TPU v7x, 256 devices: a whole 4x4x8 slice. The times are simulated.
256 devices in a mesh: row: 16 (over z_lo, x), col: 16 (over z_hi, y, core).
Axes of the slice: x: 4, y: 4, z: 8 (z_hi: 2, z_lo: 4; z = z_hi * 4 + z_lo), core: 2. Of those that a mesh axis runs over, the one named last changes fastest.
Arguments:
- feat: bfloat16 [512, 512, 256], P('row', 'col'), may hold values from -6 to 6
- noise_fine: float32 [512, 512, 256], P('row', 'col'), may hold values from -0.5 to 0.5
- noise_coarse: float32 [256, 256, 256], P('row', 'col'), may hold values from -0.5 to 0.5
- w_post: bfloat16 [2304, 256], replicated, may hold values from -0.125 to 0.125
- w_coarse: bfloat16 [2304, 256], replicated, may hold values from -0.125 to 0.125
- w_prior: bfloat16 [2304, 512], replicated, may hold values from -0.125 to 0.125
Outputs:
- grad_feat: bfloat16 [512, 512, 256], P('row', 'col')
- grad_post: float32 [589824], P(('row', 'col'))
- grad_coarse: float32 [589824], P(('row', 'col'))
- grad_prior: float32 [1179648], P(('row', 'col'))
All inputs are finite; a program needn't handle non-finite values.
Results may differ from a plain program's by a relative error of at most 0.0075.
Values may be sent and summed in bfloat16 or wider, within the bound.
No kernel may reach another device: no remote copies, remote signals or barrier semaphores. Data moves between devices by JAX's collectives and lax.ppermute only.
A program may use at most 128 MiB of HBM per device.

v0:
```python
import functools
import math

import jax
import jax.numpy as jnp
from jax import lax
from jax.experimental import pallas as pl
from jax.experimental.pallas import tpu as pltpu
from jax.sharding import PartitionSpec as P

BF = jnp.bfloat16
F32 = jnp.float32
VARIANT = ((1, -1), (0, 0), (1, 0), (0, 1))
FOLD = (3, 1, 2, 0)
VMEM_LIMIT = 60 * 1024 * 1024


def digits():
    places = []
    for d in range(256):
        row, col = d // 16, d % 16
        places.append({"zl": row // 4, "x": row % 4, "zh": col // 8, "y": (col // 2) % 4, "core": col % 2})
    return places


RADIX = {"core": 2, "x": 4, "y": 4, "zl": 4, "zh": 2}


def index_of(place):
    return (place["zl"] * 4 + place["x"]) * 16 + (place["zh"] * 4 + place["y"]) * 2 + place["core"]


def my_place():
    row, col = lax.axis_index("row"), lax.axis_index("col")
    return {"zl": row // 4, "x": row % 4, "zh": col // 8, "y": (col // 2) % 4, "core": col % 2}


def moved(place, name, step):
    return {**place, name: (place[name] + step) % RADIX[name]}


def sum_stage(part, name):
    radix = RADIX[name]
    here = my_place()[name]
    share = part.shape[0] // radix
    cut = part.reshape(radix, share, part.shape[1])
    total = lax.dynamic_index_in_dim(cut, here, 0, keepdims=False).astype(jnp.float32)
    order = (1, 3, 2) if radix == 4 else (1,)
    arrived = []
    for step in order:
        piece = lax.dynamic_index_in_dim(cut, (here + step) % radix, 0, keepdims=False)
        pairs = [(index_of(p), index_of(moved(p, name, step))) for p in digits()]
        arrived.append(lax.ppermute(piece, ("row", "col"), pairs))
    for piece in arrived:
        total = total + piece.astype(jnp.float32)
    return total.astype(jnp.bfloat16)


def reduce_scatter(part, stages):
    for name in stages:
        part = sum_stage(part, name)
    halves = part.reshape(2, part.shape[0] // 2, part.shape[1])
    last = my_place()["zh"]
    total = 0.0
    for flip in (0, 1):
        pairs = []
        for p in digits():
            chunk = 0
            for name in stages:
                chunk = chunk * RADIX[name] + p[name]
            pairs.append((index_of(p), chunk * 2 + (p["zh"] + flip) % 2))
        piece = lax.dynamic_index_in_dim(halves, (last + flip) % 2, 0, keepdims=False)
        total = total + lax.ppermute(piece, ("row", "col"), pairs).astype(jnp.float32)
    return total


def in_vmem(count):
    return [pl.BlockSpec(memory_space=pltpu.VMEM)] * count


def split_lanes(ref, value):
    for half in range(2):
        ref[:, :, half] = value[..., 128 * half:128 * (half + 1)]


def phase_of(ref, row, col):
    return jnp.concatenate([ref[:, row, half, pl.ds(col, 16, stride=2), :] for half in range(2)], axis=-1)


def line_of(ref, line, col):
    return jnp.concatenate(
        [ref[line // 2, line % 2, half, pl.ds(col, 16, stride=2), :] for half in range(2)], axis=-1)


def pack_kernel(feat_ref, fine_ref, low_ref, own_ref, top_ref, bottom_ref, left_ref, right_ref, wide, noise, side):
    split_lanes(wide, feat_ref[...].astype(F32))
    split_lanes(noise, fine_ref[...])
    for out, first, fine_first, low_first in ((top_ref, 0, 0, 0), (bottom_ref, 23, 24, 13)):
        for r in range(9):
            for col in range(2):
                out[2 * r + col] = line_of(wide, first + r, col).astype(BF)
        for r in range(8):
            for col in range(2):
                out[18 + 2 * r + col] = line_of(noise, fine_first + r, col).astype(BF)
        out[34:37] = low_ref[low_first:low_first + 3].astype(BF)
    for row in range(2):
        for col in range(2):
            own_ref[2 * row + col] = phase_of(wide, row, col).astype(BF)
    side[:, 32:40, :] = jnp.zeros((16, 8, 256), F32)
    for out, long, long_from, other_from, low_from in ((left_ref, 0, 0, 0, 0), (right_ref, 1, 11, 12, 13)):
        for row in range(2):
            at = 17 * row
            side[:, at:at + 5, :] = phase_of(wide, row, long)[:, long_from:long_from + 5]
            side[:, at + 5:at + 9, :] = phase_of(wide, row, 1 - long)[:, other_from:other_from + 4]
            for col in range(2):
                side[:, at + 9 + 4 * col:at + 13 + 4 * col, :] = (
                    phase_of(noise, row, col)[:, other_from:other_from + 4])
        side[:, 34:37, :] = low_ref[:, low_from:low_from + 3, :]
        out[...] = side[...].astype(BF)


def flat(block):
    return block.reshape(block.shape[0] * 32, block.shape[2])


def back_in_rows(block):
    return block.reshape(block.shape[0] // 32, 32, block.shape[1])


def before(block):
    return pltpu.roll(block, 1, 0)


def after(block):
    return pltpu.roll(block, block.shape[0] - 1, 0)


def dot(left, right):
    return jnp.dot(left, right, preferred_element_type=F32)


def inside(place_ref, first_row, rows):
    cell = lax.broadcasted_iota(jnp.int32, (rows * 32, 256), 0)
    line = cell // 32 + first_row + 16 * place_ref[0]
    column = cell % 32 - 8 + 16 * place_ref[1]
    return (line >= 0) & (line < 256) & (column >= 0) & (column < 256)


def three_wide(value, ref, first, rows):
    c = value.shape[1]
    for at, part in enumerate((before(value), value, after(value))):
        ref[pl.ds(first, rows), :, c * at:c * (at + 1)] = back_in_rows(part.astype(BF))


def own_cells(block):
    return block.astype(F32)[:, 8:24, :].reshape(256, block.shape[2]).astype(BF)


def turned(block):
    return own_cells(block).T


def main_kernel(scale, place_ref, own_ref, fine_ref, low_ref, up_ref, down_ref, left_ref, right_ref, ul_ref, ur_ref,
                dl_ref, dr_ref, w_post, w_coarse, fold, fold_t, w_coarse_t,
                g_post, g_coarse, g_prior, g_fine,
                field, fine, noise, low, cat, pool_cat, coarse, ctx_cat, err, d_cat, gc_cat, gf_own, turn):
    split_lanes(noise, fine_ref[...])
    for row in range(2):
        for col in range(2):
            p = 2 * row + col
            field[p, 5:21, 8:24, :] = own_ref[p].astype(F32)
            fine[p, 4:20, 8:24, :] = phase_of(noise, row, col)
    low[3:19, 8:24, :] = low_ref[...]
    for ref, first, fine_first, low_first in ((up_ref, -9, -8, 0), (down_ref, 32, 32, 19)):
        for r in range(9):
            line = first + r
            for col in range(2):
                field[2 * (line % 2) + col, line // 2 + 5, 8:24, :] = ref[2 * r + col].astype(F32)
        for r in range(8):
            line = fine_first + r
            for col in range(2):
                fine[2 * (line % 2) + col, line // 2 + 4, 8:24, :] = ref[18 + 2 * r + col].astype(F32)
        low[low_first:low_first + 3, 8:24, :] = ref[34:37].astype(F32)
    sides = (
        (left_ref, True, 0, 16, 0), (right_ref, False, 0, 16, 0),
        (ul_ref, True, -5, 5, -1), (ur_ref, False, -5, 5, -1), (dl_ref, True, 16, 5, 1), (dr_ref, False, 16, 5, 1),
    )
    for ref, on_left, first, rows, corner in sides:
        block = ref[...].astype(F32)
        fine_rows, low_rows = (slice(0, 16), slice(0, 16))
        if corner == -1:
            fine_rows, low_rows = slice(1, 5), slice(2, 5)
        if corner == 1:
            fine_rows, low_rows = slice(0, 4), slice(0, 3)
        fine_at, low_at = first + 4 + fine_rows.start, first + 3 + low_rows.start
        n_fine, n_low = fine_rows.stop - fine_rows.start, low_rows.stop - low_rows.start
        long = 1 if on_left else 0
        long_at = 3 if on_left else 24
        other_at = 4 if on_left else 24
        low_col = 5 if on_left else 24
        for row in range(2):
            at = 17 * row
            field[2 * row + long, first + 5:first + 5 + rows, long_at:long_at + 5, :] = block[:, at:at + 5, :]
            field[2 * row + 1 - long, first + 5:first + 5 + rows, other_at:other_at + 4, :] = block[:, at + 5:at + 9, :]
            for col in range(2):
                fine[2 * row + col, fine_at:fine_at + n_fine, other_at:other_at + 4, :] = (
                    block[fine_rows, at + 9 + 4 * col:at + 13 + 4 * col, :])
        low[low_at:low_at + n_low, low_col:low_col + 3, :] = block[low_rows, 34:37, :]

    @pl.loop(0, 2)
    def _(half):
        for row in range(2):
            rows = pl.ds(half * 13, 13)
            even, odd = flat(field[2 * row, rows]), flat(field[2 * row + 1, rows])
            for at, part in enumerate((before(odd), even, odd, after(even))):
                cat[row, rows, :, 256 * at:256 * (at + 1)] = back_in_rows(part.astype(BF))

    @pl.loop(0, 3)
    def _(step):
        total = jnp.zeros((256, 256), F32)
        for row in range(2):
            for col in range(2):
                p = 2 * row + col
                value = flat(fine[p, pl.ds(step * 8, 8)])
                for a in range(3):
                    phase, shift = VARIANT[row + a]
                    cells = flat(cat[phase, pl.ds(step * 8 + 1 + shift, 8), :, 256 * col:256 * col + 768])
                    value = value + dot(cells, w_post[768 * a:768 * (a + 1)])
                fine[p, pl.ds(step * 8, 8)] = back_in_rows(value)
                total = total + value
        total = jnp.where(inside(place_ref, step * 8 - 4, 8), total * 0.25, 0.0)
        three_wide(total, pool_cat, step * 8, 8)

    @pl.loop(0, 2)
    def _(step):
        value = flat(low[pl.ds(step * 11, 11)])
        for a in range(3):
            value = value + dot(flat(pool_cat[pl.ds(step * 11 + a, 11)]), w_coarse[768 * a:768 * (a + 1)])
        value = jnp.where(inside(place_ref, step * 11 - 3, 11), value, 0.0)
        coarse[pl.ds(step * 11, 11)] = back_in_rows(value)
        three_wide(value, ctx_cat, step * 11, 11)

    for row in range(2):
        @pl.loop(0, 3)
        def _(step):
            valid = inside(place_ref, step * 7 - 2 - row, 7)
            pieces = []
            for col in range(2):
                prior = jnp.zeros((224, 512), F32)
                for k in range(2):
                    cells = flat(ctx_cat[pl.ds(step * 7 + k, 7), :, 256 * col:256 * col + 512])
                    prior = prior + dot(cells, fold[2 * row + k, 512 * col:512 * col + 512])
                raw = prior[:, 256:]
                small = jnp.exp(-jnp.abs(raw))
                more = 1.0 + small
                sigma = jnp.maximum(raw, 0.0) + jnp.log(more) + 0.5
                gate = jnp.where(raw >= 0.0, 1.0, small) / more
                inverse = 1.0 / sigma
                deviation = flat(fine[2 * row + col, pl.ds(step * 7 + 2 - row, 7)]) - prior[:, :256]
                residual = deviation * inverse * inverse
                err[2 * row + col, pl.ds(step * 7, 7)] = back_in_rows(residual)
                pieces.append(jnp.where(valid, -residual, 0.0))
                pieces.append(jnp.where(valid, (inverse - residual * deviation * inverse) * gate, 0.0))
            parts = (before(pieces[2]), before(pieces[3]), pieces[0], pieces[1], pieces[2], pieces[3],
                     after(pieces[0]), after(pieces[1]))
            for at, part in enumerate(parts):
                d_cat[row, pl.ds(step * 7, 7), :, 256 * at:256 * (at + 1)] = back_in_rows(part.astype(BF))

    for i in range(3):
        for j in range(3):
            turn[3 * i + j] = turned(ctx_cat[2 + i:18 + i, :, 256 * j:256 * (j + 1)])
    for j in range(2):
        rights = []
        for row in range(2):
            for col in range(2):
                rights.append(jnp.concatenate(
                    [own_cells(d_cat[row, 2 + row:18 + row, :, 512 * (1 + col) + 256 * j:512 * (1 + col) + 256 * (j + 1)])],
                    axis=1))
        right = jnp.concatenate(rights, axis=0)
        for a in range(3):
            for b in range(3):
                lefts = [turn[3 * ((row + a + 1) // 2) + (col + b + 1) // 2] for row in range(2) for col in range(2)]
                tap = 3 * a + b
                g_prior[256 * tap:256 * (tap + 1), 256 * j:256 * (j + 1)] = (
                    dot(jnp.concatenate(lefts, axis=1), right) * scale).astype(BF)

    @pl.loop(0, 2)
    def _(step):
        value = flat(coarse[pl.ds(step * 10 + 1, 10)])
        for k in range(4):
            phase, shift = VARIANT[k]
            at = step * 10 + shift + phase
            value = value + dot(flat(d_cat[phase, pl.ds(at, 10)]), fold_t[k])
        value = jnp.where(inside(place_ref, step * 10 - 2, 10), value, 0.0)
        three_wide(value, gc_cat, step * 10, 10)

    right = own_cells(gc_cat[2:18, :, 256:512])
    for i in range(3):
        for j in range(3):
            left = turned(pool_cat[3 + i:19 + i, :, 256 * j:256 * (j + 1)])
            tap = 3 * i + j
            g_coarse[256 * tap:256 * (tap + 1), :] = (dot(left, right) * scale).astype(BF)

    @pl.loop(0, 2)
    def _(step):
        value = jnp.zeros((288, 256), F32)
        for a in range(3):
            value = value + dot(flat(gc_cat[pl.ds(step * 9 + a, 9)]), w_coarse_t[768 * a:768 * (a + 1)])
        value = value * 0.25
        valid = inside(place_ref, step * 9 - 1, 9)
        for row in range(2):
            even, odd = [
                jnp.where(valid, flat(err[2 * row + col, pl.ds(step * 9 + 1 + row, 9)]) + value, 0.0)
                for col in range(2)
            ]
            for at, part in enumerate((before(odd), even, odd, after(even))):
                compact = part.reshape(9, 32, 256)[:, 8:24, :]
                gf_own[row, pl.ds(step * 9, 9), :, 256 * at:256 * (at + 1)] = compact.astype(BF)
    g_fine[...] = gf_own[...]

    for k in range(4):
        phase, shift = VARIANT[k]
        for at in range(4):
            turn[4 * k + at] = turned(cat[phase, 5 + shift:21 + shift, :, 256 * at:256 * (at + 1)])
    right = jnp.concatenate(
        [gf_own[row, 1:17, :, 256 * (1 + col):256 * (2 + col)].reshape(256, 256) for row in range(2) for col in range(2)],
        axis=0)
    for a in range(3):
        for b in range(3):
            lefts = [turn[4 * (row + a) + col + b] for row in range(2) for col in range(2)]
            tap = 3 * a + b
            g_post[256 * tap:256 * (tap + 1), :] = (dot(jnp.concatenate(lefts, axis=1), right) * scale).astype(BF)


def feat_kernel(g_fine, w_post_t, out_ref, wide):
    for row in range(2):
        for col in range(2):
            value = jnp.zeros((256, 256), F32)
            for a in range(3):
                phase, shift = VARIANT[row + a]
                cells = g_fine[phase, 1 + shift:17 + shift, :, 256 * col:256 * col + 768].reshape(256, 768)
                value = value + dot(cells, w_post_t[768 * a:768 * (a + 1)])
            for half in range(2):
                wide[:, row, half, pl.ds(col, 16, stride=2), :] = (
                    value[:, 128 * half:128 * (half + 1)].reshape(16, 16, 128))
    for half in range(2):
        out_ref[:, :, :, 128 * half:128 * (half + 1)] = wide[:, :, half].astype(BF)


def turned_weight(weight):
    chans_in, chans_out = weight.shape[0] // 9, weight.shape[1]
    return weight.reshape(9, chans_in, chans_out)[::-1].transpose(0, 2, 1).reshape(9 * chans_out, chans_in)


def folded_weight(weight):
    taps = weight.astype(F32).reshape(3, 3, 256, 512)
    rows = jnp.stack([taps[0], taps[1] + taps[2], taps[0] + taps[1], taps[2]])
    return jnp.stack([rows[:, 0], rows[:, 1] + rows[:, 2], rows[:, 0] + rows[:, 1], rows[:, 2]], axis=1).astype(BF)


def sent(strip, down, right):
    pairs = [
        (r * 16 + c, (r + down) * 16 + c + right)
        for r in range(16) for c in range(16) if 0 <= r + down < 16 and 0 <= c + right < 16
    ]
    return lax.ppermute(strip, ("row", "col"), pairs)


def on_device(feat, noise_fine, noise_coarse, w_post, w_coarse, w_prior):
    scale = 1.0 / 512.0
    params = pltpu.CompilerParams(vmem_limit_bytes=VMEM_LIMIT)
    feat_rows = feat.reshape(16, 2, 32, 256)
    noise_rows = noise_fine.reshape(16, 2, 32, 256)
    own, top, bottom, left, right = pl.pallas_call(
        pack_kernel,
        out_shape=[
            jax.ShapeDtypeStruct((4, 16, 16, 256), BF),
            jax.ShapeDtypeStruct((37, 16, 256), BF),
            jax.ShapeDtypeStruct((37, 16, 256), BF),
            jax.ShapeDtypeStruct((16, 40, 256), BF),
            jax.ShapeDtypeStruct((16, 40, 256), BF),
        ],
        in_specs=in_vmem(3),
        out_specs=in_vmem(5),
        scratch_shapes=[
            pltpu.VMEM((16, 2, 2, 32, 128), F32),
            pltpu.VMEM((16, 2, 2, 32, 128), F32),
            pltpu.VMEM((16, 40, 256), F32),
        ],
        compiler_params=params,
        name="pack",
    )(feat_rows, noise_rows, noise_coarse)
    from_up = sent(bottom, 1, 0)
    from_down = sent(top, -1, 0)
    from_left = sent(right, 0, 1)
    from_right = sent(left, 0, -1)
    from_ul = sent(right[11:], 1, 1)
    from_ur = sent(left[11:], 1, -1)
    from_dl = sent(right[:5], -1, 1)
    from_dr = sent(left[:5], -1, -1)
    fold = folded_weight(w_prior)
    fold_t = jnp.stack([
        jnp.concatenate([fold[FOLD[k], FOLD[l]].T for l in range(4)], axis=0) for k in range(4)
    ])
    fold = fold.reshape(4, 1024, 512)
    place = jnp.stack([lax.axis_index("row"), lax.axis_index("col")]).astype(jnp.int32)
    g_post, g_coarse, g_prior, g_fine = pl.pallas_call(
        functools.partial(main_kernel, scale),
        out_shape=[
            jax.ShapeDtypeStruct((2304, 256), BF),
            jax.ShapeDtypeStruct((2304, 256), BF),
            jax.ShapeDtypeStruct((2304, 512), BF),
            jax.ShapeDtypeStruct((2, 18, 16, 1024), BF),
        ],
        in_specs=[pl.BlockSpec(memory_space=pltpu.SMEM)] + in_vmem(16),
        out_specs=in_vmem(4),
        scratch_shapes=[
            pltpu.VMEM((4, 26, 32, 256), F32),
            pltpu.VMEM((4, 24, 32, 256), F32),
            pltpu.VMEM((16, 2, 2, 32, 128), F32),
            pltpu.VMEM((22, 32, 256), F32),
            pltpu.VMEM((2, 26, 32, 1024), BF),
            pltpu.VMEM((24, 32, 768), BF),
            pltpu.VMEM((22, 32, 256), F32),
            pltpu.VMEM((22, 32, 768), BF),
            pltpu.VMEM((4, 21, 32, 256), F32),
            pltpu.VMEM((2, 21, 32, 2048), BF),
            pltpu.VMEM((20, 32, 768), BF),
            pltpu.VMEM((2, 18, 16, 1024), BF),
            pltpu.VMEM((16, 256, 256), BF),
        ],
        compiler_params=params,
        name="tile",
    )(place, own, noise_rows, noise_coarse, from_up, from_down, from_left, from_right, from_ul, from_ur,
      from_dl, from_dr, w_post, w_coarse, fold, fold_t, turned_weight(w_coarse))
    grad_feat = pl.pallas_call(
        feat_kernel,
        out_shape=jax.ShapeDtypeStruct((16, 2, 32, 256), BF),
        in_specs=in_vmem(2),
        out_specs=pl.BlockSpec(memory_space=pltpu.VMEM),
        scratch_shapes=[pltpu.VMEM((16, 2, 2, 32, 128), F32)],
        compiler_params=params,
        cost_estimate=pl.CostEstimate(flops=1200000000, bytes_accessed=3000000, transcendentals=0),
        name="feat",
    )(g_fine, turned_weight(w_post)).reshape(32, 32, 256)
    gradients = jnp.concatenate([g_prior, g_coarse, g_post], axis=1)
    summed = reduce_scatter(gradients, ("core", "x", "y", "zl"))
    return (
        grad_feat,
        summed[:, 768:].reshape(-1),
        summed[:, 512:768].reshape(-1),
        summed[:, :512].reshape(-1),
    )


def solution(mesh):
    return jax.shard_map(
        on_device,
        mesh=mesh,
        in_specs=(
            P("row", "col", None),
            P("row", "col", None),
            P("row", "col", None),
            P(),
            P(),
            P(),
        ),
        out_specs=(P("row", "col", None), P(("row", "col")), P(("row", "col")), P(("row", "col"))),
        check_vma=False,
    )
```

profile of v0, /device:TPU:6, one launch (start us, length us, event | category | flops | bytes accessed | tf_op | source)
XLA Modules:
  0.0 199.1 jit_solution(1569918838416700436)
XLA Ops:
  0.6 3.0 %pack.1 = (bf16[4,16,16,256]{3,2,1,0:T(8,128)(2,1)}, bf16[37,16,256]{2,1,0:T(8,128)(2,1)}, bf16[37,16,256]{2,1,0:T(8,128)(2,1)}, bf16[16,40,256]{2,1,0:T(8,128)(2,1)}, bf16[16,40,256]{2,1,0:T(8,128)(2,1)}) custom-call(bf16[16,2,32,256]{3,2,1,0:T(8,128)(2,1)} %bitcast.144, f32[16,2,32,256]{3,2,1,0:T(8,128)} %bitcast.139, f32[16,16,256]{2,1,0:T(8,128)} %low_ref.3), custom_call_target="tpu_custom_call" | custom-call | tf_op jit(solution)/shard_map/pack/pallas_call | solution.py:374
  3.7 3.7 %collective-permute-start = (bf16[37,16,256]{2,1,0:T(8,128)(2,1)}, bf16[37,16,256]{2,1,0:T(8,128)(2,1)}, u32[]{:S(2)}, u32[]{:S(2)}) collective-permute-start(bf16[37,16,256]{2,1,0:T(8,128)(2,1)} %get-tuple-element.14), channel_id=1, source_target_pairs={{0,16},{1,17},{2,18},{3,19},{4,20},{5,21},{6,22},{7,23},{8,24},{9,... | collective-permute-start | bytes 909320 | tf_op jit(solution)/shard_map/ppermute | solution.py:366
  7.4 2.2 %collective-permute-start.2 = (bf16[16,40,256]{2,1,0:T(8,128)(2,1)}, bf16[16,40,256]{2,1,0:T(8,128)(2,1)}, u32[]{:S(2)}, u32[]{:S(2)}) collective-permute-start(bf16[16,40,256]{2,1,0:T(8,128)(2,1)} %get-tuple-element.16), channel_id=1, source_target_pairs={{0,1},{1,2},{2,3},{3,4},{4,5},{5,6},{6,7},{7,8},{8,9},{9,10},{10,1... | collective-permute-start | bytes 983048 | tf_op jit(solution)/shard_map/ppermute | solution.py:366
  10.9 1.7 fusion.14
  12.6 5.1 %collective-permute-start.4 = (bf16[5,40,256]{2,1,0:T(8,128)(2,1)}, bf16[5,40,256]{2,1,0:T(8,128)(2,1)S(1)}, u32[]{:S(2)}, u32[]{:S(2)}) collective-permute-start(bf16[5,40,256]{2,1,0:T(8,128)(2,1)} %get-tuple-element.56), channel_id=1, source_target_pairs={{0,17},{1,18},{2,19},{3,20},{4,21},{5,22},{6,23},{7,24},{8,25},{9,... | collective-permute-start | bytes 307208 | tf_op jit(solution)/shard_map/ppermute | solution.py:366
  20.6 2.3 %fusion.11 = (f32[768,512]{1,0:T(8,128)S(1)}, f32[768,512]{1,0:T(8,128)}, f32[768,512]{1,0:T(8,128)}) fusion(bf16[2304,512]{1,0:T(8,128)(2,1)S(1)} %copy-done.2), kind=kLoop, calls=%fused_computation.55 | loop fusion | bytes 9437184 | tf_op jit(solution)/shard_map/slice | solution.py:357
  22.9 1.9 copy.13
  26.4 1.9 copy.16
  28.3 1.7 fusion.12
  35.0 2.4 %collective-permute-start.1 = (bf16[37,16,256]{2,1,0:T(8,128)(2,1)S(1)}, bf16[37,16,256]{2,1,0:T(8,128)(2,1)S(1)}, u32[]{:S(2)}, u32[]{:S(2)}) collective-permute-start(bf16[37,16,256]{2,1,0:T(8,128)(2,1)S(1)} %copy-done.12), channel_id=1, source_target_pairs={{16,0},{17,1},{18,2},{19,3},{20,4},{21,5},{22,6},{23,7},{24,8},{25... | collective-permute-start | bytes 909320 | tf_op jit(solution)/shard_map/ppermute | solution.py:366
  37.5 4.0 %collective-permute-start.6 = (bf16[5,40,256]{2,1,0:T(8,128)(2,1)S(1)}, bf16[5,40,256]{2,1,0:T(8,128)(2,1)S(1)}, u32[]{:S(2)}, u32[]{:S(2)}) collective-permute-start(bf16[5,40,256]{2,1,0:T(8,128)(2,1)S(1)} %copy-done.11), channel_id=1, source_target_pairs={{16,1},{17,2},{18,3},{19,4},{20,5},{21,6},{22,7},{23,8},{24,9},{25... | collective-permute-start | bytes 307208 | tf_op jit(solution)/shard_map/ppermute | solution.py:366
  41.5 2.3 %pad_maximum_fusion.2.fold_t = bf16[4,2048,256]{2,1,0:T(8,128)(2,1)} fusion(bf16[1,2048,256]{2,1,0:T(8,128)(2,1)S(1)} %get-tuple-element.67, bf16[1,2048,256]{2,1,0:T(8,128)(2,1)S(1)} %get-tuple-element.66, bf16[1,2048,256]{2,1,0:T(8,128)(2,1)S(1)} %get-tuple-element.65, bf16[1,2048,256]{2,1,0:T(8,128)(2,1)S(1)} %get-tuple-element.64), kind=kLoop, calls=%fused_computation.5 | loop fusion | flops 6291456 | bytes 8388608 | tf_op jit(solution)/shard_map/stack | solution.py:402
  43.8 7.4 %copy.18 = bf16[4,4,256,512]{3,2,1,0:T(8,128)(2,1)} copy(bf16[4,4,256,512]{2,3,1,0:T(8,128)(2,1)} %copy-done) | data formatting | bytes 8388608 | tf_op jit(solution)/shard_map/convert_element_type | solution.py:358
  55.1 8.1 %collective-permute-done.7.dr_ref = bf16[5,40,256]{2,1,0:T(8,128)(2,1)S(1)} collective-permute-done((bf16[5,40,256]{2,1,0:T(8,128)(2,1)S(1)}, bf16[5,40,256]{2,1,0:T(8,128)(2,1)S(1)}, u32[]{:S(2)}, u32[]{:S(2)}) %collective-permute-start.7) | collective-permute-done | bytes 102432 | tf_op jit(solution)/shard_map/ppermute | solution.py:366
  64.0 28.7 %tile.1 = (bf16[2304,256]{1,0:T(8,128)(2,1)}, bf16[2304,256]{1,0:T(8,128)(2,1)}, bf16[2304,512]{1,0:T(8,128)(2,1)}, bf16[2,18,16,1024]{3,2,1,0:T(8,128)(2,1)}) custom-call(s32[2]{0:T(128)} %pad_add_fusion.place_ref, bf16[4,16,16,256]{3,2,1,0:T(8,128)(2,1)} %get-tuple-element.13.own_ref, f32[16,2,32,256]{3,2,1,0:T(8,128)} %bitcast.140, ...), custom_call_target="tpu_custom_call" | custom-call | tf_op jit(solution)/shard_map/tile/pallas_call | solution.py:407
  92.8 2.7 %pad_maximum_fusion.1 = bf16[2304,1024]{1,0:T(8,128)(2,1)S(1)} fusion(bf16[2304,256]{1,0:T(8,128)(2,1)} %get-tuple-element.21, bf16[2304,256]{1,0:T(8,128)(2,1)} %get-tuple-element.20, bf16[2304,512]{1,0:T(8,128)(2,1)} %get-tuple-element.19), kind=kLoop, calls=%fused_computation.2 | loop fusion | flops 14155776 | bytes 9437184 | tf_op jit(solution)/shard_map/concatenate | solution.py:446
  95.7 1.9 copy-done.1
  97.6 1.9 collective-permute-start.8
  99.5 4.3 %collective-permute-done.8 = bf16[1152,1024]{1,0:T(8,128)(2,1)} collective-permute-done((bf16[1152,1024]{1,0:T(8,128)(2,1)S(1)}, bf16[1152,1024]{1,0:T(8,128)(2,1)}, u32[]{:S(2)}, u32[]{:S(2)}) %collective-permute-start.8) | collective-permute-done | bytes 2359328 | tf_op jit(solution)/shard_map/ppermute | solution.py:53
  103.8 3.5 %fusion = bf16[1152,1024]{1,0:T(8,128)(2,1)S(1)} fusion(bf16[1152,1024]{1,0:T(8,128)(2,1)} %collective-permute-done.8, bf16[2,1152,1024]{2,1,0:T(8,128)(2,1)} %bitcast.129, s32[]{:T(128)S(6)} %select_n.127), kind=kLoop, calls=%fused_computation.4 | loop fusion | flops 4718592 | bytes 7077892 | tf_op jit(solution)/shard_map/convert_element_type | solution.py:56
  108.6 3.2 %collective-permute-start.9 = (bf16[288,1024]{1,0:T(8,128)(2,1)}, bf16[288,1024]{1,0:T(8,128)(2,1)}, u32[]{:S(2)}, u32[]{:S(2)}) collective-permute-start(bf16[288,1024]{1,0:T(8,128)(2,1)} %get-tuple-element.42), channel_id=1, source_target_pairs={{0,16},{1,17},{2,18},{3,19},{4,20},{5,21},{6,22},{7,23},{8,24},{9,... | collective-permute-start | bytes 1769480 | tf_op jit(solution)/shard_map/ppermute | solution.py:53
  111.8 14.8 %collective-permute-done.11 = bf16[288,1024]{1,0:T(8,128)(2,1)} collective-permute-done((bf16[288,1024]{1,0:T(8,128)(2,1)}, bf16[288,1024]{1,0:T(8,128)(2,1)}, u32[]{:S(2)}, u32[]{:S(2)}) %collective-permute-start.11) | collective-permute-done | bytes 589856 | tf_op jit(solution)/shard_map/ppermute | solution.py:53
  126.6 11.8 %collective-permute-done.10 = bf16[288,1024]{1,0:T(8,128)(2,1)} collective-permute-done((bf16[288,1024]{1,0:T(8,128)(2,1)}, bf16[288,1024]{1,0:T(8,128)(2,1)}, u32[]{:S(2)}, u32[]{:S(2)}) %collective-permute-start.10) | collective-permute-done | bytes 589856 | tf_op jit(solution)/shard_map/ppermute | solution.py:53
  138.4 1.8 fusion.3
  141.1 10.2 %collective-permute-start.14 = (bf16[72,1024]{1,0:T(8,128)(2,1)S(1)}, bf16[72,1024]{1,0:T(8,128)(2,1)S(1)}, u32[]{:S(2)}, u32[]{:S(2)}) collective-permute-start(bf16[72,1024]{1,0:T(8,128)(2,1)S(1)} %get-tuple-element.51), channel_id=1, source_target_pairs={{0,4},{1,5},{2,6},{3,7},{4,0},{5,1},{6,2},{7,3},{8,12},{9,13},{10,... | collective-permute-start | bytes 442376 | tf_op jit(solution)/shard_map/ppermute | solution.py:53
  151.3 13.7 %collective-permute-start.13 = (bf16[72,1024]{1,0:T(8,128)(2,1)S(1)}, bf16[72,1024]{1,0:T(8,128)(2,1)S(1)}, u32[]{:S(2)}, u32[]{:S(2)}) collective-permute-start(bf16[72,1024]{1,0:T(8,128)(2,1)S(1)} %get-tuple-element.52), channel_id=1, source_target_pairs={{0,6},{1,7},{2,0},{3,1},{4,2},{5,3},{6,4},{7,5},{8,14},{9,15},{10,... | collective-permute-start | bytes 442376 | tf_op jit(solution)/shard_map/ppermute | solution.py:53
  165.7 7.0 %collective-permute-done.13 = bf16[72,1024]{1,0:T(8,128)(2,1)S(1)} collective-permute-done((bf16[72,1024]{1,0:T(8,128)(2,1)S(1)}, bf16[72,1024]{1,0:T(8,128)(2,1)S(1)}, u32[]{:S(2)}, u32[]{:S(2)}) %collective-permute-start.13) | collective-permute-done | bytes 147488 | tf_op jit(solution)/shard_map/ppermute | solution.py:53
  173.8 3.5 %collective-permute-start.17 = (bf16[18,1024]{1,0:T(8,128)(2,1)S(1)}, bf16[18,1024]{1,0:T(8,128)(2,1)S(1)}, u32[]{:S(2)}, u32[]{:S(2)}) collective-permute-start(bf16[18,1024]{1,0:T(8,128)(2,1)S(1)} %get-tuple-element.58), channel_id=1, source_target_pairs={{0,128},{1,129},{2,130},{3,131},{4,132},{5,133},{6,134},{7,135},{8... | collective-permute-start | bytes 110600 | tf_op jit(solution)/shard_map/ppermute | solution.py:53
  182.0 2.2 %collective-permute-done.15 = bf16[18,1024]{1,0:T(8,128)(2,1)S(1)} collective-permute-done((bf16[18,1024]{1,0:T(8,128)(2,1)S(1)}, bf16[18,1024]{1,0:T(8,128)(2,1)S(1)}, u32[]{:S(2)}, u32[]{:S(2)}) %collective-permute-start.15) | collective-permute-done | bytes 36896 | tf_op jit(solution)/shard_map/ppermute | solution.py:53
  184.3 1.9 collective-permute-start.18
  186.2 3.9 %feat.1 = bf16[16,2,32,256]{3,2,1,0:T(8,128)(2,1)} custom-call(bf16[2,18,16,1024]{3,2,1,0:T(8,128)(2,1)} %get-tuple-element.18.g_fine, bf16[2304,256]{1,0:T(8,128)(2,1)} %bitcast.143), custom_call_target="tpu_custom_call" | custom-call | flops 1200000000 | bytes 3000000 | tf_op jit(solution)/shard_map/feat/pallas_call | solution.py:436
  190.1 7.1 %collective-permute-done.19 = bf16[9,1024]{1,0:T(8,128)(2,1)S(1)} collective-permute-done((bf16[9,1024]{1,0:T(8,128)(2,1)S(1)}, bf16[9,1024]{1,0:T(8,128)(2,1)S(1)}, u32[]{:S(2)}, u32[]{:S(2)}) %collective-permute-start.19) | collective-permute-done | bytes 18464 | tf_op jit(solution)/shard_map/ppermute | solution.py:73
  (75 shorter events, 26.2 us)
Async XLA Ops:
  0.6 19.9 %copy-start.2 = (bf16[2304,512]{1,0:T(8,128)(2,1)S(1)}, bf16[2304,512]{1,0:T(8,128)(2,1)}, u32[]{:S(2)}) copy-start(bf16[2304,512]{1,0:T(8,128)(2,1)} %param.11) | copy-start | bytes 7077892
  3.7 59.6 %collective-permute-start = (bf16[37,16,256]{2,1,0:T(8,128)(2,1)}, bf16[37,16,256]{2,1,0:T(8,128)(2,1)}, u32[]{:S(2)}, u32[]{:S(2)}) collective-permute-start(bf16[37,16,256]{2,1,0:T(8,128)(2,1)} %get-tuple-element.14), channel_id=1, source_target_pairs={{0,16},{1,17},{2,18},{3,19},{4,20},{5,21},{6,22},{7,23},{8,24},{9,... | collective-permute-start | bytes 909320 | tf_op jit(solution)/shard_map/ppermute | solution.py:366
  7.4 55.9 %collective-permute-start.2 = (bf16[16,40,256]{2,1,0:T(8,128)(2,1)}, bf16[16,40,256]{2,1,0:T(8,128)(2,1)}, u32[]{:S(2)}, u32[]{:S(2)}) collective-permute-start(bf16[16,40,256]{2,1,0:T(8,128)(2,1)} %get-tuple-element.16), channel_id=1, source_target_pairs={{0,1},{1,2},{2,3},{3,4},{4,5},{5,6},{6,7},{7,8},{8,9},{9,10},{10,1... | collective-permute-start | bytes 983048 | tf_op jit(solution)/shard_map/ppermute | solution.py:366
  9.6 53.7 %collective-permute-start.3 = (bf16[16,40,256]{2,1,0:T(8,128)(2,1)}, bf16[16,40,256]{2,1,0:T(8,128)(2,1)}, u32[]{:S(2)}, u32[]{:S(2)}) collective-permute-start(bf16[16,40,256]{2,1,0:T(8,128)(2,1)} %get-tuple-element.17), channel_id=1, source_target_pairs={{1,0},{2,1},{3,2},{4,3},{5,4},{6,5},{7,6},{8,7},{9,8},{10,9},{11,1... | collective-permute-start | bytes 983048 | tf_op jit(solution)/shard_map/ppermute | solution.py:366
  12.6 21.6 %collective-permute-start.4 = (bf16[5,40,256]{2,1,0:T(8,128)(2,1)}, bf16[5,40,256]{2,1,0:T(8,128)(2,1)S(1)}, u32[]{:S(2)}, u32[]{:S(2)}) collective-permute-start(bf16[5,40,256]{2,1,0:T(8,128)(2,1)} %get-tuple-element.56), channel_id=1, source_target_pairs={{0,17},{1,18},{2,19},{3,20},{4,21},{5,22},{6,23},{7,24},{8,25},{9,... | collective-permute-start | bytes 307208 | tf_op jit(solution)/shard_map/ppermute | solution.py:366
  19.3 18.2 %collective-permute-start.5 = (bf16[5,40,256]{2,1,0:T(8,128)(2,1)}, bf16[5,40,256]{2,1,0:T(8,128)(2,1)}, u32[]{:S(2)}, u32[]{:S(2)}) collective-permute-start(bf16[5,40,256]{2,1,0:T(8,128)(2,1)} %get-tuple-element.54), channel_id=1, source_target_pairs={{1,16},{2,17},{3,18},{4,19},{5,20},{6,21},{7,22},{8,23},{9,24},{10... | collective-permute-start | bytes 307208 | tf_op jit(solution)/shard_map/ppermute | solution.py:366
  31.9 2.0 %copy-start = (bf16[4,4,256,512]{2,3,1,0:T(8,128)(2,1)}, bf16[4,4,256,512]{2,3,1,0:T(8,128)(2,1)S(1)}, u32[]{:S(2)}) copy-start(bf16[4,4,256,512]{2,3,1,0:T(8,128)(2,1)S(1)} %maximum_convert_fusion) | copy-start | bytes 12582916
  34.0 1.0 copy-start.12
  34.1 3.4 %copy-start.11 = (bf16[5,40,256]{2,1,0:T(8,128)(2,1)S(1)}, bf16[5,40,256]{2,1,0:T(8,128)(2,1)}, u32[]{:S(2)}) copy-start(bf16[5,40,256]{2,1,0:T(8,128)(2,1)} %get-tuple-element.55) | copy-start | bytes 307204
  34.2 9.6 %copy-start.7 = (bf16[5,40,256]{2,1,0:T(8,128)(2,1)}, bf16[5,40,256]{2,1,0:T(8,128)(2,1)S(1)}, u32[]{:S(2)}) copy-start(bf16[5,40,256]{2,1,0:T(8,128)(2,1)S(1)} %collective-permute-done.4.ul_ref) | copy-start | bytes 307204
  35.0 28.3 %collective-permute-start.1 = (bf16[37,16,256]{2,1,0:T(8,128)(2,1)S(1)}, bf16[37,16,256]{2,1,0:T(8,128)(2,1)S(1)}, u32[]{:S(2)}, u32[]{:S(2)}) collective-permute-start(bf16[37,16,256]{2,1,0:T(8,128)(2,1)S(1)} %copy-done.12), channel_id=1, source_target_pairs={{16,0},{17,1},{18,2},{19,3},{20,4},{21,5},{22,6},{23,7},{24,8},{25... | collective-permute-start | bytes 909320 | tf_op jit(solution)/shard_map/ppermute | solution.py:366
  37.5 15.6 %collective-permute-start.6 = (bf16[5,40,256]{2,1,0:T(8,128)(2,1)S(1)}, bf16[5,40,256]{2,1,0:T(8,128)(2,1)S(1)}, u32[]{:S(2)}, u32[]{:S(2)}) collective-permute-start(bf16[5,40,256]{2,1,0:T(8,128)(2,1)S(1)} %copy-done.11), channel_id=1, source_target_pairs={{16,1},{17,2},{18,3},{19,4},{20,5},{21,6},{22,7},{23,8},{24,9},{25... | collective-permute-start | bytes 307208 | tf_op jit(solution)/shard_map/ppermute | solution.py:366
  43.8 7.4 %copy-start.3 = (bf16[2304,256]{1,0:T(8,128)(2,1)S(1)}, bf16[2304,256]{1,0:T(8,128)(2,1)}, u32[]{:S(2)}) copy-start(bf16[2304,256]{1,0:T(8,128)(2,1)} %w_coarse.1) | copy-start | bytes 3538948
  51.2 1.9 copy-start.10
  53.1 10.2 %copy-start.8 = (bf16[5,40,256]{2,1,0:T(8,128)(2,1)}, bf16[5,40,256]{2,1,0:T(8,128)(2,1)S(1)}, u32[]{:S(2)}) copy-start(bf16[5,40,256]{2,1,0:T(8,128)(2,1)S(1)} %collective-permute-done.6.dl_ref) | copy-start | bytes 307204
  53.1 10.2 %collective-permute-start.7 = (bf16[5,40,256]{2,1,0:T(8,128)(2,1)S(1)}, bf16[5,40,256]{2,1,0:T(8,128)(2,1)S(1)}, u32[]{:S(2)}, u32[]{:S(2)}) collective-permute-start(bf16[5,40,256]{2,1,0:T(8,128)(2,1)S(1)} %copy-done.10), channel_id=1, source_target_pairs={{17,0},{18,1},{19,2},{20,3},{21,4},{22,5},{23,6},{24,7},{25,8},{26... | collective-permute-start | bytes 307208 | tf_op jit(solution)/shard_map/ppermute | solution.py:366
  63.3 0.8 copy-start.6
  95.5 2.2 %copy-start.1 = (bf16[2304,1024]{1,0:T(8,128)(2,1)}, bf16[2304,1024]{1,0:T(8,128)(2,1)S(1)}, u32[]{:S(2)}) copy-start(bf16[2304,1024]{1,0:T(8,128)(2,1)S(1)} %pad_maximum_fusion.1) | copy-start | bytes 14155780
  97.6 6.2 %collective-permute-start.8 = (bf16[1152,1024]{1,0:T(8,128)(2,1)S(1)}, bf16[1152,1024]{1,0:T(8,128)(2,1)}, u32[]{:S(2)}, u32[]{:S(2)}) collective-permute-start(bf16[1152,1024]{1,0:T(8,128)(2,1)S(1)} %dynamic-slice_bitcast_fusion), channel_id=1, source_target_pairs={{0,1},{1,0},{2,3},{3,2},{4,5},{5,4},{6,7},{7,6},{8,9},{9,8},{10,11... | collective-permute-start | bytes 7077896 | tf_op jit(solution)/shard_map/ppermute | solution.py:53
  108.6 18.0 %collective-permute-start.11 = (bf16[288,1024]{1,0:T(8,128)(2,1)}, bf16[288,1024]{1,0:T(8,128)(2,1)}, u32[]{:S(2)}, u32[]{:S(2)}) collective-permute-start(bf16[288,1024]{1,0:T(8,128)(2,1)} %get-tuple-element.43), channel_id=1, source_target_pairs={{0,32},{1,33},{2,34},{3,35},{4,36},{5,37},{6,38},{7,39},{8,40},{9,... | collective-permute-start | bytes 1769480 | tf_op jit(solution)/shard_map/ppermute | solution.py:53
  108.6 29.8 %collective-permute-start.10 = (bf16[288,1024]{1,0:T(8,128)(2,1)}, bf16[288,1024]{1,0:T(8,128)(2,1)}, u32[]{:S(2)}, u32[]{:S(2)}) collective-permute-start(bf16[288,1024]{1,0:T(8,128)(2,1)} %get-tuple-element.44), channel_id=1, source_target_pairs={{0,48},{1,49},{2,50},{3,51},{4,52},{5,53},{6,54},{7,55},{8,56},{9,... | collective-permute-start | bytes 1769480 | tf_op jit(solution)/shard_map/ppermute | solution.py:53
  108.6 29.8 %collective-permute-start.9 = (bf16[288,1024]{1,0:T(8,128)(2,1)}, bf16[288,1024]{1,0:T(8,128)(2,1)}, u32[]{:S(2)}, u32[]{:S(2)}) collective-permute-start(bf16[288,1024]{1,0:T(8,128)(2,1)} %get-tuple-element.42), channel_id=1, source_target_pairs={{0,16},{1,17},{2,18},{3,19},{4,20},{5,21},{6,22},{7,23},{8,24},{9,... | collective-permute-start | bytes 1769480 | tf_op jit(solution)/shard_map/ppermute | solution.py:53
  111.8 67.5 %copy-start.4 = (bf16[2304,256]{1,0:T(8,128)(2,1)S(1)}, bf16[2304,256]{1,0:T(8,128)(2,1)}, u32[]{:S(2)}) copy-start(bf16[2304,256]{1,0:T(8,128)(2,1)} %w_post.1) | copy-start | bytes 3538948
  140.2 0.8 copy-start.5
  141.1 24.7 %collective-permute-start.14 = (bf16[72,1024]{1,0:T(8,128)(2,1)S(1)}, bf16[72,1024]{1,0:T(8,128)(2,1)S(1)}, u32[]{:S(2)}, u32[]{:S(2)}) collective-permute-start(bf16[72,1024]{1,0:T(8,128)(2,1)S(1)} %get-tuple-element.51), channel_id=1, source_target_pairs={{0,4},{1,5},{2,6},{3,7},{4,0},{5,1},{6,2},{7,3},{8,12},{9,13},{10,... | collective-permute-start | bytes 442376 | tf_op jit(solution)/shard_map/ppermute | solution.py:53
  151.3 21.5 %collective-permute-start.13 = (bf16[72,1024]{1,0:T(8,128)(2,1)S(1)}, bf16[72,1024]{1,0:T(8,128)(2,1)S(1)}, u32[]{:S(2)}, u32[]{:S(2)}) collective-permute-start(bf16[72,1024]{1,0:T(8,128)(2,1)S(1)} %get-tuple-element.52), channel_id=1, source_target_pairs={{0,6},{1,7},{2,0},{3,1},{4,2},{5,3},{6,4},{7,5},{8,14},{9,15},{10,... | collective-permute-start | bytes 442376 | tf_op jit(solution)/shard_map/ppermute | solution.py:53
  165.0 7.8 %collective-permute-start.12 = (bf16[72,1024]{1,0:T(8,128)(2,1)S(1)}, bf16[72,1024]{1,0:T(8,128)(2,1)S(1)}, u32[]{:S(2)}, u32[]{:S(2)}) collective-permute-start(bf16[72,1024]{1,0:T(8,128)(2,1)S(1)} %get-tuple-element.50), channel_id=1, source_target_pairs={{0,2},{1,3},{2,4},{3,5},{4,6},{5,7},{6,0},{7,1},{8,10},{9,11},{10,... | collective-permute-start | bytes 442376 | tf_op jit(solution)/shard_map/ppermute | solution.py:53
  173.8 7.4 %collective-permute-start.17 = (bf16[18,1024]{1,0:T(8,128)(2,1)S(1)}, bf16[18,1024]{1,0:T(8,128)(2,1)S(1)}, u32[]{:S(2)}, u32[]{:S(2)}) collective-permute-start(bf16[18,1024]{1,0:T(8,128)(2,1)S(1)} %get-tuple-element.58), channel_id=1, source_target_pairs={{0,128},{1,129},{2,130},{3,131},{4,132},{5,133},{6,134},{7,135},{8... | collective-permute-start | bytes 110600 | tf_op jit(solution)/shard_map/ppermute | solution.py:53
  177.3 4.6 %collective-permute-start.16 = (bf16[18,1024]{1,0:T(8,128)(2,1)S(1)}, bf16[18,1024]{1,0:T(8,128)(2,1)S(1)}, u32[]{:S(2)}, u32[]{:S(2)}) collective-permute-start(bf16[18,1024]{1,0:T(8,128)(2,1)S(1)} %get-tuple-element.59), channel_id=1, source_target_pairs={{0,192},{1,193},{2,194},{3,195},{4,196},{5,197},{6,198},{7,199},{8... | collective-permute-start | bytes 110600 | tf_op jit(solution)/shard_map/ppermute | solution.py:53
  178.2 5.9 %collective-permute-start.15 = (bf16[18,1024]{1,0:T(8,128)(2,1)S(1)}, bf16[18,1024]{1,0:T(8,128)(2,1)S(1)}, u32[]{:S(2)}, u32[]{:S(2)}) collective-permute-start(bf16[18,1024]{1,0:T(8,128)(2,1)S(1)} %get-tuple-element.57), channel_id=1, source_target_pairs={{0,64},{1,65},{2,66},{3,67},{4,68},{5,69},{6,70},{7,71},{8,72},{9,... | collective-permute-start | bytes 110600 | tf_op jit(solution)/shard_map/ppermute | solution.py:53
  184.2 13.0 %collective-permute-start.19 = (bf16[9,1024]{1,0:T(8,128)(2,1)S(1)}, bf16[9,1024]{1,0:T(8,128)(2,1)S(1)}, u32[]{:S(2)}, u32[]{:S(2)}) collective-permute-start(bf16[9,1024]{1,0:T(8,128)(2,1)S(1)} %get-tuple-element.63), channel_id=1, source_target_pairs={{0,1},{1,129},{2,9},{3,137},{4,17},{5,145},{6,25},{7,153},{8,0},{9... | collective-permute-start | bytes 55304 | tf_op jit(solution)/shard_map/ppermute | solution.py:73
  184.3 12.9 %collective-permute-start.18 = (bf16[9,1024]{1,0:T(8,128)(2,1)S(1)}, bf16[9,1024]{1,0:T(8,128)(2,1)S(1)}, u32[]{:S(2)}, u32[]{:S(2)}) collective-permute-start(bf16[9,1024]{1,0:T(8,128)(2,1)S(1)} %get-tuple-element.62), channel_id=1, source_target_pairs={{0,0},{1,128},{2,8},{3,136},{4,16},{5,144},{6,24},{7,152},{8,1},{9... | collective-permute-start | bytes 55304 | tf_op jit(solution)/shard_map/ppermute | solution.py:73
  (1 other events, 0.6 us)
where the time goes:
time: 201 us; the launch traced here: 199 us
  starting transfers between devices  58.9 us (29%)
  waiting for transfers between devices  56 us (28%)
  Pallas kernels  35.6 us (18%)
  local copies, waits for them, and re-layouts  31.8 us (16%)
  other arithmetic  15.8 us (8%)
    ppermute x10, waiting for transfers between devices, sum_stage(): arrived.append(lax.ppermute(piece, ('row', 'col'), pairs))  40.7 us
    ppermute x10, starting transfers between devices, sum_stage(): arrived.append(lax.ppermute(piece, ('row', 'col'), pairs))  35.4 us
    pallas_call x1, Pallas kernels, on_device(): pl.pallas_call(functools.partial(main_kernel, scale), out_shape=[jax.Shap...  28.7 us
    ppermute x8, starting transfers between devices, sent(): return lax.ppermute(strip, ('row', 'col'), pairs)  21.4 us
    ppermute x8, waiting for transfers between devices, sent(): return lax.ppermute(strip, ('row', 'col'), pairs)  8.14 us
    convert_element_type x1, local copies, waits for them, and re-layouts, folded_weight(): jnp.stack([rows[:, 0], rows[:, 1] + rows[:, 2], rows[:, 0] + rows[:, 1],...  7.37 us
    ppermute x2, waiting for transfers between devices, reduce_scatter(): lax.ppermute(piece, ('row', 'col'), pairs).astype(jnp.float32)  7.12 us
    convert_element_type x4, other arithmetic, sum_stage(): return total.astype(jnp.bfloat16)  6.34 us
  transfers between devices with their start and end apart: 20, of which 8 were waited for; matrix products, arithmetic and copies ran while one was open for 15% of the time, Pallas kernels for 2%

commit v1 on v0

--- a/solution.py
+++ b/solution.py
@@ -39,38 +39,37 @@
     return {**place, name: (place[name] + step) % RADIX[name]}
 
 
-def sum_stage(part, name):
+def sum_stage(part, name, dim):
     radix = RADIX[name]
     here = my_place()[name]
-    share = part.shape[0] // radix
-    cut = part.reshape(radix, share, part.shape[1])
-    total = lax.dynamic_index_in_dim(cut, here, 0, keepdims=False).astype(jnp.float32)
-    order = (1, 3, 2) if radix == 4 else (1,)
     arrived = []
-    for step in order:
-        piece = lax.dynamic_index_in_dim(cut, (here + step) % radix, 0, keepdims=False)
+    for step in (1, 3, 2) if radix == 4 else (1,):
+        piece = lax.dynamic_index_in_dim(part, (here + step) % radix, dim, keepdims=False)
         pairs = [(index_of(p), index_of(moved(p, name, step))) for p in digits()]
         arrived.append(lax.ppermute(piece, ("row", "col"), pairs))
+    total = lax.dynamic_index_in_dim(part, here, dim, keepdims=False).astype(F32)
     for piece in arrived:
-        total = total + piece.astype(jnp.float32)
-    return total.astype(jnp.bfloat16)
-
-
-def reduce_scatter(part, stages):
-    for name in stages:
-        part = sum_stage(part, name)
-    halves = part.reshape(2, part.shape[0] // 2, part.shape[1])
+        total = total + piece.astype(F32)
+    return total.astype(BF)
+
+
+def reduce_scatter(parts):
+    parts = sum_stage(parts.reshape(2, 2, 1152, 512), "core", 1)
+    first = parts[0].reshape(4, 4, 72, 512)
+    second = parts[1].reshape(4, 4, 72, 512)
+    first, second = sum_stage(first, "x", 0), sum_stage(second, "y", 1)
+    first, second = sum_stage(first, "y", 0), sum_stage(second, "x", 0)
+    parts = sum_stage(jnp.stack([first, second]).reshape(2, 4, 18, 512), "zl", 1)
+    halves = parts.reshape(2, 2, 9, 512)
     last = my_place()["zh"]
     total = 0.0
     for flip in (0, 1):
         pairs = []
         for p in digits():
-            chunk = 0
-            for name in stages:
-                chunk = chunk * RADIX[name] + p[name]
-            pairs.append((index_of(p), chunk * 2 + (p["zh"] + flip) % 2))
-        piece = lax.dynamic_index_in_dim(halves, (last + flip) % 2, 0, keepdims=False)
-        total = total + lax.ppermute(piece, ("row", "col"), pairs).astype(jnp.float32)
+            chunk = (((p["core"] * 4 + p["x"]) * 4 + p["y"]) * 4 + p["zl"]) * 2 + (p["zh"] + flip) % 2
+            pairs.append((index_of(p), chunk))
+        piece = lax.dynamic_index_in_dim(halves, (last + flip) % 2, 1, keepdims=False)
+        total = total + lax.ppermute(piece, ("row", "col"), pairs).astype(F32)
     return total
 
 
@@ -92,7 +91,8 @@
         [ref[line // 2, line % 2, half, pl.ds(col, 16, stride=2), :] for half in range(2)], axis=-1)
 
 
-def pack_kernel(feat_ref, fine_ref, low_ref, own_ref, top_ref, bottom_ref, left_ref, right_ref, wide, noise, side):
+def pack_kernel(feat_ref, fine_ref, low_ref, own_ref, top_ref, bottom_ref, left_ref, right_ref, lu_ref, ld_ref, ru_ref, rd_ref,
+                wide, noise, side):
     split_lanes(wide, feat_ref[...].astype(F32))
     split_lanes(noise, fine_ref[...])
     for out, first, fine_first, low_first in ((top_ref, 0, 0, 0), (bottom_ref, 23, 24, 13)):
@@ -107,7 +107,8 @@
         for col in range(2):
             own_ref[2 * row + col] = phase_of(wide, row, col).astype(BF)
     side[:, 32:40, :] = jnp.zeros((16, 8, 256), F32)
-    for out, long, long_from, other_from, low_from in ((left_ref, 0, 0, 0, 0), (right_ref, 1, 11, 12, 13)):
+    for out, up, down, long, long_from, other_from, low_from in (
+            (left_ref, lu_ref, ld_ref, 0, 0, 0, 0), (right_ref, ru_ref, rd_ref, 1, 11, 12, 13)):
         for row in range(2):
             at = 17 * row
             side[:, at:at + 5, :] = phase_of(wide, row, long)[:, long_from:long_from + 5]
@@ -117,6 +118,8 @@
                     phase_of(noise, row, col)[:, other_from:other_from + 4])
         side[:, 34:37, :] = low_ref[:, low_from:low_from + 3, :]
         out[...] = side[...].astype(BF)
+        up[...] = side[0:5].astype(BF)
+        down[...] = side[11:16].astype(BF)
 
 
 def flat(block):
@@ -162,7 +165,7 @@
 
 def main_kernel(scale, place_ref, own_ref, fine_ref, low_ref, up_ref, down_ref, left_ref, right_ref, ul_ref, ur_ref,
                 dl_ref, dr_ref, w_post, w_coarse, fold, fold_t, w_coarse_t,
-                g_post, g_coarse, g_prior, g_fine,
+                grads, g_fine,
                 field, fine, noise, low, cat, pool_cat, coarse, ctx_cat, err, d_cat, gc_cat, gf_own, turn):
     split_lanes(noise, fine_ref[...])
     for row in range(2):
@@ -281,7 +284,7 @@
             for b in range(3):
                 lefts = [turn[3 * ((row + a + 1) // 2) + (col + b + 1) // 2] for row in range(2) for col in range(2)]
                 tap = 3 * a + b
-                g_prior[256 * tap:256 * (tap + 1), 256 * j:256 * (j + 1)] = (
+                grads[0, 256 * tap:256 * (tap + 1), 256 * j:256 * (j + 1)] = (
                     dot(jnp.concatenate(lefts, axis=1), right) * scale).astype(BF)
 
     @pl.loop(0, 2)
@@ -299,7 +302,7 @@
         for j in range(3):
             left = turned(pool_cat[3 + i:19 + i, :, 256 * j:256 * (j + 1)])
             tap = 3 * i + j
-            g_coarse[256 * tap:256 * (tap + 1), :] = (dot(left, right) * scale).astype(BF)
+            grads[1, 256 * tap:256 * (tap + 1), 0:256] = (dot(left, right) * scale).astype(BF)
 
     @pl.loop(0, 2)
     def _(step):
@@ -329,7 +332,7 @@
         for b in range(3):
             lefts = [turn[4 * (row + a) + col + b] for row in range(2) for col in range(2)]
             tap = 3 * a + b
-            g_post[256 * tap:256 * (tap + 1), :] = (dot(jnp.concatenate(lefts, axis=1), right) * scale).astype(BF)
+            grads[1, 256 * tap:256 * (tap + 1), 256:512] = (dot(jnp.concatenate(lefts, axis=1), right) * scale).astype(BF)
 
 
 def feat_kernel(g_fine, w_post_t, out_ref, wide):
@@ -347,15 +350,23 @@
         out_ref[:, :, :, 128 * half:128 * (half + 1)] = wide[:, :, half].astype(BF)
 
 
-def turned_weight(weight):
-    chans_in, chans_out = weight.shape[0] // 9, weight.shape[1]
-    return weight.reshape(9, chans_in, chans_out)[::-1].transpose(0, 2, 1).reshape(9 * chans_out, chans_in)
-
-
-def folded_weight(weight):
-    taps = weight.astype(F32).reshape(3, 3, 256, 512)
-    rows = jnp.stack([taps[0], taps[1] + taps[2], taps[0] + taps[1], taps[2]])
-    return jnp.stack([rows[:, 0], rows[:, 1] + rows[:, 2], rows[:, 0] + rows[:, 1], rows[:, 2]], axis=1).astype(BF)
+TAPS_OF = ((0,), (1, 2), (0, 1), (2,))
+
+
+def weight_kernel(w_post, w_coarse, w_prior, fold, fold_t, w_post_t, w_coarse_t):
+    for i in range(4):
+        for j in range(4):
+            taps = [3 * a + b for a in TAPS_OF[i] for b in TAPS_OF[j]]
+            total = w_prior[256 * taps[0]:256 * (taps[0] + 1)].astype(F32)
+            for tap in taps[1:]:
+                total = total + w_prior[256 * tap:256 * (tap + 1)].astype(F32)
+            total = total.astype(BF)
+            fold[i, 256 * j:256 * (j + 1)] = total
+            k, l = FOLD.index(i), FOLD.index(j)
+            fold_t[k, 512 * l:512 * (l + 1)] = total.T
+    for tap in range(9):
+        w_coarse_t[256 * tap:256 * (tap + 1)] = w_coarse[256 * (8 - tap):256 * (9 - tap)].T
+        w_post_t[256 * tap:256 * (tap + 1)] = w_post[256 * (8 - tap):256 * (9 - tap)].T
 
 
 def sent(strip, down, right):
@@ -371,7 +382,7 @@
     params = pltpu.CompilerParams(vmem_limit_bytes=VMEM_LIMIT)
     feat_rows = feat.reshape(16, 2, 32, 256)
     noise_rows = noise_fine.reshape(16, 2, 32, 256)
-    own, top, bottom, left, right = pl.pallas_call(
+    own, top, bottom, left, right, lu, ld, ru, rd = pl.pallas_call(
         pack_kernel,
         out_shape=[
             jax.ShapeDtypeStruct((4, 16, 16, 256), BF),
@@ -379,9 +390,9 @@
             jax.ShapeDtypeStruct((37, 16, 256), BF),
             jax.ShapeDtypeStruct((16, 40, 256), BF),
             jax.ShapeDtypeStruct((16, 40, 256), BF),
-        ],
+        ] + [jax.ShapeDtypeStruct((5, 40, 256), BF)] * 4,
         in_specs=in_vmem(3),
-        out_specs=in_vmem(5),
+        out_specs=in_vmem(9),
         scratch_shapes=[
             pltpu.VMEM((16, 2, 2, 32, 128), F32),
             pltpu.VMEM((16, 2, 2, 32, 128), F32),
@@ -394,26 +405,33 @@
     from_down = sent(top, -1, 0)
     from_left = sent(right, 0, 1)
     from_right = sent(left, 0, -1)
-    from_ul = sent(right[11:], 1, 1)
-    from_ur = sent(left[11:], 1, -1)
-    from_dl = sent(right[:5], -1, 1)
-    from_dr = sent(left[:5], -1, -1)
-    fold = folded_weight(w_prior)
-    fold_t = jnp.stack([
-        jnp.concatenate([fold[FOLD[k], FOLD[l]].T for l in range(4)], axis=0) for k in range(4)
-    ])
-    fold = fold.reshape(4, 1024, 512)
+    from_ul = sent(rd, 1, 1)
+    from_ur = sent(ld, 1, -1)
+    from_dl = sent(ru, -1, 1)
+    from_dr = sent(lu, -1, -1)
+    fold, fold_t, w_post_t, w_coarse_t = pl.pallas_call(
+        weight_kernel,
+        out_shape=[
+            jax.ShapeDtypeStruct((4, 1024, 512), BF),
+            jax.ShapeDtypeStruct((4, 2048, 256), BF),
+            jax.ShapeDtypeStruct((2304, 256), BF),
+            jax.ShapeDtypeStruct((2304, 256), BF),
+        ],
+        in_specs=in_vmem(3),
+        out_specs=in_vmem(4),
+        compiler_params=params,
+        cost_estimate=pl.CostEstimate(flops=10000000, bytes_accessed=15000000, transcendentals=0),
+        name="weights",
+    )(w_post, w_coarse, w_prior)
     place = jnp.stack([lax.axis_index("row"), lax.axis_index("col")]).astype(jnp.int32)
-    g_post, g_coarse, g_prior, g_fine = pl.pallas_call(
+    grads, g_fine = pl.pallas_call(
         functools.partial(main_kernel, scale),
         out_shape=[
-            jax.ShapeDtypeStruct((2304, 256), BF),
-            jax.ShapeDtypeStruct((2304, 256), BF),
-            jax.ShapeDtypeStruct((2304, 512), BF),
+            jax.ShapeDtypeStruct((2, 2304, 512), BF),
             jax.ShapeDtypeStruct((2, 18, 16, 1024), BF),
         ],
         in_specs=[pl.BlockSpec(memory_space=pltpu.SMEM)] + in_vmem(16),
-        out_specs=in_vmem(4),
+        out_specs=in_vmem(2),
         scratch_shapes=[
             pltpu.VMEM((4, 26, 32, 256), F32),
             pltpu.VMEM((4, 24, 32, 256), F32),
@@ -432,7 +450,7 @@
         compiler_params=params,
         name="tile",
     )(place, own, noise_rows, noise_coarse, from_up, from_down, from_left, from_right, from_ul, from_ur,
-      from_dl, from_dr, w_post, w_coarse, fold, fold_t, turned_weight(w_coarse))
+      from_dl, from_dr, w_post, w_coarse, fold, fold_t, w_coarse_t)
     grad_feat = pl.pallas_call(
         feat_kernel,
         out_shape=jax.ShapeDtypeStruct((16, 2, 32, 256), BF),
@@ -442,15 +460,9 @@
         compiler_params=params,
         cost_estimate=pl.CostEstimate(flops=1200000000, bytes_accessed=3000000, transcendentals=0),
         name="feat",
-    )(g_fine, turned_weight(w_post)).reshape(32, 32, 256)
-    gradients = jnp.concatenate([g_prior, g_coarse, g_post], axis=1)
-    summed = reduce_scatter(gradients, ("core", "x", "y", "zl"))
-    return (
-        grad_feat,
-        summed[:, 768:].reshape(-1),
-        summed[:, 512:768].reshape(-1),
-        summed[:, :512].reshape(-1),
-    )
+    )(g_fine, w_post_t).reshape(32, 32, 256)
+    summed = reduce_scatter(grads)
+    return grad_feat, summed[1, :, 256:].reshape(-1), summed[1, :, :256].reshape(-1), summed[0].reshape(-1)
 
 
 def solution(mesh):

time: 201 us -> 157 us (0.78)
  waiting for transfers between devices: 56 us -> 26.9 us
  local copies, waits for them, and re-layouts: 31.8 us -> 6.76 us
  starting transfers between devices: 58.9 us -> 71.2 us
  other arithmetic: 15.8 us -> 4.41 us
  Pallas kernels: 35.6 us -> 44.3 us
    ppermute x10 -> x16, waiting for transfers between devices: 40.7 us -> 12.3 us  [sum_stage(): arrived.append(lax.ppermute(piece, ('row', 'col'), pairs))]
    ppermute x10 -> x16, starting transfers between devices: 35.4 us -> 48.8 us  [sum_stage(): arrived.append(lax.ppermute(piece, ('row', 'col'), pairs))]
    pallas_call x0 -> x1, Pallas kernels: none -> 7.74 us  [on_device(): pl.pallas_call(weight_kernel, out_shape=[jax.ShapeDtypeStruct((4, 1024, 5...]
    convert_element_type x1, local copies, waits for them, and re-layouts: 7.37 us -> 0.03 us  [sum_stage(): return total.astype(BF)]
    slice x6 -> x3, local copies, waits for them, and re-layouts: 7.52 us -> 0.26 us  [the longest x1 0.15 us: reduce_scatter(): second = parts[1].reshape(4, 4, 72, 512)]
    unnamed x26 -> x19, local copies, waits for them, and re-layouts: 5.89 us -> 1.06 us
    reshape x7 -> x0, local copies, waits for them, and re-layouts: 3.32 us -> none  [the longest x2 1.44 us: turned_weight(): weight.reshape(9, chans_in, chans_out)[::-1].transpose(0, 2, 1)]
    convert_element_type x5 -> x6, other arithmetic: 6.91 us -> 3.81 us  [sum_stage(): return total.astype(BF)]
  transfers between devices with their start and end apart: 20 -> 26, of which waited for: 8 -> 7; matrix products, arithmetic and copies ran while one was open for 15% -> 1% of each run, Pallas kernels for 2% -> 8%
where the time goes in v1:
time: 157 us; the launch traced here: 155 us
  starting transfers between devices  71.2 us (45%)
  Pallas kernels  44.3 us (28%)
  waiting for transfers between devices  26.9 us (17%)
  local copies, waits for them, and re-layouts  6.76 us (4%)
  other arithmetic  4.41 us (3%)
    ppermute x16, starting transfers between devices, sum_stage(): arrived.append(lax.ppermute(piece, ('row', 'col'), pairs))  48.8 us
    pallas_call x1, Pallas kernels, on_device(): pl.pallas_call(functools.partial(main_kernel, scale), out_shape=[jax.Shap...  29.8 us
    ppermute x8, starting transfers between devices, sent(): return lax.ppermute(strip, ('row', 'col'), pairs)  20.4 us
    ppermute x16, waiting for transfers between devices, sum_stage(): arrived.append(lax.ppermute(piece, ('row', 'col'), pairs))  12.3 us
    ppermute x8, waiting for transfers between devices, sent(): return lax.ppermute(strip, ('row', 'col'), pairs)  7.99 us
    pallas_call x1, Pallas kernels, on_device(): pl.pallas_call(weight_kernel, out_shape=[jax.ShapeDtypeStruct((4, 1024, 5...  7.74 us
    ppermute x2, waiting for transfers between devices, reduce_scatter(): total = total + lax.ppermute(piece, ('row', 'col'), pairs).astype(F32)  6.67 us
    pallas_call x1, Pallas kernels, on_device(): pl.pallas_call(feat_kernel, out_shape=jax.ShapeDtypeStruct((16, 2, 32, 25...  3.87 us
  transfers between devices with their start and end apart: 26, of which 7 were waited for; matrix products, arithmetic and copies ran while one was open for 1% of the time, Pallas kernels for 8%

profile of v1, /device:TPU:6, one launch (start us, length us, event | category | flops | bytes accessed | tf_op | source)
XLA Modules:
  0.0 154.6 jit_solution(12456156637692633942)
XLA Ops:
  0.6 2.9 %pack.1 = (bf16[4,16,16,256]{3,2,1,0:T(8,128)(2,1)}, bf16[37,16,256]{2,1,0:T(8,128)(2,1)}, bf16[37,16,256]{2,1,0:T(8,128)(2,1)}, bf16[16,40,256]{2,1,0:T(8,128)(...) custom-call(bf16[16,2,32,256]{3,2,1,0:T(8,128)(2,1)} %bitcast.73, ...), custom_call_target="tpu_custom_call" | custom-call | tf_op jit(solution)/shard_map/pack/pallas_call | solution.py:385
  3.6 3.2 %collective-permute-start.4 = (bf16[5,40,256]{2,1,0:T(8,128)(2,1)}, bf16[5,40,256]{2,1,0:T(8,128)(2,1)S(1)}, u32[]{:S(2)}, u32[]{:S(2)}) collective-permute-start(bf16[5,40,256]{2,1,0:T(8,128)(2,1)} %get-tuple-element.24), channel_id=1, source_target_pairs={{0,17},{1,18},{2,19},{3,20},{4,21},{5,22},{6,23},{7,24},{8,25},{9,... | collective-permute-start | bytes 307208 | tf_op jit(solution)/shard_map/ppermute | solution.py:377
  6.8 3.6 %collective-permute-start.2 = (bf16[16,40,256]{2,1,0:T(8,128)(2,1)}, bf16[16,40,256]{2,1,0:T(8,128)(2,1)S(1)}, u32[]{:S(2)}, u32[]{:S(2)}) collective-permute-start(bf16[16,40,256]{2,1,0:T(8,128)(2,1)} %get-tuple-element.22), channel_id=1, source_target_pairs={{0,1},{1,2},{2,3},{3,4},{4,5},{5,6},{6,7},{7,8},{8,9},{9,10},{10,1... | collective-permute-start | bytes 983048 | tf_op jit(solution)/shard_map/ppermute | solution.py:377
  10.4 1.3 collective-permute-start.3
  11.7 1.3 collective-permute-start.5
  13.0 3.4 %collective-permute-start = (bf16[37,16,256]{2,1,0:T(8,128)(2,1)}, bf16[37,16,256]{2,1,0:T(8,128)(2,1)S(1)}, u32[]{:S(2)}, u32[]{:S(2)}) collective-permute-start(bf16[37,16,256]{2,1,0:T(8,128)(2,1)} %get-tuple-element.20), channel_id=1, source_target_pairs={{0,16},{1,17},{2,18},{3,19},{4,20},{5,21},{6,22},{7,23},{8,24},{9,... | collective-permute-start | bytes 909320 | tf_op jit(solution)/shard_map/ppermute | solution.py:377
  16.4 2.4 %collective-permute-start.1 = (bf16[37,16,256]{2,1,0:T(8,128)(2,1)}, bf16[37,16,256]{2,1,0:T(8,128)(2,1)S(1)}, u32[]{:S(2)}, u32[]{:S(2)}) collective-permute-start(bf16[37,16,256]{2,1,0:T(8,128)(2,1)} %get-tuple-element.21), channel_id=1, source_target_pairs={{16,0},{17,1},{18,2},{19,3},{20,4},{21,5},{22,6},{23,7},{24,8},{25... | collective-permute-start | bytes 909320 | tf_op jit(solution)/shard_map/ppermute | solution.py:377
  18.9 3.7 %collective-permute-start.6 = (bf16[5,40,256]{2,1,0:T(8,128)(2,1)}, bf16[5,40,256]{2,1,0:T(8,128)(2,1)S(1)}, u32[]{:S(2)}, u32[]{:S(2)}) collective-permute-start(bf16[5,40,256]{2,1,0:T(8,128)(2,1)} %get-tuple-element.26), channel_id=1, source_target_pairs={{16,1},{17,2},{18,3},{19,4},{20,5},{21,6},{22,7},{23,8},{24,9},{25... | collective-permute-start | bytes 307208 | tf_op jit(solution)/shard_map/ppermute | solution.py:377
  22.6 7.7 %weights.1 = (bf16[4,1024,512]{2,1,0:T(8,128)(2,1)}, bf16[4,2048,256]{2,1,0:T(8,128)(2,1)}, bf16[2304,256]{1,0:T(8,128)(2,1)}, bf16[2304,256]{1,0:T(8,128)(2,1)}) custom-call(bf16[2304,256]{1,0:T(8,128)(2,1)} %w_post.3, bf16[2304,256]{1,0:T(8,128)(2,1)} %w_coarse.3, bf16[2304,512]{1,0:T(8,128)(2,1)} %w_prior.1), custom_call_target="tpu_custom_call" | custom-call | flops 10000000 | bytes 15000000 | tf_op jit(solution)/shard_map/weights/pallas_call | solution.py:412
  30.4 1.5 collective-permute-start.7
  32.5 8.0 %collective-permute-done.7.dr_ref = bf16[5,40,256]{2,1,0:T(8,128)(2,1)S(1)} collective-permute-done((bf16[5,40,256]{2,1,0:T(8,128)(2,1)S(1)}, bf16[5,40,256]{2,1,0:T(8,128)(2,1)S(1)}, u32[]{:S(2)}, u32[]{:S(2)}) %collective-permute-start.7) | collective-permute-done | bytes 102432 | tf_op jit(solution)/shard_map/ppermute | solution.py:377
  41.5 29.8 %tile.1 = (bf16[2,2304,512]{2,1,0:T(8,128)(2,1)}, bf16[2,18,16,1024]{3,2,1,0:T(8,128)(2,1)}) custom-call(s32[2]{0:T(128)} %pad_add_fusion.place_ref, bf16[4,16,16,256]{3,2,1,0:T(8,128)(2,1)} %get-tuple-element.19.own_ref, f32[16,2,32,256]{3,2,1,0:T(8,128)} %bitcast.72, f32[16,16,256]{2,1,0:T(8,128)} %low_ref.3, bf16[37,16,256]{2,1,0:T(8,128)(2,1)} %copy-done.2, ...), custom_call_target="tpu_custom_call" | custom-call | tf_op jit(solution)/shard_map/tile/pallas_call | solution.py:427
  71.3 3.3 %dynamic-slice_bitcast_fusion = bf16[2,1152,512]{2,1,0:T(8,128)(2,1)} fusion(bf16[2,2,1152,512]{3,2,1,0:T(8,128)(2,1)} %bitcast.65, s32[]{:T(128)S(6)} %select_n.155), kind=kLoop, calls=%fused_computation.2 | loop fusion | bytes 4718596 | tf_op jit(solution)/shard_map/jit(dynamic_index_in_dim)/squeeze | solution.py:47
  74.6 2.3 %collective-permute-start.8 = (bf16[2,1152,512]{2,1,0:T(8,128)(2,1)}, bf16[2,1152,512]{2,1,0:T(8,128)(2,1)S(1)}, u32[]{:S(2)}, u32[]{:S(2)}) collective-permute-start(bf16[2,1152,512]{2,1,0:T(8,128)(2,1)} %dynamic-slice_bitcast_fusion), channel_id=1, source_target_pairs={{0,1},{1,0},{2,3},{3,2},{4,5},{5,4},{6,7},{7,6},{8,9},{9,8},{10,11... | collective-permute-start | bytes 7077896 | tf_op jit(solution)/shard_map/ppermute | solution.py:49
  76.9 4.4 %collective-permute-done.8 = bf16[2,1152,512]{2,1,0:T(8,128)(2,1)S(1)} collective-permute-done((bf16[2,1152,512]{2,1,0:T(8,128)(2,1)}, bf16[2,1152,512]{2,1,0:T(8,128)(2,1)S(1)}, u32[]{:S(2)}, u32[]{:S(2)}) %collective-permute-start.8) | collective-permute-done | bytes 2359328 | tf_op jit(solution)/shard_map/ppermute | solution.py:49
  81.3 2.3 %fusion = bf16[2,1152,512]{2,1,0:T(8,128)(2,1)S(1)} fusion(bf16[2,1152,512]{2,1,0:T(8,128)(2,1)S(1)} %collective-permute-done.8, bf16[2,2,1152,512]{3,2,1,0:T(8,128)(2,1)} %bitcast.66, s32[]{:T(128)S(6)} %select_n.153), kind=kLoop, calls=%fused_computation.1 | loop fusion | flops 4718592 | bytes 7077892 | tf_op jit(solution)/shard_map/convert_element_type | solution.py:53
  84.3 3.2 %collective-permute-start.9 = (bf16[4,72,512]{2,1,0:T(8,128)(2,1)S(1)}, bf16[4,72,512]{2,1,0:T(8,128)(2,1)}, u32[]{:S(2)}, u32[]{:S(2)}) collective-permute-start(bf16[4,72,512]{2,1,0:T(8,128)(2,1)S(1)} %get-tuple-element.41), channel_id=1, source_target_pairs={{0,16},{1,17},{2,18},{3,19},{4,20},{5,21},{6,22},{7,23},{8,24},{9,... | collective-permute-start | bytes 884744 | tf_op jit(solution)/shard_map/ppermute | solution.py:49
  87.6 10.1 %collective-permute-start.17 = (bf16[4,72,512]{2,1,0:T(8,128)(2,1)S(1)}, bf16[4,72,512]{2,1,0:T(8,128)(2,1)S(1)}, u32[]{:S(2)}, u32[]{:S(2)}) collective-permute-start(bf16[4,72,512]{2,1,0:T(8,128)(2,1)S(1)} %get-tuple-element.39), channel_id=1, source_target_pairs={{0,4},{1,5},{2,6},{3,7},{4,0},{5,1},{6,2},{7,3},{8,12},{9,13},{10,... | collective-permute-start | bytes 884744 | tf_op jit(solution)/shard_map/ppermute | solution.py:49
  97.7 6.8 %collective-permute-start.16 = (bf16[4,72,512]{2,1,0:T(8,128)(2,1)S(1)}, bf16[4,72,512]{2,1,0:T(8,128)(2,1)S(1)}, u32[]{:S(2)}, u32[]{:S(2)}) collective-permute-start(bf16[4,72,512]{2,1,0:T(8,128)(2,1)S(1)} %get-tuple-element.40), channel_id=1, source_target_pairs={{0,6},{1,7},{2,0},{3,1},{4,2},{5,3},{6,4},{7,5},{8,14},{9,15},{10,... | collective-permute-start | bytes 884744 | tf_op jit(solution)/shard_map/ppermute | solution.py:49
  105.3 1.2 fusion.6
  106.5 7.9 %collective-permute-start.14 = (bf16[72,512]{1,0:T(8,128)(2,1)S(1)}, bf16[72,512]{1,0:T(8,128)(2,1)S(1)}, u32[]{:S(2)}, u32[]{:S(2)}) collective-permute-start(bf16[72,512]{1,0:T(8,128)(2,1)S(1)} %get-tuple-element.48), channel_id=1, source_target_pairs={{0,4},{1,5},{2,6},{3,7},{4,0},{5,1},{6,2},{7,3},{8,12},{9,13},{10,... | collective-permute-start | bytes 221192 | tf_op jit(solution)/shard_map/ppermute | solution.py:49
  114.5 4.4 %collective-permute-start.13 = (bf16[72,512]{1,0:T(8,128)(2,1)S(1)}, bf16[72,512]{1,0:T(8,128)(2,1)S(1)}, u32[]{:S(2)}, u32[]{:S(2)}) collective-permute-start(bf16[72,512]{1,0:T(8,128)(2,1)S(1)} %get-tuple-element.49), channel_id=1, source_target_pairs={{0,6},{1,7},{2,0},{3,1},{4,2},{5,3},{6,4},{7,5},{8,14},{9,15},{10,... | collective-permute-start | bytes 221192 | tf_op jit(solution)/shard_map/ppermute | solution.py:49
  119.9 2.0 %collective-permute-start.20 = (bf16[72,512]{1,0:T(8,128)(2,1)S(1)}, bf16[72,512]{1,0:T(8,128)(2,1)S(1)}, u32[]{:S(2)}, u32[]{:S(2)}) collective-permute-start(bf16[72,512]{1,0:T(8,128)(2,1)S(1)} %get-tuple-element.45), channel_id=1, source_target_pairs={{0,32},{1,33},{2,34},{3,35},{4,36},{5,37},{6,38},{7,39},{8,40},{9,... | collective-permute-start | bytes 221192 | tf_op jit(solution)/shard_map/ppermute | solution.py:49
  121.9 3.2 %collective-permute-start.18 = (bf16[72,512]{1,0:T(8,128)(2,1)S(1)}, bf16[72,512]{1,0:T(8,128)(2,1)S(1)}, u32[]{:S(2)}, u32[]{:S(2)}) collective-permute-start(bf16[72,512]{1,0:T(8,128)(2,1)S(1)} %get-tuple-element.44), channel_id=1, source_target_pairs={{0,16},{1,17},{2,18},{3,19},{4,20},{5,21},{6,22},{7,23},{8,24},{9,... | collective-permute-start | bytes 221192 | tf_op jit(solution)/shard_map/ppermute | solution.py:49
  125.3 1.3 collective-permute-done.20
  127.6 4.6 %collective-permute-start.23 = (bf16[2,18,512]{2,1,0:T(8,128)(2,1)S(1)}, bf16[2,18,512]{2,1,0:T(8,128)(2,1)S(1)}, u32[]{:S(2)}, u32[]{:S(2)}) collective-permute-start(bf16[2,18,512]{2,1,0:T(8,128)(2,1)S(1)} %get-tuple-element.51), channel_id=1, source_target_pairs={{0,128},{1,129},{2,130},{3,131},{4,132},{5,133},{6,134},{7,135},{8... | collective-permute-start | bytes 110600 | tf_op jit(solution)/shard_map/ppermute | solution.py:49
  132.3 1.8 %collective-permute-start.22 = (bf16[2,18,512]{2,1,0:T(8,128)(2,1)S(1)}, bf16[2,18,512]{2,1,0:T(8,128)(2,1)S(1)}, u32[]{:S(2)}, u32[]{:S(2)}) collective-permute-start(bf16[2,18,512]{2,1,0:T(8,128)(2,1)S(1)} %get-tuple-element.52), channel_id=1, source_target_pairs={{0,192},{1,193},{2,194},{3,195},{4,196},{5,197},{6,198},{7,199},{8... | collective-permute-start | bytes 110600 | tf_op jit(solution)/shard_map/ppermute | solution.py:49
  134.3 2.0 %collective-permute-done.22 = bf16[2,18,512]{2,1,0:T(8,128)(2,1)S(1)} collective-permute-done((bf16[2,18,512]{2,1,0:T(8,128)(2,1)S(1)}, bf16[2,18,512]{2,1,0:T(8,128)(2,1)S(1)}, u32[]{:S(2)}, u32[]{:S(2)}) %collective-permute-start.22) | collective-permute-done | bytes 36896 | tf_op jit(solution)/shard_map/ppermute | solution.py:49
  136.4 3.6 %collective-permute-done.21 = bf16[2,18,512]{2,1,0:T(8,128)(2,1)S(1)} collective-permute-done((bf16[2,18,512]{2,1,0:T(8,128)(2,1)S(1)}, bf16[2,18,512]{2,1,0:T(8,128)(2,1)S(1)}, u32[]{:S(2)}, u32[]{:S(2)}) %collective-permute-start.21) | collective-permute-done | bytes 36896 | tf_op jit(solution)/shard_map/ppermute | solution.py:49
  140.2 1.9 %collective-permute-start.24 = (bf16[2,9,512]{2,0,1:T(2,128)(2,1)S(1)}, bf16[2,9,512]{2,0,1:T(2,128)(2,1)S(1)}, u32[]{:S(2)}, u32[]{:S(2)}) collective-permute-start(bf16[2,9,512]{2,0,1:T(2,128)(2,1)S(1)} %get-tuple-element.53), channel_id=1, source_target_pairs={{0,0},{1,128},{2,8},{3,136},{4,16},{5,144},{6,24},{7,152},{8,1},{9... | collective-permute-start | bytes 55304 | tf_op jit(solution)/shard_map/ppermute | solution.py:72
  142.1 3.9 %feat.1 = bf16[16,2,32,256]{3,2,1,0:T(8,128)(2,1)} custom-call(bf16[2,18,16,1024]{3,2,1,0:T(8,128)(2,1)} %get-tuple-element.31.g_fine, bf16[2304,256]{1,0:T(8,128)(2,1)} %get-tuple-element.32.w_post_t), custom_call_target="tpu_custom_call" | custom-call | flops 1200000000 | bytes 3000000 | tf_op jit(solution)/shard_map/feat/pallas_call | solution.py:454
  146.0 6.7 %collective-permute-done.25 = bf16[2,9,512]{2,0,1:T(2,128)(2,1)S(1)} collective-permute-done((bf16[2,9,512]{2,0,1:T(2,128)(2,1)S(1)}, bf16[2,9,512]{2,0,1:T(2,128)(2,1)S(1)}, u32[]{:S(2)}, u32[]{:S(2)}) %collective-permute-start.25) | collective-permute-done | bytes 18464 | tf_op jit(solution)/shard_map/ppermute | solution.py:72
  (68 shorter events, 7.7 us)
Async XLA Ops:
  3.6 12.8 %collective-permute-start.4 = (bf16[5,40,256]{2,1,0:T(8,128)(2,1)}, bf16[5,40,256]{2,1,0:T(8,128)(2,1)S(1)}, u32[]{:S(2)}, u32[]{:S(2)}) collective-permute-start(bf16[5,40,256]{2,1,0:T(8,128)(2,1)} %get-tuple-element.24), channel_id=1, source_target_pairs={{0,17},{1,18},{2,19},{3,20},{4,21},{5,22},{6,23},{7,24},{8,25},{9,... | collective-permute-start | bytes 307208 | tf_op jit(solution)/shard_map/ppermute | solution.py:377
  6.8 33.7 %collective-permute-start.2 = (bf16[16,40,256]{2,1,0:T(8,128)(2,1)}, bf16[16,40,256]{2,1,0:T(8,128)(2,1)S(1)}, u32[]{:S(2)}, u32[]{:S(2)}) collective-permute-start(bf16[16,40,256]{2,1,0:T(8,128)(2,1)} %get-tuple-element.22), channel_id=1, source_target_pairs={{0,1},{1,2},{2,3},{3,4},{4,5},{5,6},{6,7},{7,8},{8,9},{9,10},{10,1... | collective-permute-start | bytes 983048 | tf_op jit(solution)/shard_map/ppermute | solution.py:377
  10.4 30.1 %collective-permute-start.3 = (bf16[16,40,256]{2,1,0:T(8,128)(2,1)}, bf16[16,40,256]{2,1,0:T(8,128)(2,1)S(1)}, u32[]{:S(2)}, u32[]{:S(2)}) collective-permute-start(bf16[16,40,256]{2,1,0:T(8,128)(2,1)} %get-tuple-element.23), channel_id=1, source_target_pairs={{1,0},{2,1},{3,2},{4,3},{5,4},{6,5},{7,6},{8,7},{9,8},{10,9},{11,1... | collective-permute-start | bytes 983048 | tf_op jit(solution)/shard_map/ppermute | solution.py:377
  11.7 7.2 %collective-permute-start.5 = (bf16[5,40,256]{2,1,0:T(8,128)(2,1)}, bf16[5,40,256]{2,1,0:T(8,128)(2,1)S(1)}, u32[]{:S(2)}, u32[]{:S(2)}) collective-permute-start(bf16[5,40,256]{2,1,0:T(8,128)(2,1)} %get-tuple-element.25), channel_id=1, source_target_pairs={{1,16},{2,17},{3,18},{4,19},{5,20},{6,21},{7,22},{8,23},{9,24},{10... | collective-permute-start | bytes 307208 | tf_op jit(solution)/shard_map/ppermute | solution.py:377
  13.0 27.5 %collective-permute-start = (bf16[37,16,256]{2,1,0:T(8,128)(2,1)}, bf16[37,16,256]{2,1,0:T(8,128)(2,1)S(1)}, u32[]{:S(2)}, u32[]{:S(2)}) collective-permute-start(bf16[37,16,256]{2,1,0:T(8,128)(2,1)} %get-tuple-element.20), channel_id=1, source_target_pairs={{0,16},{1,17},{2,18},{3,19},{4,20},{5,21},{6,22},{7,23},{8,24},{9,... | collective-permute-start | bytes 909320 | tf_op jit(solution)/shard_map/ppermute | solution.py:377
  16.4 14.0 %copy-start.4 = (bf16[5,40,256]{2,1,0:T(8,128)(2,1)}, bf16[5,40,256]{2,1,0:T(8,128)(2,1)S(1)}, u32[]{:S(2)}) copy-start(bf16[5,40,256]{2,1,0:T(8,128)(2,1)S(1)} %collective-permute-done.4.ul_ref) | copy-start | bytes 307204
  16.4 24.1 %collective-permute-start.1 = (bf16[37,16,256]{2,1,0:T(8,128)(2,1)}, bf16[37,16,256]{2,1,0:T(8,128)(2,1)S(1)}, u32[]{:S(2)}, u32[]{:S(2)}) collective-permute-start(bf16[37,16,256]{2,1,0:T(8,128)(2,1)} %get-tuple-element.21), channel_id=1, source_target_pairs={{16,0},{17,1},{18,2},{19,3},{20,4},{21,5},{22,6},{23,7},{24,8},{25... | collective-permute-start | bytes 909320 | tf_op jit(solution)/shard_map/ppermute | solution.py:377
  18.9 11.5 %copy-start.5 = (bf16[5,40,256]{2,1,0:T(8,128)(2,1)}, bf16[5,40,256]{2,1,0:T(8,128)(2,1)S(1)}, u32[]{:S(2)}) copy-start(bf16[5,40,256]{2,1,0:T(8,128)(2,1)S(1)} %collective-permute-done.5.ur_ref) | copy-start | bytes 307204
  18.9 11.5 %collective-permute-start.6 = (bf16[5,40,256]{2,1,0:T(8,128)(2,1)}, bf16[5,40,256]{2,1,0:T(8,128)(2,1)S(1)}, u32[]{:S(2)}, u32[]{:S(2)}) collective-permute-start(bf16[5,40,256]{2,1,0:T(8,128)(2,1)} %get-tuple-element.26), channel_id=1, source_target_pairs={{16,1},{17,2},{18,3},{19,4},{20,5},{21,6},{22,7},{23,8},{24,9},{25... | collective-permute-start | bytes 307208 | tf_op jit(solution)/shard_map/ppermute | solution.py:377
  22.6 7.8 %copy-start.8 = (bf16[5,40,256]{2,1,0:T(8,128)(2,1)S(1)}, bf16[5,40,256]{2,1,0:T(8,128)(2,1)}, u32[]{:S(2)}) copy-start(bf16[5,40,256]{2,1,0:T(8,128)(2,1)} %get-tuple-element.27) | copy-start | bytes 307204
  30.4 10.1 %copy-start.6 = (bf16[5,40,256]{2,1,0:T(8,128)(2,1)}, bf16[5,40,256]{2,1,0:T(8,128)(2,1)S(1)}, u32[]{:S(2)}) copy-start(bf16[5,40,256]{2,1,0:T(8,128)(2,1)S(1)} %collective-permute-done.6.dl_ref) | copy-start | bytes 307204
  30.4 10.0 %collective-permute-start.7 = (bf16[5,40,256]{2,1,0:T(8,128)(2,1)S(1)}, bf16[5,40,256]{2,1,0:T(8,128)(2,1)S(1)}, u32[]{:S(2)}, u32[]{:S(2)}) collective-permute-start(bf16[5,40,256]{2,1,0:T(8,128)(2,1)S(1)} %copy-done.8), channel_id=1, source_target_pairs={{17,0},{18,1},{19,2},{20,3},{21,4},{22,5},{23,6},{24,7},{25,8},{26... | collective-permute-start | bytes 307208 | tf_op jit(solution)/shard_map/ppermute | solution.py:377
  40.5 1.0 copy-start
  40.5 1.0 copy-start.1
  74.6 6.7 %collective-permute-start.8 = (bf16[2,1152,512]{2,1,0:T(8,128)(2,1)}, bf16[2,1152,512]{2,1,0:T(8,128)(2,1)S(1)}, u32[]{:S(2)}, u32[]{:S(2)}) collective-permute-start(bf16[2,1152,512]{2,1,0:T(8,128)(2,1)} %dynamic-slice_bitcast_fusion), channel_id=1, source_target_pairs={{0,1},{1,0},{2,3},{3,2},{4,5},{5,4},{6,7},{7,6},{8,9},{9,8},{10,11... | collective-permute-start | bytes 7077896 | tf_op jit(solution)/shard_map/ppermute | solution.py:49
  83.8 20.7 %collective-permute-start.11 = (bf16[4,72,512]{2,1,0:T(8,128)(2,1)S(1)}, bf16[4,72,512]{2,1,0:T(8,128)(2,1)S(1)}, u32[]{:S(2)}, u32[]{:S(2)}) collective-permute-start(bf16[4,72,512]{2,1,0:T(8,128)(2,1)S(1)} %get-tuple-element.42), channel_id=1, source_target_pairs={{0,32},{1,33},{2,34},{3,35},{4,36},{5,37},{6,38},{7,39},{8,40},{9,... | collective-permute-start | bytes 884744 | tf_op jit(solution)/shard_map/ppermute | solution.py:49
  83.9 21.4 %collective-permute-start.10 = (bf16[4,72,512]{2,1,0:T(8,128)(2,1)S(1)}, bf16[4,72,512]{2,1,0:T(8,128)(2,1)}, u32[]{:S(2)}, u32[]{:S(2)}) collective-permute-start(bf16[4,72,512]{2,1,0:T(8,128)(2,1)S(1)} %get-tuple-element.43), channel_id=1, source_target_pairs={{0,48},{1,49},{2,50},{3,51},{4,52},{5,53},{6,54},{7,55},{8,56},{9,... | collective-permute-start | bytes 884744 | tf_op jit(solution)/shard_map/ppermute | solution.py:49
  84.3 21.0 %collective-permute-start.9 = (bf16[4,72,512]{2,1,0:T(8,128)(2,1)S(1)}, bf16[4,72,512]{2,1,0:T(8,128)(2,1)}, u32[]{:S(2)}, u32[]{:S(2)}) collective-permute-start(bf16[4,72,512]{2,1,0:T(8,128)(2,1)S(1)} %get-tuple-element.41), channel_id=1, source_target_pairs={{0,16},{1,17},{2,18},{3,19},{4,20},{5,21},{6,22},{7,23},{8,24},{9,... | collective-permute-start | bytes 884744 | tf_op jit(solution)/shard_map/ppermute | solution.py:49
  87.6 31.4 %collective-permute-start.17 = (bf16[4,72,512]{2,1,0:T(8,128)(2,1)S(1)}, bf16[4,72,512]{2,1,0:T(8,128)(2,1)S(1)}, u32[]{:S(2)}, u32[]{:S(2)}) collective-permute-start(bf16[4,72,512]{2,1,0:T(8,128)(2,1)S(1)} %get-tuple-element.39), channel_id=1, source_target_pairs={{0,4},{1,5},{2,6},{3,7},{4,0},{5,1},{6,2},{7,3},{8,12},{9,13},{10,... | collective-permute-start | bytes 884744 | tf_op jit(solution)/shard_map/ppermute | solution.py:49
  97.7 22.0 %collective-permute-start.16 = (bf16[4,72,512]{2,1,0:T(8,128)(2,1)S(1)}, bf16[4,72,512]{2,1,0:T(8,128)(2,1)S(1)}, u32[]{:S(2)}, u32[]{:S(2)}) collective-permute-start(bf16[4,72,512]{2,1,0:T(8,128)(2,1)S(1)} %get-tuple-element.40), channel_id=1, source_target_pairs={{0,6},{1,7},{2,0},{3,1},{4,2},{5,3},{6,4},{7,5},{8,14},{9,15},{10,... | collective-permute-start | bytes 884744 | tf_op jit(solution)/shard_map/ppermute | solution.py:49
  104.5 15.2 %collective-permute-start.15 = (bf16[4,72,512]{2,1,0:T(8,128)(2,1)S(1)}, bf16[4,72,512]{2,1,0:T(8,128)(2,1)S(1)}, u32[]{:S(2)}, u32[]{:S(2)}) collective-permute-start(bf16[4,72,512]{2,1,0:T(8,128)(2,1)S(1)} %get-tuple-element.38), channel_id=1, source_target_pairs={{0,2},{1,3},{2,4},{3,5},{4,6},{5,7},{6,0},{7,1},{8,10},{9,11},{10,... | collective-permute-start | bytes 884744 | tf_op jit(solution)/shard_map/ppermute | solution.py:49
  106.5 15.4 %collective-permute-start.14 = (bf16[72,512]{1,0:T(8,128)(2,1)S(1)}, bf16[72,512]{1,0:T(8,128)(2,1)S(1)}, u32[]{:S(2)}, u32[]{:S(2)}) collective-permute-start(bf16[72,512]{1,0:T(8,128)(2,1)S(1)} %get-tuple-element.48), channel_id=1, source_target_pairs={{0,4},{1,5},{2,6},{3,7},{4,0},{5,1},{6,2},{7,3},{8,12},{9,13},{10,... | collective-permute-start | bytes 221192 | tf_op jit(solution)/shard_map/ppermute | solution.py:49
  114.5 10.7 %collective-permute-start.13 = (bf16[72,512]{1,0:T(8,128)(2,1)S(1)}, bf16[72,512]{1,0:T(8,128)(2,1)S(1)}, u32[]{:S(2)}, u32[]{:S(2)}) collective-permute-start(bf16[72,512]{1,0:T(8,128)(2,1)S(1)} %get-tuple-element.49), channel_id=1, source_target_pairs={{0,6},{1,7},{2,0},{3,1},{4,2},{5,3},{6,4},{7,5},{8,14},{9,15},{10,... | collective-permute-start | bytes 221192 | tf_op jit(solution)/shard_map/ppermute | solution.py:49
  118.9 6.2 %collective-permute-start.12 = (bf16[72,512]{1,0:T(8,128)(2,1)S(1)}, bf16[72,512]{1,0:T(8,128)(2,1)S(1)}, u32[]{:S(2)}, u32[]{:S(2)}) collective-permute-start(bf16[72,512]{1,0:T(8,128)(2,1)S(1)} %get-tuple-element.47), channel_id=1, source_target_pairs={{0,2},{1,3},{2,4},{3,5},{4,6},{5,7},{6,0},{7,1},{8,10},{9,11},{10,... | collective-permute-start | bytes 221192 | tf_op jit(solution)/shard_map/ppermute | solution.py:49
  119.9 6.6 %collective-permute-start.20 = (bf16[72,512]{1,0:T(8,128)(2,1)S(1)}, bf16[72,512]{1,0:T(8,128)(2,1)S(1)}, u32[]{:S(2)}, u32[]{:S(2)}) collective-permute-start(bf16[72,512]{1,0:T(8,128)(2,1)S(1)} %get-tuple-element.45), channel_id=1, source_target_pairs={{0,32},{1,33},{2,34},{3,35},{4,36},{5,37},{6,38},{7,39},{8,40},{9,... | collective-permute-start | bytes 221192 | tf_op jit(solution)/shard_map/ppermute | solution.py:49
  121.9 5.6 %collective-permute-start.19 = (bf16[72,512]{1,0:T(8,128)(2,1)S(1)}, bf16[72,512]{1,0:T(8,128)(2,1)S(1)}, u32[]{:S(2)}, u32[]{:S(2)}) collective-permute-start(bf16[72,512]{1,0:T(8,128)(2,1)S(1)} %get-tuple-element.46), channel_id=1, source_target_pairs={{0,48},{1,49},{2,50},{3,51},{4,52},{5,53},{6,54},{7,55},{8,56},{9,... | collective-permute-start | bytes 221192 | tf_op jit(solution)/shard_map/ppermute | solution.py:49
  121.9 5.6 %collective-permute-start.18 = (bf16[72,512]{1,0:T(8,128)(2,1)S(1)}, bf16[72,512]{1,0:T(8,128)(2,1)S(1)}, u32[]{:S(2)}, u32[]{:S(2)}) collective-permute-start(bf16[72,512]{1,0:T(8,128)(2,1)S(1)} %get-tuple-element.44), channel_id=1, source_target_pairs={{0,16},{1,17},{2,18},{3,19},{4,20},{5,21},{6,22},{7,23},{8,24},{9,... | collective-permute-start | bytes 221192 | tf_op jit(solution)/shard_map/ppermute | solution.py:49
  127.6 6.7 %collective-permute-start.23 = (bf16[2,18,512]{2,1,0:T(8,128)(2,1)S(1)}, bf16[2,18,512]{2,1,0:T(8,128)(2,1)S(1)}, u32[]{:S(2)}, u32[]{:S(2)}) collective-permute-start(bf16[2,18,512]{2,1,0:T(8,128)(2,1)S(1)} %get-tuple-element.51), channel_id=1, source_target_pairs={{0,128},{1,129},{2,130},{3,131},{4,132},{5,133},{6,134},{7,135},{8... | collective-permute-start | bytes 110600 | tf_op jit(solution)/shard_map/ppermute | solution.py:49
  132.3 4.1 %collective-permute-start.22 = (bf16[2,18,512]{2,1,0:T(8,128)(2,1)S(1)}, bf16[2,18,512]{2,1,0:T(8,128)(2,1)S(1)}, u32[]{:S(2)}, u32[]{:S(2)}) collective-permute-start(bf16[2,18,512]{2,1,0:T(8,128)(2,1)S(1)} %get-tuple-element.52), channel_id=1, source_target_pairs={{0,192},{1,193},{2,194},{3,195},{4,196},{5,197},{6,198},{7,199},{8... | collective-permute-start | bytes 110600 | tf_op jit(solution)/shard_map/ppermute | solution.py:49
  134.1 5.9 %collective-permute-start.21 = (bf16[2,18,512]{2,1,0:T(8,128)(2,1)S(1)}, bf16[2,18,512]{2,1,0:T(8,128)(2,1)S(1)}, u32[]{:S(2)}, u32[]{:S(2)}) collective-permute-start(bf16[2,18,512]{2,1,0:T(8,128)(2,1)S(1)} %get-tuple-element.50), channel_id=1, source_target_pairs={{0,64},{1,65},{2,66},{3,67},{4,68},{5,69},{6,70},{7,71},{8,72},{9,... | collective-permute-start | bytes 110600 | tf_op jit(solution)/shard_map/ppermute | solution.py:49
  140.1 12.6 %collective-permute-start.25 = (bf16[2,9,512]{2,0,1:T(2,128)(2,1)S(1)}, bf16[2,9,512]{2,0,1:T(2,128)(2,1)S(1)}, u32[]{:S(2)}, u32[]{:S(2)}) collective-permute-start(bf16[2,9,512]{2,0,1:T(2,128)(2,1)S(1)} %get-tuple-element.54), channel_id=1, source_target_pairs={{0,1},{1,129},{2,9},{3,137},{4,17},{5,145},{6,25},{7,153},{8,0},{9... | collective-permute-start | bytes 55304 | tf_op jit(solution)/shard_map/ppermute | solution.py:72
  140.2 12.5 %collective-permute-start.24 = (bf16[2,9,512]{2,0,1:T(2,128)(2,1)S(1)}, bf16[2,9,512]{2,0,1:T(2,128)(2,1)S(1)}, u32[]{:S(2)}, u32[]{:S(2)}) collective-permute-start(bf16[2,9,512]{2,0,1:T(2,128)(2,1)S(1)} %get-tuple-element.53), channel_id=1, source_target_pairs={{0,0},{1,128},{2,8},{3,136},{4,16},{5,144},{6,24},{7,152},{8,1},{9... | collective-permute-start | bytes 55304 | tf_op jit(solution)/shard_map/ppermute | solution.py:72
  (3 other events, 2.3 us)

commit v2 on v1

v2 whole, which is shorter than its diff:
```python
import functools
import math

import jax
import jax.numpy as jnp
from jax import lax
from jax.experimental import pallas as pl
from jax.experimental.pallas import tpu as pltpu
from jax.sharding import PartitionSpec as P

BF = jnp.bfloat16
F32 = jnp.float32
VARIANT = ((1, -1), (0, 0), (1, 0), (0, 1))
FOLD = (3, 1, 2, 0)
VMEM_LIMIT = 60 * 1024 * 1024


def digits():
    places = []
    for d in range(256):
        row, col = d // 16, d % 16
        places.append({"zl": row // 4, "x": row % 4, "zh": col // 8, "y": (col // 2) % 4, "core": col % 2})
    return places


def index_of(place):
    return (place["zl"] * 4 + place["x"]) * 16 + (place["zh"] * 4 + place["y"]) * 2 + place["core"]


def my_place():
    row, col = lax.axis_index("row"), lax.axis_index("col")
    return {"zl": row // 4, "x": row % 4, "zh": col // 8, "y": (col // 2) % 4, "core": col % 2}


def flipped(place, name, bits):
    return {**place, name: place[name] ^ bits}


def sum_stage(part, name, dim):
    here = my_place()[name]
    arrived = []
    for bits in (1, 3, 2):
        piece = lax.dynamic_index_in_dim(part, here ^ bits, dim, keepdims=False)
        pairs = [(index_of(p), index_of(flipped(p, name, bits))) for p in digits()]
        arrived.append(lax.ppermute(piece, ("row", "col"), pairs))
    total = lax.dynamic_index_in_dim(part, here, dim, keepdims=False).astype(F32)
    for piece in arrived:
        total = total + piece.astype(F32)
    return total.astype(BF)


def reduce_scatter(parts):
    pairs = [(index_of(p), index_of(flipped(p, "core", 1))) for p in digits()]
    other = lax.ppermute(parts[1], ("row", "col"), pairs)
    parts = (parts[0].astype(F32) + other.astype(F32)).astype(BF)
    first = parts[0].reshape(4, 4, 72, 512)
    second = parts[1].reshape(4, 4, 72, 512)
    first, second = sum_stage(first, "x", 0), sum_stage(second, "y", 1)
    first, second = sum_stage(first, "y", 0), sum_stage(second, "x", 0)
    parts = sum_stage(jnp.stack([first, second]).reshape(2, 4, 18, 512), "zl", 1)
    halves = parts.reshape(2, 2, 9, 512)
    last = my_place()["zh"]
    total = 0.0
    for flip in (0, 1):
        pairs = []
        for p in digits():
            chunk = (((p["core"] * 4 + p["x"]) * 4 + p["y"]) * 4 + p["zl"]) * 2 + (p["zh"] + flip) % 2
            pairs.append((index_of(p), chunk))
        piece = lax.dynamic_index_in_dim(halves, (last + flip) % 2, 1, keepdims=False)
        total = total + lax.ppermute(piece, ("row", "col"), pairs).astype(F32)
    return total


def in_vmem(count):
    return [pl.BlockSpec(memory_space=pltpu.VMEM)] * count


def split_lanes(ref, value):
    for half in range(2):
        ref[:, :, half] = value[..., 128 * half:128 * (half + 1)]


def phase_of(ref, row, col):
    return jnp.concatenate([ref[:, row, half, pl.ds(col, 16, stride=2), :] for half in range(2)], axis=-1)


def line_of(ref, line, col):
    return jnp.concatenate(
        [ref[line // 2, line % 2, half, pl.ds(col, 16, stride=2), :] for half in range(2)], axis=-1)


def split_lanes(ref, value):
    for half in range(2):
        ref[:, :, half] = value[..., 128 * half:128 * (half + 1)]


def phase_of(ref, row, col):
    return jnp.concatenate([ref[:, row, half, pl.ds(col, 16, stride=2), :] for half in range(2)], axis=-1)


def first_kernel(feat_ref, fine_ref, low_ref, w_post, own_ref, part_ref, top_ref, bottom_ref,
                 wide, noise, field, cat, spill):
    split_lanes(wide, feat_ref[...].astype(F32))
    split_lanes(noise, fine_ref[...])
    field[...] = jnp.zeros(field.shape, F32)
    for row in range(2):
        for col in range(2):
            cells = phase_of(wide, row, col)
            own_ref[2 * row + col] = cells.astype(BF)
            field[col, 1:17, 8:24, :] = cells
        even, odd = flat(field[0]), flat(field[1])
        for at, part in enumerate((before(odd), even, odd, after(even))):
            cat[row, :, :, 256 * at:256 * (at + 1)] = back_in_rows(part.astype(BF))
    for row in range(2):
        for col in range(2):
            value = jnp.zeros((544, 256), F32)
            for a in range(3):
                phase, shift = VARIANT[row + a]
                at = 1 + shift - row
                cells = flat(cat[phase, at:at + 17, :, 256 * col:256 * col + 768])
                value = value + dot(cells, w_post[768 * a:768 * (a + 1)])
            part_ref[2 * row + col] = back_in_rows(value)
            part_ref[2 * row + col, row:row + 16, 8:24, :] += phase_of(noise, row, col)
    spill[...] = jnp.zeros(spill.shape, F32)
    for out, first, low_first in ((top_ref, -1, 0), (bottom_ref, 24, 13)):
        for r in range(9):
            line = first + r
            row = line % 2
            at = line // 2 + row
            for col in range(2):
                e = 2 * r + col
                out[e] = part_ref[2 * row + col, at, 8:24, :].astype(BF)
                edge = 7 if col else 24
                spill[e:e + 1, :] = part_ref[2 * row + col, at, edge:edge + 1, :]
        out[18:21] = low_ref[low_first:low_first + 3].astype(BF)
        out[21:23] = spill[...].reshape(2, 16, 256).astype(BF)


def middle_kernel(part_ref, low_ref, up_ref, down_ref, left_ref, right_ref, side, spill):
    lows = ((4, low_ref[...]), (1, up_ref[18:21].astype(F32)), (20, down_ref[18:21].astype(F32)))
    for out, long, long_from, other_from, low_from in ((left_ref, 1, -1, 0, 0), (right_ref, 0, 12, 12, 13)):
        side[...] = jnp.zeros(side.shape, F32)
        for row in range(2):
            at = 9 * row
            rows = slice(4 - row, 21 - row)
            side[rows, at:at + 5, :] = part_ref[2 * row + long, :, 8 + long_from:13 + long_from, :]
            side[rows, at + 5:at + 9, :] = part_ref[2 * row + 1 - long, :, 8 + other_from:12 + other_from, :]
        for ref, first in ((up_ref, -8), (down_ref, 31)):
            spill[...] = ref[21:23].astype(F32).reshape(32, 256)
            for r in range(9):
                line = first + r
                row = line % 2
                here, at = line // 2 + 4, 9 * row
                cells = ref[2 * r + long].astype(F32)
                end = spill[2 * r + long:2 * r + long + 1, :]
                if long:
                    side[here, at:at + 1, :] += end
                    side[here, at + 1:at + 5, :] += cells[0:4]
                else:
                    side[here, at:at + 4, :] += cells[12:16]
                    side[here, at + 4:at + 5, :] += end
                side[here, at + 5:at + 9, :] += ref[2 * r + 1 - long].astype(F32)[other_from:other_from + 4]
        for here, block in lows:
            side[here:here + block.shape[0], 18:21, :] = block[:, low_from:low_from + 3, :]
        out[...] = side[...].astype(BF)


def flat(block):
    return block.reshape(block.shape[0] * 32, block.shape[2])


def back_in_rows(block):
    return block.reshape(block.shape[0] // 32, 32, block.shape[1])


def before(block):
    return pltpu.roll(block, 1, 0)


def after(block):
    return pltpu.roll(block, block.shape[0] - 1, 0)


def dot(left, right):
    return jnp.dot(left, right, preferred_element_type=F32)


def inside(place_ref, first_row, rows):
    cell = lax.broadcasted_iota(jnp.int32, (rows * 32, 256), 0)
    line = cell // 32 + first_row + 16 * place_ref[0]
    column = cell % 32 - 8 + 16 * place_ref[1]
    return (line >= 0) & (line < 256) & (column >= 0) & (column < 256)


def three_wide(value, ref, first, rows):
    c = value.shape[1]
    for at, part in enumerate((before(value), value, after(value))):
        ref[pl.ds(first, rows), :, c * at:c * (at + 1)] = back_in_rows(part.astype(BF))


def own_cells(block):
    return block.astype(F32)[:, 8:24, :].reshape(256, block.shape[2]).astype(BF)


def turned(block):
    return own_cells(block).T


def main_kernel(scale, place_ref, own_ref, part_ref, low_ref, up_ref, down_ref, left_ref, right_ref,
                w_coarse, fold, fold_t, w_coarse_t, grads, g_fine,
                fine, low, pool_cat, coarse, ctx_cat, err, d_cat, d_own, gc_cat, gc_own, spill):
    def put(which, tap, lanes, value):
        value = (value * scale).astype(BF)
        for half, first, start, stop in ((0, 256 * tap, 0, 256), (1, 256 * tap - 1152, 0, 256)):
            start, stop = max(start, -first), min(stop, 1152 - first)
            if start < stop:
                slot = (place_ref[2] + half) % 2
                grads[slot, which, first + start:first + stop, lanes] = value[start:stop]

    fine[...] = jnp.zeros(fine.shape, F32)
    for row in range(2):
        for col in range(2):
            fine[2 * row + col, 4 - row:21 - row] = part_ref[2 * row + col]
    low[3:19, 8:24, :] = low_ref[...]
    for ref, first, low_first in ((up_ref, -8, 0), (down_ref, 31, 19)):
        spill[...] = ref[21:23].astype(F32).reshape(32, 256)
        for r in range(9):
            line = first + r
            for col in range(2):
                e = 2 * r + col
                edge = 7 if col else 24
                fine[2 * (line % 2) + col, line // 2 + 4, 8:24, :] += ref[e].astype(F32)
                fine[2 * (line % 2) + col, line // 2 + 4, edge:edge + 1, :] += spill[e:e + 1, :]
        low[low_first:low_first + 3, 8:24, :] = ref[18:21].astype(F32)
    for ref, long, long_at, other_at, low_at in ((left_ref, 0, 4, 4, 5), (right_ref, 1, 23, 24, 24)):
        block = ref[...].astype(F32)
        for row in range(2):
            at = 9 * row
            fine[2 * row + long, :, long_at:long_at + 5, :] += block[:, at:at + 5, :]
            fine[2 * row + 1 - long, :, other_at:other_at + 4, :] += block[:, at + 5:at + 9, :]
        low[:, low_at:low_at + 3, :] = block[1:23, 18:21, :]

    @pl.loop(0, 3)
    def _(step):
        total = flat(fine[0, pl.ds(step * 8, 8)])
        for p in range(1, 4):
            total = total + flat(fine[p, pl.ds(step * 8, 8)])
        total = jnp.where(inside(place_ref, step * 8 - 4, 8), total * 0.25, 0.0)
        three_wide(total, pool_cat, step * 8, 8)

    @pl.loop(0, 2)
    def _(step):
        value = flat(low[pl.ds(step * 11, 11)])
        for a in range(3):
            value = value + dot(flat(pool_cat[pl.ds(step * 11 + a, 11)]), w_coarse[768 * a:768 * (a + 1)])
        value = jnp.where(inside(place_ref, step * 11 - 3, 11), value, 0.0)
        coarse[pl.ds(step * 11, 11)] = back_in_rows(value)
        three_wide(value, ctx_cat, step * 11, 11)

    for row in range(2):
        @pl.loop(0, 3)
        def _(step):
            valid = inside(place_ref, step * 7 - 2 - row, 7)
            pieces = []
            for col in range(2):
                prior = jnp.zeros((224, 512), F32)
                for k in range(2):
                    cells = flat(ctx_cat[pl.ds(step * 7 + k, 7), :, 256 * col:256 * col + 512])
                    prior = prior + dot(cells, fold[2 * row + k, 512 * col:512 * col + 512])
                raw = prior[:, 256:]
                small = jnp.exp(-jnp.abs(raw))
                more = 1.0 + small
                sigma = jnp.maximum(raw, 0.0) + jnp.log(more) + 0.5
                gate = jnp.where(raw >= 0.0, 1.0, small) / more
                inverse = 1.0 / sigma
                deviation = flat(fine[2 * row + col, pl.ds(step * 7 + 2 - row, 7)]) - prior[:, :256]
                residual = deviation * inverse * inverse
                err[2 * row + col, pl.ds(step * 7, 7)] = back_in_rows(residual)
                pieces.append(jnp.where(valid, -residual, 0.0))
                pieces.append(jnp.where(valid, (inverse - residual * deviation * inverse) * gate, 0.0))
            parts = (before(pieces[2]), before(pieces[3]), pieces[0], pieces[1], pieces[2], pieces[3],
                     after(pieces[0]), after(pieces[1]))
            for at, part in enumerate(parts):
                part = back_in_rows(part)
                d_cat[row, pl.ds(step * 7, 7), :, 256 * at:256 * (at + 1)] = part.astype(BF)
                d_own[row, pl.ds(step * 7, 7), :, 256 * at:256 * (at + 1)] = part[:, 8:24, :].astype(BF)

    left = turned(ctx_cat[3:19, :, 256:512])
    left = jnp.concatenate([left] * 4, axis=1)
    for a in range(3):
        for b in range(3):
            rights = []
            for k in (2 - a, 3 - a):
                phase, shift = VARIANT[k]
                at = 2 + phase + shift
                for l in (2 - b, 3 - b):
                    rights.append(d_own[phase, at:at + 16, :, 512 * l:512 * (l + 1)].reshape(256, 512))
            put(0, 3 * a + b, slice(0, 512), dot(left, jnp.concatenate(rights, axis=0)))

    @pl.loop(0, 2)
    def _(step):
        value = flat(coarse[pl.ds(step * 10 + 1, 10)])
        for k in range(4):
            phase, shift = VARIANT[k]
            at = step * 10 + shift + phase
            value = value + dot(flat(d_cat[phase, pl.ds(at, 10)]), fold_t[k])
        value = jnp.where(inside(place_ref, step * 10 - 2, 10), value, 0.0)
        three_wide(value, gc_cat, step * 10, 10)
        for at, part in enumerate((before(value), value, after(value))):
            gc_own[pl.ds(step * 10, 10), :, 256 * at:256 * (at + 1)] = back_in_rows(part)[:, 8:24, :].astype(BF)

    left = turned(pool_cat[4:20, :, 256:512])
    for a in range(3):
        for b in range(3):
            right = gc_own[3 - a:19 - a, :, 256 * (2 - b):256 * (3 - b)].reshape(256, 256)
            put(1, 3 * a + b, slice(0, 256), dot(left, right))

    @pl.loop(0, 2)
    def _(step):
        value = jnp.zeros((288, 256), F32)
        for a in range(3):
            value = value + dot(flat(gc_cat[pl.ds(step * 9 + a, 9)]), w_coarse_t[768 * a:768 * (a + 1)])
        value = value * 0.25
        valid = inside(place_ref, step * 9 - 1, 9)
        for row in range(2):
            even, odd = [
                jnp.where(valid, flat(err[2 * row + col, pl.ds(step * 9 + 1 + row, 9)]) + value, 0.0)
                for col in range(2)
            ]
            for at, part in enumerate((before(odd), even, odd, after(even))):
                compact = part.reshape(9, 32, 256)[:, 8:24, :]
                g_fine[row, pl.ds(step * 9, 9), :, 256 * at:256 * (at + 1)] = compact.astype(BF)

    left = jnp.concatenate([own_ref[p].reshape(256, 256).T for p in range(4)], axis=1)
    for a in range(3):
        for b in range(3):
            rights = []
            for row in range(2):
                phase, shift = VARIANT[row + 2 - a]
                for col in range(2):
                    at = col + 2 - b
                    rights.append(g_fine[phase, 1 + shift:17 + shift, :, 256 * at:256 * (at + 1)].reshape(256, 256))
            put(1, 3 * a + b, slice(256, 512), dot(left, jnp.concatenate(rights, axis=0)))


def feat_kernel(g_fine, w_post_t, out_ref, wide):
    for row in range(2):
        for col in range(2):
            value = jnp.zeros((256, 256), F32)
            for a in range(3):
                phase, shift = VARIANT[row + a]
                cells = g_fine[phase, 1 + shift:17 + shift, :, 256 * col:256 * col + 768].reshape(256, 768)
                value = value + dot(cells, w_post_t[768 * a:768 * (a + 1)])
            for half in range(2):
                wide[:, row, half, pl.ds(col, 16, stride=2), :] = (
                    value[:, 128 * half:128 * (half + 1)].reshape(16, 16, 128))
    for half in range(2):
        out_ref[:, :, :, 128 * half:128 * (half + 1)] = wide[:, :, half].astype(BF)


TAPS_OF = ((0,), (1, 2), (0, 1), (2,))


def weight_kernel(w_post, w_coarse, w_prior, fold, fold_t, w_post_t, w_coarse_t):
    for i in range(4):
        for j in range(4):
            taps = [3 * a + b for a in TAPS_OF[i] for b in TAPS_OF[j]]
            total = w_prior[256 * taps[0]:256 * (taps[0] + 1)].astype(F32)
            for tap in taps[1:]:
                total = total + w_prior[256 * tap:256 * (tap + 1)].astype(F32)
            total = total.astype(BF)
            fold[i, 256 * j:256 * (j + 1)] = total
            k, l = FOLD.index(i), FOLD.index(j)
            fold_t[k, 512 * l:512 * (l + 1)] = total.T
    for tap in range(9):
        w_coarse_t[256 * tap:256 * (tap + 1)] = w_coarse[256 * (8 - tap):256 * (9 - tap)].T
        w_post_t[256 * tap:256 * (tap + 1)] = w_post[256 * (8 - tap):256 * (9 - tap)].T


def sent(strip, down, right):
    pairs = [
        (r * 16 + c, (r + down) * 16 + c + right)
        for r in range(16) for c in range(16) if 0 <= r + down < 16 and 0 <= c + right < 16
    ]
    return lax.ppermute(strip, ("row", "col"), pairs)


def on_device(feat, noise_fine, noise_coarse, w_post, w_coarse, w_prior):
    scale = 1.0 / 512.0
    params = pltpu.CompilerParams(vmem_limit_bytes=VMEM_LIMIT)
    own, part, top, bottom = pl.pallas_call(
        first_kernel,
        out_shape=[
            jax.ShapeDtypeStruct((4, 16, 16, 256), BF),
            jax.ShapeDtypeStruct((4, 17, 32, 256), F32),
            jax.ShapeDtypeStruct((23, 16, 256), BF),
            jax.ShapeDtypeStruct((23, 16, 256), BF),
        ],
        in_specs=in_vmem(4),
        out_specs=in_vmem(4),
        scratch_shapes=[
            pltpu.VMEM((16, 2, 2, 32, 128), F32),
            pltpu.VMEM((16, 2, 2, 32, 128), F32),
            pltpu.VMEM((2, 18, 32, 256), F32),
            pltpu.VMEM((2, 18, 32, 1024), BF),
            pltpu.VMEM((32, 256), F32),
        ],
        compiler_params=params,
        name="first",
    )(feat.reshape(16, 2, 32, 256), noise_fine.reshape(16, 2, 32, 256), noise_coarse, w_post)
    from_up, from_down = sent(bottom, 1, 0), sent(top, -1, 0)
    fold, fold_t, w_post_t, w_coarse_t = pl.pallas_call(
        weight_kernel,
        out_shape=[
            jax.ShapeDtypeStruct((4, 1024, 512), BF),
            jax.ShapeDtypeStruct((4, 2048, 256), BF),
            jax.ShapeDtypeStruct((2304, 256), BF),
            jax.ShapeDtypeStruct((2304, 256), BF),
        ],
        in_specs=in_vmem(3),
        out_specs=in_vmem(4),
        compiler_params=params,
        cost_estimate=pl.CostEstimate(flops=10000000, bytes_accessed=15000000, transcendentals=0),
        name="weights",
    )(w_post, w_coarse, w_prior)
    left, right = pl.pallas_call(
        middle_kernel,
        out_shape=[jax.ShapeDtypeStruct((24, 24, 256), BF)] * 2,
        in_specs=in_vmem(4),
        out_specs=in_vmem(2),
        scratch_shapes=[pltpu.VMEM((24, 24, 256), F32), pltpu.VMEM((32, 256), F32)],
        compiler_params=params,
        name="middle",
    )(part, noise_coarse, from_up, from_down)
    from_left, from_right = sent(right, 0, 1), sent(left, 0, -1)
    row, col = lax.axis_index("row"), lax.axis_index("col")
    place = jnp.stack([row, col, col % 2]).astype(jnp.int32)
    grads, g_fine = pl.pallas_call(
        functools.partial(main_kernel, scale),
        out_shape=[
            jax.ShapeDtypeStruct((2, 2, 1152, 512), BF),
            jax.ShapeDtypeStruct((2, 18, 16, 1024), BF),
        ],
        in_specs=[pl.BlockSpec(memory_space=pltpu.SMEM)] + in_vmem(11),
        out_specs=in_vmem(2),
        scratch_shapes=[
            pltpu.VMEM((4, 24, 32, 256), F32),
            pltpu.VMEM((22, 32, 256), F32),
            pltpu.VMEM((24, 32, 768), BF),
            pltpu.VMEM((22, 32, 256), F32),
            pltpu.VMEM((22, 32, 768), BF),
            pltpu.VMEM((4, 21, 32, 256), F32),
            pltpu.VMEM((2, 21, 32, 2048), BF),
            pltpu.VMEM((2, 21, 16, 2048), BF),
            pltpu.VMEM((20, 32, 768), BF),
            pltpu.VMEM((20, 16, 768), BF),
            pltpu.VMEM((32, 256), F32),
        ],
        compiler_params=params,
        name="tile",
    )(place, own, part, noise_coarse, from_up, from_down, from_left, from_right,
      w_coarse, fold, fold_t, w_coarse_t)
    grad_feat = pl.pallas_call(
        feat_kernel,
        out_shape=jax.ShapeDtypeStruct((16, 2, 32, 256), BF),
        in_specs=in_vmem(2),
        out_specs=pl.BlockSpec(memory_space=pltpu.VMEM),
        scratch_shapes=[pltpu.VMEM((16, 2, 2, 32, 128), F32)],
        compiler_params=params,
        cost_estimate=pl.CostEstimate(flops=1200000000, bytes_accessed=3000000, transcendentals=0),
        name="feat",
    )(g_fine, w_post_t).reshape(32, 32, 256)
    summed = reduce_scatter(grads)
    return grad_feat, summed[1, :, 256:].reshape(-1), summed[1, :, :256].reshape(-1), summed[0].reshape(-1)


def solution(mesh):
    return jax.shard_map(
        on_device,
        mesh=mesh,
        in_specs=(
            P("row", "col", None),
            P("row", "col", None),
            P("row", "col", None),
            P(),
            P(),
            P(),
        ),
        out_specs=(P("row", "col", None), P(("row", "col")), P(("row", "col")), P(("row", "col"))),
        check_vma=False,
    )
```

time: 157 us -> 143 us (0.911); the launches traced: 155 us -> 143 us
  starting transfers between devices: 71.2 us -> 46.6 us
  waiting for transfers between devices: 26.9 us -> 38.4 us
    ppermute x16 -> x15, starting transfers between devices: 48.8 us -> 31.7 us  [sum_stage(): arrived.append(lax.ppermute(piece, ('row', 'col'), pairs))]
    ppermute x8 -> x4, starting transfers between devices: 20.4 us -> 8.6 us  [sent(): return lax.ppermute(strip, ('row', 'col'), pairs)]
    ppermute x16 -> x15, waiting for transfers between devices: 12.3 us -> 18.5 us  [sum_stage(): arrived.append(lax.ppermute(piece, ('row', 'col'), pairs))]
    pallas_call x1 -> x2, Pallas kernels: 2.94 us -> 8.99 us  [the longest x1 6.13 us: on_device(): pl.pallas_call(first_kernel, out_shape=[jax.ShapeDtypeStruct((4, 16, 16,...]
    pallas_call x1, Pallas kernels: 29.8 us -> 24.8 us  [on_device(): pl.pallas_call(functools.partial(main_kernel, scale), out_shape=[jax.Shap...]
    ppermute x0 -> x1, waiting for transfers between devices: none -> 4.37 us  [reduce_scatter(): other = lax.ppermute(parts[1], ('row', 'col'), pairs)]
    ppermute x0 -> x1, starting transfers between devices: none -> 2.92 us  [reduce_scatter(): other = lax.ppermute(parts[1], ('row', 'col'), pairs)]
    convert_element_type x6 -> x5, other arithmetic: 3.81 us -> 1.48 us  [sum_stage(): return total.astype(BF)]
  transfers between devices with their start and end apart: 26 -> 22, of which waited for: 7 -> 12; matrix products, arithmetic and copies ran while one was open for 1% -> 2% of each run, Pallas kernels for 8% -> 8%
where the time goes in v2:
time: 143 us
  starting transfers between devices  46.6 us (33%)
  Pallas kernels  45.3 us (32%)
  waiting for transfers between devices  38.4 us (27%)
  local copies, waits for them, and re-layouts  7.2 us (5%)
  other arithmetic  4.42 us (3%)
    ppermute x15, starting transfers between devices, sum_stage(): arrived.append(lax.ppermute(piece, ('row', 'col'), pairs))  31.7 us
    pallas_call x1, Pallas kernels, on_device(): pl.pallas_call(functools.partial(main_kernel, scale), out_shape=[jax.Shap...  24.8 us
    ppermute x15, waiting for transfers between devices, sum_stage(): arrived.append(lax.ppermute(piece, ('row', 'col'), pairs))  18.5 us
    ppermute x4, starting transfers between devices, sent(): return lax.ppermute(strip, ('row', 'col'), pairs)  8.6 us
    ppermute x4, waiting for transfers between devices, sent(): return lax.ppermute(strip, ('row', 'col'), pairs)  8.29 us
    pallas_call x1, Pallas kernels, on_device(): pl.pallas_call(weight_kernel, out_shape=[jax.ShapeDtypeStruct((4, 1024, 5...  7.65 us
    ppermute x2, waiting for transfers between devices, reduce_scatter(): total = total + lax.ppermute(piece, ('row', 'col'), pairs).astype(F32)  7.19 us
    pallas_call x1, Pallas kernels, on_device(): pl.pallas_call(first_kernel, out_shape=[jax.ShapeDtypeStruct((4, 16, 16,...  6.13 us
  transfers between devices with their start and end apart: 22, of which 12 were waited for; matrix products, arithmetic and copies ran while one was open for 2% of the time, Pallas kernels for 8%

profile of v2, /device:TPU:6, one launch (start us, length us, event | category | flops | bytes accessed | tf_op | source)
XLA Modules:
  0.0 142.8 jit_solution(15170564289915817593)
XLA Ops:
  0.6 6.1 %first.1 = (bf16[4,16,16,256]{3,2,1,0:T(8,128)(2,1)}, f32[4,17,32,256]{3,2,1,0:T(8,128)}, bf16[23,16,256]{2,1,0:T(8,128)(2,1)}, bf16[23,16,256]{2,1,0:T(8,128)(2,1)}) custom-call(bf16[16,2,32,256]{3,2,1,0:T(8,128)(2,1)} %bitcast.70, f32[16,2,32,256]{3,2,1,0:T(8,128)} %bitcast.69, f32[16,16,256]{2,1,0:T(8,128)} %low_ref.5, bf16[2304,256]{1,0:T(8,128)(2,1)} %w_post.3), custom_call_target="tpu_custom_call" | custom-call | tf_op jit(solution)/shard_map/first/pallas_call | solution.py:391
  6.8 3.7 %collective-permute-start = (bf16[23,16,256]{2,1,0:T(8,128)(2,1)}, bf16[23,16,256]{2,1,0:T(8,128)(2,1)S(1)}, u32[]{:S(2)}, u32[]{:S(2)}) collective-permute-start(bf16[23,16,256]{2,1,0:T(8,128)(2,1)} %get-tuple-element.18), channel_id=1, source_target_pairs={{0,16},{1,17},{2,18},{3,19},{4,20},{5,21},{6,22},{7,23},{8,24},{9,... | collective-permute-start | bytes 565256 | tf_op jit(solution)/shard_map/ppermute | solution.py:385
  10.5 2.1 %collective-permute-start.1 = (bf16[23,16,256]{2,1,0:T(8,128)(2,1)}, bf16[23,16,256]{2,1,0:T(8,128)(2,1)S(1)}, u32[]{:S(2)}, u32[]{:S(2)}) collective-permute-start(bf16[23,16,256]{2,1,0:T(8,128)(2,1)} %get-tuple-element.19), channel_id=1, source_target_pairs={{16,0},{17,1},{18,2},{19,3},{20,4},{21,5},{22,6},{23,7},{24,8},{25... | collective-permute-start | bytes 565256 | tf_op jit(solution)/shard_map/ppermute | solution.py:385
  12.6 2.7 %collective-permute-done.up_ref = bf16[23,16,256]{2,1,0:T(8,128)(2,1)S(1)} collective-permute-done((bf16[23,16,256]{2,1,0:T(8,128)(2,1)}, bf16[23,16,256]{2,1,0:T(8,128)(2,1)S(1)}, u32[]{:S(2)}, u32[]{:S(2)}) %collective-permute-start) | collective-permute-done | bytes 188448 | tf_op jit(solution)/shard_map/ppermute | solution.py:385
  15.3 5.6 %collective-permute-done.1.down_ref = bf16[23,16,256]{2,1,0:T(8,128)(2,1)S(1)} collective-permute-done((bf16[23,16,256]{2,1,0:T(8,128)(2,1)}, bf16[23,16,256]{2,1,0:T(8,128)(2,1)S(1)}, u32[]{:S(2)}, u32[]{:S(2)}) %collective-permute-start.1) | collective-permute-done | bytes 188448 | tf_op jit(solution)/shard_map/ppermute | solution.py:385
  21.6 2.9 %middle.1 = (bf16[24,24,256]{2,1,0:T(8,128)(2,1)}, bf16[24,24,256]{2,1,0:T(8,128)(2,1)}) custom-call(f32[4,17,32,256]{3,2,1,0:T(8,128)} %get-tuple-element.17.part_ref, f32[16,16,256]{2,1,0:T(8,128)} %low_ref.5, bf16[23,16,256]{2,1,0:T(8,128)(2,1)} %copy-done, bf16[23,16,256]{2,1,0:T(8,128)(2,1)} %copy-done.1), custom_call_target="tpu_custom_call" | custom-call | tf_op jit(solution)/shard_map/middle/pallas_call | solution.py:426
  25.7 1.5 %collective-permute-start.3 = (bf16[24,24,256]{2,1,0:T(8,128)(2,1)}, bf16[24,24,256]{2,1,0:T(8,128)(2,1)S(1)}, u32[]{:S(2)}, u32[]{:S(2)}) collective-permute-start(bf16[24,24,256]{2,1,0:T(8,128)(2,1)} %get-tuple-element.21), channel_id=1, source_target_pairs={{1,0},{2,1},{3,2},{4,3},{5,4},{6,5},{7,6},{8,7},{9,8},{10,9},{11,1... | collective-permute-start | bytes 884744 | tf_op jit(solution)/shard_map/ppermute | solution.py:385
  27.2 7.7 %weights.1 = (bf16[4,1024,512]{2,1,0:T(8,128)(2,1)}, bf16[4,2048,256]{2,1,0:T(8,128)(2,1)}, bf16[2304,256]{1,0:T(8,128)(2,1)}, bf16[2304,256]{1,0:T(8,128)(2,1)}) custom-call(bf16[2304,256]{1,0:T(8,128)(2,1)} %w_post.3, bf16[2304,256]{1,0:T(8,128)(2,1)} %w_coarse.3, bf16[2304,512]{1,0:T(8,128)(2,1)} %w_prior.1), custom_call_target="tpu_custom_call" | custom-call | flops 10000000 | bytes 15000000 | tf_op jit(solution)/shard_map/weights/pallas_call | solution.py:412
  36.3 24.8 %tile.1 = (bf16[2,2,1152,512]{3,2,1,0:T(8,128)(2,1)}, bf16[2,18,16,1024]{3,2,1,0:T(8,128)(2,1)}) custom-call(s32[3]{0:T(128)} %pad_add_fusion.place_ref, bf16[4,16,16,256]{3,2,1,0:T(8,128)(2,1)} %get-tuple-element.16.own_ref, f32[4,17,32,256]{3,2,1,0:T(8,128)} %get-tuple-element.17.part_ref, f32[16,16,256]{2,1,0:T(8,128)} %low_ref.5, ...), custom_call_target="tpu_custom_call" | custom-call | tf_op jit(solution)/shard_map/tile/pallas_call | solution.py:438
  61.1 3.3 %slice_bitcast_fusion = bf16[2,1152,512]{2,1,0:T(8,128)(2,1)} fusion(bf16[2,2,1152,512]{3,2,1,0:T(8,128)(2,1)} %get-tuple-element.27), kind=kLoop, calls=%fused_computation.2 | loop fusion | bytes 4718592 | tf_op jit(solution)/shard_map/squeeze | solution.py:54
  64.3 2.9 %collective-permute-start.4 = (bf16[2,1152,512]{2,1,0:T(8,128)(2,1)}, bf16[2,1152,512]{2,1,0:T(8,128)(2,1)S(1)}, u32[]{:S(2)}, u32[]{:S(2)}) collective-permute-start(bf16[2,1152,512]{2,1,0:T(8,128)(2,1)} %slice_bitcast_fusion), channel_id=1, source_target_pairs={{0,1},{1,0},{2,3},{3,2},{4,5},{5,4},{6,7},{7,6},{8,9},{9,8},{10,11... | collective-permute-start | bytes 7077896 | tf_op jit(solution)/shard_map/ppermute | solution.py:54
  67.3 4.4 %collective-permute-done.4 = bf16[2,1152,512]{2,1,0:T(8,128)(2,1)S(1)} collective-permute-done((bf16[2,1152,512]{2,1,0:T(8,128)(2,1)}, bf16[2,1152,512]{2,1,0:T(8,128)(2,1)S(1)}, u32[]{:S(2)}, u32[]{:S(2)}) %collective-permute-start.4) | collective-permute-done | bytes 2359328 | tf_op jit(solution)/shard_map/ppermute | solution.py:54
  71.6 2.3 %fusion = bf16[2,1152,512]{2,1,0:T(8,128)(2,1)S(1)} fusion(bf16[2,1152,512]{2,1,0:T(8,128)(2,1)S(1)} %collective-permute-done.4, bf16[2,2,1152,512]{3,2,1,0:T(8,128)(2,1)} %get-tuple-element.27), kind=kLoop, calls=%fused_computation.1 | loop fusion | flops 4718592 | bytes 7077888 | tf_op jit(solution)/shard_map/convert_element_type | solution.py:55
  74.2 2.3 %collective-permute-start.11 = (bf16[4,72,512]{2,1,0:T(8,128)(2,1)S(1)}, bf16[4,72,512]{2,1,0:T(8,128)(2,1)S(1)}, u32[]{:S(2)}, u32[]{:S(2)}) collective-permute-start(bf16[4,72,512]{2,1,0:T(8,128)(2,1)S(1)} %get-tuple-element.32), channel_id=1, source_target_pairs={{0,2},{1,3},{2,0},{3,1},{4,6},{5,7},{6,4},{7,5},{8,10},{9,11},{10,... | collective-permute-start | bytes 884744 | tf_op jit(solution)/shard_map/ppermute | solution.py:45
  76.5 9.4 %collective-permute-start.12 = (bf16[4,72,512]{2,1,0:T(8,128)(2,1)S(1)}, bf16[4,72,512]{2,1,0:T(8,128)(2,1)}, u32[]{:S(2)}, u32[]{:S(2)}) collective-permute-start(bf16[4,72,512]{2,1,0:T(8,128)(2,1)S(1)} %get-tuple-element.34), channel_id=1, source_target_pairs={{0,6},{1,7},{2,4},{3,5},{4,2},{5,3},{6,0},{7,1},{8,14},{9,15},{10,... | collective-permute-start | bytes 884744 | tf_op jit(solution)/shard_map/ppermute | solution.py:45
  85.9 1.4 collective-permute-start.13
  87.9 3.7 %collective-permute-start.7 = (bf16[4,72,512]{2,1,0:T(8,128)(2,1)S(1)}, bf16[4,72,512]{2,1,0:T(8,128)(2,1)S(1)}, u32[]{:S(2)}, u32[]{:S(2)}) collective-permute-start(bf16[4,72,512]{2,1,0:T(8,128)(2,1)S(1)} %get-tuple-element.36), channel_id=1, source_target_pairs={{0,32},{1,33},{2,34},{3,35},{4,36},{5,37},{6,38},{7,39},{8,40},{9,... | collective-permute-start | bytes 884744 | tf_op jit(solution)/shard_map/ppermute | solution.py:45
  91.5 7.5 %collective-permute-done.12 = bf16[4,72,512]{2,1,0:T(8,128)(2,1)} collective-permute-done((bf16[4,72,512]{2,1,0:T(8,128)(2,1)S(1)}, bf16[4,72,512]{2,1,0:T(8,128)(2,1)}, u32[]{:S(2)}, u32[]{:S(2)}) %collective-permute-start.12) | collective-permute-done | bytes 294944 | tf_op jit(solution)/shard_map/ppermute | solution.py:45
  99.0 1.9 %collective-permute-done.13 = bf16[4,72,512]{2,1,0:T(8,128)(2,1)} collective-permute-done((bf16[4,72,512]{2,1,0:T(8,128)(2,1)S(1)}, bf16[4,72,512]{2,1,0:T(8,128)(2,1)}, u32[]{:S(2)}, u32[]{:S(2)}) %collective-permute-start.13) | collective-permute-done | bytes 294944 | tf_op jit(solution)/shard_map/ppermute | solution.py:45
  102.7 3.7 %collective-permute-start.16 = (bf16[72,512]{1,0:T(8,128)(2,1)S(1)}, bf16[72,512]{1,0:T(8,128)(2,1)S(1)}, u32[]{:S(2)}, u32[]{:S(2)}) collective-permute-start(bf16[72,512]{1,0:T(8,128)(2,1)S(1)} %get-tuple-element.39), channel_id=1, source_target_pairs={{0,32},{1,33},{2,34},{3,35},{4,36},{5,37},{6,38},{7,39},{8,40},{9,... | collective-permute-start | bytes 221192 | tf_op jit(solution)/shard_map/ppermute | solution.py:45
  106.6 1.8 %collective-permute-start.10 = (bf16[72,512]{1,0:T(8,128)(2,1)S(1)}, bf16[72,512]{1,0:T(8,128)(2,1)S(1)}, u32[]{:S(2)}, u32[]{:S(2)}) collective-permute-start(bf16[72,512]{1,0:T(8,128)(2,1)S(1)} %get-tuple-element.42), channel_id=1, source_target_pairs={{0,4},{1,5},{2,6},{3,7},{4,0},{5,1},{6,2},{7,3},{8,12},{9,13},{10,... | collective-permute-start | bytes 221192 | tf_op jit(solution)/shard_map/ppermute | solution.py:45
  110.9 1.8 %collective-permute-done.10 = bf16[72,512]{1,0:T(8,128)(2,1)S(1)} collective-permute-done((bf16[72,512]{1,0:T(8,128)(2,1)S(1)}, bf16[72,512]{1,0:T(8,128)(2,1)S(1)}, u32[]{:S(2)}, u32[]{:S(2)}) %collective-permute-start.10) | collective-permute-done | bytes 73760 | tf_op jit(solution)/shard_map/ppermute | solution.py:45
  112.8 2.2 %collective-permute-done.9 = bf16[72,512]{1,0:T(8,128)(2,1)S(1)} collective-permute-done((bf16[72,512]{1,0:T(8,128)(2,1)S(1)}, bf16[72,512]{1,0:T(8,128)(2,1)S(1)}, u32[]{:S(2)}, u32[]{:S(2)}) %collective-permute-start.9) | collective-permute-done | bytes 73760 | tf_op jit(solution)/shard_map/ppermute | solution.py:45
  115.1 1.7 %collective-permute-start.17 = (bf16[2,18,512]{2,1,0:T(8,128)(2,1)S(1)}, bf16[2,18,512]{2,1,0:T(8,128)(2,1)S(1)}, u32[]{:S(2)}, u32[]{:S(2)}) collective-permute-start(bf16[2,18,512]{2,1,0:T(8,128)(2,1)S(1)} %get-tuple-element.44), channel_id=1, source_target_pairs={{0,64},{1,65},{2,66},{3,67},{4,68},{5,69},{6,70},{7,71},{8,72},{9,... | collective-permute-start | bytes 110600 | tf_op jit(solution)/shard_map/ppermute | solution.py:45
  116.8 4.4 %collective-permute-start.18 = (bf16[2,18,512]{2,1,0:T(8,128)(2,1)S(1)}, bf16[2,18,512]{2,1,0:T(8,128)(2,1)S(1)}, u32[]{:S(2)}, u32[]{:S(2)}) collective-permute-start(bf16[2,18,512]{2,1,0:T(8,128)(2,1)S(1)} %get-tuple-element.46), channel_id=1, source_target_pairs={{0,192},{1,193},{2,194},{3,195},{4,196},{5,197},{6,198},{7,199},{8... | collective-permute-start | bytes 110600 | tf_op jit(solution)/shard_map/ppermute | solution.py:45
  121.2 2.6 %collective-permute-done.18 = bf16[2,18,512]{2,1,0:T(8,128)(2,1)S(1)} collective-permute-done((bf16[2,18,512]{2,1,0:T(8,128)(2,1)S(1)}, bf16[2,18,512]{2,1,0:T(8,128)(2,1)S(1)}, u32[]{:S(2)}, u32[]{:S(2)}) %collective-permute-start.18) | collective-permute-done | bytes 36896 | tf_op jit(solution)/shard_map/ppermute | solution.py:45
  123.8 2.4 %collective-permute-done.19 = bf16[2,18,512]{2,1,0:T(8,128)(2,1)S(1)} collective-permute-done((bf16[2,18,512]{2,1,0:T(8,128)(2,1)S(1)}, bf16[2,18,512]{2,1,0:T(8,128)(2,1)S(1)}, u32[]{:S(2)}, u32[]{:S(2)}) %collective-permute-start.19) | collective-permute-done | bytes 36896 | tf_op jit(solution)/shard_map/ppermute | solution.py:45
  126.3 1.9 %collective-permute-start.20 = (bf16[2,9,512]{2,0,1:T(2,128)(2,1)S(1)}, bf16[2,9,512]{2,0,1:T(2,128)(2,1)S(1)}, u32[]{:S(2)}, u32[]{:S(2)}) collective-permute-start(bf16[2,9,512]{2,0,1:T(2,128)(2,1)S(1)} %get-tuple-element.47), channel_id=1, source_target_pairs={{0,0},{1,128},{2,8},{3,136},{4,16},{5,144},{6,24},{7,152},{8,1},{9... | collective-permute-start | bytes 55304 | tf_op jit(solution)/shard_map/ppermute | solution.py:70
  128.2 1.5 %collective-permute-start.21 = (bf16[2,9,512]{2,0,1:T(2,128)(2,1)S(1)}, bf16[2,9,512]{2,0,1:T(2,128)(2,1)S(1)}, u32[]{:S(2)}, u32[]{:S(2)}) collective-permute-start(bf16[2,9,512]{2,0,1:T(2,128)(2,1)S(1)} %get-tuple-element.48), channel_id=1, source_target_pairs={{0,1},{1,129},{2,9},{3,137},{4,17},{5,145},{6,25},{7,153},{8,0},{9... | collective-permute-start | bytes 55304 | tf_op jit(solution)/shard_map/ppermute | solution.py:70
  129.7 3.9 %feat.1 = bf16[16,2,32,256]{3,2,1,0:T(8,128)(2,1)} custom-call(bf16[2,18,16,1024]{3,2,1,0:T(8,128)(2,1)} %get-tuple-element.25.g_fine, bf16[2304,256]{1,0:T(8,128)(2,1)} %get-tuple-element.26.w_post_t), custom_call_target="tpu_custom_call" | custom-call | flops 1200000000 | bytes 3000000 | tf_op jit(solution)/shard_map/feat/pallas_call | solution.py:463
  133.6 2.3 %collective-permute-done.20 = bf16[2,9,512]{2,0,1:T(2,128)(2,1)S(1)} collective-permute-done((bf16[2,9,512]{2,0,1:T(2,128)(2,1)S(1)}, bf16[2,9,512]{2,0,1:T(2,128)(2,1)S(1)}, u32[]{:S(2)}, u32[]{:S(2)}) %collective-permute-start.20) | collective-permute-done | bytes 18464 | tf_op jit(solution)/shard_map/ppermute | solution.py:70
  135.9 4.9 %collective-permute-done.21 = bf16[2,9,512]{2,0,1:T(2,128)(2,1)S(1)} collective-permute-done((bf16[2,9,512]{2,0,1:T(2,128)(2,1)S(1)}, bf16[2,9,512]{2,0,1:T(2,128)(2,1)S(1)}, u32[]{:S(2)}, u32[]{:S(2)}) %collective-permute-start.21) | collective-permute-done | bytes 18464 | tf_op jit(solution)/shard_map/ppermute | solution.py:70
  (51 shorter events, 10.8 us)
Async XLA Ops:
  6.8 8.6 %collective-permute-start = (bf16[23,16,256]{2,1,0:T(8,128)(2,1)}, bf16[23,16,256]{2,1,0:T(8,128)(2,1)S(1)}, u32[]{:S(2)}, u32[]{:S(2)}) collective-permute-start(bf16[23,16,256]{2,1,0:T(8,128)(2,1)} %get-tuple-element.18), channel_id=1, source_target_pairs={{0,16},{1,17},{2,18},{3,19},{4,20},{5,21},{6,22},{7,23},{8,24},{9,... | collective-permute-start | bytes 565256 | tf_op jit(solution)/shard_map/ppermute | solution.py:385
  10.5 10.4 %collective-permute-start.1 = (bf16[23,16,256]{2,1,0:T(8,128)(2,1)}, bf16[23,16,256]{2,1,0:T(8,128)(2,1)S(1)}, u32[]{:S(2)}, u32[]{:S(2)}) collective-permute-start(bf16[23,16,256]{2,1,0:T(8,128)(2,1)} %get-tuple-element.19), channel_id=1, source_target_pairs={{16,0},{17,1},{18,2},{19,3},{20,4},{21,5},{22,6},{23,7},{24,8},{25... | collective-permute-start | bytes 565256 | tf_op jit(solution)/shard_map/ppermute | solution.py:385
  15.3 5.6 %copy-start = (bf16[23,16,256]{2,1,0:T(8,128)(2,1)}, bf16[23,16,256]{2,1,0:T(8,128)(2,1)S(1)}, u32[]{:S(2)}) copy-start(bf16[23,16,256]{2,1,0:T(8,128)(2,1)S(1)} %collective-permute-done.up_ref) | copy-start | bytes 565252
  20.9 0.7 copy-start.1
  24.4 11.0 %collective-permute-start.2 = (bf16[24,24,256]{2,1,0:T(8,128)(2,1)}, bf16[24,24,256]{2,1,0:T(8,128)(2,1)S(1)}, u32[]{:S(2)}, u32[]{:S(2)}) collective-permute-start(bf16[24,24,256]{2,1,0:T(8,128)(2,1)} %get-tuple-element.20), channel_id=1, source_target_pairs={{0,1},{1,2},{2,3},{3,4},{4,5},{5,6},{6,7},{7,8},{8,9},{9,10},{10,1... | collective-permute-start | bytes 884744 | tf_op jit(solution)/shard_map/ppermute | solution.py:385
  25.7 9.8 %collective-permute-start.3 = (bf16[24,24,256]{2,1,0:T(8,128)(2,1)}, bf16[24,24,256]{2,1,0:T(8,128)(2,1)S(1)}, u32[]{:S(2)}, u32[]{:S(2)}) collective-permute-start(bf16[24,24,256]{2,1,0:T(8,128)(2,1)} %get-tuple-element.21), channel_id=1, source_target_pairs={{1,0},{2,1},{3,2},{4,3},{5,4},{6,5},{7,6},{8,7},{9,8},{10,9},{11,1... | collective-permute-start | bytes 884744 | tf_op jit(solution)/shard_map/ppermute | solution.py:385
  35.5 0.7 copy-start.2
  35.5 0.8 copy-start.3
  64.3 7.3 %collective-permute-start.4 = (bf16[2,1152,512]{2,1,0:T(8,128)(2,1)}, bf16[2,1152,512]{2,1,0:T(8,128)(2,1)S(1)}, u32[]{:S(2)}, u32[]{:S(2)}) collective-permute-start(bf16[2,1152,512]{2,1,0:T(8,128)(2,1)} %slice_bitcast_fusion), channel_id=1, source_target_pairs={{0,1},{1,0},{2,3},{3,2},{4,5},{5,4},{6,7},{7,6},{8,9},{9,8},{10,11... | collective-permute-start | bytes 7077896 | tf_op jit(solution)/shard_map/ppermute | solution.py:54
  74.2 13.7 %collective-permute-start.11 = (bf16[4,72,512]{2,1,0:T(8,128)(2,1)S(1)}, bf16[4,72,512]{2,1,0:T(8,128)(2,1)S(1)}, u32[]{:S(2)}, u32[]{:S(2)}) collective-permute-start(bf16[4,72,512]{2,1,0:T(8,128)(2,1)S(1)} %get-tuple-element.32), channel_id=1, source_target_pairs={{0,2},{1,3},{2,0},{3,1},{4,6},{5,7},{6,4},{7,5},{8,10},{9,11},{10,... | collective-permute-start | bytes 884744 | tf_op jit(solution)/shard_map/ppermute | solution.py:45
  76.5 22.5 %collective-permute-start.12 = (bf16[4,72,512]{2,1,0:T(8,128)(2,1)S(1)}, bf16[4,72,512]{2,1,0:T(8,128)(2,1)}, u32[]{:S(2)}, u32[]{:S(2)}) collective-permute-start(bf16[4,72,512]{2,1,0:T(8,128)(2,1)S(1)} %get-tuple-element.34), channel_id=1, source_target_pairs={{0,6},{1,7},{2,4},{3,5},{4,2},{5,3},{6,0},{7,1},{8,14},{9,15},{10,... | collective-permute-start | bytes 884744 | tf_op jit(solution)/shard_map/ppermute | solution.py:45
  85.9 15.0 %collective-permute-start.13 = (bf16[4,72,512]{2,1,0:T(8,128)(2,1)S(1)}, bf16[4,72,512]{2,1,0:T(8,128)(2,1)}, u32[]{:S(2)}, u32[]{:S(2)}) collective-permute-start(bf16[4,72,512]{2,1,0:T(8,128)(2,1)S(1)} %get-tuple-element.33), channel_id=1, source_target_pairs={{0,4},{1,5},{2,6},{3,7},{4,0},{5,1},{6,2},{7,3},{8,12},{9,13},{10,... | collective-permute-start | bytes 884744 | tf_op jit(solution)/shard_map/ppermute | solution.py:45
  87.4 15.3 %collective-permute-start.5 = (bf16[4,72,512]{2,1,0:T(8,128)(2,1)S(1)}, bf16[4,72,512]{2,1,0:T(8,128)(2,1)S(1)}, u32[]{:S(2)}, u32[]{:S(2)}) collective-permute-start(bf16[4,72,512]{2,1,0:T(8,128)(2,1)S(1)} %get-tuple-element.35), channel_id=1, source_target_pairs={{0,16},{1,17},{2,18},{3,19},{4,20},{5,21},{6,22},{7,23},{8,24},{9,... | collective-permute-start | bytes 884744 | tf_op jit(solution)/shard_map/ppermute | solution.py:45
  87.5 18.9 %collective-permute-start.6 = (bf16[4,72,512]{2,1,0:T(8,128)(2,1)S(1)}, bf16[4,72,512]{2,1,0:T(8,128)(2,1)S(1)}, u32[]{:S(2)}, u32[]{:S(2)}) collective-permute-start(bf16[4,72,512]{2,1,0:T(8,128)(2,1)S(1)} %get-tuple-element.37), channel_id=1, source_target_pairs={{0,48},{1,49},{2,50},{3,51},{4,52},{5,53},{6,54},{7,55},{8,56},{9,... | collective-permute-start | bytes 884744 | tf_op jit(solution)/shard_map/ppermute | solution.py:45
  87.9 18.5 %collective-permute-start.7 = (bf16[4,72,512]{2,1,0:T(8,128)(2,1)S(1)}, bf16[4,72,512]{2,1,0:T(8,128)(2,1)S(1)}, u32[]{:S(2)}, u32[]{:S(2)}) collective-permute-start(bf16[4,72,512]{2,1,0:T(8,128)(2,1)S(1)} %get-tuple-element.36), channel_id=1, source_target_pairs={{0,32},{1,33},{2,34},{3,35},{4,36},{5,37},{6,38},{7,39},{8,40},{9,... | collective-permute-start | bytes 884744 | tf_op jit(solution)/shard_map/ppermute | solution.py:45
  102.2 7.2 %collective-permute-start.14 = (bf16[72,512]{1,0:T(8,128)(2,1)S(1)}, bf16[72,512]{1,0:T(8,128)(2,1)S(1)}, u32[]{:S(2)}, u32[]{:S(2)}) collective-permute-start(bf16[72,512]{1,0:T(8,128)(2,1)S(1)} %get-tuple-element.38), channel_id=1, source_target_pairs={{0,16},{1,17},{2,18},{3,19},{4,20},{5,21},{6,22},{7,23},{8,24},{9,... | collective-permute-start | bytes 221192 | tf_op jit(solution)/shard_map/ppermute | solution.py:45
  102.3 8.5 %collective-permute-start.15 = (bf16[72,512]{1,0:T(8,128)(2,1)S(1)}, bf16[72,512]{1,0:T(8,128)(2,1)S(1)}, u32[]{:S(2)}, u32[]{:S(2)}) collective-permute-start(bf16[72,512]{1,0:T(8,128)(2,1)S(1)} %get-tuple-element.40), channel_id=1, source_target_pairs={{0,48},{1,49},{2,50},{3,51},{4,52},{5,53},{6,54},{7,55},{8,56},{9,... | collective-permute-start | bytes 221192 | tf_op jit(solution)/shard_map/ppermute | solution.py:45
  102.7 8.1 %collective-permute-start.16 = (bf16[72,512]{1,0:T(8,128)(2,1)S(1)}, bf16[72,512]{1,0:T(8,128)(2,1)S(1)}, u32[]{:S(2)}, u32[]{:S(2)}) collective-permute-start(bf16[72,512]{1,0:T(8,128)(2,1)S(1)} %get-tuple-element.39), channel_id=1, source_target_pairs={{0,32},{1,33},{2,34},{3,35},{4,36},{5,37},{6,38},{7,39},{8,40},{9,... | collective-permute-start | bytes 221192 | tf_op jit(solution)/shard_map/ppermute | solution.py:45
  106.6 6.1 %collective-permute-start.10 = (bf16[72,512]{1,0:T(8,128)(2,1)S(1)}, bf16[72,512]{1,0:T(8,128)(2,1)S(1)}, u32[]{:S(2)}, u32[]{:S(2)}) collective-permute-start(bf16[72,512]{1,0:T(8,128)(2,1)S(1)} %get-tuple-element.42), channel_id=1, source_target_pairs={{0,4},{1,5},{2,6},{3,7},{4,0},{5,1},{6,2},{7,3},{8,12},{9,13},{10,... | collective-permute-start | bytes 221192 | tf_op jit(solution)/shard_map/ppermute | solution.py:45
  108.4 4.4 %collective-permute-start.8 = (bf16[72,512]{1,0:T(8,128)(2,1)S(1)}, bf16[72,512]{1,0:T(8,128)(2,1)S(1)}, u32[]{:S(2)}, u32[]{:S(2)}) collective-permute-start(bf16[72,512]{1,0:T(8,128)(2,1)S(1)} %get-tuple-element.41), channel_id=1, source_target_pairs={{0,2},{1,3},{2,0},{3,1},{4,6},{5,7},{6,4},{7,5},{8,10},{9,11},{10,... | collective-permute-start | bytes 221192 | tf_op jit(solution)/shard_map/ppermute | solution.py:45
  109.4 5.6 %collective-permute-start.9 = (bf16[72,512]{1,0:T(8,128)(2,1)S(1)}, bf16[72,512]{1,0:T(8,128)(2,1)S(1)}, u32[]{:S(2)}, u32[]{:S(2)}) collective-permute-start(bf16[72,512]{1,0:T(8,128)(2,1)S(1)} %get-tuple-element.43), channel_id=1, source_target_pairs={{0,6},{1,7},{2,4},{3,5},{4,2},{5,3},{6,0},{7,1},{8,14},{9,15},{10,... | collective-permute-start | bytes 221192 | tf_op jit(solution)/shard_map/ppermute | solution.py:45
  115.1 6.1 %collective-permute-start.17 = (bf16[2,18,512]{2,1,0:T(8,128)(2,1)S(1)}, bf16[2,18,512]{2,1,0:T(8,128)(2,1)S(1)}, u32[]{:S(2)}, u32[]{:S(2)}) collective-permute-start(bf16[2,18,512]{2,1,0:T(8,128)(2,1)S(1)} %get-tuple-element.44), channel_id=1, source_target_pairs={{0,64},{1,65},{2,66},{3,67},{4,68},{5,69},{6,70},{7,71},{8,72},{9,... | collective-permute-start | bytes 110600 | tf_op jit(solution)/shard_map/ppermute | solution.py:45
  116.8 7.0 %collective-permute-start.18 = (bf16[2,18,512]{2,1,0:T(8,128)(2,1)S(1)}, bf16[2,18,512]{2,1,0:T(8,128)(2,1)S(1)}, u32[]{:S(2)}, u32[]{:S(2)}) collective-permute-start(bf16[2,18,512]{2,1,0:T(8,128)(2,1)S(1)} %get-tuple-element.46), channel_id=1, source_target_pairs={{0,192},{1,193},{2,194},{3,195},{4,196},{5,197},{6,198},{7,199},{8... | collective-permute-start | bytes 110600 | tf_op jit(solution)/shard_map/ppermute | solution.py:45
  121.2 5.0 %collective-permute-start.19 = (bf16[2,18,512]{2,1,0:T(8,128)(2,1)S(1)}, bf16[2,18,512]{2,1,0:T(8,128)(2,1)S(1)}, u32[]{:S(2)}, u32[]{:S(2)}) collective-permute-start(bf16[2,18,512]{2,1,0:T(8,128)(2,1)S(1)} %get-tuple-element.45), channel_id=1, source_target_pairs={{0,128},{1,129},{2,130},{3,131},{4,132},{5,133},{6,134},{7,135},{8... | collective-permute-start | bytes 110600 | tf_op jit(solution)/shard_map/ppermute | solution.py:45
  126.3 9.6 %collective-permute-start.20 = (bf16[2,9,512]{2,0,1:T(2,128)(2,1)S(1)}, bf16[2,9,512]{2,0,1:T(2,128)(2,1)S(1)}, u32[]{:S(2)}, u32[]{:S(2)}) collective-permute-start(bf16[2,9,512]{2,0,1:T(2,128)(2,1)S(1)} %get-tuple-element.47), channel_id=1, source_target_pairs={{0,0},{1,128},{2,8},{3,136},{4,16},{5,144},{6,24},{7,152},{8,1},{9... | collective-permute-start | bytes 55304 | tf_op jit(solution)/shard_map/ppermute | solution.py:70
  128.2 12.6 %collective-permute-start.21 = (bf16[2,9,512]{2,0,1:T(2,128)(2,1)S(1)}, bf16[2,9,512]{2,0,1:T(2,128)(2,1)S(1)}, u32[]{:S(2)}, u32[]{:S(2)}) collective-permute-start(bf16[2,9,512]{2,0,1:T(2,128)(2,1)S(1)} %get-tuple-element.48), channel_id=1, source_target_pairs={{0,1},{1,129},{2,9},{3,137},{4,17},{5,145},{6,25},{7,153},{8,0},{9... | collective-permute-start | bytes 55304 | tf_op jit(solution)/shard_map/ppermute | solution.py:70

commit v3 on v2

--- a/solution.py
+++ b/solution.py
@@ -12,7 +12,6 @@
 F32 = jnp.float32
 VARIANT = ((1, -1), (0, 0), (1, 0), (0, 1))
 FOLD = (3, 1, 2, 0)
-VMEM_LIMIT = 60 * 1024 * 1024
 
 
 def digits():
@@ -49,9 +48,9 @@
     return total.astype(BF)
 
 
-def reduce_scatter(parts):
+def reduce_scatter(parts, beside):
     pairs = [(index_of(p), index_of(flipped(p, "core", 1))) for p in digits()]
-    other = lax.ppermute(parts[1], ("row", "col"), pairs)
+    other, beside = lax.optimization_barrier((lax.ppermute(parts[1], ("row", "col"), pairs), beside))
     parts = (parts[0].astype(F32) + other.astype(F32)).astype(BF)
     first = parts[0].reshape(4, 4, 72, 512)
     second = parts[1].reshape(4, 4, 72, 512)
@@ -68,7 +67,11 @@
             pairs.append((index_of(p), chunk))
         piece = lax.dynamic_index_in_dim(halves, (last + flip) % 2, 1, keepdims=False)
         total = total + lax.ppermute(piece, ("row", "col"), pairs).astype(F32)
-    return total
+    return total, beside
+
+
+def room(mib):
+    return pltpu.CompilerParams(vmem_limit_bytes=mib * 1024 * 1024)
 
 
 def in_vmem(count):
@@ -387,7 +390,6 @@
 
 def on_device(feat, noise_fine, noise_coarse, w_post, w_coarse, w_prior):
     scale = 1.0 / 512.0
-    params = pltpu.CompilerParams(vmem_limit_bytes=VMEM_LIMIT)
     own, part, top, bottom = pl.pallas_call(
         first_kernel,
         out_shape=[
@@ -405,7 +407,7 @@
             pltpu.VMEM((2, 18, 32, 1024), BF),
             pltpu.VMEM((32, 256), F32),
         ],
-        compiler_params=params,
+        compiler_params=room(16),
         name="first",
     )(feat.reshape(16, 2, 32, 256), noise_fine.reshape(16, 2, 32, 256), noise_coarse, w_post)
     from_up, from_down = sent(bottom, 1, 0), sent(top, -1, 0)
@@ -419,7 +421,7 @@
         ],
         in_specs=in_vmem(3),
         out_specs=in_vmem(4),
-        compiler_params=params,
+        compiler_params=room(20),
         cost_estimate=pl.CostEstimate(flops=10000000, bytes_accessed=15000000, transcendentals=0),
         name="weights",
     )(w_post, w_coarse, w_prior)
@@ -429,7 +431,7 @@
         in_specs=in_vmem(4),
         out_specs=in_vmem(2),
         scratch_shapes=[pltpu.VMEM((24, 24, 256), F32), pltpu.VMEM((32, 256), F32)],
-        compiler_params=params,
+        compiler_params=room(10),
         name="middle",
     )(part, noise_coarse, from_up, from_down)
     from_left, from_right = sent(right, 0, 1), sent(left, 0, -1)
@@ -456,7 +458,7 @@
             pltpu.VMEM((20, 16, 768), BF),
             pltpu.VMEM((32, 256), F32),
         ],
-        compiler_params=params,
+        compiler_params=room(28),
         name="tile",
     )(place, own, part, noise_coarse, from_up, from_down, from_left, from_right,
       w_coarse, fold, fold_t, w_coarse_t)
@@ -466,11 +468,11 @@
         in_specs=in_vmem(2),
         out_specs=pl.BlockSpec(memory_space=pltpu.VMEM),
         scratch_shapes=[pltpu.VMEM((16, 2, 2, 32, 128), F32)],
-        compiler_params=params,
+        compiler_params=room(12),
         cost_estimate=pl.CostEstimate(flops=1200000000, bytes_accessed=3000000, transcendentals=0),
         name="feat",
     )(g_fine, w_post_t).reshape(32, 32, 256)
-    summed = reduce_scatter(grads)
+    summed, grad_feat = reduce_scatter(grads, grad_feat)
     return grad_feat, summed[1, :, 256:].reshape(-1), summed[1, :, :256].reshape(-1), summed[0].reshape(-1)
 
 

time: 143 us -> 137 us (0.958)
  Pallas kernels: 45.3 us -> 26.9 us
  local copies, waits for them, and re-layouts: 7.2 us -> 15 us
  waiting for transfers between devices: 38.4 us -> 40.5 us
  starting transfers between devices: 46.6 us -> 48.1 us
    unnamed x9 -> x39, local copies, waits for them, and re-layouts: 1.51 us -> 11 us
    pallas_call x1, Pallas kernels: 24.8 us -> 18.5 us  [on_device(): pl.pallas_call(functools.partial(main_kernel, scale), out_shape=[jax.Shap...]
    pallas_call x1, Pallas kernels: 7.65 us -> 2.07 us  [on_device(): pl.pallas_call(weight_kernel, out_shape=[jax.ShapeDtypeStruct((4, 1024, 5...]
    ppermute x2, waiting for transfers between devices: 7.19 us -> 11.7 us  [reduce_scatter(): total = total + lax.ppermute(piece, ('row', 'col'), pairs).astype(F32)]
    pallas_call x1, Pallas kernels: 6.13 us -> 2.85 us  [on_device(): pl.pallas_call(first_kernel, out_shape=[jax.ShapeDtypeStruct((4, 16, 16,...]
    ppermute x1, waiting for transfers between devices: 4.37 us -> 2.25 us  [reduce_scatter(): lax.ppermute(parts[1], ('row', 'col'), pairs)]
    ppermute x15, starting transfers between devices: 31.7 us -> 33.7 us  [sum_stage(): arrived.append(lax.ppermute(piece, ('row', 'col'), pairs))]
    squeeze x1, local copies, waits for them, and re-layouts: 3.26 us -> 1.6 us  [reduce_scatter(): parts[1]]
  transfers between devices with their start and end apart: 22 -> 22, of which waited for: 12 -> 12; matrix products, arithmetic and copies ran while one was open for 2% -> 1% of each run, Pallas kernels for 8% -> 3%
where the time goes in v3:
time: 137 us; the launch traced here: 136 us
  starting transfers between devices  48.1 us (35%)
  waiting for transfers between devices  40.5 us (30%)
  Pallas kernels  26.9 us (20%)
  local copies, waits for them, and re-layouts  15 us (11%)
  other arithmetic  4.61 us (3%)
    ppermute x15, starting transfers between devices, sum_stage(): arrived.append(lax.ppermute(piece, ('row', 'col'), pairs))  33.7 us
    ppermute x15, waiting for transfers between devices, sum_stage(): arrived.append(lax.ppermute(piece, ('row', 'col'), pairs))  18.5 us
    pallas_call x1, Pallas kernels, on_device(): pl.pallas_call(functools.partial(main_kernel, scale), out_shape=[jax.Shap...  18.5 us
    ppermute x2, waiting for transfers between devices, reduce_scatter(): total = total + lax.ppermute(piece, ('row', 'col'), pairs).astype(F32)  11.7 us
    unnamed x39, local copies, waits for them, and re-layouts  11 us
    ppermute x4, starting transfers between devices, sent(): return lax.ppermute(strip, ('row', 'col'), pairs)  9.32 us
    ppermute x4, waiting for transfers between devices, sent(): return lax.ppermute(strip, ('row', 'col'), pairs)  8.08 us
    convert_element_type x1, other arithmetic, reduce_scatter(): parts = (parts[0].astype(F32) + other.astype(F32)).astype(BF)  3.04 us
  transfers between devices with their start and end apart: 22, of which 12 were waited for; matrix products, arithmetic and copies ran while one was open for 1% of the time, Pallas kernels for 3%

profile of v3, /device:TPU:6, one launch (start us, length us, event | category | flops | bytes accessed | tf_op | source)
XLA Modules:
  0.0 136.1 jit_solution(9029842404911969936)
XLA Ops:
  5.1 2.8 %first.1 = (bf16[4,16,16,256]{3,2,1,0:T(8,128)(2,1)S(1)}, f32[4,17,32,256]{3,2,1,0:T(8,128)S(1)}, bf16[23,16,256]{2,1,0:T(8,128)(2,1)S(1)}, bf16[23,16,256]{2,1,0:T(8,128)(2,1)S(1)}) custom-call(bf16[16,2,32,256]{3,2,1,0:T(8,128)(2,1)S(1)} %bitcast.66, f32[16,2,32,256]{3,2,1,0:T(8,128)S(1)} %bitcast.65, f32[16,16,256]{2,1,0:T(8,128)S(1)} %copy-done.4, ...), custom_call_target="tpu_custom_call" | custom-call | tf_op jit(solution)/shard_map/first/pallas_call | solution.py:393
  8.0 3.7 %collective-permute-start = (bf16[23,16,256]{2,1,0:T(8,128)(2,1)S(1)}, bf16[23,16,256]{2,1,0:T(8,128)(2,1)S(1)}, u32[]{:S(2)}, u32[]{:S(2)}) collective-permute-start(bf16[23,16,256]{2,1,0:T(8,128)(2,1)S(1)} %get-tuple-element.20), channel_id=1, source_target_pairs={{0,16},{1,17},{2,18},{3,19},{4,20},{5,21},{6,22},{7,23},{8,24},{9,... | collective-permute-start | bytes 565256 | tf_op jit(solution)/shard_map/ppermute | solution.py:388
  11.7 2.1 %collective-permute-start.1 = (bf16[23,16,256]{2,1,0:T(8,128)(2,1)S(1)}, bf16[23,16,256]{2,1,0:T(8,128)(2,1)S(1)}, u32[]{:S(2)}, u32[]{:S(2)}) collective-permute-start(bf16[23,16,256]{2,1,0:T(8,128)(2,1)S(1)} %get-tuple-element.21), channel_id=1, source_target_pairs={{16,0},{17,1},{18,2},{19,3},{20,4},{21,5},{22,6},{23,7},{24,8},{25... | collective-permute-start | bytes 565256 | tf_op jit(solution)/shard_map/ppermute | solution.py:388
  13.8 2.5 %collective-permute-done.up_ref = bf16[23,16,256]{2,1,0:T(8,128)(2,1)S(1)} collective-permute-done((bf16[23,16,256]{2,1,0:T(8,128)(2,1)S(1)}, bf16[23,16,256]{2,1,0:T(8,128)(2,1)S(1)}, u32[]{:S(2)}, u32[]{:S(2)}) %collective-permute-start) | collective-permute-done | bytes 188448 | tf_op jit(solution)/shard_map/ppermute | solution.py:388
  16.3 5.6 %collective-permute-done.1.down_ref = bf16[23,16,256]{2,1,0:T(8,128)(2,1)S(1)} collective-permute-done((bf16[23,16,256]{2,1,0:T(8,128)(2,1)S(1)}, bf16[23,16,256]{2,1,0:T(8,128)(2,1)S(1)}, u32[]{:S(2)}, u32[]{:S(2)}) %collective-permute-start.1) | collective-permute-done | bytes 188448 | tf_op jit(solution)/shard_map/ppermute | solution.py:388
  23.2 2.0 %collective-permute-start.2 = (bf16[24,24,256]{2,1,0:T(8,128)(2,1)}, bf16[24,24,256]{2,1,0:T(8,128)(2,1)}, u32[]{:S(2)}, u32[]{:S(2)}) collective-permute-start(bf16[24,24,256]{2,1,0:T(8,128)(2,1)} %get-tuple-element.22), channel_id=1, source_target_pairs={{0,1},{1,2},{2,3},{3,4},{4,5},{5,6},{6,7},{7,8},{8,9},{9,10},{10,1... | collective-permute-start | bytes 884744 | tf_op jit(solution)/shard_map/ppermute | solution.py:388
  25.2 1.5 %collective-permute-start.3 = (bf16[24,24,256]{2,1,0:T(8,128)(2,1)}, bf16[24,24,256]{2,1,0:T(8,128)(2,1)}, u32[]{:S(2)}, u32[]{:S(2)}) collective-permute-start(bf16[24,24,256]{2,1,0:T(8,128)(2,1)} %get-tuple-element.23), channel_id=1, source_target_pairs={{1,0},{2,1},{3,2},{4,3},{5,4},{6,5},{7,6},{8,7},{9,8},{10,9},{11,1... | collective-permute-start | bytes 884744 | tf_op jit(solution)/shard_map/ppermute | solution.py:388
  28.0 1.7 %copy-done.6 = bf16[2304,512]{1,0:T(8,128)(2,1)S(1)} copy-done((bf16[2304,512]{1,0:T(8,128)(2,1)S(1)}, bf16[2304,512]{1,0:T(8,128)(2,1)}, u32[]{:S(2)}) %copy-start.6) | copy-done | bytes 2359320
  29.6 2.1 %weights.1 = (bf16[4,1024,512]{2,1,0:T(8,128)(2,1)S(1)}, bf16[4,2048,256]{2,1,0:T(8,128)(2,1)S(1)}, bf16[2304,256]{1,0:T(8,128)(2,1)S(1)}, bf16[2304,256]{1,0:T(8,128)(2,1)S(1)}) custom-call(bf16[2304,256]{1,0:T(8,128)(2,1)S(1)} %copy-done.3, bf16[2304,256]{1,0:T(8,128)(2,1)S(1)} %copy-done, bf16[2304,512]{1,0:T(8,128)(2,1)S(1)} %copy-done.6), custom_call_target="tpu_custom_call" | custom-call | flops 10000000 | bytes 15000000 | tf_op jit(solution)/shard_map/weights/pallas_call | solution.py:414
  32.8 18.5 %tile.1 = (bf16[2,2,1152,512]{3,2,1,0:T(8,128)(2,1)S(1)}, bf16[2,18,16,1024]{3,2,1,0:T(8,128)(2,1)S(1)}) custom-call(s32[3]{0:T(128)S(1)} %pad_add_fusion.place_ref, bf16[4,16,16,256]{3,2,1,0:T(8,128)(2,1)S(1)} %copy-done.13, f32[4,17,32,256]{3,2,1,0:T(8,128)S(1)} %get-tuple-element.19.part_ref, f32[16,16,256]{2,1,0:T(8,128)S(1)} %copy-done.5, ...), custom_call_target="tpu_custom_call" | custom-call | tf_op jit(solution)/shard_map/tile/pallas_call | solution.py:440
  52.4 1.6 %slice_bitcast_fusion = bf16[2,1152,512]{2,1,0:T(8,128)(2,1)} fusion(bf16[2,2,1152,512]{3,2,1,0:T(8,128)(2,1)S(1)} %get-tuple-element.27), kind=kLoop, calls=%fused_computation.2 | loop fusion | bytes 4718592 | tf_op jit(solution)/shard_map/squeeze | solution.py:53
  54.0 1.5 %copy-done.1 = bf16[2,2,1152,512]{3,2,1,0:T(8,128)(2,1)} copy-done((bf16[2,2,1152,512]{3,2,1,0:T(8,128)(2,1)}, bf16[2,2,1152,512]{3,2,1,0:T(8,128)(2,1)S(1)}, u32[]{:S(2)}) %copy-start.1) | copy-done | bytes 4718616
  55.5 2.3 %collective-permute-start.4 = (bf16[2,1152,512]{2,1,0:T(8,128)(2,1)}, bf16[2,1152,512]{2,1,0:T(8,128)(2,1)}, u32[]{:S(2)}, u32[]{:S(2)}) collective-permute-start(bf16[2,1152,512]{2,1,0:T(8,128)(2,1)} %slice_bitcast_fusion), channel_id=1, source_target_pairs={{0,1},{1,0},{2,3},{3,2},{4,5},{5,4},{6,7},{7,6},{8,9},{9,8},{10,11... | collective-permute-start | bytes 7077896 | tf_op jit(solution)/shard_map/ppermute | solution.py:53
  57.8 2.2 %feat.1 = bf16[16,2,32,256]{3,2,1,0:T(8,128)(2,1)} custom-call(bf16[2,18,16,1024]{3,2,1,0:T(8,128)(2,1)S(1)} %copy-done.18, bf16[2304,256]{1,0:T(8,128)(2,1)S(1)} %copy-done.16), custom_call_target="tpu_custom_call" | custom-call | flops 1200000000 | bytes 3000000 | tf_op jit(solution)/shard_map/feat/pallas_call | solution.py:465
  60.1 2.3 %collective-permute-done.4 = bf16[2,1152,512]{2,1,0:T(8,128)(2,1)} collective-permute-done((bf16[2,1152,512]{2,1,0:T(8,128)(2,1)}, bf16[2,1152,512]{2,1,0:T(8,128)(2,1)}, u32[]{:S(2)}, u32[]{:S(2)}) %collective-permute-start.4) | collective-permute-done | bytes 2359328 | tf_op jit(solution)/shard_map/ppermute | solution.py:53
  62.3 3.0 %fusion = bf16[2,1152,512]{2,1,0:T(8,128)(2,1)S(1)} fusion(bf16[2,1152,512]{2,1,0:T(8,128)(2,1)} %collective-permute-done.4, bf16[2,2,1152,512]{3,2,1,0:T(8,128)(2,1)} %copy-done.1), kind=kLoop, calls=%fused_computation.1 | loop fusion | flops 4718592 | bytes 7077888 | tf_op jit(solution)/shard_map/convert_element_type | solution.py:54
  65.6 2.0 %collective-permute-start.11 = (bf16[4,72,512]{2,1,0:T(8,128)(2,1)S(1)}, bf16[4,72,512]{2,1,0:T(8,128)(2,1)S(1)}, u32[]{:S(2)}, u32[]{:S(2)}) collective-permute-start(bf16[4,72,512]{2,1,0:T(8,128)(2,1)S(1)} %get-tuple-element.36), channel_id=1, source_target_pairs={{0,2},{1,3},{2,0},{3,1},{4,6},{5,7},{6,4},{7,5},{8,10},{9,11},{10,... | collective-permute-start | bytes 884744 | tf_op jit(solution)/shard_map/ppermute | solution.py:44
  67.6 11.7 %collective-permute-start.12 = (bf16[4,72,512]{2,1,0:T(8,128)(2,1)S(1)}, bf16[4,72,512]{2,1,0:T(8,128)(2,1)}, u32[]{:S(2)}, u32[]{:S(2)}) collective-permute-start(bf16[4,72,512]{2,1,0:T(8,128)(2,1)S(1)} %get-tuple-element.38), channel_id=1, source_target_pairs={{0,6},{1,7},{2,4},{3,5},{4,2},{5,3},{6,0},{7,1},{8,14},{9,15},{10,... | collective-permute-start | bytes 884744 | tf_op jit(solution)/shard_map/ppermute | solution.py:44
  81.3 3.7 %collective-permute-start.7 = (bf16[4,72,512]{2,1,0:T(8,128)(2,1)S(1)}, bf16[4,72,512]{2,1,0:T(8,128)(2,1)S(1)}, u32[]{:S(2)}, u32[]{:S(2)}) collective-permute-start(bf16[4,72,512]{2,1,0:T(8,128)(2,1)S(1)} %get-tuple-element.40), channel_id=1, source_target_pairs={{0,32},{1,33},{2,34},{3,35},{4,36},{5,37},{6,38},{7,39},{8,40},{9,... | collective-permute-start | bytes 884744 | tf_op jit(solution)/shard_map/ppermute | solution.py:44
  84.9 7.5 %collective-permute-done.12 = bf16[4,72,512]{2,1,0:T(8,128)(2,1)} collective-permute-done((bf16[4,72,512]{2,1,0:T(8,128)(2,1)S(1)}, bf16[4,72,512]{2,1,0:T(8,128)(2,1)}, u32[]{:S(2)}, u32[]{:S(2)}) %collective-permute-start.12) | collective-permute-done | bytes 294944 | tf_op jit(solution)/shard_map/ppermute | solution.py:44
  92.4 1.9 %collective-permute-done.13 = bf16[4,72,512]{2,1,0:T(8,128)(2,1)} collective-permute-done((bf16[4,72,512]{2,1,0:T(8,128)(2,1)S(1)}, bf16[4,72,512]{2,1,0:T(8,128)(2,1)}, u32[]{:S(2)}, u32[]{:S(2)}) %collective-permute-start.13) | collective-permute-done | bytes 294944 | tf_op jit(solution)/shard_map/ppermute | solution.py:44
  96.1 3.7 %collective-permute-start.16 = (bf16[72,512]{1,0:T(8,128)(2,1)S(1)}, bf16[72,512]{1,0:T(8,128)(2,1)S(1)}, u32[]{:S(2)}, u32[]{:S(2)}) collective-permute-start(bf16[72,512]{1,0:T(8,128)(2,1)S(1)} %get-tuple-element.43), channel_id=1, source_target_pairs={{0,32},{1,33},{2,34},{3,35},{4,36},{5,37},{6,38},{7,39},{8,40},{9,... | collective-permute-start | bytes 221192 | tf_op jit(solution)/shard_map/ppermute | solution.py:44
  100.0 1.8 %collective-permute-start.10 = (bf16[72,512]{1,0:T(8,128)(2,1)S(1)}, bf16[72,512]{1,0:T(8,128)(2,1)S(1)}, u32[]{:S(2)}, u32[]{:S(2)}) collective-permute-start(bf16[72,512]{1,0:T(8,128)(2,1)S(1)} %get-tuple-element.46), channel_id=1, source_target_pairs={{0,4},{1,5},{2,6},{3,7},{4,0},{5,1},{6,2},{7,3},{8,12},{9,13},{10,... | collective-permute-start | bytes 221192 | tf_op jit(solution)/shard_map/ppermute | solution.py:44
  104.2 1.8 %collective-permute-done.10 = bf16[72,512]{1,0:T(8,128)(2,1)S(1)} collective-permute-done((bf16[72,512]{1,0:T(8,128)(2,1)S(1)}, bf16[72,512]{1,0:T(8,128)(2,1)S(1)}, u32[]{:S(2)}, u32[]{:S(2)}) %collective-permute-start.10) | collective-permute-done | bytes 73760 | tf_op jit(solution)/shard_map/ppermute | solution.py:44
  106.2 2.2 %collective-permute-done.9 = bf16[72,512]{1,0:T(8,128)(2,1)S(1)} collective-permute-done((bf16[72,512]{1,0:T(8,128)(2,1)S(1)}, bf16[72,512]{1,0:T(8,128)(2,1)S(1)}, u32[]{:S(2)}, u32[]{:S(2)}) %collective-permute-start.9) | collective-permute-done | bytes 73760 | tf_op jit(solution)/shard_map/ppermute | solution.py:44
  108.5 1.6 %collective-permute-start.17 = (bf16[2,18,512]{2,1,0:T(8,128)(2,1)S(1)}, bf16[2,18,512]{2,1,0:T(8,128)(2,1)S(1)}, u32[]{:S(2)}, u32[]{:S(2)}) collective-permute-start(bf16[2,18,512]{2,1,0:T(8,128)(2,1)S(1)} %get-tuple-element.48), channel_id=1, source_target_pairs={{0,64},{1,65},{2,66},{3,67},{4,68},{5,69},{6,70},{7,71},{8,72},{9,... | collective-permute-start | bytes 110600 | tf_op jit(solution)/shard_map/ppermute | solution.py:44
  110.1 4.5 %collective-permute-start.18 = (bf16[2,18,512]{2,1,0:T(8,128)(2,1)S(1)}, bf16[2,18,512]{2,1,0:T(8,128)(2,1)S(1)}, u32[]{:S(2)}, u32[]{:S(2)}) collective-permute-start(bf16[2,18,512]{2,1,0:T(8,128)(2,1)S(1)} %get-tuple-element.50), channel_id=1, source_target_pairs={{0,192},{1,193},{2,194},{3,195},{4,196},{5,197},{6,198},{7,199},{8... | collective-permute-start | bytes 110600 | tf_op jit(solution)/shard_map/ppermute | solution.py:44
  114.6 2.6 %collective-permute-done.18 = bf16[2,18,512]{2,1,0:T(8,128)(2,1)S(1)} collective-permute-done((bf16[2,18,512]{2,1,0:T(8,128)(2,1)S(1)}, bf16[2,18,512]{2,1,0:T(8,128)(2,1)S(1)}, u32[]{:S(2)}, u32[]{:S(2)}) %collective-permute-start.18) | collective-permute-done | bytes 36896 | tf_op jit(solution)/shard_map/ppermute | solution.py:44
  117.2 2.4 %collective-permute-done.19 = bf16[2,18,512]{2,1,0:T(8,128)(2,1)S(1)} collective-permute-done((bf16[2,18,512]{2,1,0:T(8,128)(2,1)S(1)}, bf16[2,18,512]{2,1,0:T(8,128)(2,1)S(1)}, u32[]{:S(2)}, u32[]{:S(2)}) %collective-permute-start.19) | collective-permute-done | bytes 36896 | tf_op jit(solution)/shard_map/ppermute | solution.py:44
  119.7 1.9 %collective-permute-start.20 = (bf16[2,9,512]{2,0,1:T(2,128)(2,1)S(1)}, bf16[2,9,512]{2,0,1:T(2,128)(2,1)S(1)}, u32[]{:S(2)}, u32[]{:S(2)}) collective-permute-start(bf16[2,9,512]{2,0,1:T(2,128)(2,1)S(1)} %get-tuple-element.51), channel_id=1, source_target_pairs={{0,0},{1,128},{2,8},{3,136},{4,16},{5,144},{6,24},{7,152},{8,1},{9... | collective-permute-start | bytes 55304 | tf_op jit(solution)/shard_map/ppermute | solution.py:69
  122.5 6.8 %collective-permute-done.20 = bf16[2,9,512]{2,0,1:T(2,128)(2,1)S(1)} collective-permute-done((bf16[2,9,512]{2,0,1:T(2,128)(2,1)S(1)}, bf16[2,9,512]{2,0,1:T(2,128)(2,1)S(1)}, u32[]{:S(2)}, u32[]{:S(2)}) %collective-permute-start.20) | collective-permute-done | bytes 18464 | tf_op jit(solution)/shard_map/ppermute | solution.py:69
  129.3 4.9 %collective-permute-done.21 = bf16[2,9,512]{2,0,1:T(2,128)(2,1)S(1)} collective-permute-done((bf16[2,9,512]{2,0,1:T(2,128)(2,1)S(1)}, bf16[2,9,512]{2,0,1:T(2,128)(2,1)S(1)}, u32[]{:S(2)}, u32[]{:S(2)}) %collective-permute-start.21) | collective-permute-done | bytes 18464 | tf_op jit(solution)/shard_map/ppermute | solution.py:69
  (81 shorter events, 18.8 us)
Async XLA Ops:
  5.1 21.6 %copy-start = (bf16[2304,256]{1,0:T(8,128)(2,1)S(1)}, bf16[2304,256]{1,0:T(8,128)(2,1)}, u32[]{:S(2)}) copy-start(bf16[2304,256]{1,0:T(8,128)(2,1)} %w_coarse.3) | copy-start | bytes 3538948
  8.0 17.2 %copy-start.12 = (bf16[4,16,16,256]{3,2,1,0:T(8,128)(2,1)}, bf16[4,16,16,256]{3,2,1,0:T(8,128)(2,1)S(1)}, u32[]{:S(2)}) copy-start(bf16[4,16,16,256]{3,2,1,0:T(8,128)(2,1)S(1)} %get-tuple-element.18.own_ref) | copy-start | bytes 1572868
  8.0 8.4 %collective-permute-start = (bf16[23,16,256]{2,1,0:T(8,128)(2,1)S(1)}, bf16[23,16,256]{2,1,0:T(8,128)(2,1)S(1)}, u32[]{:S(2)}, u32[]{:S(2)}) collective-permute-start(bf16[23,16,256]{2,1,0:T(8,128)(2,1)S(1)} %get-tuple-element.20), channel_id=1, source_target_pairs={{0,16},{1,17},{2,18},{3,19},{4,20},{5,21},{6,22},{7,23},{8,24},{9,... | collective-permute-start | bytes 565256 | tf_op jit(solution)/shard_map/ppermute | solution.py:388
  11.7 10.2 %collective-permute-start.1 = (bf16[23,16,256]{2,1,0:T(8,128)(2,1)S(1)}, bf16[23,16,256]{2,1,0:T(8,128)(2,1)S(1)}, u32[]{:S(2)}, u32[]{:S(2)}) collective-permute-start(bf16[23,16,256]{2,1,0:T(8,128)(2,1)S(1)} %get-tuple-element.21), channel_id=1, source_target_pairs={{16,0},{17,1},{18,2},{19,3},{20,4},{21,5},{22,6},{23,7},{24,8},{25... | collective-permute-start | bytes 565256 | tf_op jit(solution)/shard_map/ppermute | solution.py:388
  16.3 6.8 %copy-start.8 = (bf16[23,16,256]{2,1,0:T(8,128)(2,1)}, bf16[23,16,256]{2,1,0:T(8,128)(2,1)S(1)}, u32[]{:S(2)}) copy-start(bf16[23,16,256]{2,1,0:T(8,128)(2,1)S(1)} %collective-permute-done.up_ref) | copy-start | bytes 565252
  23.2 9.6 %collective-permute-start.2 = (bf16[24,24,256]{2,1,0:T(8,128)(2,1)}, bf16[24,24,256]{2,1,0:T(8,128)(2,1)}, u32[]{:S(2)}, u32[]{:S(2)}) collective-permute-start(bf16[24,24,256]{2,1,0:T(8,128)(2,1)} %get-tuple-element.22), channel_id=1, source_target_pairs={{0,1},{1,2},{2,3},{3,4},{4,5},{5,6},{6,7},{7,8},{8,9},{9,10},{10,1... | collective-permute-start | bytes 884744 | tf_op jit(solution)/shard_map/ppermute | solution.py:388
  25.2 7.6 %collective-permute-start.3 = (bf16[24,24,256]{2,1,0:T(8,128)(2,1)}, bf16[24,24,256]{2,1,0:T(8,128)(2,1)}, u32[]{:S(2)}, u32[]{:S(2)}) collective-permute-start(bf16[24,24,256]{2,1,0:T(8,128)(2,1)} %get-tuple-element.23), channel_id=1, source_target_pairs={{1,0},{2,1},{3,2},{4,3},{5,4},{6,5},{7,6},{8,7},{9,8},{10,9},{11,1... | collective-permute-start | bytes 884744 | tf_op jit(solution)/shard_map/ppermute | solution.py:388
  29.6 3.2 %copy-start.5 = (f32[16,16,256]{2,1,0:T(8,128)S(1)}, f32[16,16,256]{2,1,0:T(8,128)}, u32[]{:S(2)}) copy-start(f32[16,16,256]{2,1,0:T(8,128)} %low_ref.5) | copy-start | bytes 786436
  29.6 3.2 %copy-start.9 = (bf16[23,16,256]{2,1,0:T(8,128)(2,1)S(1)}, bf16[23,16,256]{2,1,0:T(8,128)(2,1)}, u32[]{:S(2)}) copy-start(bf16[23,16,256]{2,1,0:T(8,128)(2,1)} %copy-done.8) | copy-start | bytes 565252
  29.6 3.2 %copy-start.11 = (bf16[23,16,256]{2,1,0:T(8,128)(2,1)S(1)}, bf16[23,16,256]{2,1,0:T(8,128)(2,1)}, u32[]{:S(2)}) copy-start(bf16[23,16,256]{2,1,0:T(8,128)(2,1)} %copy-done.10) | copy-start | bytes 565252
  29.6 3.2 %copy-start.13 = (bf16[4,16,16,256]{3,2,1,0:T(8,128)(2,1)S(1)}, bf16[4,16,16,256]{3,2,1,0:T(8,128)(2,1)}, u32[]{:S(2)}) copy-start(bf16[4,16,16,256]{3,2,1,0:T(8,128)(2,1)} %copy-done.12) | copy-start | bytes 1572868
  52.4 3.1 %copy-start.1 = (bf16[2,2,1152,512]{3,2,1,0:T(8,128)(2,1)}, bf16[2,2,1152,512]{3,2,1,0:T(8,128)(2,1)S(1)}, u32[]{:S(2)}) copy-start(bf16[2,2,1152,512]{3,2,1,0:T(8,128)(2,1)S(1)} %get-tuple-element.27) | copy-start | bytes 14155780
  52.4 5.5 %copy-start.16 = (bf16[2304,256]{1,0:T(8,128)(2,1)S(1)}, bf16[2304,256]{1,0:T(8,128)(2,1)}, u32[]{:S(2)}) copy-start(bf16[2304,256]{1,0:T(8,128)(2,1)} %copy-done.15) | copy-start | bytes 3538948
  52.4 5.5 %copy-start.18 = (bf16[2,18,16,1024]{3,2,1,0:T(8,128)(2,1)S(1)}, bf16[2,18,16,1024]{3,2,1,0:T(8,128)(2,1)}, u32[]{:S(2)}) copy-start(bf16[2,18,16,1024]{3,2,1,0:T(8,128)(2,1)} %copy-done.17) | copy-start | bytes 3538948
  55.5 6.8 %collective-permute-start.4 = (bf16[2,1152,512]{2,1,0:T(8,128)(2,1)}, bf16[2,1152,512]{2,1,0:T(8,128)(2,1)}, u32[]{:S(2)}, u32[]{:S(2)}) collective-permute-start(bf16[2,1152,512]{2,1,0:T(8,128)(2,1)} %slice_bitcast_fusion), channel_id=1, source_target_pairs={{0,1},{1,0},{2,3},{3,2},{4,5},{5,4},{6,7},{7,6},{8,9},{9,8},{10,11... | collective-permute-start | bytes 7077896 | tf_op jit(solution)/shard_map/ppermute | solution.py:53
  65.6 15.7 %collective-permute-start.11 = (bf16[4,72,512]{2,1,0:T(8,128)(2,1)S(1)}, bf16[4,72,512]{2,1,0:T(8,128)(2,1)S(1)}, u32[]{:S(2)}, u32[]{:S(2)}) collective-permute-start(bf16[4,72,512]{2,1,0:T(8,128)(2,1)S(1)} %get-tuple-element.36), channel_id=1, source_target_pairs={{0,2},{1,3},{2,0},{3,1},{4,6},{5,7},{6,4},{7,5},{8,10},{9,11},{10,... | collective-permute-start | bytes 884744 | tf_op jit(solution)/shard_map/ppermute | solution.py:44
  67.6 24.8 %collective-permute-start.12 = (bf16[4,72,512]{2,1,0:T(8,128)(2,1)S(1)}, bf16[4,72,512]{2,1,0:T(8,128)(2,1)}, u32[]{:S(2)}, u32[]{:S(2)}) collective-permute-start(bf16[4,72,512]{2,1,0:T(8,128)(2,1)S(1)} %get-tuple-element.38), channel_id=1, source_target_pairs={{0,6},{1,7},{2,4},{3,5},{4,2},{5,3},{6,0},{7,1},{8,14},{9,15},{10,... | collective-permute-start | bytes 884744 | tf_op jit(solution)/shard_map/ppermute | solution.py:44
  79.3 15.0 %collective-permute-start.13 = (bf16[4,72,512]{2,1,0:T(8,128)(2,1)S(1)}, bf16[4,72,512]{2,1,0:T(8,128)(2,1)}, u32[]{:S(2)}, u32[]{:S(2)}) collective-permute-start(bf16[4,72,512]{2,1,0:T(8,128)(2,1)S(1)} %get-tuple-element.37), channel_id=1, source_target_pairs={{0,4},{1,5},{2,6},{3,7},{4,0},{5,1},{6,2},{7,3},{8,12},{9,13},{10,... | collective-permute-start | bytes 884744 | tf_op jit(solution)/shard_map/ppermute | solution.py:44
  80.7 15.3 %collective-permute-start.5 = (bf16[4,72,512]{2,1,0:T(8,128)(2,1)S(1)}, bf16[4,72,512]{2,1,0:T(8,128)(2,1)S(1)}, u32[]{:S(2)}, u32[]{:S(2)}) collective-permute-start(bf16[4,72,512]{2,1,0:T(8,128)(2,1)S(1)} %get-tuple-element.39), channel_id=1, source_target_pairs={{0,16},{1,17},{2,18},{3,19},{4,20},{5,21},{6,22},{7,23},{8,24},{9,... | collective-permute-start | bytes 884744 | tf_op jit(solution)/shard_map/ppermute | solution.py:44
  80.8 18.9 %collective-permute-start.6 = (bf16[4,72,512]{2,1,0:T(8,128)(2,1)S(1)}, bf16[4,72,512]{2,1,0:T(8,128)(2,1)S(1)}, u32[]{:S(2)}, u32[]{:S(2)}) collective-permute-start(bf16[4,72,512]{2,1,0:T(8,128)(2,1)S(1)} %get-tuple-element.41), channel_id=1, source_target_pairs={{0,48},{1,49},{2,50},{3,51},{4,52},{5,53},{6,54},{7,55},{8,56},{9,... | collective-permute-start | bytes 884744 | tf_op jit(solution)/shard_map/ppermute | solution.py:44
  81.3 18.5 %collective-permute-start.7 = (bf16[4,72,512]{2,1,0:T(8,128)(2,1)S(1)}, bf16[4,72,512]{2,1,0:T(8,128)(2,1)S(1)}, u32[]{:S(2)}, u32[]{:S(2)}) collective-permute-start(bf16[4,72,512]{2,1,0:T(8,128)(2,1)S(1)} %get-tuple-element.40), channel_id=1, source_target_pairs={{0,32},{1,33},{2,34},{3,35},{4,36},{5,37},{6,38},{7,39},{8,40},{9,... | collective-permute-start | bytes 884744 | tf_op jit(solution)/shard_map/ppermute | solution.py:44
  95.6 7.2 %collective-permute-start.14 = (bf16[72,512]{1,0:T(8,128)(2,1)S(1)}, bf16[72,512]{1,0:T(8,128)(2,1)S(1)}, u32[]{:S(2)}, u32[]{:S(2)}) collective-permute-start(bf16[72,512]{1,0:T(8,128)(2,1)S(1)} %get-tuple-element.42), channel_id=1, source_target_pairs={{0,16},{1,17},{2,18},{3,19},{4,20},{5,21},{6,22},{7,23},{8,24},{9,... | collective-permute-start | bytes 221192 | tf_op jit(solution)/shard_map/ppermute | solution.py:44
  95.7 8.5 %collective-permute-start.15 = (bf16[72,512]{1,0:T(8,128)(2,1)S(1)}, bf16[72,512]{1,0:T(8,128)(2,1)S(1)}, u32[]{:S(2)}, u32[]{:S(2)}) collective-permute-start(bf16[72,512]{1,0:T(8,128)(2,1)S(1)} %get-tuple-element.44), channel_id=1, source_target_pairs={{0,48},{1,49},{2,50},{3,51},{4,52},{5,53},{6,54},{7,55},{8,56},{9,... | collective-permute-start | bytes 221192 | tf_op jit(solution)/shard_map/ppermute | solution.py:44
  96.1 8.1 %collective-permute-start.16 = (bf16[72,512]{1,0:T(8,128)(2,1)S(1)}, bf16[72,512]{1,0:T(8,128)(2,1)S(1)}, u32[]{:S(2)}, u32[]{:S(2)}) collective-permute-start(bf16[72,512]{1,0:T(8,128)(2,1)S(1)} %get-tuple-element.43), channel_id=1, source_target_pairs={{0,32},{1,33},{2,34},{3,35},{4,36},{5,37},{6,38},{7,39},{8,40},{9,... | collective-permute-start | bytes 221192 | tf_op jit(solution)/shard_map/ppermute | solution.py:44
  100.0 6.1 %collective-permute-start.10 = (bf16[72,512]{1,0:T(8,128)(2,1)S(1)}, bf16[72,512]{1,0:T(8,128)(2,1)S(1)}, u32[]{:S(2)}, u32[]{:S(2)}) collective-permute-start(bf16[72,512]{1,0:T(8,128)(2,1)S(1)} %get-tuple-element.46), channel_id=1, source_target_pairs={{0,4},{1,5},{2,6},{3,7},{4,0},{5,1},{6,2},{7,3},{8,12},{9,13},{10,... | collective-permute-start | bytes 221192 | tf_op jit(solution)/shard_map/ppermute | solution.py:44
  101.8 4.4 %collective-permute-start.8 = (bf16[72,512]{1,0:T(8,128)(2,1)S(1)}, bf16[72,512]{1,0:T(8,128)(2,1)S(1)}, u32[]{:S(2)}, u32[]{:S(2)}) collective-permute-start(bf16[72,512]{1,0:T(8,128)(2,1)S(1)} %get-tuple-element.45), channel_id=1, source_target_pairs={{0,2},{1,3},{2,0},{3,1},{4,6},{5,7},{6,4},{7,5},{8,10},{9,11},{10,... | collective-permute-start | bytes 221192 | tf_op jit(solution)/shard_map/ppermute | solution.py:44
  102.8 5.6 %collective-permute-start.9 = (bf16[72,512]{1,0:T(8,128)(2,1)S(1)}, bf16[72,512]{1,0:T(8,128)(2,1)S(1)}, u32[]{:S(2)}, u32[]{:S(2)}) collective-permute-start(bf16[72,512]{1,0:T(8,128)(2,1)S(1)} %get-tuple-element.47), channel_id=1, source_target_pairs={{0,6},{1,7},{2,4},{3,5},{4,2},{5,3},{6,0},{7,1},{8,14},{9,15},{10,... | collective-permute-start | bytes 221192 | tf_op jit(solution)/shard_map/ppermute | solution.py:44
  108.5 6.1 %collective-permute-start.17 = (bf16[2,18,512]{2,1,0:T(8,128)(2,1)S(1)}, bf16[2,18,512]{2,1,0:T(8,128)(2,1)S(1)}, u32[]{:S(2)}, u32[]{:S(2)}) collective-permute-start(bf16[2,18,512]{2,1,0:T(8,128)(2,1)S(1)} %get-tuple-element.48), channel_id=1, source_target_pairs={{0,64},{1,65},{2,66},{3,67},{4,68},{5,69},{6,70},{7,71},{8,72},{9,... | collective-permute-start | bytes 110600 | tf_op jit(solution)/shard_map/ppermute | solution.py:44
  110.1 7.1 %collective-permute-start.18 = (bf16[2,18,512]{2,1,0:T(8,128)(2,1)S(1)}, bf16[2,18,512]{2,1,0:T(8,128)(2,1)S(1)}, u32[]{:S(2)}, u32[]{:S(2)}) collective-permute-start(bf16[2,18,512]{2,1,0:T(8,128)(2,1)S(1)} %get-tuple-element.50), channel_id=1, source_target_pairs={{0,192},{1,193},{2,194},{3,195},{4,196},{5,197},{6,198},{7,199},{8... | collective-permute-start | bytes 110600 | tf_op jit(solution)/shard_map/ppermute | solution.py:44
  114.6 5.0 %collective-permute-start.19 = (bf16[2,18,512]{2,1,0:T(8,128)(2,1)S(1)}, bf16[2,18,512]{2,1,0:T(8,128)(2,1)S(1)}, u32[]{:S(2)}, u32[]{:S(2)}) collective-permute-start(bf16[2,18,512]{2,1,0:T(8,128)(2,1)S(1)} %get-tuple-element.49), channel_id=1, source_target_pairs={{0,128},{1,129},{2,130},{3,131},{4,132},{5,133},{6,134},{7,135},{8... | collective-permute-start | bytes 110600 | tf_op jit(solution)/shard_map/ppermute | solution.py:44
  119.7 9.6 %collective-permute-start.20 = (bf16[2,9,512]{2,0,1:T(2,128)(2,1)S(1)}, bf16[2,9,512]{2,0,1:T(2,128)(2,1)S(1)}, u32[]{:S(2)}, u32[]{:S(2)}) collective-permute-start(bf16[2,9,512]{2,0,1:T(2,128)(2,1)S(1)} %get-tuple-element.51), channel_id=1, source_target_pairs={{0,0},{1,128},{2,8},{3,136},{4,16},{5,144},{6,24},{7,152},{8,1},{9... | collective-permute-start | bytes 55304 | tf_op jit(solution)/shard_map/ppermute | solution.py:69
  121.6 12.6 %collective-permute-start.21 = (bf16[2,9,512]{2,0,1:T(2,128)(2,1)S(1)}, bf16[2,9,512]{2,0,1:T(2,128)(2,1)S(1)}, u32[]{:S(2)}, u32[]{:S(2)}) collective-permute-start(bf16[2,9,512]{2,0,1:T(2,128)(2,1)S(1)} %get-tuple-element.52), channel_id=1, source_target_pairs={{0,1},{1,129},{2,9},{3,137},{4,17},{5,145},{6,25},{7,153},{8,0},{9... | collective-permute-start | bytes 55304 | tf_op jit(solution)/shard_map/ppermute | solution.py:69
  (9 other events, 10.7 us)

commit v4 on v3

--- a/solution.py
+++ b/solution.py
@@ -48,10 +48,17 @@
     return total.astype(BF)
 
 
-def reduce_scatter(parts, beside):
+def reduce_scatter(keep, send, beside):
     pairs = [(index_of(p), index_of(flipped(p, "core", 1))) for p in digits()]
-    other, beside = lax.optimization_barrier((lax.ppermute(parts[1], ("row", "col"), pairs), beside))
-    parts = (parts[0].astype(F32) + other.astype(F32)).astype(BF)
+    other, beside = lax.optimization_barrier((lax.ppermute(send, ("row", "col"), pairs), beside))
+    parts = pl.pallas_call(
+        join_kernel,
+        out_shape=jax.ShapeDtypeStruct((2, 1152, 512), BF),
+        in_specs=in_vmem(2),
+        out_specs=pl.BlockSpec(memory_space=pltpu.VMEM),
+        compiler_params=room(9),
+        name="join",
+    )(keep, other)
     first = parts[0].reshape(4, 4, 72, 512)
     second = parts[1].reshape(4, 4, 72, 512)
     first, second = sum_stage(first, "x", 0), sum_stage(second, "y", 1)
@@ -101,11 +108,18 @@
     return jnp.concatenate([ref[:, row, half, pl.ds(col, 16, stride=2), :] for half in range(2)], axis=-1)
 
 
-def first_kernel(feat_ref, fine_ref, low_ref, w_post, own_ref, part_ref, top_ref, bottom_ref,
-                 wide, noise, field, cat, spill):
+def first_kernel(feat_hbm, fine_hbm, low_hbm, post_hbm, own_ref, part_ref, top_ref, bottom_ref,
+                 feat_ref, fine_ref, low_ref, w_post, wide, noise, field, cat, spill, sems):
+    pairs = ((feat_hbm, feat_ref), (post_hbm.at[:768], w_post.at[:768]), (post_hbm.at[768:1536], w_post.at[768:1536]),
+             (post_hbm.at[1536:], w_post.at[1536:]), (fine_hbm.at[:8], fine_ref.at[:8]),
+             (fine_hbm.at[8:], fine_ref.at[8:]), (low_hbm, low_ref))
+    copies = [pltpu.make_async_copy(source, target, sems.at[at]) for at, (source, target) in enumerate(pairs)]
+    for copy in copies:
+        copy.start()
+    field[...] = jnp.zeros(field.shape, F32)
+    spill[...] = jnp.zeros(spill.shape, F32)
+    copies[0].wait()
     split_lanes(wide, feat_ref[...].astype(F32))
-    split_lanes(noise, fine_ref[...])
-    field[...] = jnp.zeros(field.shape, F32)
     for row in range(2):
         for col in range(2):
             cells = phase_of(wide, row, col)
@@ -114,6 +128,9 @@
         even, odd = flat(field[0]), flat(field[1])
         for at, part in enumerate((before(odd), even, odd, after(even))):
             cat[row, :, :, 256 * at:256 * (at + 1)] = back_in_rows(part.astype(BF))
+    for copy in copies[1:]:
+        copy.wait()
+    split_lanes(noise, fine_ref[...])
     for row in range(2):
         for col in range(2):
             value = jnp.zeros((544, 256), F32)
@@ -124,7 +141,6 @@
                 value = value + dot(cells, w_post[768 * a:768 * (a + 1)])
             part_ref[2 * row + col] = back_in_rows(value)
             part_ref[2 * row + col, row:row + 16, 8:24, :] += phase_of(noise, row, col)
-    spill[...] = jnp.zeros(spill.shape, F32)
     for out, first, low_first in ((top_ref, -1, 0), (bottom_ref, 24, 13)):
         for r in range(9):
             line = first + r
@@ -210,8 +226,8 @@
 
 
 def main_kernel(scale, place_ref, own_ref, part_ref, low_ref, up_ref, down_ref, left_ref, right_ref,
-                w_coarse, fold, fold_t, w_coarse_t, grads, g_fine,
-                fine, low, pool_cat, coarse, ctx_cat, err, d_cat, d_own, gc_cat, gc_own, spill):
+                w_coarse, fold, fold_t, w_coarse_t, keep_ref, send_ref, g_fine,
+                fine, low, pool_cat, coarse, ctx_cat, err, d_cat, d_own, gc_cat, gc_own, spill, grads):
     def put(which, tap, lanes, value):
         value = (value * scale).astype(BF)
         for half, first, start, stop in ((0, 256 * tap, 0, 256), (1, 256 * tap - 1152, 0, 256)):
@@ -344,6 +360,12 @@
                     at = col + 2 - b
                     rights.append(g_fine[phase, 1 + shift:17 + shift, :, 256 * at:256 * (at + 1)].reshape(256, 256))
             put(1, 3 * a + b, slice(256, 512), dot(left, jnp.concatenate(rights, axis=0)))
+    keep_ref[...] = grads[0]
+    send_ref[...] = grads[1]
+
+
+def join_kernel(keep_ref, other_ref, out_ref):
+    out_ref[...] = (keep_ref[...].astype(F32) + other_ref[...].astype(F32)).astype(BF)
 
 
 def feat_kernel(g_fine, w_post_t, out_ref, wide):
@@ -398,16 +420,21 @@
             jax.ShapeDtypeStruct((23, 16, 256), BF),
             jax.ShapeDtypeStruct((23, 16, 256), BF),
         ],
-        in_specs=in_vmem(4),
+        in_specs=[pl.BlockSpec(memory_space=pltpu.HBM)] * 4,
         out_specs=in_vmem(4),
         scratch_shapes=[
+            pltpu.VMEM((16, 2, 32, 256), BF),
+            pltpu.VMEM((16, 2, 32, 256), F32),
+            pltpu.VMEM((16, 16, 256), F32),
+            pltpu.VMEM((2304, 256), BF),
             pltpu.VMEM((16, 2, 2, 32, 128), F32),
             pltpu.VMEM((16, 2, 2, 32, 128), F32),
             pltpu.VMEM((2, 18, 32, 256), F32),
             pltpu.VMEM((2, 18, 32, 1024), BF),
             pltpu.VMEM((32, 256), F32),
+            pltpu.SemaphoreType.DMA((7,)),
         ],
-        compiler_params=room(16),
+        compiler_params=room(59),
         name="first",
     )(feat.reshape(16, 2, 32, 256), noise_fine.reshape(16, 2, 32, 256), noise_coarse, w_post)
     from_up, from_down = sent(bottom, 1, 0), sent(top, -1, 0)
@@ -437,14 +464,15 @@
     from_left, from_right = sent(right, 0, 1), sent(left, 0, -1)
     row, col = lax.axis_index("row"), lax.axis_index("col")
     place = jnp.stack([row, col, col % 2]).astype(jnp.int32)
-    grads, g_fine = pl.pallas_call(
+    keep, send, g_fine = pl.pallas_call(
         functools.partial(main_kernel, scale),
         out_shape=[
-            jax.ShapeDtypeStruct((2, 2, 1152, 512), BF),
+            jax.ShapeDtypeStruct((2, 1152, 512), BF),
+            jax.ShapeDtypeStruct((2, 1152, 512), BF),
             jax.ShapeDtypeStruct((2, 18, 16, 1024), BF),
         ],
         in_specs=[pl.BlockSpec(memory_space=pltpu.SMEM)] + in_vmem(11),
-        out_specs=in_vmem(2),
+        out_specs=in_vmem(3),
         scratch_shapes=[
             pltpu.VMEM((4, 24, 32, 256), F32),
             pltpu.VMEM((22, 32, 256), F32),
@@ -457,8 +485,9 @@
             pltpu.VMEM((20, 32, 768), BF),
             pltpu.VMEM((20, 16, 768), BF),
             pltpu.VMEM((32, 256), F32),
+            pltpu.VMEM((2, 2, 1152, 512), BF),
         ],
-        compiler_params=room(28),
+        compiler_params=room(32),
         name="tile",
     )(place, own, part, noise_coarse, from_up, from_down, from_left, from_right,
       w_coarse, fold, fold_t, w_coarse_t)
@@ -468,11 +497,11 @@
         in_specs=in_vmem(2),
         out_specs=pl.BlockSpec(memory_space=pltpu.VMEM),
         scratch_shapes=[pltpu.VMEM((16, 2, 2, 32, 128), F32)],
-        compiler_params=room(12),
+        compiler_params=room(8),
         cost_estimate=pl.CostEstimate(flops=1200000000, bytes_accessed=3000000, transcendentals=0),
         name="feat",
     )(g_fine, w_post_t).reshape(32, 32, 256)
-    summed, grad_feat = reduce_scatter(grads, grad_feat)
+    summed, grad_feat = reduce_scatter(keep, send, grad_feat)
     return grad_feat, summed[1, :, 256:].reshape(-1), summed[1, :, :256].reshape(-1), summed[0].reshape(-1)
 
 

time: 137 us -> 135 us (0.985)
  Pallas kernels: 26.9 us -> 32.6 us
  local copies, waits for them, and re-layouts: 15 us -> 10.8 us
  other arithmetic: 4.61 us -> 1.58 us
  waiting for transfers between devices: 40.5 us -> 37.7 us
  starting transfers between devices: 48.1 us -> 50.7 us
    pallas_call x1, Pallas kernels: 2.85 us -> 6.16 us  [on_device(): pl.pallas_call(first_kernel, out_shape=[jax.ShapeDtypeStruct((4, 16, 16,...]
    convert_element_type x1 -> x0, other arithmetic: 3.04 us -> none  [reduce_scatter(): parts = (parts[0].astype(F32) + other.astype(F32)).astype(BF)]
    unnamed x39 -> x27, local copies, waits for them, and re-layouts: 11 us -> 8.32 us
    ppermute x1, starting transfers between devices: 2.32 us -> 4.94 us  [reduce_scatter(): lax.ppermute(send, ('row', 'col'), pairs)]
    ppermute x1, waiting for transfers between devices: 2.25 us -> 0.01 us  [reduce_scatter(): lax.ppermute(send, ('row', 'col'), pairs)]
    pallas_call x1, Pallas kernels: 18.5 us -> 20.3 us  [on_device(): pl.pallas_call(functools.partial(main_kernel, scale), out_shape=[jax.Shap...]
    squeeze x1 -> x0, local copies, waits for them, and re-layouts: 1.6 us -> none  [reduce_scatter(): parts[1]]
where the time goes in v4:
time: 135 us; the launch traced here: 134 us
  starting transfers between devices  50.7 us (38%)
  waiting for transfers between devices  37.7 us (28%)
  Pallas kernels  32.6 us (24%)
  local copies, waits for them, and re-layouts  10.8 us (8%)
  other arithmetic  1.58 us (1%)
    ppermute x15, starting transfers between devices, sum_stage(): arrived.append(lax.ppermute(piece, ('row', 'col'), pairs))  33.7 us
    pallas_call x1, Pallas kernels, on_device(): pl.pallas_call(functools.partial(main_kernel, scale), out_shape=[jax.Shap...  20.3 us
    ppermute x15, waiting for transfers between devices, sum_stage(): arrived.append(lax.ppermute(piece, ('row', 'col'), pairs))  18.2 us
    ppermute x2, waiting for transfers between devices, reduce_scatter(): total = total + lax.ppermute(piece, ('row', 'col'), pairs).astype(F32)  11 us
    ppermute x4, starting transfers between devices, sent(): return lax.ppermute(strip, ('row', 'col'), pairs)  8.61 us
    ppermute x4, waiting for transfers between devices, sent(): return lax.ppermute(strip, ('row', 'col'), pairs)  8.5 us
    unnamed x27, local copies, waits for them, and re-layouts  8.32 us
    pallas_call x1, Pallas kernels, on_device(): pl.pallas_call(first_kernel, out_shape=[jax.ShapeDtypeStruct((4, 16, 16,...  6.16 us
  transfers between devices with their start and end apart: 22, of which 12 were waited for; matrix products, arithmetic and copies ran while one was open for 1% of the time, Pallas kernels for 3%

profile of v4, /device:TPU:6, one launch (start us, length us, event | category | flops | bytes accessed | tf_op | source)
XLA Modules:
  0.0 134.2 jit_solution(13393175180567572640)
XLA Ops:
  0.6 6.2 %first.1 = (bf16[4,16,16,256]{3,2,1,0:T(8,128)(2,1)}, f32[4,17,32,256]{3,2,1,0:T(8,128)}, bf16[23,16,256]{2,1,0:T(8,128)(2,1)}, bf16[23,16,256]{2,1,0:T(8,128)(2,1)}) custom-call(bf16[16,2,32,256]{3,2,1,0:T(8,128)(2,1)} %bitcast.65, f32[16,2,32,256]{3,2,1,0:T(8,128)} %bitcast.64, f32[16,16,256]{2,1,0:T(8,128)} %low_ref.3, bf16[2304,256]{1,0:T(8,128)(2,1)} %w_post.1), custom_call_target="tpu_custom_call" | custom-call | tf_op jit(solution)/shard_map/first/pallas_call | solution.py:415
  6.8 3.7 %collective-permute-start = (bf16[23,16,256]{2,1,0:T(8,128)(2,1)}, bf16[23,16,256]{2,1,0:T(8,128)(2,1)S(1)}, u32[]{:S(2)}, u32[]{:S(2)}) collective-permute-start(bf16[23,16,256]{2,1,0:T(8,128)(2,1)} %get-tuple-element.21), channel_id=1, source_target_pairs={{0,16},{1,17},{2,18},{3,19},{4,20},{5,21},{6,22},{7,23},{8,24},{9,... | collective-permute-start | bytes 565256 | tf_op jit(solution)/shard_map/ppermute | solution.py:410
  10.6 2.1 %collective-permute-start.1 = (bf16[23,16,256]{2,1,0:T(8,128)(2,1)}, bf16[23,16,256]{2,1,0:T(8,128)(2,1)S(1)}, u32[]{:S(2)}, u32[]{:S(2)}) collective-permute-start(bf16[23,16,256]{2,1,0:T(8,128)(2,1)} %get-tuple-element.22), channel_id=1, source_target_pairs={{16,0},{17,1},{18,2},{19,3},{20,4},{21,5},{22,6},{23,7},{24,8},{25... | collective-permute-start | bytes 565256 | tf_op jit(solution)/shard_map/ppermute | solution.py:410
  12.7 2.7 %collective-permute-done.up_ref = bf16[23,16,256]{2,1,0:T(8,128)(2,1)S(1)} collective-permute-done((bf16[23,16,256]{2,1,0:T(8,128)(2,1)}, bf16[23,16,256]{2,1,0:T(8,128)(2,1)S(1)}, u32[]{:S(2)}, u32[]{:S(2)}) %collective-permute-start) | collective-permute-done | bytes 188448 | tf_op jit(solution)/shard_map/ppermute | solution.py:410
  15.4 5.6 %collective-permute-done.1.down_ref = bf16[23,16,256]{2,1,0:T(8,128)(2,1)S(1)} collective-permute-done((bf16[23,16,256]{2,1,0:T(8,128)(2,1)}, bf16[23,16,256]{2,1,0:T(8,128)(2,1)S(1)}, u32[]{:S(2)}, u32[]{:S(2)}) %collective-permute-start.1) | collective-permute-done | bytes 188448 | tf_op jit(solution)/shard_map/ppermute | solution.py:410
  21.0 1.6 %copy-done = f32[4,17,32,256]{3,2,1,0:T(8,128)S(1)} copy-done((f32[4,17,32,256]{3,2,1,0:T(8,128)S(1)}, f32[4,17,32,256]{3,2,1,0:T(8,128)}, u32[]{:S(2)}) %copy-start) | copy-done | bytes 2228248
  25.1 1.5 %collective-permute-start.3 = (bf16[24,24,256]{2,1,0:T(8,128)(2,1)}, bf16[24,24,256]{2,1,0:T(8,128)(2,1)}, u32[]{:S(2)}, u32[]{:S(2)}) collective-permute-start(bf16[24,24,256]{2,1,0:T(8,128)(2,1)} %get-tuple-element.24), channel_id=1, source_target_pairs={{1,0},{2,1},{3,2},{4,3},{5,4},{6,5},{7,6},{8,7},{9,8},{10,9},{11,1... | collective-permute-start | bytes 884744 | tf_op jit(solution)/shard_map/ppermute | solution.py:410
  26.7 1.7 %copy-done.7 = bf16[2304,512]{1,0:T(8,128)(2,1)S(1)} copy-done((bf16[2304,512]{1,0:T(8,128)(2,1)S(1)}, bf16[2304,512]{1,0:T(8,128)(2,1)}, u32[]{:S(2)}) %copy-start.7) | copy-done | bytes 2359320
  28.3 2.1 %weights.1 = (bf16[4,1024,512]{2,1,0:T(8,128)(2,1)S(1)}, bf16[4,2048,256]{2,1,0:T(8,128)(2,1)S(1)}, bf16[2304,256]{1,0:T(8,128)(2,1)S(1)}, bf16[2304,256]{1,0:T(8,128)(2,1)S(1)}) custom-call(bf16[2304,256]{1,0:T(8,128)(2,1)S(1)} %copy-done.3, bf16[2304,256]{1,0:T(8,128)(2,1)S(1)} %copy-done.2, bf16[2304,512]{1,0:T(8,128)(2,1)S(1)} %copy-done.7), custom_call_target="tpu_custom_call" | custom-call | flops 10000000 | bytes 15000000 | tf_op jit(solution)/shard_map/weights/pallas_call | solution.py:441
  30.8 20.3 %tile.1 = (bf16[2,1152,512]{2,1,0:T(8,128)(2,1)S(1)}, bf16[2,1152,512]{2,1,0:T(8,128)(2,1)}, bf16[2,18,16,1024]{3,2,1,0:T(8,128)(2,1)S(1)}) custom-call(s32[3]{0:T(128)S(1)} %pad_add_fusion.place_ref, bf16[4,16,16,256]{3,2,1,0:T(8,128)(2,1)S(1)} %copy-done.8, f32[4,17,32,256]{3,2,1,0:T(8,128)S(1)} %copy-done.1, f32[16,16,256]{2,1,0:T(8,128)S(1)} %copy-done.4, ...), custom_call_target="tpu_custom_call" | custom-call | tf_op jit(solution)/shard_map/tile/pallas_call | solution.py:467
  51.1 1.4 %copy-done.5 = bf16[2,1152,512]{2,1,0:T(8,128)(2,1)} copy-done((bf16[2,1152,512]{2,1,0:T(8,128)(2,1)}, bf16[2,1152,512]{2,1,0:T(8,128)(2,1)S(1)}, u32[]{:S(2)}) %copy-start.5) | copy-done | bytes 2359320
  53.5 4.9 %collective-permute-start.4 = (bf16[2,1152,512]{2,1,0:T(8,128)(2,1)}, bf16[2,1152,512]{2,1,0:T(8,128)(2,1)S(1)}, u32[]{:S(2)}, u32[]{:S(2)}) collective-permute-start(bf16[2,1152,512]{2,1,0:T(8,128)(2,1)} %get-tuple-element.28), channel_id=1, source_target_pairs={{0,1},{1,0},{2,3},{3,2},{4,5},{5,4},{6,7},{7,6},{8,9},{9,8},{10,11... | collective-permute-start | bytes 7077896 | tf_op jit(solution)/shard_map/ppermute | solution.py:53
  61.0 2.2 %feat.1 = bf16[16,2,32,256]{3,2,1,0:T(8,128)(2,1)} custom-call(bf16[2,18,16,1024]{3,2,1,0:T(8,128)(2,1)S(1)} %copy-done.12, bf16[2304,256]{1,0:T(8,128)(2,1)S(1)} %copy-done.10), custom_call_target="tpu_custom_call" | custom-call | flops 1200000000 | bytes 3000000 | tf_op jit(solution)/shard_map/feat/pallas_call | solution.py:494
  64.0 1.7 %collective-permute-start.11 = (bf16[4,72,512]{2,1,0:T(8,128)(2,1)S(1)}, bf16[4,72,512]{2,1,0:T(8,128)(2,1)S(1)}, u32[]{:S(2)}, u32[]{:S(2)}) collective-permute-start(bf16[4,72,512]{2,1,0:T(8,128)(2,1)S(1)} %get-tuple-element.38), channel_id=1, source_target_pairs={{0,2},{1,3},{2,0},{3,1},{4,6},{5,7},{6,4},{7,5},{8,10},{9,11},{10,... | collective-permute-start | bytes 884744 | tf_op jit(solution)/shard_map/ppermute | solution.py:44
  65.7 12.0 %collective-permute-start.12 = (bf16[4,72,512]{2,1,0:T(8,128)(2,1)S(1)}, bf16[4,72,512]{2,1,0:T(8,128)(2,1)}, u32[]{:S(2)}, u32[]{:S(2)}) collective-permute-start(bf16[4,72,512]{2,1,0:T(8,128)(2,1)S(1)} %get-tuple-element.40), channel_id=1, source_target_pairs={{0,6},{1,7},{2,4},{3,5},{4,2},{5,3},{6,0},{7,1},{8,14},{9,15},{10,... | collective-permute-start | bytes 884744 | tf_op jit(solution)/shard_map/ppermute | solution.py:44
  77.7 1.4 %collective-permute-start.13 = (bf16[4,72,512]{2,1,0:T(8,128)(2,1)S(1)}, bf16[4,72,512]{2,1,0:T(8,128)(2,1)}, u32[]{:S(2)}, u32[]{:S(2)}) collective-permute-start(bf16[4,72,512]{2,1,0:T(8,128)(2,1)S(1)} %get-tuple-element.39), channel_id=1, source_target_pairs={{0,4},{1,5},{2,6},{3,7},{4,0},{5,1},{6,2},{7,3},{8,12},{9,13},{10,... | collective-permute-start | bytes 884744 | tf_op jit(solution)/shard_map/ppermute | solution.py:44
  79.7 3.7 %collective-permute-start.7 = (bf16[4,72,512]{2,1,0:T(8,128)(2,1)S(1)}, bf16[4,72,512]{2,1,0:T(8,128)(2,1)S(1)}, u32[]{:S(2)}, u32[]{:S(2)}) collective-permute-start(bf16[4,72,512]{2,1,0:T(8,128)(2,1)S(1)} %get-tuple-element.42), channel_id=1, source_target_pairs={{0,32},{1,33},{2,34},{3,35},{4,36},{5,37},{6,38},{7,39},{8,40},{9,... | collective-permute-start | bytes 884744 | tf_op jit(solution)/shard_map/ppermute | solution.py:44
  83.3 7.1 %collective-permute-done.12 = bf16[4,72,512]{2,1,0:T(8,128)(2,1)} collective-permute-done((bf16[4,72,512]{2,1,0:T(8,128)(2,1)S(1)}, bf16[4,72,512]{2,1,0:T(8,128)(2,1)}, u32[]{:S(2)}, u32[]{:S(2)}) %collective-permute-start.12) | collective-permute-done | bytes 294944 | tf_op jit(solution)/shard_map/ppermute | solution.py:44
  90.5 1.9 %collective-permute-done.13 = bf16[4,72,512]{2,1,0:T(8,128)(2,1)} collective-permute-done((bf16[4,72,512]{2,1,0:T(8,128)(2,1)S(1)}, bf16[4,72,512]{2,1,0:T(8,128)(2,1)}, u32[]{:S(2)}, u32[]{:S(2)}) %collective-permute-start.13) | collective-permute-done | bytes 294944 | tf_op jit(solution)/shard_map/ppermute | solution.py:44
  94.1 3.7 %collective-permute-start.16 = (bf16[72,512]{1,0:T(8,128)(2,1)S(1)}, bf16[72,512]{1,0:T(8,128)(2,1)S(1)}, u32[]{:S(2)}, u32[]{:S(2)}) collective-permute-start(bf16[72,512]{1,0:T(8,128)(2,1)S(1)} %get-tuple-element.45), channel_id=1, source_target_pairs={{0,32},{1,33},{2,34},{3,35},{4,36},{5,37},{6,38},{7,39},{8,40},{9,... | collective-permute-start | bytes 221192 | tf_op jit(solution)/shard_map/ppermute | solution.py:44
  98.0 1.8 %collective-permute-start.10 = (bf16[72,512]{1,0:T(8,128)(2,1)S(1)}, bf16[72,512]{1,0:T(8,128)(2,1)S(1)}, u32[]{:S(2)}, u32[]{:S(2)}) collective-permute-start(bf16[72,512]{1,0:T(8,128)(2,1)S(1)} %get-tuple-element.48), channel_id=1, source_target_pairs={{0,4},{1,5},{2,6},{3,7},{4,0},{5,1},{6,2},{7,3},{8,12},{9,13},{10,... | collective-permute-start | bytes 221192 | tf_op jit(solution)/shard_map/ppermute | solution.py:44
  100.8 1.4 %collective-permute-start.9 = (bf16[72,512]{1,0:T(8,128)(2,1)S(1)}, bf16[72,512]{1,0:T(8,128)(2,1)S(1)}, u32[]{:S(2)}, u32[]{:S(2)}) collective-permute-start(bf16[72,512]{1,0:T(8,128)(2,1)S(1)} %get-tuple-element.49), channel_id=1, source_target_pairs={{0,6},{1,7},{2,4},{3,5},{4,2},{5,3},{6,0},{7,1},{8,14},{9,15},{10,... | collective-permute-start | bytes 221192 | tf_op jit(solution)/shard_map/ppermute | solution.py:44
  102.3 1.8 %collective-permute-done.10 = bf16[72,512]{1,0:T(8,128)(2,1)S(1)} collective-permute-done((bf16[72,512]{1,0:T(8,128)(2,1)S(1)}, bf16[72,512]{1,0:T(8,128)(2,1)S(1)}, u32[]{:S(2)}, u32[]{:S(2)}) %collective-permute-start.10) | collective-permute-done | bytes 73760 | tf_op jit(solution)/shard_map/ppermute | solution.py:44
  104.2 2.2 %collective-permute-done.9 = bf16[72,512]{1,0:T(8,128)(2,1)S(1)} collective-permute-done((bf16[72,512]{1,0:T(8,128)(2,1)S(1)}, bf16[72,512]{1,0:T(8,128)(2,1)S(1)}, u32[]{:S(2)}, u32[]{:S(2)}) %collective-permute-start.9) | collective-permute-done | bytes 73760 | tf_op jit(solution)/shard_map/ppermute | solution.py:44
  106.6 1.7 %collective-permute-start.17 = (bf16[2,18,512]{2,1,0:T(8,128)(2,1)S(1)}, bf16[2,18,512]{2,1,0:T(8,128)(2,1)S(1)}, u32[]{:S(2)}, u32[]{:S(2)}) collective-permute-start(bf16[2,18,512]{2,1,0:T(8,128)(2,1)S(1)} %get-tuple-element.50), channel_id=1, source_target_pairs={{0,64},{1,65},{2,66},{3,67},{4,68},{5,69},{6,70},{7,71},{8,72},{9,... | collective-permute-start | bytes 110600 | tf_op jit(solution)/shard_map/ppermute | solution.py:44
  108.2 4.4 %collective-permute-start.18 = (bf16[2,18,512]{2,1,0:T(8,128)(2,1)S(1)}, bf16[2,18,512]{2,1,0:T(8,128)(2,1)S(1)}, u32[]{:S(2)}, u32[]{:S(2)}) collective-permute-start(bf16[2,18,512]{2,1,0:T(8,128)(2,1)S(1)} %get-tuple-element.52), channel_id=1, source_target_pairs={{0,192},{1,193},{2,194},{3,195},{4,196},{5,197},{6,198},{7,199},{8... | collective-permute-start | bytes 110600 | tf_op jit(solution)/shard_map/ppermute | solution.py:44
  112.7 2.6 %collective-permute-done.18 = bf16[2,18,512]{2,1,0:T(8,128)(2,1)S(1)} collective-permute-done((bf16[2,18,512]{2,1,0:T(8,128)(2,1)S(1)}, bf16[2,18,512]{2,1,0:T(8,128)(2,1)S(1)}, u32[]{:S(2)}, u32[]{:S(2)}) %collective-permute-start.18) | collective-permute-done | bytes 36896 | tf_op jit(solution)/shard_map/ppermute | solution.py:44
  115.2 2.4 %collective-permute-done.19 = bf16[2,18,512]{2,1,0:T(8,128)(2,1)S(1)} collective-permute-done((bf16[2,18,512]{2,1,0:T(8,128)(2,1)S(1)}, bf16[2,18,512]{2,1,0:T(8,128)(2,1)S(1)}, u32[]{:S(2)}, u32[]{:S(2)}) %collective-permute-start.19) | collective-permute-done | bytes 36896 | tf_op jit(solution)/shard_map/ppermute | solution.py:44
  117.8 1.9 %collective-permute-start.20 = (bf16[2,9,512]{2,0,1:T(2,128)(2,1)S(1)}, bf16[2,9,512]{2,0,1:T(2,128)(2,1)S(1)}, u32[]{:S(2)}, u32[]{:S(2)}) collective-permute-start(bf16[2,9,512]{2,0,1:T(2,128)(2,1)S(1)} %get-tuple-element.53), channel_id=1, source_target_pairs={{0,0},{1,128},{2,8},{3,136},{4,16},{5,144},{6,24},{7,152},{8,1},{9... | collective-permute-start | bytes 55304 | tf_op jit(solution)/shard_map/ppermute | solution.py:76
  119.7 1.5 %collective-permute-start.21 = (bf16[2,9,512]{2,0,1:T(2,128)(2,1)S(1)}, bf16[2,9,512]{2,0,1:T(2,128)(2,1)S(1)}, u32[]{:S(2)}, u32[]{:S(2)}) collective-permute-start(bf16[2,9,512]{2,0,1:T(2,128)(2,1)S(1)} %get-tuple-element.54), channel_id=1, source_target_pairs={{0,1},{1,129},{2,9},{3,137},{4,17},{5,145},{6,25},{7,153},{8,0},{9... | collective-permute-start | bytes 55304 | tf_op jit(solution)/shard_map/ppermute | solution.py:76
  121.2 6.1 %collective-permute-done.20 = bf16[2,9,512]{2,0,1:T(2,128)(2,1)S(1)} collective-permute-done((bf16[2,9,512]{2,0,1:T(2,128)(2,1)S(1)}, bf16[2,9,512]{2,0,1:T(2,128)(2,1)S(1)}, u32[]{:S(2)}, u32[]{:S(2)}) %collective-permute-start.20) | collective-permute-done | bytes 18464 | tf_op jit(solution)/shard_map/ppermute | solution.py:76
  127.3 4.9 %collective-permute-done.21 = bf16[2,9,512]{2,0,1:T(2,128)(2,1)S(1)} collective-permute-done((bf16[2,9,512]{2,0,1:T(2,128)(2,1)S(1)}, bf16[2,9,512]{2,0,1:T(2,128)(2,1)S(1)}, u32[]{:S(2)}, u32[]{:S(2)}) %collective-permute-start.21) | collective-permute-done | bytes 18464 | tf_op jit(solution)/shard_map/ppermute | solution.py:76
  (68 shorter events, 13.0 us)
Async XLA Ops:
  0.6 20.3 %copy-start.4 = (f32[16,16,256]{2,1,0:T(8,128)S(1)}, f32[16,16,256]{2,1,0:T(8,128)}, u32[]{:S(2)}) copy-start(f32[16,16,256]{2,1,0:T(8,128)} %low_ref.3) | copy-start | bytes 786436
  6.8 8.6 %collective-permute-start = (bf16[23,16,256]{2,1,0:T(8,128)(2,1)}, bf16[23,16,256]{2,1,0:T(8,128)(2,1)S(1)}, u32[]{:S(2)}, u32[]{:S(2)}) collective-permute-start(bf16[23,16,256]{2,1,0:T(8,128)(2,1)} %get-tuple-element.21), channel_id=1, source_target_pairs={{0,16},{1,17},{2,18},{3,19},{4,20},{5,21},{6,22},{7,23},{8,24},{9,... | collective-permute-start | bytes 565256 | tf_op jit(solution)/shard_map/ppermute | solution.py:410
  10.6 10.4 %collective-permute-start.1 = (bf16[23,16,256]{2,1,0:T(8,128)(2,1)}, bf16[23,16,256]{2,1,0:T(8,128)(2,1)S(1)}, u32[]{:S(2)}, u32[]{:S(2)}) collective-permute-start(bf16[23,16,256]{2,1,0:T(8,128)(2,1)} %get-tuple-element.22), channel_id=1, source_target_pairs={{16,0},{17,1},{18,2},{19,3},{20,4},{21,5},{22,6},{23,7},{24,8},{25... | collective-permute-start | bytes 565256 | tf_op jit(solution)/shard_map/ppermute | solution.py:410
  21.0 1.6 %copy-start = (f32[4,17,32,256]{3,2,1,0:T(8,128)S(1)}, f32[4,17,32,256]{3,2,1,0:T(8,128)}, u32[]{:S(2)}) copy-start(f32[4,17,32,256]{3,2,1,0:T(8,128)} %get-tuple-element.20.part_ref) | copy-start | bytes 6684676
  22.6 4.0 %copy-start.2 = (bf16[2304,256]{1,0:T(8,128)(2,1)S(1)}, bf16[2304,256]{1,0:T(8,128)(2,1)}, u32[]{:S(2)}) copy-start(bf16[2304,256]{1,0:T(8,128)(2,1)} %w_coarse.3) | copy-start | bytes 3538948
  22.6 4.1 %copy-start.3 = (bf16[2304,256]{1,0:T(8,128)(2,1)S(1)}, bf16[2304,256]{1,0:T(8,128)(2,1)}, u32[]{:S(2)}) copy-start(bf16[2304,256]{1,0:T(8,128)(2,1)} %w_post.1) | copy-start | bytes 3538948
  23.8 6.7 %collective-permute-start.2 = (bf16[24,24,256]{2,1,0:T(8,128)(2,1)}, bf16[24,24,256]{2,1,0:T(8,128)(2,1)S(1)}, u32[]{:S(2)}, u32[]{:S(2)}) collective-permute-start(bf16[24,24,256]{2,1,0:T(8,128)(2,1)} %get-tuple-element.23), channel_id=1, source_target_pairs={{0,1},{1,2},{2,3},{3,4},{4,5},{5,6},{6,7},{7,8},{8,9},{9,10},{10,1... | collective-permute-start | bytes 884744 | tf_op jit(solution)/shard_map/ppermute | solution.py:410
  25.1 5.6 %collective-permute-start.3 = (bf16[24,24,256]{2,1,0:T(8,128)(2,1)}, bf16[24,24,256]{2,1,0:T(8,128)(2,1)}, u32[]{:S(2)}, u32[]{:S(2)}) collective-permute-start(bf16[24,24,256]{2,1,0:T(8,128)(2,1)} %get-tuple-element.24), channel_id=1, source_target_pairs={{1,0},{2,1},{3,2},{4,3},{5,4},{6,5},{7,6},{8,7},{9,8},{10,9},{11,1... | collective-permute-start | bytes 884744 | tf_op jit(solution)/shard_map/ppermute | solution.py:410
  26.6 1.7 %copy-start.7 = (bf16[2304,512]{1,0:T(8,128)(2,1)S(1)}, bf16[2304,512]{1,0:T(8,128)(2,1)}, u32[]{:S(2)}) copy-start(bf16[2304,512]{1,0:T(8,128)(2,1)} %w_prior.1) | copy-start | bytes 7077892
  28.3 2.4 %copy-start.1 = (f32[4,17,32,256]{3,2,1,0:T(8,128)S(1)}, f32[4,17,32,256]{3,2,1,0:T(8,128)}, u32[]{:S(2)}) copy-start(f32[4,17,32,256]{3,2,1,0:T(8,128)} %get-tuple-element.20.part_ref) | copy-start | bytes 6684676
  28.3 2.4 %copy-start.8 = (bf16[4,16,16,256]{3,2,1,0:T(8,128)(2,1)S(1)}, bf16[4,16,16,256]{3,2,1,0:T(8,128)(2,1)}, u32[]{:S(2)}) copy-start(bf16[4,16,16,256]{3,2,1,0:T(8,128)(2,1)} %get-tuple-element.19.own_ref) | copy-start | bytes 1572868
  30.4 20.6 %copy-start.9 = (bf16[2304,256]{1,0:T(8,128)(2,1)}, bf16[2304,256]{1,0:T(8,128)(2,1)S(1)}, u32[]{:S(2)}) copy-start(bf16[2304,256]{1,0:T(8,128)(2,1)S(1)} %get-tuple-element.30.w_post_t) | copy-start | bytes 3538948
  51.1 1.4 %copy-start.5 = (bf16[2,1152,512]{2,1,0:T(8,128)(2,1)}, bf16[2,1152,512]{2,1,0:T(8,128)(2,1)S(1)}, u32[]{:S(2)}) copy-start(bf16[2,1152,512]{2,1,0:T(8,128)(2,1)S(1)} %get-tuple-element.32.keep_ref) | copy-start | bytes 7077892
  53.5 9.7 %collective-permute-start.4 = (bf16[2,1152,512]{2,1,0:T(8,128)(2,1)}, bf16[2,1152,512]{2,1,0:T(8,128)(2,1)S(1)}, u32[]{:S(2)}, u32[]{:S(2)}) collective-permute-start(bf16[2,1152,512]{2,1,0:T(8,128)(2,1)} %get-tuple-element.28), channel_id=1, source_target_pairs={{0,1},{1,0},{2,3},{3,2},{4,5},{5,4},{6,7},{7,6},{8,9},{9,8},{10,11... | collective-permute-start | bytes 7077896 | tf_op jit(solution)/shard_map/ppermute | solution.py:53
  61.0 2.2 %copy-start.6 = (bf16[2,1152,512]{2,1,0:T(8,128)(2,1)S(1)}, bf16[2,1152,512]{2,1,0:T(8,128)(2,1)}, u32[]{:S(2)}) copy-start(bf16[2,1152,512]{2,1,0:T(8,128)(2,1)} %copy-done.5) | copy-start | bytes 7077892
  64.0 15.6 %collective-permute-start.11 = (bf16[4,72,512]{2,1,0:T(8,128)(2,1)S(1)}, bf16[4,72,512]{2,1,0:T(8,128)(2,1)S(1)}, u32[]{:S(2)}, u32[]{:S(2)}) collective-permute-start(bf16[4,72,512]{2,1,0:T(8,128)(2,1)S(1)} %get-tuple-element.38), channel_id=1, source_target_pairs={{0,2},{1,3},{2,0},{3,1},{4,6},{5,7},{6,4},{7,5},{8,10},{9,11},{10,... | collective-permute-start | bytes 884744 | tf_op jit(solution)/shard_map/ppermute | solution.py:44
  65.7 24.8 %collective-permute-start.12 = (bf16[4,72,512]{2,1,0:T(8,128)(2,1)S(1)}, bf16[4,72,512]{2,1,0:T(8,128)(2,1)}, u32[]{:S(2)}, u32[]{:S(2)}) collective-permute-start(bf16[4,72,512]{2,1,0:T(8,128)(2,1)S(1)} %get-tuple-element.40), channel_id=1, source_target_pairs={{0,6},{1,7},{2,4},{3,5},{4,2},{5,3},{6,0},{7,1},{8,14},{9,15},{10,... | collective-permute-start | bytes 884744 | tf_op jit(solution)/shard_map/ppermute | solution.py:44
  77.7 14.7 %collective-permute-start.13 = (bf16[4,72,512]{2,1,0:T(8,128)(2,1)S(1)}, bf16[4,72,512]{2,1,0:T(8,128)(2,1)}, u32[]{:S(2)}, u32[]{:S(2)}) collective-permute-start(bf16[4,72,512]{2,1,0:T(8,128)(2,1)S(1)} %get-tuple-element.39), channel_id=1, source_target_pairs={{0,4},{1,5},{2,6},{3,7},{4,0},{5,1},{6,2},{7,3},{8,12},{9,13},{10,... | collective-permute-start | bytes 884744 | tf_op jit(solution)/shard_map/ppermute | solution.py:44
  79.2 15.0 %collective-permute-start.5 = (bf16[4,72,512]{2,1,0:T(8,128)(2,1)S(1)}, bf16[4,72,512]{2,1,0:T(8,128)(2,1)S(1)}, u32[]{:S(2)}, u32[]{:S(2)}) collective-permute-start(bf16[4,72,512]{2,1,0:T(8,128)(2,1)S(1)} %get-tuple-element.41), channel_id=1, source_target_pairs={{0,16},{1,17},{2,18},{3,19},{4,20},{5,21},{6,22},{7,23},{8,24},{9,... | collective-permute-start | bytes 884744 | tf_op jit(solution)/shard_map/ppermute | solution.py:44
  79.3 18.6 %collective-permute-start.6 = (bf16[4,72,512]{2,1,0:T(8,128)(2,1)S(1)}, bf16[4,72,512]{2,1,0:T(8,128)(2,1)S(1)}, u32[]{:S(2)}, u32[]{:S(2)}) collective-permute-start(bf16[4,72,512]{2,1,0:T(8,128)(2,1)S(1)} %get-tuple-element.43), channel_id=1, source_target_pairs={{0,48},{1,49},{2,50},{3,51},{4,52},{5,53},{6,54},{7,55},{8,56},{9,... | collective-permute-start | bytes 884744 | tf_op jit(solution)/shard_map/ppermute | solution.py:44
  79.7 18.2 %collective-permute-start.7 = (bf16[4,72,512]{2,1,0:T(8,128)(2,1)S(1)}, bf16[4,72,512]{2,1,0:T(8,128)(2,1)S(1)}, u32[]{:S(2)}, u32[]{:S(2)}) collective-permute-start(bf16[4,72,512]{2,1,0:T(8,128)(2,1)S(1)} %get-tuple-element.42), channel_id=1, source_target_pairs={{0,32},{1,33},{2,34},{3,35},{4,36},{5,37},{6,38},{7,39},{8,40},{9,... | collective-permute-start | bytes 884744 | tf_op jit(solution)/shard_map/ppermute | solution.py:44
  93.6 7.2 %collective-permute-start.14 = (bf16[72,512]{1,0:T(8,128)(2,1)S(1)}, bf16[72,512]{1,0:T(8,128)(2,1)S(1)}, u32[]{:S(2)}, u32[]{:S(2)}) collective-permute-start(bf16[72,512]{1,0:T(8,128)(2,1)S(1)} %get-tuple-element.44), channel_id=1, source_target_pairs={{0,16},{1,17},{2,18},{3,19},{4,20},{5,21},{6,22},{7,23},{8,24},{9,... | collective-permute-start | bytes 221192 | tf_op jit(solution)/shard_map/ppermute | solution.py:44
  93.7 8.5 %collective-permute-start.15 = (bf16[72,512]{1,0:T(8,128)(2,1)S(1)}, bf16[72,512]{1,0:T(8,128)(2,1)S(1)}, u32[]{:S(2)}, u32[]{:S(2)}) collective-permute-start(bf16[72,512]{1,0:T(8,128)(2,1)S(1)} %get-tuple-element.46), channel_id=1, source_target_pairs={{0,48},{1,49},{2,50},{3,51},{4,52},{5,53},{6,54},{7,55},{8,56},{9,... | collective-permute-start | bytes 221192 | tf_op jit(solution)/shard_map/ppermute | solution.py:44
  94.1 8.1 %collective-permute-start.16 = (bf16[72,512]{1,0:T(8,128)(2,1)S(1)}, bf16[72,512]{1,0:T(8,128)(2,1)S(1)}, u32[]{:S(2)}, u32[]{:S(2)}) collective-permute-start(bf16[72,512]{1,0:T(8,128)(2,1)S(1)} %get-tuple-element.45), channel_id=1, source_target_pairs={{0,32},{1,33},{2,34},{3,35},{4,36},{5,37},{6,38},{7,39},{8,40},{9,... | collective-permute-start | bytes 221192 | tf_op jit(solution)/shard_map/ppermute | solution.py:44
  98.0 6.0 %collective-permute-start.10 = (bf16[72,512]{1,0:T(8,128)(2,1)S(1)}, bf16[72,512]{1,0:T(8,128)(2,1)S(1)}, u32[]{:S(2)}, u32[]{:S(2)}) collective-permute-start(bf16[72,512]{1,0:T(8,128)(2,1)S(1)} %get-tuple-element.48), channel_id=1, source_target_pairs={{0,4},{1,5},{2,6},{3,7},{4,0},{5,1},{6,2},{7,3},{8,12},{9,13},{10,... | collective-permute-start | bytes 221192 | tf_op jit(solution)/shard_map/ppermute | solution.py:44
  99.9 4.4 %collective-permute-start.8 = (bf16[72,512]{1,0:T(8,128)(2,1)S(1)}, bf16[72,512]{1,0:T(8,128)(2,1)S(1)}, u32[]{:S(2)}, u32[]{:S(2)}) collective-permute-start(bf16[72,512]{1,0:T(8,128)(2,1)S(1)} %get-tuple-element.47), channel_id=1, source_target_pairs={{0,2},{1,3},{2,0},{3,1},{4,6},{5,7},{6,4},{7,5},{8,10},{9,11},{10,... | collective-permute-start | bytes 221192 | tf_op jit(solution)/shard_map/ppermute | solution.py:44
  100.8 5.6 %collective-permute-start.9 = (bf16[72,512]{1,0:T(8,128)(2,1)S(1)}, bf16[72,512]{1,0:T(8,128)(2,1)S(1)}, u32[]{:S(2)}, u32[]{:S(2)}) collective-permute-start(bf16[72,512]{1,0:T(8,128)(2,1)S(1)} %get-tuple-element.49), channel_id=1, source_target_pairs={{0,6},{1,7},{2,4},{3,5},{4,2},{5,3},{6,0},{7,1},{8,14},{9,15},{10,... | collective-permute-start | bytes 221192 | tf_op jit(solution)/shard_map/ppermute | solution.py:44
  106.6 6.1 %collective-permute-start.17 = (bf16[2,18,512]{2,1,0:T(8,128)(2,1)S(1)}, bf16[2,18,512]{2,1,0:T(8,128)(2,1)S(1)}, u32[]{:S(2)}, u32[]{:S(2)}) collective-permute-start(bf16[2,18,512]{2,1,0:T(8,128)(2,1)S(1)} %get-tuple-element.50), channel_id=1, source_target_pairs={{0,64},{1,65},{2,66},{3,67},{4,68},{5,69},{6,70},{7,71},{8,72},{9,... | collective-permute-start | bytes 110600 | tf_op jit(solution)/shard_map/ppermute | solution.py:44
  108.2 7.0 %collective-permute-start.18 = (bf16[2,18,512]{2,1,0:T(8,128)(2,1)S(1)}, bf16[2,18,512]{2,1,0:T(8,128)(2,1)S(1)}, u32[]{:S(2)}, u32[]{:S(2)}) collective-permute-start(bf16[2,18,512]{2,1,0:T(8,128)(2,1)S(1)} %get-tuple-element.52), channel_id=1, source_target_pairs={{0,192},{1,193},{2,194},{3,195},{4,196},{5,197},{6,198},{7,199},{8... | collective-permute-start | bytes 110600 | tf_op jit(solution)/shard_map/ppermute | solution.py:44
  112.7 5.0 %collective-permute-start.19 = (bf16[2,18,512]{2,1,0:T(8,128)(2,1)S(1)}, bf16[2,18,512]{2,1,0:T(8,128)(2,1)S(1)}, u32[]{:S(2)}, u32[]{:S(2)}) collective-permute-start(bf16[2,18,512]{2,1,0:T(8,128)(2,1)S(1)} %get-tuple-element.51), channel_id=1, source_target_pairs={{0,128},{1,129},{2,130},{3,131},{4,132},{5,133},{6,134},{7,135},{8... | collective-permute-start | bytes 110600 | tf_op jit(solution)/shard_map/ppermute | solution.py:44
  117.8 9.6 %collective-permute-start.20 = (bf16[2,9,512]{2,0,1:T(2,128)(2,1)S(1)}, bf16[2,9,512]{2,0,1:T(2,128)(2,1)S(1)}, u32[]{:S(2)}, u32[]{:S(2)}) collective-permute-start(bf16[2,9,512]{2,0,1:T(2,128)(2,1)S(1)} %get-tuple-element.53), channel_id=1, source_target_pairs={{0,0},{1,128},{2,8},{3,136},{4,16},{5,144},{6,24},{7,152},{8,1},{9... | collective-permute-start | bytes 55304 | tf_op jit(solution)/shard_map/ppermute | solution.py:76
  119.7 12.6 %collective-permute-start.21 = (bf16[2,9,512]{2,0,1:T(2,128)(2,1)S(1)}, bf16[2,9,512]{2,0,1:T(2,128)(2,1)S(1)}, u32[]{:S(2)}, u32[]{:S(2)}) collective-permute-start(bf16[2,9,512]{2,0,1:T(2,128)(2,1)S(1)} %get-tuple-element.54), channel_id=1, source_target_pairs={{0,1},{1,129},{2,9},{3,137},{4,17},{5,145},{6,25},{7,153},{8,0},{9... | collective-permute-start | bytes 55304 | tf_op jit(solution)/shard_map/ppermute | solution.py:76
  (3 other events, 3.6 us)

commit v5 on v4

--- a/solution.py
+++ b/solution.py
@@ -109,7 +109,7 @@
 
 
 def first_kernel(feat_hbm, fine_hbm, low_hbm, post_hbm, own_ref, part_ref, top_ref, bottom_ref,
-                 feat_ref, fine_ref, low_ref, w_post, wide, noise, field, cat, spill, sems):
+                 left_ref, right_ref, feat_ref, fine_ref, low_ref, w_post, wide, noise, field, cat, spill, side, sems):
     pairs = ((feat_hbm, feat_ref), (post_hbm.at[:768], w_post.at[:768]), (post_hbm.at[768:1536], w_post.at[768:1536]),
              (post_hbm.at[1536:], w_post.at[1536:]), (fine_hbm.at[:8], fine_ref.at[:8]),
              (fine_hbm.at[8:], fine_ref.at[8:]), (low_hbm, low_ref))
@@ -153,34 +153,37 @@
                 spill[e:e + 1, :] = part_ref[2 * row + col, at, edge:edge + 1, :]
         out[18:21] = low_ref[low_first:low_first + 3].astype(BF)
         out[21:23] = spill[...].reshape(2, 16, 256).astype(BF)
-
-
-def middle_kernel(part_ref, low_ref, up_ref, down_ref, left_ref, right_ref, side, spill):
-    lows = ((4, low_ref[...]), (1, up_ref[18:21].astype(F32)), (20, down_ref[18:21].astype(F32)))
     for out, long, long_from, other_from, low_from in ((left_ref, 1, -1, 0, 0), (right_ref, 0, 12, 12, 13)):
         side[...] = jnp.zeros(side.shape, F32)
         for row in range(2):
             at = 9 * row
-            rows = slice(4 - row, 21 - row)
+            rows = slice(1 - row, 18 - row)
             side[rows, at:at + 5, :] = part_ref[2 * row + long, :, 8 + long_from:13 + long_from, :]
             side[rows, at + 5:at + 9, :] = part_ref[2 * row + 1 - long, :, 8 + other_from:12 + other_from, :]
-        for ref, first in ((up_ref, -8), (down_ref, 31)):
+        side[1:17, 18:21, :] = low_ref[:, low_from:low_from + 3, :]
+        out[...] = side[...].astype(BF)
+
+
+def middle_kernel(up_ref, down_ref, left_ref, right_ref, side, spill):
+    for out, long, other_from, low_from in ((left_ref, 1, 0, 0), (right_ref, 0, 12, 13)):
+        side[...] = jnp.zeros(side.shape, F32)
+        for ref, first, offset in ((up_ref, -8, 4), (down_ref, 31, -10)):
             spill[...] = ref[21:23].astype(F32).reshape(32, 256)
             for r in range(9):
                 line = first + r
                 row = line % 2
-                here, at = line // 2 + 4, 9 * row
+                here, at = line // 2 + offset, 9 * row
                 cells = ref[2 * r + long].astype(F32)
                 end = spill[2 * r + long:2 * r + long + 1, :]
                 if long:
-                    side[here, at:at + 1, :] += end
-                    side[here, at + 1:at + 5, :] += cells[0:4]
+                    side[here, at:at + 1, :] = end
+                    side[here, at + 1:at + 5, :] = cells[0:4]
                 else:
-                    side[here, at:at + 4, :] += cells[12:16]
-                    side[here, at + 4:at + 5, :] += end
-                side[here, at + 5:at + 9, :] += ref[2 * r + 1 - long].astype(F32)[other_from:other_from + 4]
-        for here, block in lows:
-            side[here:here + block.shape[0], 18:21, :] = block[:, low_from:low_from + 3, :]
+                    side[here, at:at + 4, :] = cells[12:16]
+                    side[here, at + 4:at + 5, :] = end
+                side[here, at + 5:at + 9, :] = ref[2 * r + 1 - long].astype(F32)[other_from:other_from + 4]
+        side[1:4, 18:21, :] = up_ref[18:21].astype(F32)[:, low_from:low_from + 3, :]
+        side[6:9, 18:21, :] = down_ref[18:21].astype(F32)[:, low_from:low_from + 3, :]
         out[...] = side[...].astype(BF)
 
 
@@ -225,7 +228,7 @@
     return own_cells(block).T
 
 
-def main_kernel(scale, place_ref, own_ref, part_ref, low_ref, up_ref, down_ref, left_ref, right_ref,
+def main_kernel(scale, place_ref, own_ref, part_ref, low_ref, up_ref, down_ref, left_ref, right_ref, more_left_ref, more_right_ref,
                 w_coarse, fold, fold_t, w_coarse_t, keep_ref, send_ref, g_fine,
                 fine, low, pool_cat, coarse, ctx_cat, err, d_cat, d_own, gc_cat, gc_own, spill, grads):
     def put(which, tap, lanes, value):
@@ -251,13 +254,17 @@
                 fine[2 * (line % 2) + col, line // 2 + 4, 8:24, :] += ref[e].astype(F32)
                 fine[2 * (line % 2) + col, line // 2 + 4, edge:edge + 1, :] += spill[e:e + 1, :]
         low[low_first:low_first + 3, 8:24, :] = ref[18:21].astype(F32)
-    for ref, long, long_at, other_at, low_at in ((left_ref, 0, 4, 4, 5), (right_ref, 1, 23, 24, 24)):
-        block = ref[...].astype(F32)
-        for row in range(2):
-            at = 9 * row
-            fine[2 * row + long, :, long_at:long_at + 5, :] += block[:, at:at + 5, :]
-            fine[2 * row + 1 - long, :, other_at:other_at + 4, :] += block[:, at + 5:at + 9, :]
-        low[:, low_at:low_at + 3, :] = block[1:23, 18:21, :]
+    for ref, more, long, long_at, other_at, low_at in (
+            (left_ref, more_left_ref, 0, 4, 4, 5), (right_ref, more_right_ref, 1, 23, 24, 24)):
+        block, rest = ref[...].astype(F32), more[...].astype(F32)
+        for rows, cells in ((slice(3, 21), block), (slice(0, 5), rest[0:5]), (slice(19, 24), rest[5:10])):
+            for row in range(2):
+                at = 9 * row
+                fine[2 * row + long, rows, long_at:long_at + 5, :] += cells[:, at:at + 5, :]
+                fine[2 * row + 1 - long, rows, other_at:other_at + 4, :] += cells[:, at + 5:at + 9, :]
+        low[3:19, low_at:low_at + 3, :] = block[1:17, 18:21, :]
+        low[0:3, low_at:low_at + 3, :] = rest[1:4, 18:21, :]
+        low[19:22, low_at:low_at + 3, :] = rest[6:9, 18:21, :]
 
     @pl.loop(0, 3)
     def _(step):
@@ -412,16 +419,18 @@
 
 def on_device(feat, noise_fine, noise_coarse, w_post, w_coarse, w_prior):
     scale = 1.0 / 512.0
-    own, part, top, bottom = pl.pallas_call(
+    own, part, top, bottom, left, right = pl.pallas_call(
         first_kernel,
         out_shape=[
             jax.ShapeDtypeStruct((4, 16, 16, 256), BF),
             jax.ShapeDtypeStruct((4, 17, 32, 256), F32),
             jax.ShapeDtypeStruct((23, 16, 256), BF),
             jax.ShapeDtypeStruct((23, 16, 256), BF),
+            jax.ShapeDtypeStruct((18, 24, 256), BF),
+            jax.ShapeDtypeStruct((18, 24, 256), BF),
         ],
         in_specs=[pl.BlockSpec(memory_space=pltpu.HBM)] * 4,
-        out_specs=in_vmem(4),
+        out_specs=in_vmem(6),
         scratch_shapes=[
             pltpu.VMEM((16, 2, 32, 256), BF),
             pltpu.VMEM((16, 2, 32, 256), F32),
@@ -432,11 +441,13 @@
             pltpu.VMEM((2, 18, 32, 256), F32),
             pltpu.VMEM((2, 18, 32, 1024), BF),
             pltpu.VMEM((32, 256), F32),
+            pltpu.VMEM((18, 24, 256), F32),
             pltpu.SemaphoreType.DMA((7,)),
         ],
         compiler_params=room(59),
         name="first",
     )(feat.reshape(16, 2, 32, 256), noise_fine.reshape(16, 2, 32, 256), noise_coarse, w_post)
+    from_left, from_right = sent(right, 0, 1), sent(left, 0, -1)
     from_up, from_down = sent(bottom, 1, 0), sent(top, -1, 0)
     fold, fold_t, w_post_t, w_coarse_t = pl.pallas_call(
         weight_kernel,
@@ -454,14 +465,14 @@
     )(w_post, w_coarse, w_prior)
     left, right = pl.pallas_call(
         middle_kernel,
-        out_shape=[jax.ShapeDtypeStruct((24, 24, 256), BF)] * 2,
-        in_specs=in_vmem(4),
+        out_shape=[jax.ShapeDtypeStruct((10, 24, 256), BF)] * 2,
+        in_specs=in_vmem(2),
         out_specs=in_vmem(2),
-        scratch_shapes=[pltpu.VMEM((24, 24, 256), F32), pltpu.VMEM((32, 256), F32)],
-        compiler_params=room(10),
+        scratch_shapes=[pltpu.VMEM((10, 24, 256), F32), pltpu.VMEM((32, 256), F32)],
+        compiler_params=room(6),
         name="middle",
-    )(part, noise_coarse, from_up, from_down)
-    from_left, from_right = sent(right, 0, 1), sent(left, 0, -1)
+    )(from_up, from_down)
+    more_left, more_right = sent(right, 0, 1), sent(left, 0, -1)
     row, col = lax.axis_index("row"), lax.axis_index("col")
     place = jnp.stack([row, col, col % 2]).astype(jnp.int32)
     keep, send, g_fine = pl.pallas_call(
@@ -471,7 +482,7 @@
             jax.ShapeDtypeStruct((2, 1152, 512), BF),
             jax.ShapeDtypeStruct((2, 18, 16, 1024), BF),
         ],
-        in_specs=[pl.BlockSpec(memory_space=pltpu.SMEM)] + in_vmem(11),
+        in_specs=[pl.BlockSpec(memory_space=pltpu.SMEM)] + in_vmem(13),
         out_specs=in_vmem(3),
         scratch_shapes=[
             pltpu.VMEM((4, 24, 32, 256), F32),
@@ -490,7 +501,7 @@
         compiler_params=room(32),
         name="tile",
     )(place, own, part, noise_coarse, from_up, from_down, from_left, from_right,
-      w_coarse, fold, fold_t, w_coarse_t)
+      more_left, more_right, w_coarse, fold, fold_t, w_coarse_t)
     grad_feat = pl.pallas_call(
         feat_kernel,
         out_shape=jax.ShapeDtypeStruct((16, 2, 32, 256), BF),

time: 135 us -> 139 us (1.030)
  waiting for transfers between devices: 37.7 us -> 31.7 us
  local copies, waits for them, and re-layouts: 10.8 us -> 16.3 us
  starting transfers between devices: 50.7 us -> 54.2 us
    unnamed x27 -> x45, local copies, waits for them, and re-layouts: 8.32 us -> 13.8 us
    ppermute x2, starting transfers between devices: 3.43 us -> 6.9 us  [reduce_scatter(): total = total + lax.ppermute(piece, ('row', 'col'), pairs).astype(F32)]
    ppermute x2, waiting for transfers between devices: 11 us -> 7.88 us  [reduce_scatter(): total = total + lax.ppermute(piece, ('row', 'col'), pairs).astype(F32)]
    ppermute x4 -> x6, waiting for transfers between devices: 8.5 us -> 5.69 us  [sent(): return lax.ppermute(strip, ('row', 'col'), pairs)]
    ppermute x4 -> x6, starting transfers between devices: 8.61 us -> 11.2 us  [sent(): return lax.ppermute(strip, ('row', 'col'), pairs)]
    ppermute x1, starting transfers between devices: 4.94 us -> 2.93 us  [reduce_scatter(): lax.ppermute(send, ('row', 'col'), pairs)]
    pallas_call x1, Pallas kernels: 0.53 us -> 2.2 us  [reduce_scatter(): pl.pallas_call(join_kernel, out_shape=jax.ShapeDtypeStruct((2, 1152, 512)...]
  transfers between devices with their start and end apart: 22 -> 24, of which waited for: 12 -> 12; matrix products, arithmetic and copies ran while one was open for 1% -> 1% of each run, Pallas kernels for 3% -> 3%
where the time goes in v5:
time: 139 us; the launch traced here: 138 us
  starting transfers between devices  54.2 us (39%)
  Pallas kernels  33 us (24%)
  waiting for transfers between devices  31.7 us (23%)
  local copies, waits for them, and re-layouts  16.3 us (12%)
  other arithmetic  1.57 us (1%)
    ppermute x15, starting transfers between devices, sum_stage(): arrived.append(lax.ppermute(piece, ('row', 'col'), pairs))  33.2 us
    pallas_call x1, Pallas kernels, on_device(): pl.pallas_call(functools.partial(main_kernel, scale), out_shape=[jax.Shap...  19.8 us
    ppermute x15, waiting for transfers between devices, sum_stage(): arrived.append(lax.ppermute(piece, ('row', 'col'), pairs))  18.2 us
    unnamed x45, local copies, waits for them, and re-layouts  13.8 us
    ppermute x6, starting transfers between devices, sent(): return lax.ppermute(strip, ('row', 'col'), pairs)  11.2 us
    ppermute x2, waiting for transfers between devices, reduce_scatter(): total = total + lax.ppermute(piece, ('row', 'col'), pairs).astype(F32)  7.88 us
    ppermute x2, starting transfers between devices, reduce_scatter(): total = total + lax.ppermute(piece, ('row', 'col'), pairs).astype(F32)  6.9 us
    pallas_call x1, Pallas kernels, on_device(): pl.pallas_call(first_kernel, out_shape=[jax.ShapeDtypeStruct((4, 16, 16,...  6.61 us
  transfers between devices with their start and end apart: 24, of which 12 were waited for; matrix products, arithmetic and copies ran while one was open for 1% of the time, Pallas kernels for 3%

profile of v5, /device:TPU:6, one launch (start us, length us, event | category | flops | bytes accessed | tf_op | source)
XLA Modules:
  0.0 137.8 jit_solution(8080157509049287042)
XLA Ops:
  0.7 6.6 %first.1 = (bf16[4,16,16,256]{3,2,1,0:T(8,128)(2,1)}, f32[4,17,32,256]{3,2,1,0:T(8,128)}, bf16[23,16,256]{2,1,0:T(8,128)(2,1)}, bf16[23,16,256]{2,1,0:T(8,128)(2...) custom-call(bf16[16,2,32,256]{3,2,1,0:T(8,128)(2,1)} %bitcast.65, f32[16,2,32,256]{3,2,1,0:T(8,128)} %bitcast.64, ...), custom_call_target="tpu_custom_call" | custom-call | tf_op jit(solution)/shard_map/first/pallas_call | solution.py:422
  7.3 3.7 %collective-permute-start = (bf16[23,16,256]{2,1,0:T(8,128)(2,1)}, bf16[23,16,256]{2,1,0:T(8,128)(2,1)S(1)}, u32[]{:S(2)}, u32[]{:S(2)}) collective-permute-start(bf16[23,16,256]{2,1,0:T(8,128)(2,1)} %get-tuple-element.23), channel_id=1, source_target_pairs={{0,16},{1,17},{2,18},{3,19},{4,20},{5,21},{6,22},{7,23},{8,24},{9,... | collective-permute-start | bytes 565256 | tf_op jit(solution)/shard_map/ppermute | solution.py:417
  11.0 2.1 %collective-permute-start.1 = (bf16[23,16,256]{2,1,0:T(8,128)(2,1)}, bf16[23,16,256]{2,1,0:T(8,128)(2,1)S(1)}, u32[]{:S(2)}, u32[]{:S(2)}) collective-permute-start(bf16[23,16,256]{2,1,0:T(8,128)(2,1)} %get-tuple-element.24), channel_id=1, source_target_pairs={{16,0},{17,1},{18,2},{19,3},{20,4},{21,5},{22,6},{23,7},{24,8},{25... | collective-permute-start | bytes 565256 | tf_op jit(solution)/shard_map/ppermute | solution.py:417
  13.1 1.3 collective-permute-start.2
  14.4 1.3 collective-permute-start.3
  15.8 5.6 %collective-permute-done.1.down_ref = bf16[23,16,256]{2,1,0:T(8,128)(2,1)S(1)} collective-permute-done((bf16[23,16,256]{2,1,0:T(8,128)(2,1)}, bf16[23,16,256]{2,1,0:T(8,128)(2,1)S(1)}, u32[]{:S(2)}, u32[]{:S(2)}) %collective-permute-start.1) | collective-permute-done | bytes 188448 | tf_op jit(solution)/shard_map/ppermute | solution.py:417
  22.8 1.3 collective-permute-start.4
  24.0 1.5 %collective-permute-start.5 = (bf16[10,24,256]{2,1,0:T(8,128)(2,1)S(1)}, bf16[10,24,256]{2,1,0:T(8,128)(2,1)S(1)}, u32[]{:S(2)}, u32[]{:S(2)}) collective-permute-start(bf16[10,24,256]{2,1,0:T(8,128)(2,1)S(1)} %get-tuple-element.28), channel_id=1, source_target_pairs={{1,0},{2,1},{3,2},{4,3},{5,4},{6,5},{7,6},{8,7},{9,8},{10,9},{11,1... | collective-permute-start | bytes 368648 | tf_op jit(solution)/shard_map/ppermute | solution.py:417
  25.6 1.7 %copy-done.2 = bf16[2304,512]{1,0:T(8,128)(2,1)S(1)} copy-done((bf16[2304,512]{1,0:T(8,128)(2,1)S(1)}, bf16[2304,512]{1,0:T(8,128)(2,1)}, u32[]{:S(2)}) %copy-start.2) | copy-done | bytes 2359320
  27.3 2.1 %weights.1 = (bf16[4,1024,512]{2,1,0:T(8,128)(2,1)S(1)}, bf16[4,2048,256]{2,1,0:T(8,128)(2,1)S(1)}, bf16[2304,256]{1,0:T(8,128)(2,1)S(1)}, bf16[2304,256]{1,0:T(8,128)(2,1)S(1)}) custom-call(bf16[2304,256]{1,0:T(8,128)(2,1)S(1)} %copy-done.1, bf16[2304,256]{1,0:T(8,128)(2,1)S(1)} %copy-done, bf16[2304,512]{1,0:T(8,128)(2,1)S(1)} %copy-done.2), custom_call_target="tpu_custom_call" | custom-call | flops 10000000 | bytes 15000000 | tf_op jit(solution)/shard_map/weights/pallas_call | solution.py:452
  36.9 19.8 %tile.1 = (bf16[2,1152,512]{2,1,0:T(8,128)(2,1)S(1)}, bf16[2,1152,512]{2,1,0:T(8,128)(2,1)}, bf16[2,18,16,1024]{3,2,1,0:T(8,128)(2,1)S(1)}) custom-call(s32[3]{0:T(128)S(1)} %pad_add_fusion.place_ref, bf16[4,16,16,256]{3,2,1,0:T(8,128)(2,1)S(1)} %copy-done.9, f32[4,17,32,256]{3,2,1,0:T(8,128)S(1)} %copy-done.3, f32[16,16,256]{2,1,0:T(8,128)S(1)} %copy-done.4, ...), custom_call_target="tpu_custom_call" | custom-call | tf_op jit(solution)/shard_map/tile/pallas_call | solution.py:478
  57.6 2.9 %collective-permute-start.6 = (bf16[2,1152,512]{2,1,0:T(8,128)(2,1)}, bf16[2,1152,512]{2,1,0:T(8,128)(2,1)}, u32[]{:S(2)}, u32[]{:S(2)}) collective-permute-start(bf16[2,1152,512]{2,1,0:T(8,128)(2,1)} %get-tuple-element.32), channel_id=1, source_target_pairs={{0,1},{1,0},{2,3},{3,2},{4,5},{5,4},{6,7},{7,6},{8,9},{9,8},{10,11... | collective-permute-start | bytes 7077896 | tf_op jit(solution)/shard_map/ppermute | solution.py:53
  63.1 2.2 %feat.1 = bf16[16,2,32,256]{3,2,1,0:T(8,128)(2,1)} custom-call(bf16[2,18,16,1024]{3,2,1,0:T(8,128)(2,1)S(1)} %copy-done.21, bf16[2304,256]{1,0:T(8,128)(2,1)S(1)} %copy-done.19), custom_call_target="tpu_custom_call" | custom-call | flops 1200000000 | bytes 3000000 | tf_op jit(solution)/shard_map/feat/pallas_call | solution.py:505
  65.4 2.2 %join.1 = bf16[2,1152,512]{2,1,0:T(8,128)(2,1)S(1)} custom-call(bf16[2,1152,512]{2,1,0:T(8,128)(2,1)S(1)} %get-tuple-element.36.keep_ref, bf16[2,1152,512]{2,1,0:T(8,128)(2,1)} %collective-permute-done.6.other_ref), custom_call_target="tpu_custom_call" | custom-call | tf_op jit(solution)/shard_map/join/pallas_call | solution.py:54
  67.8 1.8 %collective-permute-start.13 = (bf16[4,72,512]{2,1,0:T(8,128)(2,1)S(1)}, bf16[4,72,512]{2,1,0:T(8,128)(2,1)S(1)}, u32[]{:S(2)}, u32[]{:S(2)}) collective-permute-start(bf16[4,72,512]{2,1,0:T(8,128)(2,1)S(1)} %get-tuple-element.42), channel_id=1, source_target_pairs={{0,2},{1,3},{2,0},{3,1},{4,6},{5,7},{6,4},{7,5},{8,10},{9,11},{10,... | collective-permute-start | bytes 884744 | tf_op jit(solution)/shard_map/ppermute | solution.py:44
  69.6 13.2 %collective-permute-start.14 = (bf16[4,72,512]{2,1,0:T(8,128)(2,1)S(1)}, bf16[4,72,512]{2,1,0:T(8,128)(2,1)}, u32[]{:S(2)}, u32[]{:S(2)}) collective-permute-start(bf16[4,72,512]{2,1,0:T(8,128)(2,1)S(1)} %get-tuple-element.44), channel_id=1, source_target_pairs={{0,6},{1,7},{2,4},{3,5},{4,2},{5,3},{6,0},{7,1},{8,14},{9,15},{10,... | collective-permute-start | bytes 884744 | tf_op jit(solution)/shard_map/ppermute | solution.py:44
  82.8 1.4 collective-permute-start.15
  86.3 2.1 %collective-permute-start.9 = (bf16[4,72,512]{2,1,0:T(8,128)(2,1)S(1)}, bf16[4,72,512]{2,1,0:T(8,128)(2,1)S(1)}, u32[]{:S(2)}, u32[]{:S(2)}) collective-permute-start(bf16[4,72,512]{2,1,0:T(8,128)(2,1)S(1)} %get-tuple-element.46), channel_id=1, source_target_pairs={{0,32},{1,33},{2,34},{3,35},{4,36},{5,37},{6,38},{7,39},{8,40},{9,... | collective-permute-start | bytes 884744 | tf_op jit(solution)/shard_map/ppermute | solution.py:44
  88.5 7.2 %collective-permute-done.14 = bf16[4,72,512]{2,1,0:T(8,128)(2,1)} collective-permute-done((bf16[4,72,512]{2,1,0:T(8,128)(2,1)S(1)}, bf16[4,72,512]{2,1,0:T(8,128)(2,1)}, u32[]{:S(2)}, u32[]{:S(2)}) %collective-permute-start.14) | collective-permute-done | bytes 294944 | tf_op jit(solution)/shard_map/ppermute | solution.py:44
  95.7 1.9 %collective-permute-done.15 = bf16[4,72,512]{2,1,0:T(8,128)(2,1)} collective-permute-done((bf16[4,72,512]{2,1,0:T(8,128)(2,1)S(1)}, bf16[4,72,512]{2,1,0:T(8,128)(2,1)}, u32[]{:S(2)}, u32[]{:S(2)}) %collective-permute-start.15) | collective-permute-done | bytes 294944 | tf_op jit(solution)/shard_map/ppermute | solution.py:44
  100.9 2.1 %collective-permute-start.18 = (bf16[72,512]{1,0:T(8,128)(2,1)S(1)}, bf16[72,512]{1,0:T(8,128)(2,1)S(1)}, u32[]{:S(2)}, u32[]{:S(2)}) collective-permute-start(bf16[72,512]{1,0:T(8,128)(2,1)S(1)} %get-tuple-element.49), channel_id=1, source_target_pairs={{0,32},{1,33},{2,34},{3,35},{4,36},{5,37},{6,38},{7,39},{8,40},{9,... | collective-permute-start | bytes 221192 | tf_op jit(solution)/shard_map/ppermute | solution.py:44
  103.3 2.3 %collective-permute-start.11 = (bf16[72,512]{1,0:T(8,128)(2,1)S(1)}, bf16[72,512]{1,0:T(8,128)(2,1)S(1)}, u32[]{:S(2)}, u32[]{:S(2)}) collective-permute-start(bf16[72,512]{1,0:T(8,128)(2,1)S(1)} %get-tuple-element.53), channel_id=1, source_target_pairs={{0,6},{1,7},{2,4},{3,5},{4,2},{5,3},{6,0},{7,1},{8,14},{9,15},{10,... | collective-permute-start | bytes 221192 | tf_op jit(solution)/shard_map/ppermute | solution.py:44
  105.6 1.8 %collective-permute-start.12 = (bf16[72,512]{1,0:T(8,128)(2,1)S(1)}, bf16[72,512]{1,0:T(8,128)(2,1)S(1)}, u32[]{:S(2)}, u32[]{:S(2)}) collective-permute-start(bf16[72,512]{1,0:T(8,128)(2,1)S(1)} %get-tuple-element.52), channel_id=1, source_target_pairs={{0,4},{1,5},{2,6},{3,7},{4,0},{5,1},{6,2},{7,3},{8,12},{9,13},{10,... | collective-permute-start | bytes 221192 | tf_op jit(solution)/shard_map/ppermute | solution.py:44
  107.8 1.6 %collective-permute-done.11 = bf16[72,512]{1,0:T(8,128)(2,1)S(1)} collective-permute-done((bf16[72,512]{1,0:T(8,128)(2,1)S(1)}, bf16[72,512]{1,0:T(8,128)(2,1)S(1)}, u32[]{:S(2)}, u32[]{:S(2)}) %collective-permute-start.11) | collective-permute-done | bytes 73760 | tf_op jit(solution)/shard_map/ppermute | solution.py:44
  109.4 2.1 %collective-permute-done.12 = bf16[72,512]{1,0:T(8,128)(2,1)S(1)} collective-permute-done((bf16[72,512]{1,0:T(8,128)(2,1)S(1)}, bf16[72,512]{1,0:T(8,128)(2,1)S(1)}, u32[]{:S(2)}, u32[]{:S(2)}) %collective-permute-start.12) | collective-permute-done | bytes 73760 | tf_op jit(solution)/shard_map/ppermute | solution.py:44
  111.6 2.3 %collective-permute-start.19 = (bf16[2,18,512]{2,1,0:T(8,128)(2,1)S(1)}, bf16[2,18,512]{2,1,0:T(8,128)(2,1)S(1)}, u32[]{:S(2)}, u32[]{:S(2)}) collective-permute-start(bf16[2,18,512]{2,1,0:T(8,128)(2,1)S(1)} %get-tuple-element.54), channel_id=1, source_target_pairs={{0,64},{1,65},{2,66},{3,67},{4,68},{5,69},{6,70},{7,71},{8,72},{9,... | collective-permute-start | bytes 110600 | tf_op jit(solution)/shard_map/ppermute | solution.py:44
  114.0 1.9 %collective-permute-start.20 = (bf16[2,18,512]{2,1,0:T(8,128)(2,1)S(1)}, bf16[2,18,512]{2,1,0:T(8,128)(2,1)S(1)}, u32[]{:S(2)}, u32[]{:S(2)}) collective-permute-start(bf16[2,18,512]{2,1,0:T(8,128)(2,1)S(1)} %get-tuple-element.56), channel_id=1, source_target_pairs={{0,192},{1,193},{2,194},{3,195},{4,196},{5,197},{6,198},{7,199},{8... | collective-permute-start | bytes 110600 | tf_op jit(solution)/shard_map/ppermute | solution.py:44
  116.6 3.3 %collective-permute-done.20 = bf16[2,18,512]{2,1,0:T(8,128)(2,1)S(1)} collective-permute-done((bf16[2,18,512]{2,1,0:T(8,128)(2,1)S(1)}, bf16[2,18,512]{2,1,0:T(8,128)(2,1)S(1)}, u32[]{:S(2)}, u32[]{:S(2)}) %collective-permute-start.20) | collective-permute-done | bytes 36896 | tf_op jit(solution)/shard_map/ppermute | solution.py:44
  121.0 2.2 %collective-permute-start.22 = (bf16[2,9,512]{2,0,1:T(2,128)(2,1)S(1)}, bf16[2,9,512]{2,0,1:T(2,128)(2,1)S(1)}, u32[]{:S(2)}, u32[]{:S(2)}) collective-permute-start(bf16[2,9,512]{2,0,1:T(2,128)(2,1)S(1)} %get-tuple-element.57), channel_id=1, source_target_pairs={{0,0},{1,128},{2,8},{3,136},{4,16},{5,144},{6,24},{7,152},{8,1},{9... | collective-permute-start | bytes 55304 | tf_op jit(solution)/shard_map/ppermute | solution.py:76
  123.2 4.7 %collective-permute-start.23 = (bf16[2,9,512]{2,0,1:T(2,128)(2,1)S(1)}, bf16[2,9,512]{2,0,1:T(2,128)(2,1)S(1)}, u32[]{:S(2)}, u32[]{:S(2)}) collective-permute-start(bf16[2,9,512]{2,0,1:T(2,128)(2,1)S(1)} %get-tuple-element.58), channel_id=1, source_target_pairs={{0,1},{1,129},{2,9},{3,137},{4,17},{5,145},{6,25},{7,153},{8,0},{9... | collective-permute-start | bytes 55304 | tf_op jit(solution)/shard_map/ppermute | solution.py:76
  127.9 2.7 %collective-permute-done.22 = bf16[2,9,512]{2,0,1:T(2,128)(2,1)S(1)} collective-permute-done((bf16[2,9,512]{2,0,1:T(2,128)(2,1)S(1)}, bf16[2,9,512]{2,0,1:T(2,128)(2,1)S(1)}, u32[]{:S(2)}, u32[]{:S(2)}) %collective-permute-start.22) | collective-permute-done | bytes 18464 | tf_op jit(solution)/shard_map/ppermute | solution.py:76
  130.6 5.2 %collective-permute-done.23 = bf16[2,9,512]{2,0,1:T(2,128)(2,1)S(1)} collective-permute-done((bf16[2,9,512]{2,0,1:T(2,128)(2,1)S(1)}, bf16[2,9,512]{2,0,1:T(2,128)(2,1)S(1)}, u32[]{:S(2)}, u32[]{:S(2)}) %collective-permute-start.23) | collective-permute-done | bytes 18464 | tf_op jit(solution)/shard_map/ppermute | solution.py:76
  (90 shorter events, 22.7 us)
Async XLA Ops:
  0.6 24.9 %copy-start = (bf16[2304,256]{1,0:T(8,128)(2,1)S(1)}, bf16[2304,256]{1,0:T(8,128)(2,1)}, u32[]{:S(2)}) copy-start(bf16[2304,256]{1,0:T(8,128)(2,1)} %w_coarse.3) | copy-start | bytes 3538948
  0.6 24.9 %copy-start.1 = (bf16[2304,256]{1,0:T(8,128)(2,1)S(1)}, bf16[2304,256]{1,0:T(8,128)(2,1)}, u32[]{:S(2)}) copy-start(bf16[2304,256]{1,0:T(8,128)(2,1)} %w_post.1) | copy-start | bytes 3538948
  7.3 8.6 %collective-permute-start = (bf16[23,16,256]{2,1,0:T(8,128)(2,1)}, bf16[23,16,256]{2,1,0:T(8,128)(2,1)S(1)}, u32[]{:S(2)}, u32[]{:S(2)}) collective-permute-start(bf16[23,16,256]{2,1,0:T(8,128)(2,1)} %get-tuple-element.23), channel_id=1, source_target_pairs={{0,16},{1,17},{2,18},{3,19},{4,20},{5,21},{6,22},{7,23},{8,24},{9,... | collective-permute-start | bytes 565256 | tf_op jit(solution)/shard_map/ppermute | solution.py:417
  11.0 10.4 %collective-permute-start.1 = (bf16[23,16,256]{2,1,0:T(8,128)(2,1)}, bf16[23,16,256]{2,1,0:T(8,128)(2,1)S(1)}, u32[]{:S(2)}, u32[]{:S(2)}) collective-permute-start(bf16[23,16,256]{2,1,0:T(8,128)(2,1)} %get-tuple-element.24), channel_id=1, source_target_pairs={{16,0},{17,1},{18,2},{19,3},{20,4},{21,5},{22,6},{23,7},{24,8},{25... | collective-permute-start | bytes 565256 | tf_op jit(solution)/shard_map/ppermute | solution.py:417
  13.1 17.3 %collective-permute-start.2 = (bf16[18,24,256]{2,1,0:T(8,128)(2,1)}, bf16[18,24,256]{2,1,0:T(8,128)(2,1)S(1)}, u32[]{:S(2)}, u32[]{:S(2)}) collective-permute-start(bf16[18,24,256]{2,1,0:T(8,128)(2,1)} %get-tuple-element.25), channel_id=1, source_target_pairs={{0,1},{1,2},{2,3},{3,4},{4,5},{5,6},{6,7},{7,8},{8,9},{9,10},{10,1... | collective-permute-start | bytes 663560 | tf_op jit(solution)/shard_map/ppermute | solution.py:417
  14.4 16.7 %collective-permute-start.3 = (bf16[18,24,256]{2,1,0:T(8,128)(2,1)}, bf16[18,24,256]{2,1,0:T(8,128)(2,1)S(1)}, u32[]{:S(2)}, u32[]{:S(2)}) collective-permute-start(bf16[18,24,256]{2,1,0:T(8,128)(2,1)} %get-tuple-element.26), channel_id=1, source_target_pairs={{1,0},{2,1},{3,2},{4,3},{5,4},{6,5},{7,6},{8,7},{9,8},{10,9},{11,1... | collective-permute-start | bytes 663560 | tf_op jit(solution)/shard_map/ppermute | solution.py:417
  22.8 9.1 %collective-permute-start.4 = (bf16[10,24,256]{2,1,0:T(8,128)(2,1)S(1)}, bf16[10,24,256]{2,1,0:T(8,128)(2,1)S(1)}, u32[]{:S(2)}, u32[]{:S(2)}) collective-permute-start(bf16[10,24,256]{2,1,0:T(8,128)(2,1)S(1)} %get-tuple-element.27), channel_id=1, source_target_pairs={{0,1},{1,2},{2,3},{3,4},{4,5},{5,6},{6,7},{7,8},{8,9},{9,10},{10,1... | collective-permute-start | bytes 368648 | tf_op jit(solution)/shard_map/ppermute | solution.py:417
  24.0 8.5 %collective-permute-start.5 = (bf16[10,24,256]{2,1,0:T(8,128)(2,1)S(1)}, bf16[10,24,256]{2,1,0:T(8,128)(2,1)S(1)}, u32[]{:S(2)}, u32[]{:S(2)}) collective-permute-start(bf16[10,24,256]{2,1,0:T(8,128)(2,1)S(1)} %get-tuple-element.28), channel_id=1, source_target_pairs={{1,0},{2,1},{3,2},{4,3},{5,4},{6,5},{7,6},{8,7},{9,8},{10,9},{11,1... | collective-permute-start | bytes 368648 | tf_op jit(solution)/shard_map/ppermute | solution.py:417
  25.6 1.7 %copy-start.2 = (bf16[2304,512]{1,0:T(8,128)(2,1)S(1)}, bf16[2304,512]{1,0:T(8,128)(2,1)}, u32[]{:S(2)}) copy-start(bf16[2304,512]{1,0:T(8,128)(2,1)} %w_prior.1) | copy-start | bytes 7077892
  27.2 5.9 %copy-start.3 = (f32[4,17,32,256]{3,2,1,0:T(8,128)S(1)}, f32[4,17,32,256]{3,2,1,0:T(8,128)}, u32[]{:S(2)}) copy-start(f32[4,17,32,256]{3,2,1,0:T(8,128)} %get-tuple-element.22.part_ref) | copy-start | bytes 6684676
  27.2 5.9 %copy-start.4 = (f32[16,16,256]{2,1,0:T(8,128)S(1)}, f32[16,16,256]{2,1,0:T(8,128)}, u32[]{:S(2)}) copy-start(f32[16,16,256]{2,1,0:T(8,128)} %low_ref.1) | copy-start | bytes 786436
  27.2 5.9 %copy-start.6 = (bf16[23,16,256]{2,1,0:T(8,128)(2,1)S(1)}, bf16[23,16,256]{2,1,0:T(8,128)(2,1)}, u32[]{:S(2)}) copy-start(bf16[23,16,256]{2,1,0:T(8,128)(2,1)} %copy-done.5) | copy-start | bytes 565252
  27.2 5.9 %copy-start.8 = (bf16[23,16,256]{2,1,0:T(8,128)(2,1)S(1)}, bf16[23,16,256]{2,1,0:T(8,128)(2,1)}, u32[]{:S(2)}) copy-start(bf16[23,16,256]{2,1,0:T(8,128)(2,1)} %copy-done.7) | copy-start | bytes 565252
  27.2 5.9 %copy-start.9 = (bf16[4,16,16,256]{3,2,1,0:T(8,128)(2,1)S(1)}, bf16[4,16,16,256]{3,2,1,0:T(8,128)(2,1)}, u32[]{:S(2)}) copy-start(bf16[4,16,16,256]{3,2,1,0:T(8,128)(2,1)} %get-tuple-element.21.own_ref) | copy-start | bytes 1572868
  57.6 7.7 %collective-permute-start.6 = (bf16[2,1152,512]{2,1,0:T(8,128)(2,1)}, bf16[2,1152,512]{2,1,0:T(8,128)(2,1)}, u32[]{:S(2)}, u32[]{:S(2)}) collective-permute-start(bf16[2,1152,512]{2,1,0:T(8,128)(2,1)} %get-tuple-element.32), channel_id=1, source_target_pairs={{0,1},{1,0},{2,3},{3,2},{4,5},{5,4},{6,7},{7,6},{8,9},{9,8},{10,11... | collective-permute-start | bytes 7077896 | tf_op jit(solution)/shard_map/ppermute | solution.py:53
  67.8 18.5 %collective-permute-start.13 = (bf16[4,72,512]{2,1,0:T(8,128)(2,1)S(1)}, bf16[4,72,512]{2,1,0:T(8,128)(2,1)S(1)}, u32[]{:S(2)}, u32[]{:S(2)}) collective-permute-start(bf16[4,72,512]{2,1,0:T(8,128)(2,1)S(1)} %get-tuple-element.42), channel_id=1, source_target_pairs={{0,2},{1,3},{2,0},{3,1},{4,6},{5,7},{6,4},{7,5},{8,10},{9,11},{10,... | collective-permute-start | bytes 884744 | tf_op jit(solution)/shard_map/ppermute | solution.py:44
  69.6 26.1 %collective-permute-start.14 = (bf16[4,72,512]{2,1,0:T(8,128)(2,1)S(1)}, bf16[4,72,512]{2,1,0:T(8,128)(2,1)}, u32[]{:S(2)}, u32[]{:S(2)}) collective-permute-start(bf16[4,72,512]{2,1,0:T(8,128)(2,1)S(1)} %get-tuple-element.44), channel_id=1, source_target_pairs={{0,6},{1,7},{2,4},{3,5},{4,2},{5,3},{6,0},{7,1},{8,14},{9,15},{10,... | collective-permute-start | bytes 884744 | tf_op jit(solution)/shard_map/ppermute | solution.py:44
  82.8 14.8 %collective-permute-start.15 = (bf16[4,72,512]{2,1,0:T(8,128)(2,1)S(1)}, bf16[4,72,512]{2,1,0:T(8,128)(2,1)}, u32[]{:S(2)}, u32[]{:S(2)}) collective-permute-start(bf16[4,72,512]{2,1,0:T(8,128)(2,1)S(1)} %get-tuple-element.43), channel_id=1, source_target_pairs={{0,4},{1,5},{2,6},{3,7},{4,0},{5,1},{6,2},{7,3},{8,12},{9,13},{10,... | collective-permute-start | bytes 884744 | tf_op jit(solution)/shard_map/ppermute | solution.py:44
  84.3 16.6 %collective-permute-start.7 = (bf16[4,72,512]{2,1,0:T(8,128)(2,1)S(1)}, bf16[4,72,512]{2,1,0:T(8,128)(2,1)S(1)}, u32[]{:S(2)}, u32[]{:S(2)}) collective-permute-start(bf16[4,72,512]{2,1,0:T(8,128)(2,1)S(1)} %get-tuple-element.45), channel_id=1, source_target_pairs={{0,16},{1,17},{2,18},{3,19},{4,20},{5,21},{6,22},{7,23},{8,24},{9,... | collective-permute-start | bytes 884744 | tf_op jit(solution)/shard_map/ppermute | solution.py:44
  85.2 17.8 %collective-permute-start.8 = (bf16[4,72,512]{2,1,0:T(8,128)(2,1)S(1)}, bf16[4,72,512]{2,1,0:T(8,128)(2,1)S(1)}, u32[]{:S(2)}, u32[]{:S(2)}) collective-permute-start(bf16[4,72,512]{2,1,0:T(8,128)(2,1)S(1)} %get-tuple-element.47), channel_id=1, source_target_pairs={{0,48},{1,49},{2,50},{3,51},{4,52},{5,53},{6,54},{7,55},{8,56},{9,... | collective-permute-start | bytes 884744 | tf_op jit(solution)/shard_map/ppermute | solution.py:44
  86.3 16.7 %collective-permute-start.9 = (bf16[4,72,512]{2,1,0:T(8,128)(2,1)S(1)}, bf16[4,72,512]{2,1,0:T(8,128)(2,1)S(1)}, u32[]{:S(2)}, u32[]{:S(2)}) collective-permute-start(bf16[4,72,512]{2,1,0:T(8,128)(2,1)S(1)} %get-tuple-element.46), channel_id=1, source_target_pairs={{0,32},{1,33},{2,34},{3,35},{4,36},{5,37},{6,38},{7,39},{8,40},{9,... | collective-permute-start | bytes 884744 | tf_op jit(solution)/shard_map/ppermute | solution.py:44
  98.8 6.8 %collective-permute-start.16 = (bf16[72,512]{1,0:T(8,128)(2,1)S(1)}, bf16[72,512]{1,0:T(8,128)(2,1)S(1)}, u32[]{:S(2)}, u32[]{:S(2)}) collective-permute-start(bf16[72,512]{1,0:T(8,128)(2,1)S(1)} %get-tuple-element.48), channel_id=1, source_target_pairs={{0,16},{1,17},{2,18},{3,19},{4,20},{5,21},{6,22},{7,23},{8,24},{9,... | collective-permute-start | bytes 221192 | tf_op jit(solution)/shard_map/ppermute | solution.py:44
  99.8 7.6 %collective-permute-start.17 = (bf16[72,512]{1,0:T(8,128)(2,1)S(1)}, bf16[72,512]{1,0:T(8,128)(2,1)S(1)}, u32[]{:S(2)}, u32[]{:S(2)}) collective-permute-start(bf16[72,512]{1,0:T(8,128)(2,1)S(1)} %get-tuple-element.50), channel_id=1, source_target_pairs={{0,48},{1,49},{2,50},{3,51},{4,52},{5,53},{6,54},{7,55},{8,56},{9,... | collective-permute-start | bytes 221192 | tf_op jit(solution)/shard_map/ppermute | solution.py:44
  100.9 6.5 %collective-permute-start.18 = (bf16[72,512]{1,0:T(8,128)(2,1)S(1)}, bf16[72,512]{1,0:T(8,128)(2,1)S(1)}, u32[]{:S(2)}, u32[]{:S(2)}) collective-permute-start(bf16[72,512]{1,0:T(8,128)(2,1)S(1)} %get-tuple-element.49), channel_id=1, source_target_pairs={{0,32},{1,33},{2,34},{3,35},{4,36},{5,37},{6,38},{7,39},{8,40},{9,... | collective-permute-start | bytes 221192 | tf_op jit(solution)/shard_map/ppermute | solution.py:44
  103.2 4.6 %collective-permute-start.10 = (bf16[72,512]{1,0:T(8,128)(2,1)S(1)}, bf16[72,512]{1,0:T(8,128)(2,1)S(1)}, u32[]{:S(2)}, u32[]{:S(2)}) collective-permute-start(bf16[72,512]{1,0:T(8,128)(2,1)S(1)} %get-tuple-element.51), channel_id=1, source_target_pairs={{0,2},{1,3},{2,0},{3,1},{4,6},{5,7},{6,4},{7,5},{8,10},{9,11},{10,... | collective-permute-start | bytes 221192 | tf_op jit(solution)/shard_map/ppermute | solution.py:44
  103.3 6.1 %collective-permute-start.11 = (bf16[72,512]{1,0:T(8,128)(2,1)S(1)}, bf16[72,512]{1,0:T(8,128)(2,1)S(1)}, u32[]{:S(2)}, u32[]{:S(2)}) collective-permute-start(bf16[72,512]{1,0:T(8,128)(2,1)S(1)} %get-tuple-element.53), channel_id=1, source_target_pairs={{0,6},{1,7},{2,4},{3,5},{4,2},{5,3},{6,0},{7,1},{8,14},{9,15},{10,... | collective-permute-start | bytes 221192 | tf_op jit(solution)/shard_map/ppermute | solution.py:44
  105.6 5.9 %collective-permute-start.12 = (bf16[72,512]{1,0:T(8,128)(2,1)S(1)}, bf16[72,512]{1,0:T(8,128)(2,1)S(1)}, u32[]{:S(2)}, u32[]{:S(2)}) collective-permute-start(bf16[72,512]{1,0:T(8,128)(2,1)S(1)} %get-tuple-element.52), channel_id=1, source_target_pairs={{0,4},{1,5},{2,6},{3,7},{4,0},{5,1},{6,2},{7,3},{8,12},{9,13},{10,... | collective-permute-start | bytes 221192 | tf_op jit(solution)/shard_map/ppermute | solution.py:44
  111.6 4.9 %collective-permute-start.19 = (bf16[2,18,512]{2,1,0:T(8,128)(2,1)S(1)}, bf16[2,18,512]{2,1,0:T(8,128)(2,1)S(1)}, u32[]{:S(2)}, u32[]{:S(2)}) collective-permute-start(bf16[2,18,512]{2,1,0:T(8,128)(2,1)S(1)} %get-tuple-element.54), channel_id=1, source_target_pairs={{0,64},{1,65},{2,66},{3,67},{4,68},{5,69},{6,70},{7,71},{8,72},{9,... | collective-permute-start | bytes 110600 | tf_op jit(solution)/shard_map/ppermute | solution.py:44
  114.0 5.9 %collective-permute-start.20 = (bf16[2,18,512]{2,1,0:T(8,128)(2,1)S(1)}, bf16[2,18,512]{2,1,0:T(8,128)(2,1)S(1)}, u32[]{:S(2)}, u32[]{:S(2)}) collective-permute-start(bf16[2,18,512]{2,1,0:T(8,128)(2,1)S(1)} %get-tuple-element.56), channel_id=1, source_target_pairs={{0,192},{1,193},{2,194},{3,195},{4,196},{5,197},{6,198},{7,199},{8... | collective-permute-start | bytes 110600 | tf_op jit(solution)/shard_map/ppermute | solution.py:44
  115.9 5.0 %collective-permute-start.21 = (bf16[2,18,512]{2,1,0:T(8,128)(2,1)S(1)}, bf16[2,18,512]{2,1,0:T(8,128)(2,1)S(1)}, u32[]{:S(2)}, u32[]{:S(2)}) collective-permute-start(bf16[2,18,512]{2,1,0:T(8,128)(2,1)S(1)} %get-tuple-element.55), channel_id=1, source_target_pairs={{0,128},{1,129},{2,130},{3,131},{4,132},{5,133},{6,134},{7,135},{8... | collective-permute-start | bytes 110600 | tf_op jit(solution)/shard_map/ppermute | solution.py:44
  121.0 9.6 %collective-permute-start.22 = (bf16[2,9,512]{2,0,1:T(2,128)(2,1)S(1)}, bf16[2,9,512]{2,0,1:T(2,128)(2,1)S(1)}, u32[]{:S(2)}, u32[]{:S(2)}) collective-permute-start(bf16[2,9,512]{2,0,1:T(2,128)(2,1)S(1)} %get-tuple-element.57), channel_id=1, source_target_pairs={{0,0},{1,128},{2,8},{3,136},{4,16},{5,144},{6,24},{7,152},{8,1},{9... | collective-permute-start | bytes 55304 | tf_op jit(solution)/shard_map/ppermute | solution.py:76
  123.2 12.6 %collective-permute-start.23 = (bf16[2,9,512]{2,0,1:T(2,128)(2,1)S(1)}, bf16[2,9,512]{2,0,1:T(2,128)(2,1)S(1)}, u32[]{:S(2)}, u32[]{:S(2)}) collective-permute-start(bf16[2,9,512]{2,0,1:T(2,128)(2,1)S(1)} %get-tuple-element.58), channel_id=1, source_target_pairs={{0,1},{1,129},{2,9},{3,137},{4,17},{5,145},{6,25},{7,153},{8,0},{9... | collective-permute-start | bytes 55304 | tf_op jit(solution)/shard_map/ppermute | solution.py:76
  (14 other events, 12.3 us)

commit v6 on v4

--- a/solution.py
+++ b/solution.py
@@ -35,17 +35,20 @@
     return {**place, name: place[name] ^ bits}
 
 
-def sum_stage(part, name, dim):
+def sum_stage(part, name, cut):
     here = my_place()[name]
     arrived = []
     for bits in (1, 3, 2):
-        piece = lax.dynamic_index_in_dim(part, here ^ bits, dim, keepdims=False)
         pairs = [(index_of(p), index_of(flipped(p, name, bits))) for p in digits()]
-        arrived.append(lax.ppermute(piece, ("row", "col"), pairs))
-    total = lax.dynamic_index_in_dim(part, here, dim, keepdims=False).astype(F32)
+        arrived.append(lax.ppermute(cut(part, here ^ bits), ("row", "col"), pairs))
+    total = cut(part, here).astype(F32)
     for piece in arrived:
         total = total + piece.astype(F32)
     return total.astype(BF)
+
+
+def pick(dim):
+    return lambda part, at: lax.dynamic_index_in_dim(part, at, dim, keepdims=False)
 
 
 def reduce_scatter(keep, send, beside):
@@ -59,19 +62,20 @@
         compiler_params=room(9),
         name="join",
     )(keep, other)
-    first = parts[0].reshape(4, 4, 72, 512)
-    second = parts[1].reshape(4, 4, 72, 512)
-    first, second = sum_stage(first, "x", 0), sum_stage(second, "y", 1)
-    first, second = sum_stage(first, "y", 0), sum_stage(second, "x", 0)
-    parts = sum_stage(jnp.stack([first, second]).reshape(2, 4, 18, 512), "zl", 1)
+    first = sum_stage(parts[0].reshape(2, 4, 144, 512), "x", pick(1))
+    second = sum_stage(parts[1].reshape(2, 4, 2, 72, 512), "y", lambda part, at: pick(1)(pick(0)(part, at // 2), at % 2))
+    first = sum_stage(first.reshape(4, 72, 512), "y", pick(0))
+    second = sum_stage(second, "x", pick(0))
+    parts = sum_stage(jnp.stack([first, second]).reshape(2, 4, 18, 512), "zl", pick(1))
     halves = parts.reshape(2, 2, 9, 512)
     last = my_place()["zh"]
     total = 0.0
     for flip in (0, 1):
         pairs = []
         for p in digits():
-            chunk = (((p["core"] * 4 + p["x"]) * 4 + p["y"]) * 4 + p["zl"]) * 2 + (p["zh"] + flip) % 2
-            pairs.append((index_of(p), chunk))
+            owner = {"zl": 2 * p["core"] + p["y"] // 2, "x": p["x"], "zh": p["y"] % 2, "y": p["zl"],
+                     "core": p["zh"] ^ flip}
+            pairs.append((index_of(p), index_of(owner)))
         piece = lax.dynamic_index_in_dim(halves, (last + flip) % 2, 1, keepdims=False)
         total = total + lax.ppermute(piece, ("row", "col"), pairs).astype(F32)
     return total, beside

time: 135 us -> 128 us (0.948)
  the two profiles are of different devices: /device:TPU:6 before, /device:TPU:1 now
where the time goes in v6:
time: 128 us
  starting transfers between devices  59.1 us (46%)
  Pallas kernels  32.5 us (25%)
  waiting for transfers between devices  22.8 us (18%)
  local copies, waits for them, and re-layouts  10.8 us (8%)
  other arithmetic  1.59 us (1%)
    ppermute x15, starting transfers between devices, sum_stage(): arrived.append(lax.ppermute(cut(part, here ^ bits), ('row', 'col'), pairs))  40.7 us
    pallas_call x1, Pallas kernels, on_device(): pl.pallas_call(functools.partial(main_kernel, scale), out_shape=[jax.Shap...  20.2 us
    ppermute x4, starting transfers between devices, sent(): return lax.ppermute(strip, ('row', 'col'), pairs)  12.3 us
    ppermute x4, waiting for transfers between devices, sent(): return lax.ppermute(strip, ('row', 'col'), pairs)  8.4 us
    ppermute x15, waiting for transfers between devices, sum_stage(): arrived.append(lax.ppermute(cut(part, here ^ bits), ('row', 'col'), pairs))  8.36 us
    unnamed x27, local copies, waits for them, and re-layouts  8.32 us
    ppermute x2, starting transfers between devices, reduce_scatter(): total = total + lax.ppermute(piece, ('row', 'col'), pairs).astype(F32)  6.16 us
    pallas_call x1, Pallas kernels, on_device(): pl.pallas_call(first_kernel, out_shape=[jax.ShapeDtypeStruct((4, 16, 16,...  6.16 us
  transfers between devices with their start and end apart: 22, of which 9 were waited for; matrix products, arithmetic and copies ran while one was open for 1% of the time, Pallas kernels for 3%

profile of v6, /device:TPU:1, one launch (start us, length us, event | category | flops | bytes accessed | tf_op | source)
XLA Modules:
  0.0 127.7 jit_solution(8375537973672245460)
XLA Ops:
  0.6 6.2 %first.1 = (bf16[4,16,16,256]{3,2,1,0:T(8,128)(2,1)}, f32[4,17,32,256]{3,2,1,0:T(8,128)}, bf16[23,16,256]{2,1,0:T(8,128)(2,1)}, bf16[23,16,256]{2,1,0:T(8,128)(2,1)}) custom-call(bf16[16,2,32,256]{3,2,1,0:T(8,128)(2,1)} %bitcast.68, f32[16,2,32,256]{3,2,1,0:T(8,128)} %bitcast.67, f32[16,16,256]{2,1,0:T(8,128)} %low_ref.3, bf16[2304,256]{1,0:T(8,128)(2,1)} %w_post.1), custom_call_target="tpu_custom_call" | custom-call | tf_op jit(solution)/shard_map/first/pallas_call | solution.py:419
  6.8 4.0 %collective-permute-start = (bf16[23,16,256]{2,1,0:T(8,128)(2,1)}, bf16[23,16,256]{2,1,0:T(8,128)(2,1)S(1)}, u32[]{:S(2)}, u32[]{:S(2)}) collective-permute-start(bf16[23,16,256]{2,1,0:T(8,128)(2,1)} %get-tuple-element.21), channel_id=1, source_target_pairs={{0,16},{1,17},{2,18},{3,19},{4,20},{5,21},{6,22},{7,23},{8,24},{9,... | collective-permute-start | bytes 565256 | tf_op jit(solution)/shard_map/ppermute | solution.py:414
  10.8 1.3 %collective-permute-start.1 = (bf16[23,16,256]{2,1,0:T(8,128)(2,1)}, bf16[23,16,256]{2,1,0:T(8,128)(2,1)S(1)}, u32[]{:S(2)}, u32[]{:S(2)}) collective-permute-start(bf16[23,16,256]{2,1,0:T(8,128)(2,1)} %get-tuple-element.22), channel_id=1, source_target_pairs={{16,0},{17,1},{18,2},{19,3},{20,4},{21,5},{22,6},{23,7},{24,8},{25... | collective-permute-start | bytes 565256 | tf_op jit(solution)/shard_map/ppermute | solution.py:414
  12.1 2.4 %collective-permute-done.up_ref = bf16[23,16,256]{2,1,0:T(8,128)(2,1)S(1)} collective-permute-done((bf16[23,16,256]{2,1,0:T(8,128)(2,1)}, bf16[23,16,256]{2,1,0:T(8,128)(2,1)S(1)}, u32[]{:S(2)}, u32[]{:S(2)}) %collective-permute-start) | collective-permute-done | bytes 188448 | tf_op jit(solution)/shard_map/ppermute | solution.py:414
  14.4 3.7 %collective-permute-done.1.down_ref = bf16[23,16,256]{2,1,0:T(8,128)(2,1)S(1)} collective-permute-done((bf16[23,16,256]{2,1,0:T(8,128)(2,1)}, bf16[23,16,256]{2,1,0:T(8,128)(2,1)S(1)}, u32[]{:S(2)}, u32[]{:S(2)}) %collective-permute-start.1) | collective-permute-done | bytes 188448 | tf_op jit(solution)/shard_map/ppermute | solution.py:414
  18.1 1.6 %copy-done = f32[4,17,32,256]{3,2,1,0:T(8,128)S(1)} copy-done((f32[4,17,32,256]{3,2,1,0:T(8,128)S(1)}, f32[4,17,32,256]{3,2,1,0:T(8,128)}, u32[]{:S(2)}) %copy-start) | copy-done | bytes 2228248
  19.8 1.2 middle.1
  21.0 4.9 %collective-permute-start.2 = (bf16[24,24,256]{2,1,0:T(8,128)(2,1)}, bf16[24,24,256]{2,1,0:T(8,128)(2,1)S(1)}, u32[]{:S(2)}, u32[]{:S(2)}) collective-permute-start(bf16[24,24,256]{2,1,0:T(8,128)(2,1)} %get-tuple-element.23), channel_id=1, source_target_pairs={{0,1},{1,2},{2,3},{3,4},{4,5},{5,6},{6,7},{7,8},{8,9},{9,10},{10,1... | collective-permute-start | bytes 884744 | tf_op jit(solution)/shard_map/ppermute | solution.py:414
  26.0 2.1 %collective-permute-start.3 = (bf16[24,24,256]{2,1,0:T(8,128)(2,1)}, bf16[24,24,256]{2,1,0:T(8,128)(2,1)}, u32[]{:S(2)}, u32[]{:S(2)}) collective-permute-start(bf16[24,24,256]{2,1,0:T(8,128)(2,1)} %get-tuple-element.24), channel_id=1, source_target_pairs={{1,0},{2,1},{3,2},{4,3},{5,4},{6,5},{7,6},{8,7},{9,8},{10,9},{11,1... | collective-permute-start | bytes 884744 | tf_op jit(solution)/shard_map/ppermute | solution.py:414
  28.1 1.7 %copy-done.7 = bf16[2304,512]{1,0:T(8,128)(2,1)S(1)} copy-done((bf16[2304,512]{1,0:T(8,128)(2,1)S(1)}, bf16[2304,512]{1,0:T(8,128)(2,1)}, u32[]{:S(2)}) %copy-start.7) | copy-done | bytes 2359320
  29.8 2.1 %weights.1 = (bf16[4,1024,512]{2,1,0:T(8,128)(2,1)S(1)}, bf16[4,2048,256]{2,1,0:T(8,128)(2,1)S(1)}, bf16[2304,256]{1,0:T(8,128)(2,1)S(1)}, bf16[2304,256]{1,0:T(8,128)(2,1)S(1)}) custom-call(bf16[2304,256]{1,0:T(8,128)(2,1)S(1)} %copy-done.3, bf16[2304,256]{1,0:T(8,128)(2,1)S(1)} %copy-done.2, bf16[2304,512]{1,0:T(8,128)(2,1)S(1)} %copy-done.7), custom_call_target="tpu_custom_call" | custom-call | flops 10000000 | bytes 15000000 | tf_op jit(solution)/shard_map/weights/pallas_call | solution.py:445
  32.0 2.3 %collective-permute-done.3.right_ref = bf16[24,24,256]{2,1,0:T(8,128)(2,1)} collective-permute-done((bf16[24,24,256]{2,1,0:T(8,128)(2,1)}, bf16[24,24,256]{2,1,0:T(8,128)(2,1)}, u32[]{:S(2)}, u32[]{:S(2)}) %collective-permute-start.3) | collective-permute-done | bytes 294944 | tf_op jit(solution)/shard_map/ppermute | solution.py:414
  34.3 20.2 %tile.1 = (bf16[2,1152,512]{2,1,0:T(8,128)(2,1)S(1)}, bf16[2,1152,512]{2,1,0:T(8,128)(2,1)}, bf16[2,18,16,1024]{3,2,1,0:T(8,128)(2,1)S(1)}) custom-call(s32[3]{0:T(128)S(1)} %pad_add_fusion.place_ref, bf16[4,16,16,256]{3,2,1,0:T(8,128)(2,1)S(1)} %copy-done.8, f32[4,17,32,256]{3,2,1,0:T(8,128)S(1)} %copy-done.1, f32[16,16,256]{2,1,0:T(8,128)S(1)} %copy-done.4, ...), custom_call_target="tpu_custom_call" | custom-call | tf_op jit(solution)/shard_map/tile/pallas_call | solution.py:471
  54.6 1.4 %copy-done.5 = bf16[2,1152,512]{2,1,0:T(8,128)(2,1)} copy-done((bf16[2,1152,512]{2,1,0:T(8,128)(2,1)}, bf16[2,1152,512]{2,1,0:T(8,128)(2,1)S(1)}, u32[]{:S(2)}) %copy-start.5) | copy-done | bytes 2359320
  57.0 1.3 copy-done.10
  58.3 1.3 copy-done.12
  59.6 2.2 %feat.1 = bf16[16,2,32,256]{3,2,1,0:T(8,128)(2,1)} custom-call(bf16[2,18,16,1024]{3,2,1,0:T(8,128)(2,1)S(1)} %copy-done.12, bf16[2304,256]{1,0:T(8,128)(2,1)S(1)} %copy-done.10), custom_call_target="tpu_custom_call" | custom-call | flops 1200000000 | bytes 3000000 | tf_op jit(solution)/shard_map/feat/pallas_call | solution.py:498
  62.6 2.6 %collective-permute-start.7 = (bf16[2,144,512]{2,1,0:T(8,128)(2,1)S(1)}, bf16[2,144,512]{2,1,0:T(8,128)(2,1)S(1)}, u32[]{:S(2)}, u32[]{:S(2)}) collective-permute-start(bf16[2,144,512]{2,1,0:T(8,128)(2,1)S(1)} %get-tuple-element.42), channel_id=1, source_target_pairs={{0,32},{1,33},{2,34},{3,35},{4,36},{5,37},{6,38},{7,39},{8,40},{9,... | collective-permute-start | bytes 884744 | tf_op jit(solution)/shard_map/ppermute | solution.py:43
  65.2 2.5 %collective-permute-start.6 = (bf16[2,144,512]{2,1,0:T(8,128)(2,1)S(1)}, bf16[2,144,512]{2,1,0:T(8,128)(2,1)}, u32[]{:S(2)}, u32[]{:S(2)}) collective-permute-start(bf16[2,144,512]{2,1,0:T(8,128)(2,1)S(1)} %get-tuple-element.43), channel_id=1, source_target_pairs={{0,48},{1,49},{2,50},{3,51},{4,52},{5,53},{6,54},{7,55},{8,56},{9,... | collective-permute-start | bytes 884744 | tf_op jit(solution)/shard_map/ppermute | solution.py:43
  68.3 2.7 %collective-permute-start.13 = (bf16[4,72,512]{2,1,0:T(8,128)(2,1)S(1)}, bf16[4,72,512]{2,1,0:T(8,128)(2,1)S(1)}, u32[]{:S(2)}, u32[]{:S(2)}) collective-permute-start(bf16[4,72,512]{2,1,0:T(8,128)(2,1)S(1)} %get-tuple-element.39), channel_id=1, source_target_pairs={{0,4},{1,5},{2,6},{3,7},{4,0},{5,1},{6,2},{7,3},{8,12},{9,13},{10,... | collective-permute-start | bytes 884744 | tf_op jit(solution)/shard_map/ppermute | solution.py:43
  71.0 10.7 %collective-permute-start.12 = (bf16[4,72,512]{2,1,0:T(8,128)(2,1)S(1)}, bf16[4,72,512]{2,1,0:T(8,128)(2,1)S(1)}, u32[]{:S(2)}, u32[]{:S(2)}) collective-permute-start(bf16[4,72,512]{2,1,0:T(8,128)(2,1)S(1)} %get-tuple-element.40), channel_id=1, source_target_pairs={{0,6},{1,7},{2,4},{3,5},{4,2},{5,3},{6,0},{7,1},{8,14},{9,15},{10,... | collective-permute-start | bytes 884744 | tf_op jit(solution)/shard_map/ppermute | solution.py:43
  83.4 5.5 %collective-permute-start.10 = (bf16[72,512]{1,0:T(8,128)(2,1)S(1)}, bf16[72,512]{1,0:T(8,128)(2,1)S(1)}, u32[]{:S(2)}, u32[]{:S(2)}) collective-permute-start(bf16[72,512]{1,0:T(8,128)(2,1)S(1)} %get-tuple-element.48), channel_id=1, source_target_pairs={{0,4},{1,5},{2,6},{3,7},{4,0},{5,1},{6,2},{7,3},{8,12},{9,13},{10,... | collective-permute-start | bytes 221192 | tf_op jit(solution)/shard_map/ppermute | solution.py:43
  88.9 7.0 %collective-permute-start.9 = (bf16[72,512]{1,0:T(8,128)(2,1)S(1)}, bf16[72,512]{1,0:T(8,128)(2,1)S(1)}, u32[]{:S(2)}, u32[]{:S(2)}) collective-permute-start(bf16[72,512]{1,0:T(8,128)(2,1)S(1)} %get-tuple-element.49), channel_id=1, source_target_pairs={{0,6},{1,7},{2,4},{3,5},{4,2},{5,3},{6,0},{7,1},{8,14},{9,15},{10,... | collective-permute-start | bytes 221192 | tf_op jit(solution)/shard_map/ppermute | solution.py:43
  96.6 1.7 %collective-permute-start.16 = (bf16[72,512]{1,0:T(8,128)(2,1)S(1)}, bf16[72,512]{1,0:T(8,128)(2,1)S(1)}, u32[]{:S(2)}, u32[]{:S(2)}) collective-permute-start(bf16[72,512]{1,0:T(8,128)(2,1)S(1)} %get-tuple-element.45), channel_id=1, source_target_pairs={{0,32},{1,33},{2,34},{3,35},{4,36},{5,37},{6,38},{7,39},{8,40},{9,... | collective-permute-start | bytes 221192 | tf_op jit(solution)/shard_map/ppermute | solution.py:43
  98.3 1.6 %collective-permute-start.15 = (bf16[72,512]{1,0:T(8,128)(2,1)S(1)}, bf16[72,512]{1,0:T(8,128)(2,1)S(1)}, u32[]{:S(2)}, u32[]{:S(2)}) collective-permute-start(bf16[72,512]{1,0:T(8,128)(2,1)S(1)} %get-tuple-element.46), channel_id=1, source_target_pairs={{0,48},{1,49},{2,50},{3,51},{4,52},{5,53},{6,54},{7,55},{8,56},{9,... | collective-permute-start | bytes 221192 | tf_op jit(solution)/shard_map/ppermute | solution.py:43
  101.4 1.3 %collective-permute-done.15 = bf16[72,512]{1,0:T(8,128)(2,1)S(1)} collective-permute-done((bf16[72,512]{1,0:T(8,128)(2,1)S(1)}, bf16[72,512]{1,0:T(8,128)(2,1)S(1)}, u32[]{:S(2)}, u32[]{:S(2)}) %collective-permute-start.15) | collective-permute-done | bytes 73760 | tf_op jit(solution)/shard_map/ppermute | solution.py:43
  104.0 4.4 %collective-permute-start.19 = (bf16[2,18,512]{2,1,0:T(8,128)(2,1)S(1)}, bf16[2,18,512]{2,1,0:T(8,128)(2,1)S(1)}, u32[]{:S(2)}, u32[]{:S(2)}) collective-permute-start(bf16[2,18,512]{2,1,0:T(8,128)(2,1)S(1)} %get-tuple-element.51), channel_id=1, source_target_pairs={{0,128},{1,129},{2,130},{3,131},{4,132},{5,133},{6,134},{7,135},{8... | collective-permute-start | bytes 110600 | tf_op jit(solution)/shard_map/ppermute | solution.py:43
  108.7 1.6 %collective-permute-done.19 = bf16[2,18,512]{2,1,0:T(8,128)(2,1)S(1)} collective-permute-done((bf16[2,18,512]{2,1,0:T(8,128)(2,1)S(1)}, bf16[2,18,512]{2,1,0:T(8,128)(2,1)S(1)}, u32[]{:S(2)}, u32[]{:S(2)}) %collective-permute-start.19) | collective-permute-done | bytes 36896 | tf_op jit(solution)/shard_map/ppermute | solution.py:43
  110.3 3.1 %collective-permute-done.18 = bf16[2,18,512]{2,1,0:T(8,128)(2,1)S(1)} collective-permute-done((bf16[2,18,512]{2,1,0:T(8,128)(2,1)S(1)}, bf16[2,18,512]{2,1,0:T(8,128)(2,1)S(1)}, u32[]{:S(2)}, u32[]{:S(2)}) %collective-permute-start.18) | collective-permute-done | bytes 36896 | tf_op jit(solution)/shard_map/ppermute | solution.py:43
  113.5 1.4 %collective-permute-start.21 = (bf16[2,9,512]{2,0,1:T(2,128)(2,1)S(1)}, bf16[2,9,512]{2,0,1:T(2,128)(2,1)S(1)}, u32[]{:S(2)}, u32[]{:S(2)}) collective-permute-start(bf16[2,9,512]{2,0,1:T(2,128)(2,1)S(1)} %get-tuple-element.54), channel_id=1, source_target_pairs={{0,1},{1,129},{2,9},{3,137},{4,65},{5,193},{6,73},{7,201},{8,0},{9... | collective-permute-start | bytes 55304 | tf_op jit(solution)/shard_map/ppermute | solution.py:80
  114.9 4.8 %collective-permute-start.20 = (bf16[2,9,512]{2,0,1:T(2,128)(2,1)S(1)}, bf16[2,9,512]{2,0,1:T(2,128)(2,1)S(1)}, u32[]{:S(2)}, u32[]{:S(2)}) collective-permute-start(bf16[2,9,512]{2,0,1:T(2,128)(2,1)S(1)} %get-tuple-element.53), channel_id=1, source_target_pairs={{0,0},{1,128},{2,8},{3,136},{4,64},{5,192},{6,72},{7,200},{8,1},{9... | collective-permute-start | bytes 55304 | tf_op jit(solution)/shard_map/ppermute | solution.py:80
  119.7 6.0 %collective-permute-done.20 = bf16[2,9,512]{2,0,1:T(2,128)(2,1)S(1)} collective-permute-done((bf16[2,9,512]{2,0,1:T(2,128)(2,1)S(1)}, bf16[2,9,512]{2,0,1:T(2,128)(2,1)S(1)}, u32[]{:S(2)}, u32[]{:S(2)}) %collective-permute-start.20) | collective-permute-done | bytes 18464 | tf_op jit(solution)/shard_map/ppermute | solution.py:80
  (68 shorter events, 10.0 us)
Async XLA Ops:
  0.6 17.5 %copy-start.4 = (f32[16,16,256]{2,1,0:T(8,128)S(1)}, f32[16,16,256]{2,1,0:T(8,128)}, u32[]{:S(2)}) copy-start(f32[16,16,256]{2,1,0:T(8,128)} %low_ref.3) | copy-start | bytes 786436
  6.8 7.6 %collective-permute-start = (bf16[23,16,256]{2,1,0:T(8,128)(2,1)}, bf16[23,16,256]{2,1,0:T(8,128)(2,1)S(1)}, u32[]{:S(2)}, u32[]{:S(2)}) collective-permute-start(bf16[23,16,256]{2,1,0:T(8,128)(2,1)} %get-tuple-element.21), channel_id=1, source_target_pairs={{0,16},{1,17},{2,18},{3,19},{4,20},{5,21},{6,22},{7,23},{8,24},{9,... | collective-permute-start | bytes 565256 | tf_op jit(solution)/shard_map/ppermute | solution.py:414
  10.8 7.4 %collective-permute-start.1 = (bf16[23,16,256]{2,1,0:T(8,128)(2,1)}, bf16[23,16,256]{2,1,0:T(8,128)(2,1)S(1)}, u32[]{:S(2)}, u32[]{:S(2)}) collective-permute-start(bf16[23,16,256]{2,1,0:T(8,128)(2,1)} %get-tuple-element.22), channel_id=1, source_target_pairs={{16,0},{17,1},{18,2},{19,3},{20,4},{21,5},{22,6},{23,7},{24,8},{25... | collective-permute-start | bytes 565256 | tf_op jit(solution)/shard_map/ppermute | solution.py:414
  18.1 1.6 %copy-start = (f32[4,17,32,256]{3,2,1,0:T(8,128)S(1)}, f32[4,17,32,256]{3,2,1,0:T(8,128)}, u32[]{:S(2)}) copy-start(f32[4,17,32,256]{3,2,1,0:T(8,128)} %get-tuple-element.20.part_ref) | copy-start | bytes 6684676
  19.8 8.3 %copy-start.2 = (bf16[2304,256]{1,0:T(8,128)(2,1)S(1)}, bf16[2304,256]{1,0:T(8,128)(2,1)}, u32[]{:S(2)}) copy-start(bf16[2304,256]{1,0:T(8,128)(2,1)} %w_coarse.3) | copy-start | bytes 3538948
  19.8 8.3 %copy-start.3 = (bf16[2304,256]{1,0:T(8,128)(2,1)S(1)}, bf16[2304,256]{1,0:T(8,128)(2,1)}, u32[]{:S(2)}) copy-start(bf16[2304,256]{1,0:T(8,128)(2,1)} %w_post.1) | copy-start | bytes 3538948
  21.0 11.0 %collective-permute-start.2 = (bf16[24,24,256]{2,1,0:T(8,128)(2,1)}, bf16[24,24,256]{2,1,0:T(8,128)(2,1)S(1)}, u32[]{:S(2)}, u32[]{:S(2)}) collective-permute-start(bf16[24,24,256]{2,1,0:T(8,128)(2,1)} %get-tuple-element.23), channel_id=1, source_target_pairs={{0,1},{1,2},{2,3},{3,4},{4,5},{5,6},{6,7},{7,8},{8,9},{9,10},{10,1... | collective-permute-start | bytes 884744 | tf_op jit(solution)/shard_map/ppermute | solution.py:414
  26.0 8.4 %collective-permute-start.3 = (bf16[24,24,256]{2,1,0:T(8,128)(2,1)}, bf16[24,24,256]{2,1,0:T(8,128)(2,1)}, u32[]{:S(2)}, u32[]{:S(2)}) collective-permute-start(bf16[24,24,256]{2,1,0:T(8,128)(2,1)} %get-tuple-element.24), channel_id=1, source_target_pairs={{1,0},{2,1},{3,2},{4,3},{5,4},{6,5},{7,6},{8,7},{9,8},{10,9},{11,1... | collective-permute-start | bytes 884744 | tf_op jit(solution)/shard_map/ppermute | solution.py:414
  28.1 1.7 %copy-start.7 = (bf16[2304,512]{1,0:T(8,128)(2,1)S(1)}, bf16[2304,512]{1,0:T(8,128)(2,1)}, u32[]{:S(2)}) copy-start(bf16[2304,512]{1,0:T(8,128)(2,1)} %w_prior.1) | copy-start | bytes 7077892
  29.8 4.5 %copy-start.1 = (f32[4,17,32,256]{3,2,1,0:T(8,128)S(1)}, f32[4,17,32,256]{3,2,1,0:T(8,128)}, u32[]{:S(2)}) copy-start(f32[4,17,32,256]{3,2,1,0:T(8,128)} %get-tuple-element.20.part_ref) | copy-start | bytes 6684676
  29.8 4.5 %copy-start.8 = (bf16[4,16,16,256]{3,2,1,0:T(8,128)(2,1)S(1)}, bf16[4,16,16,256]{3,2,1,0:T(8,128)(2,1)}, u32[]{:S(2)}) copy-start(bf16[4,16,16,256]{3,2,1,0:T(8,128)(2,1)} %get-tuple-element.19.own_ref) | copy-start | bytes 1572868
  31.9 22.6 %copy-start.9 = (bf16[2304,256]{1,0:T(8,128)(2,1)}, bf16[2304,256]{1,0:T(8,128)(2,1)S(1)}, u32[]{:S(2)}) copy-start(bf16[2304,256]{1,0:T(8,128)(2,1)S(1)} %get-tuple-element.30.w_post_t) | copy-start | bytes 3538948
  54.6 1.4 %copy-start.5 = (bf16[2,1152,512]{2,1,0:T(8,128)(2,1)}, bf16[2,1152,512]{2,1,0:T(8,128)(2,1)S(1)}, u32[]{:S(2)}) copy-start(bf16[2,1152,512]{2,1,0:T(8,128)(2,1)S(1)} %get-tuple-element.32.keep_ref) | copy-start | bytes 7077892
  57.0 4.8 %collective-permute-start.4 = (bf16[2,1152,512]{2,1,0:T(8,128)(2,1)}, bf16[2,1152,512]{2,1,0:T(8,128)(2,1)S(1)}, u32[]{:S(2)}, u32[]{:S(2)}) collective-permute-start(bf16[2,1152,512]{2,1,0:T(8,128)(2,1)} %get-tuple-element.28), channel_id=1, source_target_pairs={{0,1},{1,0},{2,3},{3,2},{4,5},{5,4},{6,7},{7,6},{8,9},{9,8},{10,11... | collective-permute-start | bytes 7077896 | tf_op jit(solution)/shard_map/ppermute | solution.py:56
  59.6 2.2 %copy-start.6 = (bf16[2,1152,512]{2,1,0:T(8,128)(2,1)S(1)}, bf16[2,1152,512]{2,1,0:T(8,128)(2,1)}, u32[]{:S(2)}) copy-start(bf16[2,1152,512]{2,1,0:T(8,128)(2,1)} %copy-done.5) | copy-start | bytes 7077892
  62.6 19.1 %collective-permute-start.7 = (bf16[2,144,512]{2,1,0:T(8,128)(2,1)S(1)}, bf16[2,144,512]{2,1,0:T(8,128)(2,1)S(1)}, u32[]{:S(2)}, u32[]{:S(2)}) collective-permute-start(bf16[2,144,512]{2,1,0:T(8,128)(2,1)S(1)} %get-tuple-element.42), channel_id=1, source_target_pairs={{0,32},{1,33},{2,34},{3,35},{4,36},{5,37},{6,38},{7,39},{8,40},{9,... | collective-permute-start | bytes 884744 | tf_op jit(solution)/shard_map/ppermute | solution.py:43
  65.2 16.9 %collective-permute-start.6 = (bf16[2,144,512]{2,1,0:T(8,128)(2,1)S(1)}, bf16[2,144,512]{2,1,0:T(8,128)(2,1)}, u32[]{:S(2)}, u32[]{:S(2)}) collective-permute-start(bf16[2,144,512]{2,1,0:T(8,128)(2,1)S(1)} %get-tuple-element.43), channel_id=1, source_target_pairs={{0,48},{1,49},{2,50},{3,51},{4,52},{5,53},{6,54},{7,55},{8,56},{9,... | collective-permute-start | bytes 884744 | tf_op jit(solution)/shard_map/ppermute | solution.py:43
  67.7 14.4 %collective-permute-start.5 = (bf16[2,144,512]{2,1,0:T(8,128)(2,1)S(1)}, bf16[2,144,512]{2,1,0:T(8,128)(2,1)}, u32[]{:S(2)}, u32[]{:S(2)}) collective-permute-start(bf16[2,144,512]{2,1,0:T(8,128)(2,1)S(1)} %get-tuple-element.41), channel_id=1, source_target_pairs={{0,16},{1,17},{2,18},{3,19},{4,20},{5,21},{6,22},{7,23},{8,24},{9,... | collective-permute-start | bytes 884744 | tf_op jit(solution)/shard_map/ppermute | solution.py:43
  68.3 27.6 %collective-permute-start.13 = (bf16[4,72,512]{2,1,0:T(8,128)(2,1)S(1)}, bf16[4,72,512]{2,1,0:T(8,128)(2,1)S(1)}, u32[]{:S(2)}, u32[]{:S(2)}) collective-permute-start(bf16[4,72,512]{2,1,0:T(8,128)(2,1)S(1)} %get-tuple-element.39), channel_id=1, source_target_pairs={{0,4},{1,5},{2,6},{3,7},{4,0},{5,1},{6,2},{7,3},{8,12},{9,13},{10,... | collective-permute-start | bytes 884744 | tf_op jit(solution)/shard_map/ppermute | solution.py:43
  71.0 25.4 %collective-permute-start.12 = (bf16[4,72,512]{2,1,0:T(8,128)(2,1)S(1)}, bf16[4,72,512]{2,1,0:T(8,128)(2,1)S(1)}, u32[]{:S(2)}, u32[]{:S(2)}) collective-permute-start(bf16[4,72,512]{2,1,0:T(8,128)(2,1)S(1)} %get-tuple-element.40), channel_id=1, source_target_pairs={{0,6},{1,7},{2,4},{3,5},{4,2},{5,3},{6,0},{7,1},{8,14},{9,15},{10,... | collective-permute-start | bytes 884744 | tf_op jit(solution)/shard_map/ppermute | solution.py:43
  81.7 14.7 %collective-permute-start.11 = (bf16[4,72,512]{2,1,0:T(8,128)(2,1)S(1)}, bf16[4,72,512]{2,1,0:T(8,128)(2,1)S(1)}, u32[]{:S(2)}, u32[]{:S(2)}) collective-permute-start(bf16[4,72,512]{2,1,0:T(8,128)(2,1)S(1)} %get-tuple-element.38), channel_id=1, source_target_pairs={{0,2},{1,3},{2,0},{3,1},{4,6},{5,7},{6,4},{7,5},{8,10},{9,11},{10,... | collective-permute-start | bytes 884744 | tf_op jit(solution)/shard_map/ppermute | solution.py:43
  83.4 16.5 %collective-permute-start.10 = (bf16[72,512]{1,0:T(8,128)(2,1)S(1)}, bf16[72,512]{1,0:T(8,128)(2,1)S(1)}, u32[]{:S(2)}, u32[]{:S(2)}) collective-permute-start(bf16[72,512]{1,0:T(8,128)(2,1)S(1)} %get-tuple-element.48), channel_id=1, source_target_pairs={{0,4},{1,5},{2,6},{3,7},{4,0},{5,1},{6,2},{7,3},{8,12},{9,13},{10,... | collective-permute-start | bytes 221192 | tf_op jit(solution)/shard_map/ppermute | solution.py:43
  88.9 11.2 %collective-permute-start.9 = (bf16[72,512]{1,0:T(8,128)(2,1)S(1)}, bf16[72,512]{1,0:T(8,128)(2,1)S(1)}, u32[]{:S(2)}, u32[]{:S(2)}) collective-permute-start(bf16[72,512]{1,0:T(8,128)(2,1)S(1)} %get-tuple-element.49), channel_id=1, source_target_pairs={{0,6},{1,7},{2,4},{3,5},{4,2},{5,3},{6,0},{7,1},{8,14},{9,15},{10,... | collective-permute-start | bytes 221192 | tf_op jit(solution)/shard_map/ppermute | solution.py:43
  95.9 4.2 %collective-permute-start.8 = (bf16[72,512]{1,0:T(8,128)(2,1)S(1)}, bf16[72,512]{1,0:T(8,128)(2,1)S(1)}, u32[]{:S(2)}, u32[]{:S(2)}) collective-permute-start(bf16[72,512]{1,0:T(8,128)(2,1)S(1)} %get-tuple-element.47), channel_id=1, source_target_pairs={{0,2},{1,3},{2,0},{3,1},{4,6},{5,7},{6,4},{7,5},{8,10},{9,11},{10,... | collective-permute-start | bytes 221192 | tf_op jit(solution)/shard_map/ppermute | solution.py:43
  96.6 4.8 %collective-permute-start.16 = (bf16[72,512]{1,0:T(8,128)(2,1)S(1)}, bf16[72,512]{1,0:T(8,128)(2,1)S(1)}, u32[]{:S(2)}, u32[]{:S(2)}) collective-permute-start(bf16[72,512]{1,0:T(8,128)(2,1)S(1)} %get-tuple-element.45), channel_id=1, source_target_pairs={{0,32},{1,33},{2,34},{3,35},{4,36},{5,37},{6,38},{7,39},{8,40},{9,... | collective-permute-start | bytes 221192 | tf_op jit(solution)/shard_map/ppermute | solution.py:43
  98.3 4.4 %collective-permute-start.15 = (bf16[72,512]{1,0:T(8,128)(2,1)S(1)}, bf16[72,512]{1,0:T(8,128)(2,1)S(1)}, u32[]{:S(2)}, u32[]{:S(2)}) collective-permute-start(bf16[72,512]{1,0:T(8,128)(2,1)S(1)} %get-tuple-element.46), channel_id=1, source_target_pairs={{0,48},{1,49},{2,50},{3,51},{4,52},{5,53},{6,54},{7,55},{8,56},{9,... | collective-permute-start | bytes 221192 | tf_op jit(solution)/shard_map/ppermute | solution.py:43
  99.9 3.9 %collective-permute-start.14 = (bf16[72,512]{1,0:T(8,128)(2,1)S(1)}, bf16[72,512]{1,0:T(8,128)(2,1)S(1)}, u32[]{:S(2)}, u32[]{:S(2)}) collective-permute-start(bf16[72,512]{1,0:T(8,128)(2,1)S(1)} %get-tuple-element.44), channel_id=1, source_target_pairs={{0,16},{1,17},{2,18},{3,19},{4,20},{5,21},{6,22},{7,23},{8,24},{9,... | collective-permute-start | bytes 221192 | tf_op jit(solution)/shard_map/ppermute | solution.py:43
  104.0 6.4 %collective-permute-start.19 = (bf16[2,18,512]{2,1,0:T(8,128)(2,1)S(1)}, bf16[2,18,512]{2,1,0:T(8,128)(2,1)S(1)}, u32[]{:S(2)}, u32[]{:S(2)}) collective-permute-start(bf16[2,18,512]{2,1,0:T(8,128)(2,1)S(1)} %get-tuple-element.51), channel_id=1, source_target_pairs={{0,128},{1,129},{2,130},{3,131},{4,132},{5,133},{6,134},{7,135},{8... | collective-permute-start | bytes 110600 | tf_op jit(solution)/shard_map/ppermute | solution.py:43
  108.3 5.1 %collective-permute-start.18 = (bf16[2,18,512]{2,1,0:T(8,128)(2,1)S(1)}, bf16[2,18,512]{2,1,0:T(8,128)(2,1)S(1)}, u32[]{:S(2)}, u32[]{:S(2)}) collective-permute-start(bf16[2,18,512]{2,1,0:T(8,128)(2,1)S(1)} %get-tuple-element.52), channel_id=1, source_target_pairs={{0,192},{1,193},{2,194},{3,195},{4,196},{5,197},{6,198},{7,199},{8... | collective-permute-start | bytes 110600 | tf_op jit(solution)/shard_map/ppermute | solution.py:43
  108.4 5.0 %collective-permute-start.17 = (bf16[2,18,512]{2,1,0:T(8,128)(2,1)S(1)}, bf16[2,18,512]{2,1,0:T(8,128)(2,1)S(1)}, u32[]{:S(2)}, u32[]{:S(2)}) collective-permute-start(bf16[2,18,512]{2,1,0:T(8,128)(2,1)S(1)} %get-tuple-element.50), channel_id=1, source_target_pairs={{0,64},{1,65},{2,66},{3,67},{4,68},{5,69},{6,70},{7,71},{8,72},{9,... | collective-permute-start | bytes 110600 | tf_op jit(solution)/shard_map/ppermute | solution.py:43
  113.5 6.2 %collective-permute-start.21 = (bf16[2,9,512]{2,0,1:T(2,128)(2,1)S(1)}, bf16[2,9,512]{2,0,1:T(2,128)(2,1)S(1)}, u32[]{:S(2)}, u32[]{:S(2)}) collective-permute-start(bf16[2,9,512]{2,0,1:T(2,128)(2,1)S(1)} %get-tuple-element.54), channel_id=1, source_target_pairs={{0,1},{1,129},{2,9},{3,137},{4,65},{5,193},{6,73},{7,201},{8,0},{9... | collective-permute-start | bytes 55304 | tf_op jit(solution)/shard_map/ppermute | solution.py:80
  114.9 10.8 %collective-permute-start.20 = (bf16[2,9,512]{2,0,1:T(2,128)(2,1)S(1)}, bf16[2,9,512]{2,0,1:T(2,128)(2,1)S(1)}, u32[]{:S(2)}, u32[]{:S(2)}) collective-permute-start(bf16[2,9,512]{2,0,1:T(2,128)(2,1)S(1)} %get-tuple-element.53), channel_id=1, source_target_pairs={{0,0},{1,128},{2,8},{3,136},{4,64},{5,192},{6,72},{7,200},{8,1},{9... | collective-permute-start | bytes 55304 | tf_op jit(solution)/shard_map/ppermute | solution.py:80
  (3 other events, 3.6 us)

commit v7 on v6

--- a/solution.py
+++ b/solution.py
@@ -69,7 +69,7 @@
     parts = sum_stage(jnp.stack([first, second]).reshape(2, 4, 18, 512), "zl", pick(1))
     halves = parts.reshape(2, 2, 9, 512)
     last = my_place()["zh"]
-    total = 0.0
+    arrived = []
     for flip in (0, 1):
         pairs = []
         for p in digits():
@@ -77,8 +77,16 @@
                      "core": p["zh"] ^ flip}
             pairs.append((index_of(p), index_of(owner)))
         piece = lax.dynamic_index_in_dim(halves, (last + flip) % 2, 1, keepdims=False)
-        total = total + lax.ppermute(piece, ("row", "col"), pairs).astype(F32)
-    return total, beside
+        arrived.append(lax.ppermute(piece, ("row", "col"), pairs))
+    prior, coarse, post = pl.pallas_call(
+        last_kernel,
+        out_shape=[jax.ShapeDtypeStruct((rows, 128), F32) for rows in (36, 18, 18)],
+        in_specs=in_vmem(2),
+        out_specs=in_vmem(3),
+        compiler_params=room(4),
+        name="last",
+    )(*arrived)
+    return prior.reshape(-1), coarse.reshape(-1), post.reshape(-1), beside
 
 
 def room(mib):
@@ -370,6 +378,16 @@
 
 def join_kernel(keep_ref, other_ref, out_ref):
     out_ref[...] = (keep_ref[...].astype(F32) + other_ref[...].astype(F32)).astype(BF)
+
+
+def last_kernel(one_ref, two_ref, prior_ref, coarse_ref, post_ref):
+    total = one_ref[...].astype(F32) + two_ref[...].astype(F32)
+    for line in range(9):
+        for at in range(4):
+            lanes = slice(128 * at, 128 * (at + 1))
+            prior_ref[4 * line + at:4 * line + at + 1, :] = total[0, line:line + 1, lanes]
+            out, first = (coarse_ref, 2 * line + at) if at < 2 else (post_ref, 2 * line + at - 2)
+            out[first:first + 1, :] = total[1, line:line + 1, lanes]
 
 
 def feat_kernel(g_fine, w_post_t, out_ref, wide):
@@ -501,12 +519,12 @@
         in_specs=in_vmem(2),
         out_specs=pl.BlockSpec(memory_space=pltpu.VMEM),
         scratch_shapes=[pltpu.VMEM((16, 2, 2, 32, 128), F32)],
-        compiler_params=room(8),
+        compiler_params=room(6),
         cost_estimate=pl.CostEstimate(flops=1200000000, bytes_accessed=3000000, transcendentals=0),
         name="feat",
     )(g_fine, w_post_t).reshape(32, 32, 256)
-    summed, grad_feat = reduce_scatter(keep, send, grad_feat)
-    return grad_feat, summed[1, :, 256:].reshape(-1), summed[1, :, :256].reshape(-1), summed[0].reshape(-1)
+    prior, coarse, post, grad_feat = reduce_scatter(keep, send, grad_feat)
+    return grad_feat, post, coarse, prior
 
 
 def solution(mesh):

time: 128 us -> 129 us (level)
  the two profiles are of different devices: /device:TPU:1 before, /device:TPU:32 now
where the time goes in v7:
time: 129 us; the launch traced here: 128 us
  starting transfers between devices  63 us (49%)
  Pallas kernels  33.2 us (26%)
  waiting for transfers between devices  20.7 us (16%)
  local copies, waits for them, and re-layouts  8.86 us (7%)
  other arithmetic  1.57 us (1%)
    ppermute x15, starting transfers between devices, sum_stage(): arrived.append(lax.ppermute(cut(part, here ^ bits), ('row', 'col'), pairs))  42.6 us
    pallas_call x1, Pallas kernels, on_device(): pl.pallas_call(functools.partial(main_kernel, scale), out_shape=[jax.Shap...  20.3 us
    ppermute x4, starting transfers between devices, sent(): return lax.ppermute(strip, ('row', 'col'), pairs)  10.7 us
    ppermute x2, waiting for transfers between devices, reduce_scatter(): arrived.append(lax.ppermute(piece, ('row', 'col'), pairs))  9.66 us
    unnamed x27, local copies, waits for them, and re-layouts  8.33 us
    ppermute x15, waiting for transfers between devices, sum_stage(): arrived.append(lax.ppermute(cut(part, here ^ bits), ('row', 'col'), pairs))  6.84 us
    pallas_call x1, Pallas kernels, on_device(): pl.pallas_call(first_kernel, out_shape=[jax.ShapeDtypeStruct((4, 16, 16,...  6.14 us
    ppermute x1, starting transfers between devices, reduce_scatter(): lax.ppermute(send, ('row', 'col'), pairs)  4.92 us
  transfers between devices with their start and end apart: 22, of which 10 were waited for; matrix products, arithmetic and copies ran while one was open for 1% of the time, Pallas kernels for 3%

profile of v7, /device:TPU:32, one launch (start us, length us, event | category | flops | bytes accessed | tf_op | source)
XLA Modules:
  0.0 128.2 jit_solution(4272780972540589078)
XLA Ops:
  0.6 6.1 %first.1 = (bf16[4,16,16,256]{3,2,1,0:T(8,128)(2,1)}, f32[4,17,32,256]{3,2,1,0:T(8,128)}, bf16[23,16,256]{2,1,0:T(8,128)(2,1)}, bf16[23,16,256]{2,1,0:T(8,128)(2,1)}) custom-call(bf16[16,2,32,256]{3,2,1,0:T(8,128)(2,1)} %bitcast.73, f32[16,2,32,256]{3,2,1,0:T(8,128)} %bitcast.72, f32[16,16,256]{2,1,0:T(8,128)} %low_ref.3, bf16[2304,256]{1,0:T(8,128)(2,1)} %w_post.1), custom_call_target="tpu_custom_call" | custom-call | tf_op jit(solution)/shard_map/first/pallas_call | solution.py:437
  6.8 3.4 %collective-permute-start = (bf16[23,16,256]{2,1,0:T(8,128)(2,1)}, bf16[23,16,256]{2,1,0:T(8,128)(2,1)S(1)}, u32[]{:S(2)}, u32[]{:S(2)}) collective-permute-start(bf16[23,16,256]{2,1,0:T(8,128)(2,1)} %get-tuple-element.24), channel_id=1, source_target_pairs={{0,16},{1,17},{2,18},{3,19},{4,20},{5,21},{6,22},{7,23},{8,24},{9,... | collective-permute-start | bytes 565256 | tf_op jit(solution)/shard_map/ppermute | solution.py:432
  10.2 4.6 %collective-permute-start.1 = (bf16[23,16,256]{2,1,0:T(8,128)(2,1)}, bf16[23,16,256]{2,1,0:T(8,128)(2,1)S(1)}, u32[]{:S(2)}, u32[]{:S(2)}) collective-permute-start(bf16[23,16,256]{2,1,0:T(8,128)(2,1)} %get-tuple-element.25), channel_id=1, source_target_pairs={{16,0},{17,1},{18,2},{19,3},{20,4},{21,5},{22,6},{23,7},{24,8},{25... | collective-permute-start | bytes 565256 | tf_op jit(solution)/shard_map/ppermute | solution.py:432
  14.8 2.7 %collective-permute-done.up_ref = bf16[23,16,256]{2,1,0:T(8,128)(2,1)S(1)} collective-permute-done((bf16[23,16,256]{2,1,0:T(8,128)(2,1)}, bf16[23,16,256]{2,1,0:T(8,128)(2,1)S(1)}, u32[]{:S(2)}, u32[]{:S(2)}) %collective-permute-start) | collective-permute-done | bytes 188448 | tf_op jit(solution)/shard_map/ppermute | solution.py:432
  17.5 1.3 %collective-permute-done.1.down_ref = bf16[23,16,256]{2,1,0:T(8,128)(2,1)S(1)} collective-permute-done((bf16[23,16,256]{2,1,0:T(8,128)(2,1)}, bf16[23,16,256]{2,1,0:T(8,128)(2,1)S(1)}, u32[]{:S(2)}, u32[]{:S(2)}) %collective-permute-start.1) | collective-permute-done | bytes 188448 | tf_op jit(solution)/shard_map/ppermute | solution.py:432
  18.8 1.6 %copy-done = f32[4,17,32,256]{3,2,1,0:T(8,128)S(1)} copy-done((f32[4,17,32,256]{3,2,1,0:T(8,128)S(1)}, f32[4,17,32,256]{3,2,1,0:T(8,128)}, u32[]{:S(2)}) %copy-start) | copy-done | bytes 2228248
  20.4 1.2 middle.1
  21.6 1.3 %collective-permute-start.2 = (bf16[24,24,256]{2,1,0:T(8,128)(2,1)}, bf16[24,24,256]{2,1,0:T(8,128)(2,1)S(1)}, u32[]{:S(2)}, u32[]{:S(2)}) collective-permute-start(bf16[24,24,256]{2,1,0:T(8,128)(2,1)} %get-tuple-element.26), channel_id=1, source_target_pairs={{0,1},{1,2},{2,3},{3,4},{4,5},{5,6},{6,7},{7,8},{8,9},{9,10},{10,1... | collective-permute-start | bytes 884744 | tf_op jit(solution)/shard_map/ppermute | solution.py:432
  22.9 1.5 %collective-permute-start.3 = (bf16[24,24,256]{2,1,0:T(8,128)(2,1)}, bf16[24,24,256]{2,1,0:T(8,128)(2,1)}, u32[]{:S(2)}, u32[]{:S(2)}) collective-permute-start(bf16[24,24,256]{2,1,0:T(8,128)(2,1)} %get-tuple-element.27), channel_id=1, source_target_pairs={{1,0},{2,1},{3,2},{4,3},{5,4},{6,5},{7,6},{8,7},{9,8},{10,9},{11,1... | collective-permute-start | bytes 884744 | tf_op jit(solution)/shard_map/ppermute | solution.py:432
  24.4 1.7 %copy-done.7 = bf16[2304,512]{1,0:T(8,128)(2,1)S(1)} copy-done((bf16[2304,512]{1,0:T(8,128)(2,1)S(1)}, bf16[2304,512]{1,0:T(8,128)(2,1)}, u32[]{:S(2)}) %copy-start.7) | copy-done | bytes 2359320
  26.1 2.1 %weights.1 = (bf16[4,1024,512]{2,1,0:T(8,128)(2,1)S(1)}, bf16[4,2048,256]{2,1,0:T(8,128)(2,1)S(1)}, bf16[2304,256]{1,0:T(8,128)(2,1)S(1)}, bf16[2304,256]{1,0:T(8,128)(2,1)S(1)}) custom-call(bf16[2304,256]{1,0:T(8,128)(2,1)S(1)} %copy-done.3, bf16[2304,256]{1,0:T(8,128)(2,1)S(1)} %copy-done.2, bf16[2304,512]{1,0:T(8,128)(2,1)S(1)} %copy-done.7), custom_call_target="tpu_custom_call" | custom-call | flops 10000000 | bytes 15000000 | tf_op jit(solution)/shard_map/weights/pallas_call | solution.py:463
  28.5 20.3 %tile.1 = (bf16[2,1152,512]{2,1,0:T(8,128)(2,1)S(1)}, bf16[2,1152,512]{2,1,0:T(8,128)(2,1)}, bf16[2,18,16,1024]{3,2,1,0:T(8,128)(2,1)S(1)}) custom-call(s32[3]{0:T(128)S(1)} %pad_add_fusion.place_ref, bf16[4,16,16,256]{3,2,1,0:T(8,128)(2,1)S(1)} %copy-done.8, f32[4,17,32,256]{3,2,1,0:T(8,128)S(1)} %copy-done.1, f32[16,16,256]{2,1,0:T(8,128)S(1)} %copy-done.4, ...), custom_call_target="tpu_custom_call" | custom-call | tf_op jit(solution)/shard_map/tile/pallas_call | solution.py:489
  48.9 1.4 %copy-done.5 = bf16[2,1152,512]{2,1,0:T(8,128)(2,1)} copy-done((bf16[2,1152,512]{2,1,0:T(8,128)(2,1)}, bf16[2,1152,512]{2,1,0:T(8,128)(2,1)S(1)}, u32[]{:S(2)}) %copy-start.5) | copy-done | bytes 2359320
  51.3 4.9 %collective-permute-start.4 = (bf16[2,1152,512]{2,1,0:T(8,128)(2,1)}, bf16[2,1152,512]{2,1,0:T(8,128)(2,1)S(1)}, u32[]{:S(2)}, u32[]{:S(2)}) collective-permute-start(bf16[2,1152,512]{2,1,0:T(8,128)(2,1)} %get-tuple-element.31), channel_id=1, source_target_pairs={{0,1},{1,0},{2,3},{3,2},{4,5},{5,4},{6,7},{7,6},{8,9},{9,8},{10,11... | collective-permute-start | bytes 7077896 | tf_op jit(solution)/shard_map/ppermute | solution.py:56
  56.2 1.3 copy-done.10
  57.5 1.3 copy-done.12
  58.8 2.2 %feat.1 = bf16[16,2,32,256]{3,2,1,0:T(8,128)(2,1)} custom-call(bf16[2,18,16,1024]{3,2,1,0:T(8,128)(2,1)S(1)} %copy-done.12, bf16[2304,256]{1,0:T(8,128)(2,1)S(1)} %copy-done.10), custom_call_target="tpu_custom_call" | custom-call | flops 1200000000 | bytes 3000000 | tf_op jit(solution)/shard_map/feat/pallas_call | solution.py:516
  61.8 2.7 %collective-permute-start.7 = (bf16[2,144,512]{2,1,0:T(8,128)(2,1)S(1)}, bf16[2,144,512]{2,1,0:T(8,128)(2,1)S(1)}, u32[]{:S(2)}, u32[]{:S(2)}) collective-permute-start(bf16[2,144,512]{2,1,0:T(8,128)(2,1)S(1)} %get-tuple-element.46), channel_id=1, source_target_pairs={{0,32},{1,33},{2,34},{3,35},{4,36},{5,37},{6,38},{7,39},{8,40},{9,... | collective-permute-start | bytes 884744 | tf_op jit(solution)/shard_map/ppermute | solution.py:43
  64.5 2.5 %collective-permute-start.6 = (bf16[2,144,512]{2,1,0:T(8,128)(2,1)S(1)}, bf16[2,144,512]{2,1,0:T(8,128)(2,1)}, u32[]{:S(2)}, u32[]{:S(2)}) collective-permute-start(bf16[2,144,512]{2,1,0:T(8,128)(2,1)S(1)} %get-tuple-element.47), channel_id=1, source_target_pairs={{0,48},{1,49},{2,50},{3,51},{4,52},{5,53},{6,54},{7,55},{8,56},{9,... | collective-permute-start | bytes 884744 | tf_op jit(solution)/shard_map/ppermute | solution.py:43
  67.8 3.0 %collective-permute-start.13 = (bf16[4,72,512]{2,1,0:T(8,128)(2,1)S(1)}, bf16[4,72,512]{2,1,0:T(8,128)(2,1)S(1)}, u32[]{:S(2)}, u32[]{:S(2)}) collective-permute-start(bf16[4,72,512]{2,1,0:T(8,128)(2,1)S(1)} %get-tuple-element.43), channel_id=1, source_target_pairs={{0,4},{1,5},{2,6},{3,7},{4,0},{5,1},{6,2},{7,3},{8,12},{9,13},{10,... | collective-permute-start | bytes 884744 | tf_op jit(solution)/shard_map/ppermute | solution.py:43
  70.8 11.9 %collective-permute-start.12 = (bf16[4,72,512]{2,1,0:T(8,128)(2,1)S(1)}, bf16[4,72,512]{2,1,0:T(8,128)(2,1)S(1)}, u32[]{:S(2)}, u32[]{:S(2)}) collective-permute-start(bf16[4,72,512]{2,1,0:T(8,128)(2,1)S(1)} %get-tuple-element.44), channel_id=1, source_target_pairs={{0,6},{1,7},{2,4},{3,5},{4,2},{5,3},{6,0},{7,1},{8,14},{9,15},{10,... | collective-permute-start | bytes 884744 | tf_op jit(solution)/shard_map/ppermute | solution.py:43
  84.7 8.0 %collective-permute-start.10 = (bf16[72,512]{1,0:T(8,128)(2,1)S(1)}, bf16[72,512]{1,0:T(8,128)(2,1)S(1)}, u32[]{:S(2)}, u32[]{:S(2)}) collective-permute-start(bf16[72,512]{1,0:T(8,128)(2,1)S(1)} %get-tuple-element.52), channel_id=1, source_target_pairs={{0,4},{1,5},{2,6},{3,7},{4,0},{5,1},{6,2},{7,3},{8,12},{9,13},{10,... | collective-permute-start | bytes 221192 | tf_op jit(solution)/shard_map/ppermute | solution.py:43
  92.7 4.1 %collective-permute-start.9 = (bf16[72,512]{1,0:T(8,128)(2,1)S(1)}, bf16[72,512]{1,0:T(8,128)(2,1)S(1)}, u32[]{:S(2)}, u32[]{:S(2)}) collective-permute-start(bf16[72,512]{1,0:T(8,128)(2,1)S(1)} %get-tuple-element.53), channel_id=1, source_target_pairs={{0,6},{1,7},{2,4},{3,5},{4,2},{5,3},{6,0},{7,1},{8,14},{9,15},{10,... | collective-permute-start | bytes 221192 | tf_op jit(solution)/shard_map/ppermute | solution.py:43
  97.7 2.0 %collective-permute-start.16 = (bf16[72,512]{1,0:T(8,128)(2,1)S(1)}, bf16[72,512]{1,0:T(8,128)(2,1)S(1)}, u32[]{:S(2)}, u32[]{:S(2)}) collective-permute-start(bf16[72,512]{1,0:T(8,128)(2,1)S(1)} %get-tuple-element.49), channel_id=1, source_target_pairs={{0,32},{1,33},{2,34},{3,35},{4,36},{5,37},{6,38},{7,39},{8,40},{9,... | collective-permute-start | bytes 221192 | tf_op jit(solution)/shard_map/ppermute | solution.py:43
  99.7 1.8 %collective-permute-start.15 = (bf16[72,512]{1,0:T(8,128)(2,1)S(1)}, bf16[72,512]{1,0:T(8,128)(2,1)S(1)}, u32[]{:S(2)}, u32[]{:S(2)}) collective-permute-start(bf16[72,512]{1,0:T(8,128)(2,1)S(1)} %get-tuple-element.50), channel_id=1, source_target_pairs={{0,48},{1,49},{2,50},{3,51},{4,52},{5,53},{6,54},{7,55},{8,56},{9,... | collective-permute-start | bytes 221192 | tf_op jit(solution)/shard_map/ppermute | solution.py:43
  101.6 2.7 %collective-permute-done.16 = bf16[72,512]{1,0:T(8,128)(2,1)S(1)} collective-permute-done((bf16[72,512]{1,0:T(8,128)(2,1)S(1)}, bf16[72,512]{1,0:T(8,128)(2,1)S(1)}, u32[]{:S(2)}, u32[]{:S(2)}) %collective-permute-start.16) | collective-permute-done | bytes 73760 | tf_op jit(solution)/shard_map/ppermute | solution.py:43
  106.1 1.7 %collective-permute-start.18 = (bf16[2,18,512]{2,1,0:T(8,128)(2,1)S(1)}, bf16[2,18,512]{2,1,0:T(8,128)(2,1)S(1)}, u32[]{:S(2)}, u32[]{:S(2)}) collective-permute-start(bf16[2,18,512]{2,1,0:T(8,128)(2,1)S(1)} %get-tuple-element.56), channel_id=1, source_target_pairs={{0,192},{1,193},{2,194},{3,195},{4,196},{5,197},{6,198},{7,199},{8... | collective-permute-start | bytes 110600 | tf_op jit(solution)/shard_map/ppermute | solution.py:43
  107.8 2.6 %collective-permute-start.17 = (bf16[2,18,512]{2,1,0:T(8,128)(2,1)S(1)}, bf16[2,18,512]{2,1,0:T(8,128)(2,1)S(1)}, u32[]{:S(2)}, u32[]{:S(2)}) collective-permute-start(bf16[2,18,512]{2,1,0:T(8,128)(2,1)S(1)} %get-tuple-element.54), channel_id=1, source_target_pairs={{0,64},{1,65},{2,66},{3,67},{4,68},{5,69},{6,70},{7,71},{8,72},{9,... | collective-permute-start | bytes 110600 | tf_op jit(solution)/shard_map/ppermute | solution.py:43
  111.6 1.5 %collective-permute-done.17 = bf16[2,18,512]{2,1,0:T(8,128)(2,1)S(1)} collective-permute-done((bf16[2,18,512]{2,1,0:T(8,128)(2,1)S(1)}, bf16[2,18,512]{2,1,0:T(8,128)(2,1)S(1)}, u32[]{:S(2)}, u32[]{:S(2)}) %collective-permute-start.17) | collective-permute-done | bytes 36896 | tf_op jit(solution)/shard_map/ppermute | solution.py:43
  113.2 4.6 %collective-permute-start.20 = (bf16[2,9,512]{2,1,0:T(8,128)(2,1)S(1)}, bf16[2,9,512]{2,1,0:T(8,128)(2,1)S(1)}, u32[]{:S(2)}, u32[]{:S(2)}) collective-permute-start(bf16[2,9,512]{2,1,0:T(8,128)(2,1)S(1)} %bitcast.75), channel_id=1, source_target_pairs={{0,0},{1,128},{2,8},{3,136},{4,64},{5,192},{6,72},{7,200},{8,1},{9... | collective-permute-start | bytes 55304 | tf_op jit(solution)/shard_map/ppermute | solution.py:80
  118.0 3.4 %collective-permute-done.20.one_ref = bf16[2,9,512]{2,1,0:T(8,128)(2,1)S(1)} collective-permute-done((bf16[2,9,512]{2,1,0:T(8,128)(2,1)S(1)}, bf16[2,9,512]{2,1,0:T(8,128)(2,1)S(1)}, u32[]{:S(2)}, u32[]{:S(2)}) %collective-permute-start.20) | collective-permute-done | bytes 18464 | tf_op jit(solution)/shard_map/ppermute | solution.py:80
  121.4 6.2 %collective-permute-done.21.two_ref = bf16[2,9,512]{2,1,0:T(8,128)(2,1)S(1)} collective-permute-done((bf16[2,9,512]{2,1,0:T(8,128)(2,1)S(1)}, bf16[2,9,512]{2,1,0:T(8,128)(2,1)S(1)}, u32[]{:S(2)}, u32[]{:S(2)}) %collective-permute-start.21) | collective-permute-done | bytes 18464 | tf_op jit(solution)/shard_map/ppermute | solution.py:80
  (65 shorter events, 9.7 us)
Async XLA Ops:
  0.6 18.1 %copy-start.4 = (f32[16,16,256]{2,1,0:T(8,128)S(1)}, f32[16,16,256]{2,1,0:T(8,128)}, u32[]{:S(2)}) copy-start(f32[16,16,256]{2,1,0:T(8,128)} %low_ref.3) | copy-start | bytes 786436
  6.8 10.7 %collective-permute-start = (bf16[23,16,256]{2,1,0:T(8,128)(2,1)}, bf16[23,16,256]{2,1,0:T(8,128)(2,1)S(1)}, u32[]{:S(2)}, u32[]{:S(2)}) collective-permute-start(bf16[23,16,256]{2,1,0:T(8,128)(2,1)} %get-tuple-element.24), channel_id=1, source_target_pairs={{0,16},{1,17},{2,18},{3,19},{4,20},{5,21},{6,22},{7,23},{8,24},{9,... | collective-permute-start | bytes 565256 | tf_op jit(solution)/shard_map/ppermute | solution.py:432
  10.2 8.6 %collective-permute-start.1 = (bf16[23,16,256]{2,1,0:T(8,128)(2,1)}, bf16[23,16,256]{2,1,0:T(8,128)(2,1)S(1)}, u32[]{:S(2)}, u32[]{:S(2)}) collective-permute-start(bf16[23,16,256]{2,1,0:T(8,128)(2,1)} %get-tuple-element.25), channel_id=1, source_target_pairs={{16,0},{17,1},{18,2},{19,3},{20,4},{21,5},{22,6},{23,7},{24,8},{25... | collective-permute-start | bytes 565256 | tf_op jit(solution)/shard_map/ppermute | solution.py:432
  18.8 1.6 %copy-start = (f32[4,17,32,256]{3,2,1,0:T(8,128)S(1)}, f32[4,17,32,256]{3,2,1,0:T(8,128)}, u32[]{:S(2)}) copy-start(f32[4,17,32,256]{3,2,1,0:T(8,128)} %get-tuple-element.23.part_ref) | copy-start | bytes 6684676
  20.4 4.0 %copy-start.2 = (bf16[2304,256]{1,0:T(8,128)(2,1)S(1)}, bf16[2304,256]{1,0:T(8,128)(2,1)}, u32[]{:S(2)}) copy-start(bf16[2304,256]{1,0:T(8,128)(2,1)} %w_coarse.3) | copy-start | bytes 3538948
  20.4 4.0 %copy-start.3 = (bf16[2304,256]{1,0:T(8,128)(2,1)S(1)}, bf16[2304,256]{1,0:T(8,128)(2,1)}, u32[]{:S(2)}) copy-start(bf16[2304,256]{1,0:T(8,128)(2,1)} %w_post.1) | copy-start | bytes 3538948
  21.6 6.7 %collective-permute-start.2 = (bf16[24,24,256]{2,1,0:T(8,128)(2,1)}, bf16[24,24,256]{2,1,0:T(8,128)(2,1)S(1)}, u32[]{:S(2)}, u32[]{:S(2)}) collective-permute-start(bf16[24,24,256]{2,1,0:T(8,128)(2,1)} %get-tuple-element.26), channel_id=1, source_target_pairs={{0,1},{1,2},{2,3},{3,4},{4,5},{5,6},{6,7},{7,8},{8,9},{9,10},{10,1... | collective-permute-start | bytes 884744 | tf_op jit(solution)/shard_map/ppermute | solution.py:432
  22.9 5.6 %collective-permute-start.3 = (bf16[24,24,256]{2,1,0:T(8,128)(2,1)}, bf16[24,24,256]{2,1,0:T(8,128)(2,1)}, u32[]{:S(2)}, u32[]{:S(2)}) collective-permute-start(bf16[24,24,256]{2,1,0:T(8,128)(2,1)} %get-tuple-element.27), channel_id=1, source_target_pairs={{1,0},{2,1},{3,2},{4,3},{5,4},{6,5},{7,6},{8,7},{9,8},{10,9},{11,1... | collective-permute-start | bytes 884744 | tf_op jit(solution)/shard_map/ppermute | solution.py:432
  24.4 1.7 %copy-start.7 = (bf16[2304,512]{1,0:T(8,128)(2,1)S(1)}, bf16[2304,512]{1,0:T(8,128)(2,1)}, u32[]{:S(2)}) copy-start(bf16[2304,512]{1,0:T(8,128)(2,1)} %w_prior.1) | copy-start | bytes 7077892
  26.1 2.4 %copy-start.1 = (f32[4,17,32,256]{3,2,1,0:T(8,128)S(1)}, f32[4,17,32,256]{3,2,1,0:T(8,128)}, u32[]{:S(2)}) copy-start(f32[4,17,32,256]{3,2,1,0:T(8,128)} %get-tuple-element.23.part_ref) | copy-start | bytes 6684676
  26.1 2.4 %copy-start.8 = (bf16[4,16,16,256]{3,2,1,0:T(8,128)(2,1)S(1)}, bf16[4,16,16,256]{3,2,1,0:T(8,128)(2,1)}, u32[]{:S(2)}) copy-start(bf16[4,16,16,256]{3,2,1,0:T(8,128)(2,1)} %get-tuple-element.22.own_ref) | copy-start | bytes 1572868
  28.2 20.6 %copy-start.9 = (bf16[2304,256]{1,0:T(8,128)(2,1)}, bf16[2304,256]{1,0:T(8,128)(2,1)S(1)}, u32[]{:S(2)}) copy-start(bf16[2304,256]{1,0:T(8,128)(2,1)S(1)} %get-tuple-element.33.w_post_t) | copy-start | bytes 3538948
  48.9 1.4 %copy-start.5 = (bf16[2,1152,512]{2,1,0:T(8,128)(2,1)}, bf16[2,1152,512]{2,1,0:T(8,128)(2,1)S(1)}, u32[]{:S(2)}) copy-start(bf16[2,1152,512]{2,1,0:T(8,128)(2,1)S(1)} %get-tuple-element.35.keep_ref) | copy-start | bytes 7077892
  51.3 9.7 %collective-permute-start.4 = (bf16[2,1152,512]{2,1,0:T(8,128)(2,1)}, bf16[2,1152,512]{2,1,0:T(8,128)(2,1)S(1)}, u32[]{:S(2)}, u32[]{:S(2)}) collective-permute-start(bf16[2,1152,512]{2,1,0:T(8,128)(2,1)} %get-tuple-element.31), channel_id=1, source_target_pairs={{0,1},{1,0},{2,3},{3,2},{4,5},{5,4},{6,7},{7,6},{8,9},{9,8},{10,11... | collective-permute-start | bytes 7077896 | tf_op jit(solution)/shard_map/ppermute | solution.py:56
  58.8 2.2 %copy-start.6 = (bf16[2,1152,512]{2,1,0:T(8,128)(2,1)S(1)}, bf16[2,1152,512]{2,1,0:T(8,128)(2,1)}, u32[]{:S(2)}) copy-start(bf16[2,1152,512]{2,1,0:T(8,128)(2,1)} %copy-done.5) | copy-start | bytes 7077892
  61.8 20.8 %collective-permute-start.7 = (bf16[2,144,512]{2,1,0:T(8,128)(2,1)S(1)}, bf16[2,144,512]{2,1,0:T(8,128)(2,1)S(1)}, u32[]{:S(2)}, u32[]{:S(2)}) collective-permute-start(bf16[2,144,512]{2,1,0:T(8,128)(2,1)S(1)} %get-tuple-element.46), channel_id=1, source_target_pairs={{0,32},{1,33},{2,34},{3,35},{4,36},{5,37},{6,38},{7,39},{8,40},{9,... | collective-permute-start | bytes 884744 | tf_op jit(solution)/shard_map/ppermute | solution.py:43
  64.5 18.9 %collective-permute-start.6 = (bf16[2,144,512]{2,1,0:T(8,128)(2,1)S(1)}, bf16[2,144,512]{2,1,0:T(8,128)(2,1)}, u32[]{:S(2)}, u32[]{:S(2)}) collective-permute-start(bf16[2,144,512]{2,1,0:T(8,128)(2,1)S(1)} %get-tuple-element.47), channel_id=1, source_target_pairs={{0,48},{1,49},{2,50},{3,51},{4,52},{5,53},{6,54},{7,55},{8,56},{9,... | collective-permute-start | bytes 884744 | tf_op jit(solution)/shard_map/ppermute | solution.py:43
  67.0 16.4 %collective-permute-start.5 = (bf16[2,144,512]{2,1,0:T(8,128)(2,1)S(1)}, bf16[2,144,512]{2,1,0:T(8,128)(2,1)}, u32[]{:S(2)}, u32[]{:S(2)}) collective-permute-start(bf16[2,144,512]{2,1,0:T(8,128)(2,1)S(1)} %get-tuple-element.45), channel_id=1, source_target_pairs={{0,16},{1,17},{2,18},{3,19},{4,20},{5,21},{6,22},{7,23},{8,24},{9,... | collective-permute-start | bytes 884744 | tf_op jit(solution)/shard_map/ppermute | solution.py:43
  67.8 28.9 %collective-permute-start.13 = (bf16[4,72,512]{2,1,0:T(8,128)(2,1)S(1)}, bf16[4,72,512]{2,1,0:T(8,128)(2,1)S(1)}, u32[]{:S(2)}, u32[]{:S(2)}) collective-permute-start(bf16[4,72,512]{2,1,0:T(8,128)(2,1)S(1)} %get-tuple-element.43), channel_id=1, source_target_pairs={{0,4},{1,5},{2,6},{3,7},{4,0},{5,1},{6,2},{7,3},{8,12},{9,13},{10,... | collective-permute-start | bytes 884744 | tf_op jit(solution)/shard_map/ppermute | solution.py:43
  70.8 26.7 %collective-permute-start.12 = (bf16[4,72,512]{2,1,0:T(8,128)(2,1)S(1)}, bf16[4,72,512]{2,1,0:T(8,128)(2,1)S(1)}, u32[]{:S(2)}, u32[]{:S(2)}) collective-permute-start(bf16[4,72,512]{2,1,0:T(8,128)(2,1)S(1)} %get-tuple-element.44), channel_id=1, source_target_pairs={{0,6},{1,7},{2,4},{3,5},{4,2},{5,3},{6,0},{7,1},{8,14},{9,15},{10,... | collective-permute-start | bytes 884744 | tf_op jit(solution)/shard_map/ppermute | solution.py:43
  82.6 14.9 %collective-permute-start.11 = (bf16[4,72,512]{2,1,0:T(8,128)(2,1)S(1)}, bf16[4,72,512]{2,1,0:T(8,128)(2,1)S(1)}, u32[]{:S(2)}, u32[]{:S(2)}) collective-permute-start(bf16[4,72,512]{2,1,0:T(8,128)(2,1)S(1)} %get-tuple-element.42), channel_id=1, source_target_pairs={{0,2},{1,3},{2,0},{3,1},{4,6},{5,7},{6,4},{7,5},{8,10},{9,11},{10,... | collective-permute-start | bytes 884744 | tf_op jit(solution)/shard_map/ppermute | solution.py:43
  84.7 16.8 %collective-permute-start.10 = (bf16[72,512]{1,0:T(8,128)(2,1)S(1)}, bf16[72,512]{1,0:T(8,128)(2,1)S(1)}, u32[]{:S(2)}, u32[]{:S(2)}) collective-permute-start(bf16[72,512]{1,0:T(8,128)(2,1)S(1)} %get-tuple-element.52), channel_id=1, source_target_pairs={{0,4},{1,5},{2,6},{3,7},{4,0},{5,1},{6,2},{7,3},{8,12},{9,13},{10,... | collective-permute-start | bytes 221192 | tf_op jit(solution)/shard_map/ppermute | solution.py:43
  92.7 8.8 %collective-permute-start.9 = (bf16[72,512]{1,0:T(8,128)(2,1)S(1)}, bf16[72,512]{1,0:T(8,128)(2,1)S(1)}, u32[]{:S(2)}, u32[]{:S(2)}) collective-permute-start(bf16[72,512]{1,0:T(8,128)(2,1)S(1)} %get-tuple-element.53), channel_id=1, source_target_pairs={{0,6},{1,7},{2,4},{3,5},{4,2},{5,3},{6,0},{7,1},{8,14},{9,15},{10,... | collective-permute-start | bytes 221192 | tf_op jit(solution)/shard_map/ppermute | solution.py:43
  96.7 4.8 %collective-permute-start.8 = (bf16[72,512]{1,0:T(8,128)(2,1)S(1)}, bf16[72,512]{1,0:T(8,128)(2,1)S(1)}, u32[]{:S(2)}, u32[]{:S(2)}) collective-permute-start(bf16[72,512]{1,0:T(8,128)(2,1)S(1)} %get-tuple-element.51), channel_id=1, source_target_pairs={{0,2},{1,3},{2,0},{3,1},{4,6},{5,7},{6,4},{7,5},{8,10},{9,11},{10,... | collective-permute-start | bytes 221192 | tf_op jit(solution)/shard_map/ppermute | solution.py:43
  97.7 6.6 %collective-permute-start.16 = (bf16[72,512]{1,0:T(8,128)(2,1)S(1)}, bf16[72,512]{1,0:T(8,128)(2,1)S(1)}, u32[]{:S(2)}, u32[]{:S(2)}) collective-permute-start(bf16[72,512]{1,0:T(8,128)(2,1)S(1)} %get-tuple-element.49), channel_id=1, source_target_pairs={{0,32},{1,33},{2,34},{3,35},{4,36},{5,37},{6,38},{7,39},{8,40},{9,... | collective-permute-start | bytes 221192 | tf_op jit(solution)/shard_map/ppermute | solution.py:43
  99.7 5.6 %collective-permute-start.15 = (bf16[72,512]{1,0:T(8,128)(2,1)S(1)}, bf16[72,512]{1,0:T(8,128)(2,1)S(1)}, u32[]{:S(2)}, u32[]{:S(2)}) collective-permute-start(bf16[72,512]{1,0:T(8,128)(2,1)S(1)} %get-tuple-element.50), channel_id=1, source_target_pairs={{0,48},{1,49},{2,50},{3,51},{4,52},{5,53},{6,54},{7,55},{8,56},{9,... | collective-permute-start | bytes 221192 | tf_op jit(solution)/shard_map/ppermute | solution.py:43
  101.5 4.4 %collective-permute-start.14 = (bf16[72,512]{1,0:T(8,128)(2,1)S(1)}, bf16[72,512]{1,0:T(8,128)(2,1)S(1)}, u32[]{:S(2)}, u32[]{:S(2)}) collective-permute-start(bf16[72,512]{1,0:T(8,128)(2,1)S(1)} %get-tuple-element.48), channel_id=1, source_target_pairs={{0,16},{1,17},{2,18},{3,19},{4,20},{5,21},{6,22},{7,23},{8,24},{9,... | collective-permute-start | bytes 221192 | tf_op jit(solution)/shard_map/ppermute | solution.py:43
  106.0 5.6 %collective-permute-start.19 = (bf16[2,18,512]{2,1,0:T(8,128)(2,1)S(1)}, bf16[2,18,512]{2,1,0:T(8,128)(2,1)S(1)}, u32[]{:S(2)}, u32[]{:S(2)}) collective-permute-start(bf16[2,18,512]{2,1,0:T(8,128)(2,1)S(1)} %get-tuple-element.55), channel_id=1, source_target_pairs={{0,128},{1,129},{2,130},{3,131},{4,132},{5,133},{6,134},{7,135},{8... | collective-permute-start | bytes 110600 | tf_op jit(solution)/shard_map/ppermute | solution.py:43
  106.1 5.5 %collective-permute-start.18 = (bf16[2,18,512]{2,1,0:T(8,128)(2,1)S(1)}, bf16[2,18,512]{2,1,0:T(8,128)(2,1)S(1)}, u32[]{:S(2)}, u32[]{:S(2)}) collective-permute-start(bf16[2,18,512]{2,1,0:T(8,128)(2,1)S(1)} %get-tuple-element.56), channel_id=1, source_target_pairs={{0,192},{1,193},{2,194},{3,195},{4,196},{5,197},{6,198},{7,199},{8... | collective-permute-start | bytes 110600 | tf_op jit(solution)/shard_map/ppermute | solution.py:43
  107.8 5.2 %collective-permute-start.17 = (bf16[2,18,512]{2,1,0:T(8,128)(2,1)S(1)}, bf16[2,18,512]{2,1,0:T(8,128)(2,1)S(1)}, u32[]{:S(2)}, u32[]{:S(2)}) collective-permute-start(bf16[2,18,512]{2,1,0:T(8,128)(2,1)S(1)} %get-tuple-element.54), channel_id=1, source_target_pairs={{0,64},{1,65},{2,66},{3,67},{4,68},{5,69},{6,70},{7,71},{8,72},{9,... | collective-permute-start | bytes 110600 | tf_op jit(solution)/shard_map/ppermute | solution.py:43
  113.2 8.2 %collective-permute-start.20 = (bf16[2,9,512]{2,1,0:T(8,128)(2,1)S(1)}, bf16[2,9,512]{2,1,0:T(8,128)(2,1)S(1)}, u32[]{:S(2)}, u32[]{:S(2)}) collective-permute-start(bf16[2,9,512]{2,1,0:T(8,128)(2,1)S(1)} %bitcast.75), channel_id=1, source_target_pairs={{0,0},{1,128},{2,8},{3,136},{4,64},{5,192},{6,72},{7,200},{8,1},{9... | collective-permute-start | bytes 55304 | tf_op jit(solution)/shard_map/ppermute | solution.py:80
  117.9 9.8 %collective-permute-start.21 = (bf16[2,9,512]{2,1,0:T(8,128)(2,1)S(1)}, bf16[2,9,512]{2,1,0:T(8,128)(2,1)S(1)}, u32[]{:S(2)}, u32[]{:S(2)}) collective-permute-start(bf16[2,9,512]{2,1,0:T(8,128)(2,1)S(1)} %bitcast.76), channel_id=1, source_target_pairs={{0,1},{1,129},{2,9},{3,137},{4,65},{5,193},{6,73},{7,201},{8,0},{9... | collective-permute-start | bytes 55304 | tf_op jit(solution)/shard_map/ppermute | solution.py:80
  (3 other events, 3.6 us)

commit v8 on v7

--- a/solution.py
+++ b/solution.py
@@ -35,16 +35,19 @@
     return {**place, name: place[name] ^ bits}
 
 
-def sum_stage(part, name, cut):
+def sum_stage(part, name, cut, beside=None):
     here = my_place()[name]
     arrived = []
     for bits in (1, 3, 2):
         pairs = [(index_of(p), index_of(flipped(p, name, bits))) for p in digits()]
         arrived.append(lax.ppermute(cut(part, here ^ bits), ("row", "col"), pairs))
+    if beside is not None:
+        arrived, beside = lax.optimization_barrier((arrived, beside))
     total = cut(part, here).astype(F32)
     for piece in arrived:
         total = total + piece.astype(F32)
-    return total.astype(BF)
+    total = total.astype(BF)
+    return total if beside is None else (total, beside)
 
 
 def pick(dim):
@@ -53,7 +56,7 @@
 
 def reduce_scatter(keep, send, beside):
     pairs = [(index_of(p), index_of(flipped(p, "core", 1))) for p in digits()]
-    other, beside = lax.optimization_barrier((lax.ppermute(send, ("row", "col"), pairs), beside))
+    other = lax.ppermute(send, ("row", "col"), pairs)
     parts = pl.pallas_call(
         join_kernel,
         out_shape=jax.ShapeDtypeStruct((2, 1152, 512), BF),
@@ -62,7 +65,7 @@
         compiler_params=room(9),
         name="join",
     )(keep, other)
-    first = sum_stage(parts[0].reshape(2, 4, 144, 512), "x", pick(1))
+    first, beside = sum_stage(parts[0].reshape(2, 4, 144, 512), "x", pick(1), beside)
     second = sum_stage(parts[1].reshape(2, 4, 2, 72, 512), "y", lambda part, at: pick(1)(pick(0)(part, at // 2), at % 2))
     first = sum_stage(first.reshape(4, 72, 512), "y", pick(0))
     second = sum_stage(second, "x", pick(0))

time: 129 us -> 133 us (1.031)
  waiting for transfers between devices: 20.7 us -> 24.8 us
    ppermute x1, waiting for transfers between devices: 0.01 us -> 4.37 us  [reduce_scatter(): other = lax.ppermute(send, ('row', 'col'), pairs)]
    unnamed x27 -> x29, local copies, waits for them, and re-layouts: 8.33 us -> 7.44 us
where the time goes in v8:
time: 133 us; the launch traced here: 132 us
  starting transfers between devices  61.9 us (47%)
  Pallas kernels  33.2 us (25%)
  waiting for transfers between devices  24.8 us (19%)
  local copies, waits for them, and re-layouts  9.89 us (7%)
  other arithmetic  1.65 us (1%)
    ppermute x15, starting transfers between devices, sum_stage(): arrived.append(lax.ppermute(cut(part, here ^ bits), ('row', 'col'), pairs))  42.6 us
    pallas_call x1, Pallas kernels, on_device(): pl.pallas_call(functools.partial(main_kernel, scale), out_shape=[jax.Shap...  20.3 us
    ppermute x4, starting transfers between devices, sent(): return lax.ppermute(strip, ('row', 'col'), pairs)  10.7 us
    ppermute x2, waiting for transfers between devices, reduce_scatter(): arrived.append(lax.ppermute(piece, ('row', 'col'), pairs))  9.31 us
    unnamed x29, local copies, waits for them, and re-layouts  7.44 us
    ppermute x15, waiting for transfers between devices, sum_stage(): arrived.append(lax.ppermute(cut(part, here ^ bits), ('row', 'col'), pairs))  6.93 us
    pallas_call x1, Pallas kernels, on_device(): pl.pallas_call(first_kernel, out_shape=[jax.ShapeDtypeStruct((4, 16, 16,...  6.13 us
    ppermute x1, starting transfers between devices, reduce_scatter(): other = lax.ppermute(send, ('row', 'col'), pairs)  4.94 us
  transfers between devices with their start and end apart: 22, of which 10 were waited for; matrix products, arithmetic and copies ran while one was open for 1% of the time, Pallas kernels for 3%

profile of v8, /device:TPU:32, one launch (start us, length us, event | category | flops | bytes accessed | tf_op | source)
XLA Modules:
  0.0 132.3 jit_solution(13578735981720122241)
XLA Ops:
  0.6 6.1 %first.1 = (bf16[4,16,16,256]{3,2,1,0:T(8,128)(2,1)}, f32[4,17,32,256]{3,2,1,0:T(8,128)}, bf16[23,16,256]{2,1,0:T(8,128)(2,1)}, bf16[23,16,256]{2,1,0:T(8,128)(2,1)}) custom-call(bf16[16,2,32,256]{3,2,1,0:T(8,128)(2,1)} %bitcast.73, f32[16,2,32,256]{3,2,1,0:T(8,128)} %bitcast.72, f32[16,16,256]{2,1,0:T(8,128)} %low_ref.3, bf16[2304,256]{1,0:T(8,128)(2,1)} %w_post.1), custom_call_target="tpu_custom_call" | custom-call | tf_op jit(solution)/shard_map/first/pallas_call | solution.py:440
  6.8 3.4 %collective-permute-start = (bf16[23,16,256]{2,1,0:T(8,128)(2,1)}, bf16[23,16,256]{2,1,0:T(8,128)(2,1)S(1)}, u32[]{:S(2)}, u32[]{:S(2)}) collective-permute-start(bf16[23,16,256]{2,1,0:T(8,128)(2,1)} %get-tuple-element.26), channel_id=1, source_target_pairs={{0,16},{1,17},{2,18},{3,19},{4,20},{5,21},{6,22},{7,23},{8,24},{9,... | collective-permute-start | bytes 565256 | tf_op jit(solution)/shard_map/ppermute | solution.py:435
  10.2 4.6 %collective-permute-start.1 = (bf16[23,16,256]{2,1,0:T(8,128)(2,1)}, bf16[23,16,256]{2,1,0:T(8,128)(2,1)S(1)}, u32[]{:S(2)}, u32[]{:S(2)}) collective-permute-start(bf16[23,16,256]{2,1,0:T(8,128)(2,1)} %get-tuple-element.27), channel_id=1, source_target_pairs={{16,0},{17,1},{18,2},{19,3},{20,4},{21,5},{22,6},{23,7},{24,8},{25... | collective-permute-start | bytes 565256 | tf_op jit(solution)/shard_map/ppermute | solution.py:435
  14.7 2.7 %collective-permute-done.up_ref = bf16[23,16,256]{2,1,0:T(8,128)(2,1)S(1)} collective-permute-done((bf16[23,16,256]{2,1,0:T(8,128)(2,1)}, bf16[23,16,256]{2,1,0:T(8,128)(2,1)S(1)}, u32[]{:S(2)}, u32[]{:S(2)}) %collective-permute-start) | collective-permute-done | bytes 188448 | tf_op jit(solution)/shard_map/ppermute | solution.py:435
  17.5 1.3 collective-permute-done.1.down_ref
  18.8 1.6 %copy-done = f32[4,17,32,256]{3,2,1,0:T(8,128)S(1)} copy-done((f32[4,17,32,256]{3,2,1,0:T(8,128)S(1)}, f32[4,17,32,256]{3,2,1,0:T(8,128)}, u32[]{:S(2)}) %copy-start) | copy-done | bytes 2228248
  21.6 1.3 collective-permute-start.2
  22.9 1.5 %collective-permute-start.3 = (bf16[24,24,256]{2,1,0:T(8,128)(2,1)}, bf16[24,24,256]{2,1,0:T(8,128)(2,1)}, u32[]{:S(2)}, u32[]{:S(2)}) collective-permute-start(bf16[24,24,256]{2,1,0:T(8,128)(2,1)} %get-tuple-element.29), channel_id=1, source_target_pairs={{1,0},{2,1},{3,2},{4,3},{5,4},{6,5},{7,6},{8,7},{9,8},{10,9},{11,1... | collective-permute-start | bytes 884744 | tf_op jit(solution)/shard_map/ppermute | solution.py:435
  24.4 1.7 %copy-done.7 = bf16[2304,512]{1,0:T(8,128)(2,1)S(1)} copy-done((bf16[2304,512]{1,0:T(8,128)(2,1)S(1)}, bf16[2304,512]{1,0:T(8,128)(2,1)}, u32[]{:S(2)}) %copy-start.7) | copy-done | bytes 2359320
  26.1 2.1 %weights.1 = (bf16[4,1024,512]{2,1,0:T(8,128)(2,1)S(1)}, bf16[4,2048,256]{2,1,0:T(8,128)(2,1)S(1)}, bf16[2304,256]{1,0:T(8,128)(2,1)S(1)}, bf16[2304,256]{1,0:T(8,128)(2,1)S(1)}) custom-call(bf16[2304,256]{1,0:T(8,128)(2,1)S(1)} %copy-done.3, bf16[2304,256]{1,0:T(8,128)(2,1)S(1)} %copy-done.2, bf16[2304,512]{1,0:T(8,128)(2,1)S(1)} %copy-done.7), custom_call_target="tpu_custom_call" | custom-call | flops 10000000 | bytes 15000000 | tf_op jit(solution)/shard_map/weights/pallas_call | solution.py:466
  28.5 20.3 %tile.1 = (bf16[2,1152,512]{2,1,0:T(8,128)(2,1)S(1)}, bf16[2,1152,512]{2,1,0:T(8,128)(2,1)}, bf16[2,18,16,1024]{3,2,1,0:T(8,128)(2,1)S(1)}) custom-call(s32[3]{0:T(128)S(1)} %pad_add_fusion.place_ref, bf16[4,16,16,256]{3,2,1,0:T(8,128)(2,1)S(1)} %copy-done.8, f32[4,17,32,256]{3,2,1,0:T(8,128)S(1)} %copy-done.1, f32[16,16,256]{2,1,0:T(8,128)S(1)} %copy-done.4, ...), custom_call_target="tpu_custom_call" | custom-call | tf_op jit(solution)/shard_map/tile/pallas_call | solution.py:492
  48.8 1.4 %copy-done.5 = bf16[2,1152,512]{2,1,0:T(8,128)(2,1)} copy-done((bf16[2,1152,512]{2,1,0:T(8,128)(2,1)}, bf16[2,1152,512]{2,1,0:T(8,128)(2,1)S(1)}, u32[]{:S(2)}) %copy-start.5) | copy-done | bytes 2359320
  51.3 4.9 %collective-permute-start.4 = (bf16[2,1152,512]{2,1,0:T(8,128)(2,1)}, bf16[2,1152,512]{2,1,0:T(8,128)(2,1)S(1)}, u32[]{:S(2)}, u32[]{:S(2)}) collective-permute-start(bf16[2,1152,512]{2,1,0:T(8,128)(2,1)} %get-tuple-element.34), channel_id=1, source_target_pairs={{0,1},{1,0},{2,3},{3,2},{4,5},{5,4},{6,7},{7,6},{8,9},{9,8},{10,11... | collective-permute-start | bytes 7077896 | tf_op jit(solution)/shard_map/ppermute | solution.py:59
  56.2 4.4 %collective-permute-done.4.other_ref = bf16[2,1152,512]{2,1,0:T(8,128)(2,1)S(1)} collective-permute-done((bf16[2,1152,512]{2,1,0:T(8,128)(2,1)}, bf16[2,1152,512]{2,1,0:T(8,128)(2,1)S(1)}, u32[]{:S(2)}, u32[]{:S(2)}) %collective-permute-start.4) | collective-permute-done | bytes 2359328 | tf_op jit(solution)/shard_map/ppermute | solution.py:59
  60.6 1.7 %copy-done.6 = bf16[2,1152,512]{2,1,0:T(8,128)(2,1)S(1)} copy-done((bf16[2,1152,512]{2,1,0:T(8,128)(2,1)S(1)}, bf16[2,1152,512]{2,1,0:T(8,128)(2,1)}, u32[]{:S(2)}) %copy-start.6) | copy-done | bytes 2359320
  65.0 1.2 collective-permute-start.5
  66.2 3.7 %collective-permute-start.6 = (bf16[2,144,512]{2,1,0:T(8,128)(2,1)}, bf16[2,144,512]{2,1,0:T(8,128)(2,1)}, u32[]{:S(2)}, u32[]{:S(2)}) collective-permute-start(bf16[2,144,512]{2,1,0:T(8,128)(2,1)} %get-tuple-element.50), channel_id=1, source_target_pairs={{0,48},{1,49},{2,50},{3,51},{4,52},{5,53},{6,54},{7,55},{8,56},{9,... | collective-permute-start | bytes 884744 | tf_op jit(solution)/shard_map/ppermute | solution.py:43
  69.9 1.5 %collective-permute-start.7 = (bf16[2,144,512]{2,1,0:T(8,128)(2,1)}, bf16[2,144,512]{2,1,0:T(8,128)(2,1)}, u32[]{:S(2)}, u32[]{:S(2)}) collective-permute-start(bf16[2,144,512]{2,1,0:T(8,128)(2,1)} %get-tuple-element.49), channel_id=1, source_target_pairs={{0,32},{1,33},{2,34},{3,35},{4,36},{5,37},{6,38},{7,39},{8,40},{9,... | collective-permute-start | bytes 884744 | tf_op jit(solution)/shard_map/ppermute | solution.py:43
  71.4 2.2 %feat.1 = bf16[16,2,32,256]{3,2,1,0:T(8,128)(2,1)} custom-call(bf16[2,18,16,1024]{3,2,1,0:T(8,128)(2,1)S(1)} %copy-done.12, bf16[2304,256]{1,0:T(8,128)(2,1)S(1)} %copy-done.10), custom_call_target="tpu_custom_call" | custom-call | flops 1200000000 | bytes 3000000 | tf_op jit(solution)/shard_map/feat/pallas_call | solution.py:519
  73.7 3.0 %collective-permute-start.13 = (bf16[4,72,512]{2,1,0:T(8,128)(2,1)S(1)}, bf16[4,72,512]{2,1,0:T(8,128)(2,1)S(1)}, u32[]{:S(2)}, u32[]{:S(2)}) collective-permute-start(bf16[4,72,512]{2,1,0:T(8,128)(2,1)S(1)} %get-tuple-element.47), channel_id=1, source_target_pairs={{0,4},{1,5},{2,6},{3,7},{4,0},{5,1},{6,2},{7,3},{8,12},{9,13},{10,... | collective-permute-start | bytes 884744 | tf_op jit(solution)/shard_map/ppermute | solution.py:43
  76.7 11.4 %collective-permute-start.12 = (bf16[4,72,512]{2,1,0:T(8,128)(2,1)S(1)}, bf16[4,72,512]{2,1,0:T(8,128)(2,1)S(1)}, u32[]{:S(2)}, u32[]{:S(2)}) collective-permute-start(bf16[4,72,512]{2,1,0:T(8,128)(2,1)S(1)} %get-tuple-element.48), channel_id=1, source_target_pairs={{0,6},{1,7},{2,4},{3,5},{4,2},{5,3},{6,0},{7,1},{8,14},{9,15},{10,... | collective-permute-start | bytes 884744 | tf_op jit(solution)/shard_map/ppermute | solution.py:43
  88.9 1.3 fusion.5
  90.2 4.3 %collective-permute-start.10 = (bf16[72,512]{1,0:T(8,128)(2,1)S(1)}, bf16[72,512]{1,0:T(8,128)(2,1)S(1)}, u32[]{:S(2)}, u32[]{:S(2)}) collective-permute-start(bf16[72,512]{1,0:T(8,128)(2,1)S(1)} %get-tuple-element.56), channel_id=1, source_target_pairs={{0,4},{1,5},{2,6},{3,7},{4,0},{5,1},{6,2},{7,3},{8,12},{9,13},{10,... | collective-permute-start | bytes 221192 | tf_op jit(solution)/shard_map/ppermute | solution.py:43
  94.6 6.6 %collective-permute-start.9 = (bf16[72,512]{1,0:T(8,128)(2,1)S(1)}, bf16[72,512]{1,0:T(8,128)(2,1)S(1)}, u32[]{:S(2)}, u32[]{:S(2)}) collective-permute-start(bf16[72,512]{1,0:T(8,128)(2,1)S(1)} %get-tuple-element.57), channel_id=1, source_target_pairs={{0,6},{1,7},{2,4},{3,5},{4,2},{5,3},{6,0},{7,1},{8,14},{9,15},{10,... | collective-permute-start | bytes 221192 | tf_op jit(solution)/shard_map/ppermute | solution.py:43
  102.1 3.8 %collective-permute-start.16 = (bf16[72,512]{1,0:T(8,128)(2,1)S(1)}, bf16[72,512]{1,0:T(8,128)(2,1)S(1)}, u32[]{:S(2)}, u32[]{:S(2)}) collective-permute-start(bf16[72,512]{1,0:T(8,128)(2,1)S(1)} %get-tuple-element.53), channel_id=1, source_target_pairs={{0,32},{1,33},{2,34},{3,35},{4,36},{5,37},{6,38},{7,39},{8,40},{9,... | collective-permute-start | bytes 221192 | tf_op jit(solution)/shard_map/ppermute | solution.py:43
  108.4 3.1 %collective-permute-done.15 = bf16[72,512]{1,0:T(8,128)(2,1)S(1)} collective-permute-done((bf16[72,512]{1,0:T(8,128)(2,1)S(1)}, bf16[72,512]{1,0:T(8,128)(2,1)S(1)}, u32[]{:S(2)}, u32[]{:S(2)}) %collective-permute-start.15) | collective-permute-done | bytes 73760 | tf_op jit(solution)/shard_map/ppermute | solution.py:43
  111.7 1.6 %collective-permute-start.18 = (bf16[2,18,512]{2,1,0:T(8,128)(2,1)S(1)}, bf16[2,18,512]{2,1,0:T(8,128)(2,1)S(1)}, u32[]{:S(2)}, u32[]{:S(2)}) collective-permute-start(bf16[2,18,512]{2,1,0:T(8,128)(2,1)S(1)} %get-tuple-element.60), channel_id=1, source_target_pairs={{0,192},{1,193},{2,194},{3,195},{4,196},{5,197},{6,198},{7,199},{8... | collective-permute-start | bytes 110600 | tf_op jit(solution)/shard_map/ppermute | solution.py:43
  113.3 2.8 %collective-permute-start.17 = (bf16[2,18,512]{2,1,0:T(8,128)(2,1)S(1)}, bf16[2,18,512]{2,1,0:T(8,128)(2,1)S(1)}, u32[]{:S(2)}, u32[]{:S(2)}) collective-permute-start(bf16[2,18,512]{2,1,0:T(8,128)(2,1)S(1)} %get-tuple-element.58), channel_id=1, source_target_pairs={{0,64},{1,65},{2,66},{3,67},{4,68},{5,69},{6,70},{7,71},{8,72},{9,... | collective-permute-start | bytes 110600 | tf_op jit(solution)/shard_map/ppermute | solution.py:43
  116.8 1.8 %collective-permute-done.17 = bf16[2,18,512]{2,1,0:T(8,128)(2,1)S(1)} collective-permute-done((bf16[2,18,512]{2,1,0:T(8,128)(2,1)S(1)}, bf16[2,18,512]{2,1,0:T(8,128)(2,1)S(1)}, u32[]{:S(2)}, u32[]{:S(2)}) %collective-permute-start.17) | collective-permute-done | bytes 36896 | tf_op jit(solution)/shard_map/ppermute | solution.py:43
  118.8 3.5 %collective-permute-start.20 = (bf16[2,9,512]{2,1,0:T(8,128)(2,1)S(1)}, bf16[2,9,512]{2,1,0:T(8,128)(2,1)S(1)}, u32[]{:S(2)}, u32[]{:S(2)}) collective-permute-start(bf16[2,9,512]{2,1,0:T(8,128)(2,1)S(1)} %bitcast.75), channel_id=1, source_target_pairs={{0,0},{1,128},{2,8},{3,136},{4,64},{5,192},{6,72},{7,200},{8,1},{9... | collective-permute-start | bytes 55304 | tf_op jit(solution)/shard_map/ppermute | solution.py:83
  122.4 4.6 %collective-permute-done.20.one_ref = bf16[2,9,512]{2,1,0:T(8,128)(2,1)S(1)} collective-permute-done((bf16[2,9,512]{2,1,0:T(8,128)(2,1)S(1)}, bf16[2,9,512]{2,1,0:T(8,128)(2,1)S(1)}, u32[]{:S(2)}, u32[]{:S(2)}) %collective-permute-start.20) | collective-permute-done | bytes 18464 | tf_op jit(solution)/shard_map/ppermute | solution.py:83
  127.0 4.7 %collective-permute-done.21.two_ref = bf16[2,9,512]{2,1,0:T(8,128)(2,1)S(1)} collective-permute-done((bf16[2,9,512]{2,1,0:T(8,128)(2,1)S(1)}, bf16[2,9,512]{2,1,0:T(8,128)(2,1)S(1)}, u32[]{:S(2)}, u32[]{:S(2)}) %collective-permute-start.21) | collective-permute-done | bytes 18464 | tf_op jit(solution)/shard_map/ppermute | solution.py:83
  (67 shorter events, 11.3 us)
Async XLA Ops:
  0.6 18.1 %copy-start.4 = (f32[16,16,256]{2,1,0:T(8,128)S(1)}, f32[16,16,256]{2,1,0:T(8,128)}, u32[]{:S(2)}) copy-start(f32[16,16,256]{2,1,0:T(8,128)} %low_ref.3) | copy-start | bytes 786436
  6.8 10.7 %collective-permute-start = (bf16[23,16,256]{2,1,0:T(8,128)(2,1)}, bf16[23,16,256]{2,1,0:T(8,128)(2,1)S(1)}, u32[]{:S(2)}, u32[]{:S(2)}) collective-permute-start(bf16[23,16,256]{2,1,0:T(8,128)(2,1)} %get-tuple-element.26), channel_id=1, source_target_pairs={{0,16},{1,17},{2,18},{3,19},{4,20},{5,21},{6,22},{7,23},{8,24},{9,... | collective-permute-start | bytes 565256 | tf_op jit(solution)/shard_map/ppermute | solution.py:435
  10.2 8.6 %collective-permute-start.1 = (bf16[23,16,256]{2,1,0:T(8,128)(2,1)}, bf16[23,16,256]{2,1,0:T(8,128)(2,1)S(1)}, u32[]{:S(2)}, u32[]{:S(2)}) collective-permute-start(bf16[23,16,256]{2,1,0:T(8,128)(2,1)} %get-tuple-element.27), channel_id=1, source_target_pairs={{16,0},{17,1},{18,2},{19,3},{20,4},{21,5},{22,6},{23,7},{24,8},{25... | collective-permute-start | bytes 565256 | tf_op jit(solution)/shard_map/ppermute | solution.py:435
  20.4 4.0 %copy-start.2 = (bf16[2304,256]{1,0:T(8,128)(2,1)S(1)}, bf16[2304,256]{1,0:T(8,128)(2,1)}, u32[]{:S(2)}) copy-start(bf16[2304,256]{1,0:T(8,128)(2,1)} %w_coarse.3) | copy-start | bytes 3538948
  20.4 4.0 %copy-start.3 = (bf16[2304,256]{1,0:T(8,128)(2,1)S(1)}, bf16[2304,256]{1,0:T(8,128)(2,1)}, u32[]{:S(2)}) copy-start(bf16[2304,256]{1,0:T(8,128)(2,1)} %w_post.1) | copy-start | bytes 3538948
  21.6 6.7 %collective-permute-start.2 = (bf16[24,24,256]{2,1,0:T(8,128)(2,1)}, bf16[24,24,256]{2,1,0:T(8,128)(2,1)S(1)}, u32[]{:S(2)}, u32[]{:S(2)}) collective-permute-start(bf16[24,24,256]{2,1,0:T(8,128)(2,1)} %get-tuple-element.28), channel_id=1, source_target_pairs={{0,1},{1,2},{2,3},{3,4},{4,5},{5,6},{6,7},{7,8},{8,9},{9,10},{10,1... | collective-permute-start | bytes 884744 | tf_op jit(solution)/shard_map/ppermute | solution.py:435
  22.9 5.6 %collective-permute-start.3 = (bf16[24,24,256]{2,1,0:T(8,128)(2,1)}, bf16[24,24,256]{2,1,0:T(8,128)(2,1)}, u32[]{:S(2)}, u32[]{:S(2)}) collective-permute-start(bf16[24,24,256]{2,1,0:T(8,128)(2,1)} %get-tuple-element.29), channel_id=1, source_target_pairs={{1,0},{2,1},{3,2},{4,3},{5,4},{6,5},{7,6},{8,7},{9,8},{10,9},{11,1... | collective-permute-start | bytes 884744 | tf_op jit(solution)/shard_map/ppermute | solution.py:435
  24.4 1.7 %copy-start.7 = (bf16[2304,512]{1,0:T(8,128)(2,1)S(1)}, bf16[2304,512]{1,0:T(8,128)(2,1)}, u32[]{:S(2)}) copy-start(bf16[2304,512]{1,0:T(8,128)(2,1)} %w_prior.1) | copy-start | bytes 7077892
  26.1 2.4 %copy-start.1 = (f32[4,17,32,256]{3,2,1,0:T(8,128)S(1)}, f32[4,17,32,256]{3,2,1,0:T(8,128)}, u32[]{:S(2)}) copy-start(f32[4,17,32,256]{3,2,1,0:T(8,128)} %get-tuple-element.25.part_ref) | copy-start | bytes 6684676
  26.1 2.4 %copy-start.8 = (bf16[4,16,16,256]{3,2,1,0:T(8,128)(2,1)S(1)}, bf16[4,16,16,256]{3,2,1,0:T(8,128)(2,1)}, u32[]{:S(2)}) copy-start(bf16[4,16,16,256]{3,2,1,0:T(8,128)(2,1)} %get-tuple-element.24.own_ref) | copy-start | bytes 1572868
  28.2 20.6 %copy-start.9 = (bf16[2304,256]{1,0:T(8,128)(2,1)}, bf16[2304,256]{1,0:T(8,128)(2,1)S(1)}, u32[]{:S(2)}) copy-start(bf16[2304,256]{1,0:T(8,128)(2,1)S(1)} %get-tuple-element.36.w_post_t) | copy-start | bytes 3538948
  51.3 9.3 %collective-permute-start.4 = (bf16[2,1152,512]{2,1,0:T(8,128)(2,1)}, bf16[2,1152,512]{2,1,0:T(8,128)(2,1)S(1)}, u32[]{:S(2)}, u32[]{:S(2)}) collective-permute-start(bf16[2,1152,512]{2,1,0:T(8,128)(2,1)} %get-tuple-element.34), channel_id=1, source_target_pairs={{0,1},{1,0},{2,3},{3,2},{4,5},{5,4},{6,7},{7,6},{8,9},{9,8},{10,11... | collective-permute-start | bytes 7077896 | tf_op jit(solution)/shard_map/ppermute | solution.py:59
  62.8 8.6 %copy-start.12 = (bf16[2,18,16,1024]{3,2,1,0:T(8,128)(2,1)S(1)}, bf16[2,18,16,1024]{3,2,1,0:T(8,128)(2,1)}, u32[]{:S(2)}) copy-start(bf16[2,18,16,1024]{3,2,1,0:T(8,128)(2,1)} %copy-done.11) | copy-start | bytes 3538948
  64.0 7.4 %copy-start.10 = (bf16[2304,256]{1,0:T(8,128)(2,1)S(1)}, bf16[2304,256]{1,0:T(8,128)(2,1)}, u32[]{:S(2)}) copy-start(bf16[2304,256]{1,0:T(8,128)(2,1)} %copy-done.9) | copy-start | bytes 3538948
  65.0 23.2 %collective-permute-start.5 = (bf16[2,144,512]{2,1,0:T(8,128)(2,1)}, bf16[2,144,512]{2,1,0:T(8,128)(2,1)}, u32[]{:S(2)}, u32[]{:S(2)}) collective-permute-start(bf16[2,144,512]{2,1,0:T(8,128)(2,1)} %get-tuple-element.51), channel_id=1, source_target_pairs={{0,16},{1,17},{2,18},{3,19},{4,20},{5,21},{6,22},{7,23},{8,24},{9,... | collective-permute-start | bytes 884744 | tf_op jit(solution)/shard_map/ppermute | solution.py:43
  66.2 22.7 %collective-permute-start.6 = (bf16[2,144,512]{2,1,0:T(8,128)(2,1)}, bf16[2,144,512]{2,1,0:T(8,128)(2,1)}, u32[]{:S(2)}, u32[]{:S(2)}) collective-permute-start(bf16[2,144,512]{2,1,0:T(8,128)(2,1)} %get-tuple-element.50), channel_id=1, source_target_pairs={{0,48},{1,49},{2,50},{3,51},{4,52},{5,53},{6,54},{7,55},{8,56},{9,... | collective-permute-start | bytes 884744 | tf_op jit(solution)/shard_map/ppermute | solution.py:43
  69.9 19.0 %collective-permute-start.7 = (bf16[2,144,512]{2,1,0:T(8,128)(2,1)}, bf16[2,144,512]{2,1,0:T(8,128)(2,1)}, u32[]{:S(2)}, u32[]{:S(2)}) collective-permute-start(bf16[2,144,512]{2,1,0:T(8,128)(2,1)} %get-tuple-element.49), channel_id=1, source_target_pairs={{0,32},{1,33},{2,34},{3,35},{4,36},{5,37},{6,38},{7,39},{8,40},{9,... | collective-permute-start | bytes 884744 | tf_op jit(solution)/shard_map/ppermute | solution.py:43
  71.4 2.2 %copy-start.13 = (bf16[1,1152,512]{2,1,0:T(8,128)(2,1)S(1)}, bf16[1,1152,512]{2,1,0:T(8,128)(2,1)}, u32[]{:S(2)}) copy-start(bf16[1,1152,512]{2,1,0:T(8,128)(2,1)} %get-tuple-element.44) | copy-start | bytes 3538948
  73.7 27.4 %collective-permute-start.13 = (bf16[4,72,512]{2,1,0:T(8,128)(2,1)S(1)}, bf16[4,72,512]{2,1,0:T(8,128)(2,1)S(1)}, u32[]{:S(2)}, u32[]{:S(2)}) collective-permute-start(bf16[4,72,512]{2,1,0:T(8,128)(2,1)S(1)} %get-tuple-element.47), channel_id=1, source_target_pairs={{0,4},{1,5},{2,6},{3,7},{4,0},{5,1},{6,2},{7,3},{8,12},{9,13},{10,... | collective-permute-start | bytes 884744 | tf_op jit(solution)/shard_map/ppermute | solution.py:43
  76.7 25.2 %collective-permute-start.12 = (bf16[4,72,512]{2,1,0:T(8,128)(2,1)S(1)}, bf16[4,72,512]{2,1,0:T(8,128)(2,1)S(1)}, u32[]{:S(2)}, u32[]{:S(2)}) collective-permute-start(bf16[4,72,512]{2,1,0:T(8,128)(2,1)S(1)} %get-tuple-element.48), channel_id=1, source_target_pairs={{0,6},{1,7},{2,4},{3,5},{4,2},{5,3},{6,0},{7,1},{8,14},{9,15},{10,... | collective-permute-start | bytes 884744 | tf_op jit(solution)/shard_map/ppermute | solution.py:43
  88.2 13.7 %collective-permute-start.11 = (bf16[4,72,512]{2,1,0:T(8,128)(2,1)S(1)}, bf16[4,72,512]{2,1,0:T(8,128)(2,1)S(1)}, u32[]{:S(2)}, u32[]{:S(2)}) collective-permute-start(bf16[4,72,512]{2,1,0:T(8,128)(2,1)S(1)} %get-tuple-element.46), channel_id=1, source_target_pairs={{0,2},{1,3},{2,0},{3,1},{4,6},{5,7},{6,4},{7,5},{8,10},{9,11},{10,... | collective-permute-start | bytes 884744 | tf_op jit(solution)/shard_map/ppermute | solution.py:43
  90.2 16.8 %collective-permute-start.10 = (bf16[72,512]{1,0:T(8,128)(2,1)S(1)}, bf16[72,512]{1,0:T(8,128)(2,1)S(1)}, u32[]{:S(2)}, u32[]{:S(2)}) collective-permute-start(bf16[72,512]{1,0:T(8,128)(2,1)S(1)} %get-tuple-element.56), channel_id=1, source_target_pairs={{0,4},{1,5},{2,6},{3,7},{4,0},{5,1},{6,2},{7,3},{8,12},{9,13},{10,... | collective-permute-start | bytes 221192 | tf_op jit(solution)/shard_map/ppermute | solution.py:43
  94.6 12.5 %collective-permute-start.9 = (bf16[72,512]{1,0:T(8,128)(2,1)S(1)}, bf16[72,512]{1,0:T(8,128)(2,1)S(1)}, u32[]{:S(2)}, u32[]{:S(2)}) collective-permute-start(bf16[72,512]{1,0:T(8,128)(2,1)S(1)} %get-tuple-element.57), channel_id=1, source_target_pairs={{0,6},{1,7},{2,4},{3,5},{4,2},{5,3},{6,0},{7,1},{8,14},{9,15},{10,... | collective-permute-start | bytes 221192 | tf_op jit(solution)/shard_map/ppermute | solution.py:43
  101.1 5.9 %collective-permute-start.8 = (bf16[72,512]{1,0:T(8,128)(2,1)S(1)}, bf16[72,512]{1,0:T(8,128)(2,1)S(1)}, u32[]{:S(2)}, u32[]{:S(2)}) collective-permute-start(bf16[72,512]{1,0:T(8,128)(2,1)S(1)} %get-tuple-element.55), channel_id=1, source_target_pairs={{0,2},{1,3},{2,0},{3,1},{4,6},{5,7},{6,4},{7,5},{8,10},{9,11},{10,... | collective-permute-start | bytes 221192 | tf_op jit(solution)/shard_map/ppermute | solution.py:43
  102.1 6.3 %collective-permute-start.16 = (bf16[72,512]{1,0:T(8,128)(2,1)S(1)}, bf16[72,512]{1,0:T(8,128)(2,1)S(1)}, u32[]{:S(2)}, u32[]{:S(2)}) collective-permute-start(bf16[72,512]{1,0:T(8,128)(2,1)S(1)} %get-tuple-element.53), channel_id=1, source_target_pairs={{0,32},{1,33},{2,34},{3,35},{4,36},{5,37},{6,38},{7,39},{8,40},{9,... | collective-permute-start | bytes 221192 | tf_op jit(solution)/shard_map/ppermute | solution.py:43
  105.9 5.6 %collective-permute-start.15 = (bf16[72,512]{1,0:T(8,128)(2,1)S(1)}, bf16[72,512]{1,0:T(8,128)(2,1)S(1)}, u32[]{:S(2)}, u32[]{:S(2)}) collective-permute-start(bf16[72,512]{1,0:T(8,128)(2,1)S(1)} %get-tuple-element.54), channel_id=1, source_target_pairs={{0,48},{1,49},{2,50},{3,51},{4,52},{5,53},{6,54},{7,55},{8,56},{9,... | collective-permute-start | bytes 221192 | tf_op jit(solution)/shard_map/ppermute | solution.py:43
  107.0 4.4 %collective-permute-start.14 = (bf16[72,512]{1,0:T(8,128)(2,1)S(1)}, bf16[72,512]{1,0:T(8,128)(2,1)S(1)}, u32[]{:S(2)}, u32[]{:S(2)}) collective-permute-start(bf16[72,512]{1,0:T(8,128)(2,1)S(1)} %get-tuple-element.52), channel_id=1, source_target_pairs={{0,16},{1,17},{2,18},{3,19},{4,20},{5,21},{6,22},{7,23},{8,24},{9,... | collective-permute-start | bytes 221192 | tf_op jit(solution)/shard_map/ppermute | solution.py:43
  111.6 5.2 %collective-permute-start.19 = (bf16[2,18,512]{2,1,0:T(8,128)(2,1)S(1)}, bf16[2,18,512]{2,1,0:T(8,128)(2,1)S(1)}, u32[]{:S(2)}, u32[]{:S(2)}) collective-permute-start(bf16[2,18,512]{2,1,0:T(8,128)(2,1)S(1)} %get-tuple-element.59), channel_id=1, source_target_pairs={{0,128},{1,129},{2,130},{3,131},{4,132},{5,133},{6,134},{7,135},{8... | collective-permute-start | bytes 110600 | tf_op jit(solution)/shard_map/ppermute | solution.py:43
  111.7 5.1 %collective-permute-start.18 = (bf16[2,18,512]{2,1,0:T(8,128)(2,1)S(1)}, bf16[2,18,512]{2,1,0:T(8,128)(2,1)S(1)}, u32[]{:S(2)}, u32[]{:S(2)}) collective-permute-start(bf16[2,18,512]{2,1,0:T(8,128)(2,1)S(1)} %get-tuple-element.60), channel_id=1, source_target_pairs={{0,192},{1,193},{2,194},{3,195},{4,196},{5,197},{6,198},{7,199},{8... | collective-permute-start | bytes 110600 | tf_op jit(solution)/shard_map/ppermute | solution.py:43
  113.3 5.4 %collective-permute-start.17 = (bf16[2,18,512]{2,1,0:T(8,128)(2,1)S(1)}, bf16[2,18,512]{2,1,0:T(8,128)(2,1)S(1)}, u32[]{:S(2)}, u32[]{:S(2)}) collective-permute-start(bf16[2,18,512]{2,1,0:T(8,128)(2,1)S(1)} %get-tuple-element.58), channel_id=1, source_target_pairs={{0,64},{1,65},{2,66},{3,67},{4,68},{5,69},{6,70},{7,71},{8,72},{9,... | collective-permute-start | bytes 110600 | tf_op jit(solution)/shard_map/ppermute | solution.py:43
  118.8 8.2 %collective-permute-start.20 = (bf16[2,9,512]{2,1,0:T(8,128)(2,1)S(1)}, bf16[2,9,512]{2,1,0:T(8,128)(2,1)S(1)}, u32[]{:S(2)}, u32[]{:S(2)}) collective-permute-start(bf16[2,9,512]{2,1,0:T(8,128)(2,1)S(1)} %bitcast.75), channel_id=1, source_target_pairs={{0,0},{1,128},{2,8},{3,136},{4,64},{5,192},{6,72},{7,200},{8,1},{9... | collective-permute-start | bytes 55304 | tf_op jit(solution)/shard_map/ppermute | solution.py:83
  122.3 9.4 %collective-permute-start.21 = (bf16[2,9,512]{2,1,0:T(8,128)(2,1)S(1)}, bf16[2,9,512]{2,1,0:T(8,128)(2,1)S(1)}, u32[]{:S(2)}, u32[]{:S(2)}) collective-permute-start(bf16[2,9,512]{2,1,0:T(8,128)(2,1)S(1)} %bitcast.76), channel_id=1, source_target_pairs={{0,1},{1,129},{2,9},{3,137},{4,65},{5,193},{6,73},{7,201},{8,0},{9... | collective-permute-start | bytes 55304 | tf_op jit(solution)/shard_map/ppermute | solution.py:83
  (4 other events, 5.7 us)
